TPU v7x, 256 devices: a whole 4x4x8 slice. The times are simulated.
256 devices in a mesh: batch: 32 (over x, z), feat: 8 (over y, core).
Axes of the slice: x: 4, y: 4, z: 8, core: 2. Of those that a mesh axis runs over, the one named last changes fastest.
Arguments:
- queries: bfloat16 [4096, 4096], P('batch', 'feat'), may hold values from -8 to 8
- passages: bfloat16 [4096, 4096], P('batch', 'feat'), may hold values from -8 to 8
- positives: int32 [4096], P('batch'), may hold values from 0 to 4095, each once
- level_weight: float32 [7], replicated, may hold values from 0.5 to 2
Outputs:
- loss: float32 [], replicated
- grad_queries: bfloat16 [4096, 4096], P('batch', 'feat')
- grad_passages: bfloat16 [4096, 4096], P('batch', 'feat')
Inputs may be any that keep to these rules, and one draw needn't show every extreme that they name: `positives`: each passage is the positive of exactly one query.
All inputs are finite; a program needn't handle non-finite values.
Results may differ from a plain program's by a relative error of at most 0.022.
Values may be sent and summed in bfloat16 or wider, within the bound.
No kernel may reach another device: no remote copies, remote signals or barrier semaphores. Data moves between devices by JAX's collectives and lax.ppermute only.
A program may use at most 128 MiB of HBM per device.

v0:
```python
import jax
import jax.numpy as jnp
from jax import lax
from jax.sharding import PartitionSpec as P

SMALLEST = 64
LEVELS = 7


SHARPNESS = 3.0


def prefix_2(part, axis, combine, identity):
    place = lax.axis_index(axis)
    gathered = lax.all_gather(part, axis)
    state = jnp.zeros_like(part) + jnp.asarray(identity, part.dtype)

    def one(hop, state):
        return combine(state, lax.dynamic_index_in_dim(gathered, hop, 0, False))

    return lax.fori_loop(0, place, one, state)


def for_sending(value):
    return jax.tree.map(lambda a: a.astype(jnp.bfloat16) if a.dtype == jnp.float32 else a, value)


def add_terms(earlier, later):
    return earlier + later


def slot_layout(shard_width):
    slot_count = shard_width.bit_length() - SMALLEST.bit_length() + 1
    slot_ends = [SMALLEST * 2**slot_id for slot_id in range(slot_count)]
    slot_starts = [0] + slot_ends[:-1]
    return (slot_starts, slot_ends)


def per_device(queries, passages, positives, level_weight):
    row_count, shard_width = queries.shape
    slot_starts, slot_ends = slot_layout(shard_width)
    contract = (((1,), (1,)), ((), ()))
    contract_rows = (((0,), (0,)), ((), ()))
    gathered = lax.all_gather(passages, "batch", axis=0, tiled=True)
    pair_total = gathered.shape[0]
    running = jnp.zeros((row_count, pair_total), jnp.float32)
    partials = []
    for seg_begin, seg_end in zip(slot_starts, slot_ends):
        running = running + lax.dot_general(
            queries[:, seg_begin:seg_end],
            gathered[:, seg_begin:seg_end],
            contract,
            preferred_element_type=jnp.float32,
        )
        partials.append(running)
    prefix = prefix_2(running, "feat", add_terms, jnp.zeros_like(running))
    feat_index = lax.axis_index("feat")
    offset = feat_index * shard_width
    widths = SMALLEST * 2 ** jnp.arange(LEVELS, dtype=jnp.int32)
    columns = jnp.arange(pair_total, dtype=jnp.int32)
    onehot = (columns[None, :] == positives[:, None]).astype(jnp.float32)
    loss_local = jnp.zeros((), jnp.float32)
    slot_grads = []
    for seg_end, partial_sum in zip(slot_ends, partials):
        global_end = offset + seg_end
        weight = jnp.sum(jnp.where(widths == global_end, level_weight, 0.0))
        factor = SHARPNESS / jnp.sqrt(global_end.astype(jnp.float32))
        scores = (prefix + partial_sum) * factor
        row_max = jnp.max(scores, axis=1, keepdims=True)
        log_total = row_max + jnp.log(jnp.sum(jnp.exp(scores - row_max), axis=1, keepdims=True))
        picked = jnp.sum(scores * onehot, axis=1, keepdims=True)
        loss_local = loss_local + weight * jnp.sum(log_total - picked)
        slot_grads.append(weight * factor * (jnp.exp(scores - log_total) - onehot))
    grand = slot_grads[0]
    for extra in slot_grads[1:]:
        grand = grand + extra
    piece = lax.all_gather(for_sending(grand[None]), "feat", axis=0, tiled=True)
    sources = jnp.arange(piece.shape[0], dtype=jnp.int32)
    keep = (sources > feat_index).astype(jnp.float32)
    incoming = jnp.zeros_like(grand) + jnp.sum(piece * keep[:, None, None], axis=0)
    tail_sums = [None] * len(slot_grads)
    accumulated = incoming
    for slot_id in reversed(range(len(slot_grads))):
        accumulated = accumulated + slot_grads[slot_id]
        tail_sums[slot_id] = accumulated.astype(jnp.bfloat16)
    query_parts = []
    for slot_id, (seg_begin, seg_end) in enumerate(zip(slot_starts, slot_ends)):
        query_parts.append(
            jnp.dot(
                tail_sums[slot_id],
                gathered[:, seg_begin:seg_end],
                preferred_element_type=jnp.float32,
            )
        )
    grad_queries = jnp.concatenate(query_parts, axis=1).astype(jnp.bfloat16)
    pieces = []
    for slot_id, (seg_begin, seg_end) in enumerate(zip(slot_starts, slot_ends)):
        selected = tail_sums[slot_id]
        pieces.append(
            lax.dot_general(
                selected,
                queries[:, seg_begin:seg_end],
                contract_rows,
                preferred_element_type=jnp.float32,
            )
        )
    grad_sum = lax.psum_scatter(
        jnp.concatenate(pieces, axis=1).astype(jnp.bfloat16),
        "batch",
        scatter_dimension=0,
        tiled=True,
    )
    loss = lax.psum(loss_local, ("batch", "feat")) / pair_total
    return (loss, grad_queries, grad_sum)


def solution(mesh):
    in_specs = (P("batch", "feat"), P("batch", "feat"), P("batch"), P())
    out_specs = (P(), P("batch", "feat"), P("batch", "feat"))
    return jax.shard_map(
        per_device, mesh=mesh, in_specs=in_specs, out_specs=out_specs, check_vma=False
    )
```

profile of v0, /device:TPU:1, one launch (start us, length us, event | category | flops | bytes accessed | tf_op | source)
XLA Modules:
  0.0 512.3 jit_solution(11529864320501316830)
XLA Ops:
  8.0 85.6 %all-gather.6.cloned.1.call-done = bf16[4096,512]{1,0:T(8,128)(2,1)} async-done(((bf16[128,512]{1,0:T(8,128)(2,1)}), bf16[4096,512]{1,0:T(8,128)(2,1)}) %all-gather.6.cloned.1.call-update) | async-done | bytes 4194320 | tf_op jit(solution)/shard_map/all_gather | solution.py:44
  93.5 1.7 fusion.19
  95.2 2.6 convolution_add_fusion.2
  99.0 0.8 copy-done.10
  99.8 1.4 copy-done.8
  101.2 2.1 convolution_add_fusion
  107.3 84.1 %all-gather.8.cloned.1.call-done = f32[1024,4096]{1,0:T(8,128)} async-done(((f32[128,4096]{1,0:T(8,128)}), f32[1024,4096]{1,0:T(8,128)}) %all-gather.8.cloned.1.call-update) | async-done | bytes 16777232 | tf_op jit(solution)/shard_map/all_gather | solution.py:15
  191.6 2.1 while.10
  191.6 2.1 bitcast_add_fusion.2
  193.8 4.5 fusion.48
  198.3 2.6 select_reduce_fusion
  202.3 2.8 add_convert_fusion.1
  205.2 64.8 %all-gather.10.cloned.1.call-done = bf16[1024,4096]{1,0:T(8,128)(2,1)} async-done(((bf16[128,4096]{1,0:T(8,128)(2,1)}), bf16[1024,4096]{1,0:T(8,128)(2,1)}) %all-gather.10.cloned.1.call-update) | async-done | bytes 8388624 | tf_op jit(solution)/shard_map/all_gather | solution.py:77
  269.9 5.6 %fusion = f32[128,4096]{1,0:T(8,128)S(1)} fusion(bf16[8,128,4096]{2,1,0:T(8,128)(2,1)} %bitcast.16, f32[8]{0:T(128)S(1)} %compare_convert_fusion), kind=kLoop, calls=%fused_computation.2 | loop fusion | flops 12058624 | bytes 10485792 | tf_op jit(solution)/shard_map/reduce_sum | solution.py:80
  275.8 2.3 add_convert_fusion
  278.1 0.8 convolution_convert_fusion
  280.1 2.1 pad_maximum_fusion
  282.2 6.5 %copy.15 = bf16[4096,512]{1,0:T(8,128)(2,1)} copy(bf16[4096,512]{0,1:T(8,128)(2,1)} %pad_maximum_fusion) | data formatting | bytes 8388608
  293.8 77.0 %psum.7 = f32[]{:T(128)} all-reduce(f32[]{:T(128)S(6)} %add.134), channel_id=1, replica_groups=mesh['batch'=32,'feat'=8] {'batch','feat'}, use_global_device_ids=true, to_apply=%region_22.23 | all-reduce | flops 1 | bytes 8 | tf_op jit(solution)/shard_map/psum | solution.py:113
  371.5 1.7 convolution_convert_fusion.4
  373.4 1.9 convolution_convert_fusion.6
  375.4 2.3 convolution_convert_fusion.5
  377.8 2.0 fusion.11
  380.6 124.0 %reduce-scatter.4.cloned.1.call-done = bf16[128,512]{1,0:T(8,128)(2,1)} async-done(((bf16[4096,512]{1,0:T(8,128)(2,1)}), bf16[128,512]{1,0:T(8,128)(2,1)}) %reduce-scatter.4.cloned.1.call-update) | async-done | bytes 131088
  (53 shorter events, 7.3 us)
Async XLA Ops:
  7.2 88.1 %copy-start.14 = (bf16[128,512]{1,0:T(8,128)(2,1)S(1)}, bf16[128,512]{1,0:T(8,128)(2,1)}, u32[]{:S(2)}) copy-start(bf16[128,512]{1,0:T(8,128)(2,1)} %param.6) | copy-start | bytes 393220
  7.2 86.4 %all-gather.6.cloned.1.call-start = ((), (), s32[]{:S(2)}) async-start(), calls=%async_computation.1 | async-start | bytes 4325376 | tf_op jit(solution)/shard_map/all_gather | solution.py:44
  7.9 183.5 %all-gather.8.cloned.1.call-start = ((), (), s32[]{:S(2)}) async-start(), calls=%async_computation.2 | async-start | bytes 18874368 | tf_op jit(solution)/shard_map/all_gather | solution.py:15
  95.2 2.6 copy-start.9
  95.2 3.3 copy-start.11
  98.5 1.3 copy-start.10
  99.8 1.4 copy-start.8
  103.3 0.7 copy-start.16
  103.4 166.6 %all-gather.10.cloned.1.call-start = ((), (), s32[]{:S(2)}) async-start(), calls=%async_computation.3 | async-start | bytes 9437184 | tf_op jit(solution)/shard_map/all_gather | solution.py:77
  193.8 4.5 copy-start.15
  198.2 4.0 copy-start
  198.3 4.0 copy-start.2
  198.3 4.0 copy-start.4
  198.3 4.0 copy-start.6
  205.1 299.5 %reduce-scatter.4.cloned.1.call-start = ((), (), s32[]{:S(2)}) async-start(), calls=%async_computation.4 | async-start | bytes 4325376
  269.9 5.6 %copy-start.1 = (f32[128,4096]{1,0:T(8,128)S(1)}, f32[128,4096]{1,0:T(8,128)}, u32[]{:S(2)}) copy-start(f32[128,4096]{1,0:T(8,128)} %copy-done) | copy-start | bytes 6291460
  269.9 5.6 %copy-start.3 = (f32[128,4096]{1,0:T(8,128)S(1)}, f32[128,4096]{1,0:T(8,128)}, u32[]{:S(2)}) copy-start(f32[128,4096]{1,0:T(8,128)} %copy-done.2) | copy-start | bytes 6291460
  269.9 5.7 %copy-start.5 = (f32[128,4096]{1,0:T(8,128)S(1)}, f32[128,4096]{1,0:T(8,128)}, u32[]{:S(2)}) copy-start(f32[128,4096]{1,0:T(8,128)} %copy-done.4) | copy-start | bytes 6291460
  269.9 5.8 %copy-start.7 = (f32[128,4096]{1,0:T(8,128)S(1)}, f32[128,4096]{1,0:T(8,128)}, u32[]{:S(2)}) copy-start(f32[128,4096]{1,0:T(8,128)} %copy-done.6) | copy-start | bytes 6291460
  278.1 1.2 copy-start.12
  373.4 4.4 copy-start.13
Sparse Core Ops, SparseCore 0:
  10.6 82.8 all-gather.5
  103.5 87.8 all-gather.7
  205.2 64.6 all-gather.9
  288.9 215.7 reduce-scatter.3
where the time goes:
time: 517 us; the launch traced here: 512 us
  waiting for transfers between devices  359 us (69%)
  blocking collectives  77 us (15%)
  other arithmetic  24.9 us (5%)
  between operations  23.7 us (5%)
  matrix products  16.7 us (3%)
  local copies, waits for them, and re-layouts  10.6 us (2%)
    unnamed x5, waiting for transfers between devices  125 us
    all_gather x1, waiting for transfers between devices, per_device(): gathered = lax.all_gather(passages, 'batch', axis=0, tiled=True)  85.6 us
    all_gather x1, waiting for transfers between devices, prefix_2(): gathered = lax.all_gather(part, axis)  84.1 us
    psum x1, blocking collectives, per_device(): loss = lax.psum(loss_local, ('batch', 'feat')) / pair_total  77 us
    all_gather x1, waiting for transfers between devices, per_device(): piece = lax.all_gather(for_sending(grand[None]), 'feat', axis=0, tiled=True)  64.8 us
  transfers between devices with their start and end apart: 4, of which 4 were waited for; matrix products, arithmetic and copies ran while one was open for 2% of the time, Pallas kernels for 0%

commit v1 on v0

v1 whole, which is shorter than its diff:
```python
import math

import jax
import jax.numpy as jnp
from jax import lax
from jax.experimental import pallas as pl
from jax.experimental.pallas import tpu as pltpu
from jax.sharding import PartitionSpec as P

SMALLEST = 64
LEVELS = 7
LOW = 5
SHARPNESS = 3.0
WIDTHS = [SMALLEST * 2**k for k in range(LEVELS)]
FACTORS = [SHARPNESS / math.sqrt(w) for w in WIDTHS]
SPANS = list(zip([0] + WIDTHS[: LOW - 1], WIDTHS[:LOW]))
EXTRA = 16
PAIR = 2 * SMALLEST

BATCH = 32
FEAT = 8
BOTH = ("batch", "feat")
XZH_GROUPS = [[x * 8 + zl * 2 + zh for x in range(4) for zh in range(2)] for zl in range(4)]
Y_GROUPS = [[y * 2 + c for y in range(4)] for c in range(2)]
X, Y, ZL, ZH, CORE = range(5)

f32 = jnp.float32
bf16 = jnp.bfloat16


def shift_x(a, s):
    return lax.ppermute(a, "batch", [(b, (b + 8 * s) % BATCH) for b in range(BATCH)])


def shift_zl(a, s):
    return lax.ppermute(
        a, "batch", [(b, b // 8 * 8 + (b + 2 * s) % 8) for b in range(BATCH)]
    )


def shift_y(a, s):
    return lax.ppermute(a, "feat", [(f, (f + 2 * s) % FEAT) for f in range(FEAT)])


def swap_core(a):
    return lax.ppermute(a, "feat", [(f, f ^ 1) for f in range(FEAT)])


def move_zh(a, first):
    pairs = []
    for b in range(BATCH):
        for f in range(FEAT):
            if (b % 2 == f % 2) == first:
                pairs.append((b * FEAT + f, (b ^ 1) * FEAT + f))
    return lax.ppermute(a, BOTH, pairs)


def dot(a, b, ca, cb):
    return lax.dot_general(
        a, b, (((ca,), (cb,)), ((), ())), preferred_element_type=f32
    )


def shape(*dims_dtype):
    return jax.ShapeDtypeStruct(dims_dtype[:-1], dims_dtype[-1])


def call(body, smem, args, outs, scratch=(), flops=0):
    vmem = pl.BlockSpec(memory_space=pltpu.VMEM)
    scalar = pl.BlockSpec(memory_space=pltpu.SMEM)
    moved = sum(a.size * a.dtype.itemsize for a in (*args, *outs))
    return pl.pallas_call(
        body,
        out_shape=outs,
        in_specs=[scalar] * len(smem) + [vmem] * len(args),
        out_specs=[vmem] * len(outs),
        scratch_shapes=list(scratch),
        cost_estimate=pl.CostEstimate(
            flops=flops, bytes_accessed=moved, transcendentals=0
        ),
        compiler_params=pltpu.CompilerParams(vmem_limit_bytes=40 << 20),
    )(*smem, *args)


def find_positives(ids, pos, n):
    rows = lax.broadcasted_iota(jnp.int32, (4 * n, n), 0)
    bits = n.bit_length() - 1
    block = ids[X] * 8 + ids[ZH] + 2 * ((ids[ZL] + 4 - (rows >> bits)) & 3)
    return (block << bits) + (rows & (n - 1)) == pos


def score_kernel(ids, p_own, p_other, q0, q1, q2, q3, partial, p, q_all, pos):
    n = q_all.shape[1]
    width = p_own.shape[1]

    @pl.when(ids[CORE] == 0)
    def _():
        p[:, :width] = p_own[...]
        p[:, width:] = p_other[...]

    @pl.when(ids[CORE] != 0)
    def _():
        p[:, :width] = p_other[...]
        p[:, width:] = p_own[...]

    for s, q in enumerate((q0, q1, q2, q3)):
        j = (ids[X] + 4 - s) & 3
        q_all[j] = q[:n]
        digits = q[n:, :n].astype(f32)
        pos[j] = (digits[0:1] * 64.0 + digits[1:2]).astype(jnp.int32)
        partial[j] = dot(p[...], q[:n], 1, 1)


def low_kernel(ids, p, q_all, pos, e_low, stats):
    n = q_all.shape[1]
    first = lax.broadcasted_iota(jnp.int32, (n, PAIR), 1) < SMALLEST
    for j in range(4):
        hot = find_positives(ids, pos[j], n)
        tops, sums, picks = [], [], []
        running = None
        for k, (begin, end) in enumerate(SPANS):
            if k == 0:
                q_part = q_all[j, :, :PAIR]
                q_part = jnp.where(first, q_part, jnp.zeros_like(q_part))
                running = dot(p[:, :PAIR], q_part, 1, 1)
            elif k == 1:
                running = dot(p[:, :PAIR], q_all[j, :, :PAIR], 1, 1)
            else:
                running = running + dot(p[:, begin:end], q_all[j, :, begin:end], 1, 1)
            scores = running * FACTORS[k]
            top = jnp.max(scores, axis=0, keepdims=True)
            e = jnp.exp(scores - top)
            e_low[k, j] = e
            tops.append(top)
            sums.append(jnp.sum(e, axis=0, keepdims=True))
            picks.append(jnp.sum(jnp.where(hot, scores, 0.0), axis=0, keepdims=True))
        stats[j] = jnp.concatenate(tops + sums + picks + [tops[0]], axis=0)


def owner_kernel(ids, pieces, pos, low_stats, e_high, message):
    n = pos.shape[2]
    hot = find_positives(ids, pos[ids[Y]], n)
    sum5 = pieces[0] + pieces[1]
    sum6 = sum5 + (pieces[2] + pieces[3])
    rows = []
    for i, total in enumerate((sum5, sum6)):
        scores = total * FACTORS[LOW + i]
        top = jnp.max(scores, axis=0, keepdims=True)
        e = jnp.exp(scores - top)
        e_high[i] = e
        rows += [
            top,
            jnp.sum(e, axis=0, keepdims=True),
            jnp.sum(jnp.where(hot, scores, 0.0), axis=0, keepdims=True),
        ]
    high = jnp.concatenate(rows + rows[:2], axis=0)
    for i in range(8):
        for j in range(4):
            message[i, 16 * j : 16 * j + 16] = low_stats[j]
        message[i, 64:72] = high


def put_terms(ref, row, v):
    hi = v.astype(bf16).astype(f32)
    mid = (v - hi).astype(bf16).astype(f32)
    lo = v - hi - mid
    zero = jnp.zeros((EXTRA - 3, v.shape[1]), f32)
    ref[row:, : v.shape[1]] = jnp.concatenate([hi, mid, lo, zero], axis=0).astype(bf16)


def tail_kernel(ids, weight, stats, local, e_high, pos, m0, m1, m2, m3, rates):
    n = pos.shape[2]

    def merged(top, total, picked):
        best = jnp.max(top, axis=0)
        mass = jnp.sum(total * jnp.exp(top - best[None]), axis=0)
        return best + jnp.log(mass), jnp.sum(picked, axis=0)

    on = ids[Y] == 0
    low_loss = jnp.zeros((1, n), f32)
    for j in range(4):
        at = 16 * j
        lse, picked = merged(
            stats[:, at : at + 5], stats[:, at + 5 : at + 10], stats[:, at + 10 : at + 15]
        )
        rows = []
        for k in range(LOW):
            low_loss += weight[k] * (lse[k : k + 1] - picked[k : k + 1])
            scale = jnp.where(on, weight[k] * FACTORS[k], 0.0)
            rows.append(scale * jnp.exp(local[at + k : at + k + 1] - lse[k : k + 1]))
        rates[j] = jnp.concatenate(rows + rows[:3], axis=0)

    hot = find_positives(ids, pos[ids[Y]], n)
    loss = jnp.where(on, low_loss, 0.0)
    tail = None
    tails = []
    for i in (1, 0):
        at = 64 + 3 * i
        lse, picked = merged(
            stats[:, at : at + 1], stats[:, at + 1 : at + 2], stats[:, at + 2 : at + 3]
        )
        loss += weight[LOW + i] * (lse - picked)
        scale = weight[LOW + i] * FACTORS[LOW + i]
        rate = scale * jnp.exp(local[at : at + 1] - lse)
        g = e_high[i] * rate - jnp.where(hot, scale, 0.0)
        tail = g if tail is None else tail + g
        tails.append(tail.astype(bf16))
    lane = lax.broadcasted_iota(jnp.int32, (1, n), 1)
    mine = ids[ZL] * FEAT + ids[Y] * 2 + ids[CORE]
    loss = jnp.where(lane == mine, jnp.sum(loss, axis=1, keepdims=True), 0.0)
    for t, m in enumerate((m0, m1, m2, m3)):
        narrow = ((ids[Y] + t) & 3) <= 1

        @pl.when(narrow)
        def _():
            m[: 4 * n] = tails[1]

        @pl.when(jnp.logical_not(narrow))
        def _():
            m[: 4 * n] = tails[0]

        put_terms(m, 4 * n, loss)


def get_terms(ref, row, lanes):
    v = ref[row:, :lanes].astype(f32)
    return v[0:1] + v[1:2] + v[2:3]


def grad_kernel(
    ids, weight, t0, t1, t2, t3, e_low, rates, pos, p, q_all,
    gq0, gq1, gq2, gq3, gp_own, gp_message, tails, gq,
):
    n = pos.shape[2]
    width = gp_own.shape[1]
    on = ids[Y] == 0
    loss = jnp.zeros((1, n), f32)
    for t, ref in enumerate((t0, t1, t2, t3)):
        j = (ids[Y] + 4 - t) & 3
        lanes = pl.ds(pl.multiple_of(j * n, n), n)
        loss += get_terms(ref, 4 * n, n)
        hot = find_positives(ids, pos[j], n)
        acc = ref[: 4 * n].astype(f32)
        for k in reversed(range(LOW)):
            scale = jnp.where(on, weight[k] * FACTORS[k], 0.0)
            acc = acc + (e_low[k, j] * rates[j, k : k + 1] - jnp.where(hot, scale, 0.0))
            tails[k, :, lanes] = acc.astype(bf16)

    q = q_all[...].reshape(4 * n, 2 * width)
    first = lax.broadcasted_iota(jnp.int32, (4 * n, PAIR), 1) < SMALLEST

    def by_span(fn):
        yield 0, PAIR, jnp.where(first, fn(0, 0, PAIR), fn(1, 0, PAIR))
        for k in range(2, LOW):
            begin, end = SPANS[k]
            yield begin, end, fn(k, begin, end)

    for begin, end, v in by_span(lambda k, a, b: dot(tails[k], q[:, a:b], 1, 0)):
        mine = (begin < width) == (ids[CORE] == 0)
        at = begin % width

        @pl.when(mine)
        def _():
            gp_own[:, at : at + end - begin] = v

        @pl.when(jnp.logical_not(mine))
        def _():
            gp_message[: 4 * n, at : at + end - begin] = v.astype(bf16)

    gp_message[4 * n :] = jnp.zeros((EXTRA, width), bf16)
    put_terms(gp_message, 4 * n, loss)
    for begin, end, v in by_span(lambda k, a, b: dot(tails[k], p[:, a:b], 0, 0)):
        gq[:, begin:end] = v
    for s, out in enumerate((gq0, gq1, gq2, gq3)):
        j = (ids[X] + 4 - s) & 3
        out[...] = gq[pl.ds(pl.multiple_of(j * n, n), n), :].astype(out.dtype)


def core_sum_kernel(gp_own, own_message, other_message, own, m1, m2, m3, loss):
    n, width = own.shape
    total = get_terms(own_message, 4 * n, n) + get_terms(other_message, 4 * n, n)
    loss[...] = jnp.broadcast_to(total, loss.shape)
    for s, out in enumerate((own, m1, m2, m3)):
        rows = slice(s * n, s * n + n)
        v = gp_own[rows] + other_message[rows].astype(f32)
        out[:n] = v.astype(out.dtype)
        if s:
            out[n:] = jnp.zeros((EXTRA, width), bf16)
            put_terms(out, n, total)


def per_device(queries, passages, positives, level_weight):
    n, width = queries.shape
    wide = 2 * width
    bi = lax.axis_index("batch")
    fi = lax.axis_index("feat")
    core = fi % 2
    same = bi % 2 == core
    ids = jnp.stack([bi // 8, fi // 2, bi % 8 // 2, bi % 2, core]).astype(jnp.int32)

    q_core = swap_core(queries)
    rows = jnp.stack([positives // 64, positives % 64]).astype(bf16)
    q_chip = jnp.concatenate(
        [
            jnp.concatenate(
                [jnp.where(core == 0, queries, q_core), jnp.where(core == 0, q_core, queries)],
                axis=1,
            ),
            jnp.pad(rows, ((0, EXTRA - 2), (0, wide - n))),
        ],
        axis=0,
    )
    q_msg = jnp.where(same, q_chip, move_zh(q_chip, True))
    q_msgs = [q_msg] + [shift_x(q_msg, s) for s in (1, 2, 3)]

    p_half = jnp.concatenate([passages] + [shift_zl(passages, s) for s in (1, 2, 3)], axis=0)
    p_other = swap_core(p_half)

    tile = 4 * n * 4 * n
    partial, p, q, pos = call(
        score_kernel, [ids], [p_half, p_other, *q_msgs],
        [
            shape(4, 4 * n, n, f32),
            shape(4 * n, wide, bf16),
            shape(4, n, wide, bf16),
            shape(4, 1, n, jnp.int32),
        ],
        flops=2 * tile * wide,
    )
    pieces = lax.all_to_all(partial, "feat", 0, 0, axis_index_groups=Y_GROUPS)
    e_low, low_stats = call(
        low_kernel, [ids], [p, q, pos],
        [shape(LOW, 4, 4 * n, n, f32), shape(4, 16, n, f32)],
        flops=2 * tile * wide,
    )
    e_high, message = call(
        owner_kernel, [ids], [pieces, pos, low_stats],
        [shape(2, 4 * n, n, f32), shape(8, 72, n, f32)],
    )
    stats = lax.all_to_all(message, "batch", 0, 0, axis_index_groups=XZH_GROUPS)
    *tails, rates = call(
        tail_kernel, [ids, level_weight], [stats, message[0], e_high, pos],
        [shape(4 * n + EXTRA, n, bf16)] * 4 + [shape(4, 8, n, f32)],
    )
    tails = [tails[0]] + [shift_y(tails[t], t) for t in (1, 2, 3)]
    *gq, gp_own, gp_message = call(
        grad_kernel, [ids, level_weight], [*tails, e_low, rates, pos, p, q],
        [shape(n, wide, f32)]
        + [shape(n, wide, bf16)] * 3
        + [shape(4 * n, width, f32), shape(4 * n + EXTRA, width, bf16)],
        scratch=[pltpu.VMEM((LOW, 4 * n, 4 * n), bf16), pltpu.VMEM((4 * n, wide), f32)],
        flops=4 * tile * wide,
    )

    own, *messages, loss_row = call(
        core_sum_kernel, [], [gp_own, gp_message, swap_core(gp_message)],
        [shape(n, width, f32)] + [shape(n + EXTRA, width, bf16)] * 3 + [shape(8, n, f32)],
    )
    grad_passages = own
    loss_row = loss_row[0]
    for s, message in zip((1, 2, 3), messages):
        other = shift_zl(message, -s).astype(f32)
        grad_passages = grad_passages + other[:n]
        loss_row = loss_row + (other[n, :n] + other[n + 1, :n] + other[n + 2, :n])
    loss = jnp.sum(loss_row) / (n * BATCH)

    gq_sum = gq[0]
    for s in (1, 2, 3):
        gq_sum = gq_sum + shift_x(gq[s], -s).astype(f32)
    gq_sum = gq_sum + move_zh(gq_sum.astype(bf16), False).astype(f32)
    gq_sum = gq_sum.astype(bf16)
    left, right = gq_sum[:, :width], gq_sum[:, width:]
    other = swap_core(jnp.where(core == 0, right, left))
    grad_queries = jnp.where(same, jnp.where(core == 0, left, right), other)
    return loss, grad_queries, grad_passages.astype(bf16)


def solution(mesh):
    in_specs = (P("batch", "feat"), P("batch", "feat"), P("batch"), P())
    out_specs = (P(), P("batch", "feat"), P("batch", "feat"))
    return jax.shard_map(
        per_device, mesh=mesh, in_specs=in_specs, out_specs=out_specs, check_vma=False
    )
```

time: 517 us -> 146 us (0.28)
  waiting for transfers between devices: 359 us -> 67.1 us
  blocking collectives: 77 us -> 0 us
  starting transfers between devices: 0.16 us -> 44.5 us
  between operations: 23.7 us -> 2.64 us
  other arithmetic: 24.9 us -> 4.15 us
  matrix products: 16.7 us -> 0 us
  Pallas kernels: 0 us -> 12.8 us
    all_gather x3 -> x0, waiting for transfers between devices: 234 us -> none  [the longest x1 85.6 us: per_device(): gathered = lax.all_gather(passages, 'batch', axis=0, tiled=True)]
    unnamed x5 -> x0, waiting for transfers between devices: 125 us -> none
    psum x1 -> x0, blocking collectives: 77 us -> none  [per_device(): loss = lax.psum(loss_local, ('batch', 'feat')) / pair_total]
    ppermute x0 -> x21, waiting for transfers between devices: none -> 52.9 us  [the longest x6 25.8 us: shift_x(): lax.ppermute(a, 'batch', [(b, (b + 8 * s) % BATCH) for b in range(BATCH)])]
    ppermute x0 -> x21, starting transfers between devices: none -> 36.9 us  [the longest x6 16.1 us: shift_zl(): lax.ppermute(a, 'batch', [(b, b // 8 * 8 + (b + 2 * s) % 8) for b in rang...]
    dot_general x12 -> x0, matrix products: 16.7 us -> none  [the longest x4 7.92 us: per_device(): jnp.dot(tail_sums[slot_id], gathered[:, seg_begin:seg_end], preferred_ele...]
    all_to_all x0 -> x2, waiting for transfers between devices: none -> 14.2 us  [the longest x1 8.64 us: per_device(): pieces = lax.all_to_all(partial, 'feat', 0, 0, axis_index_groups=Y_GROUPS)]
    pallas_call x0 -> x6, Pallas kernels: none -> 12.8 us  [call(): pl.pallas_call(body, out_shape=outs, in_specs=[scalar] * len(smem) + [vme...]
  transfers between devices with their start and end apart: 4 -> 23, of which waited for: 4 -> 15; matrix products, arithmetic and copies ran while one was open for 2% -> 3% of each run, Pallas kernels for 0% -> 2%
where the time goes in v1:
time: 146 us
  waiting for transfers between devices  67.1 us (46%)
  starting transfers between devices  44.5 us (30%)
  local copies, waits for them, and re-layouts  14.5 us (10%)
  Pallas kernels  12.8 us (9%)
  other arithmetic  4.15 us (3%)
  between operations  2.64 us (2%)
    ppermute x6, waiting for transfers between devices, shift_x(): lax.ppermute(a, 'batch', [(b, (b + 8 * s) % BATCH) for b in range(BATCH)])  25.8 us
    ppermute x6, waiting for transfers between devices, shift_zl(): lax.ppermute(a, 'batch', [(b, b // 8 * 8 + (b + 2 * s) % 8) for b in rang...  18 us
    ppermute x6, starting transfers between devices, shift_zl(): lax.ppermute(a, 'batch', [(b, b // 8 * 8 + (b + 2 * s) % 8) for b in rang...  16.1 us
    unnamed x27, local copies, waits for them, and re-layouts  13.6 us
    pallas_call x6, Pallas kernels, call(): pl.pallas_call(body, out_shape=outs, in_specs=[scalar] * len(smem) + [vme...  12.8 us
    all_to_all x1, waiting for transfers between devices, per_device(): pieces = lax.all_to_all(partial, 'feat', 0, 0, axis_index_groups=Y_GROUPS)  8.64 us
    ppermute x4, starting transfers between devices, swap_core(): return lax.ppermute(a, 'feat', [(f, f ^ 1) for f in range(FEAT)])  8.2 us
    ppermute x6, starting transfers between devices, shift_x(): lax.ppermute(a, 'batch', [(b, (b + 8 * s) % BATCH) for b in range(BATCH)])  5.59 us
  transfers between devices with their start and end apart: 23, of which 15 were waited for; matrix products, arithmetic and copies ran while one was open for 3% of the time, Pallas kernels for 2%

profile of v1, /device:TPU:1, one launch (start us, length us, event | category | flops | bytes accessed | tf_op | source)
XLA Modules:
  0.0 145.7 jit_solution(10207135929653035773)
XLA Ops:
  0.6 7.8 %collective-permute-start.1 = (bf16[128,512]{1,0:T(8,128)(2,1)}, bf16[128,512]{1,0:T(8,128)(2,1)S(1)}, u32[]{:S(2)}, u32[]{:S(2)}) collective-permute-start(bf16[128,512]{1,0:T(8,128)(2,1)} %param.5), channel_id=1, source_target_pairs={{0,32},{8,40},{16,48},{24,56},{32,0},{40,8},{48,16},{56,24},{64,96... | collective-permute-start | bytes 393224 | tf_op jit(solution)/shard_map/ppermute | solution.py:36
  9.6 2.4 %collective-permute-start.2 = (bf16[128,512]{1,0:T(8,128)(2,1)}, bf16[128,512]{1,0:T(8,128)(2,1)S(1)}, u32[]{:S(2)}, u32[]{:S(2)}) collective-permute-start(bf16[128,512]{1,0:T(8,128)(2,1)} %param.5), channel_id=1, source_target_pairs={{0,48},{8,56},{16,0},{24,8},{32,16},{40,24},{48,32},{56,40},{64,11... | collective-permute-start | bytes 393224 | tf_op jit(solution)/shard_map/ppermute | solution.py:36
  17.6 4.0 %collective-permute-done.2 = bf16[128,512]{1,0:T(8,128)(2,1)S(1)} collective-permute-done((bf16[128,512]{1,0:T(8,128)(2,1)}, bf16[128,512]{1,0:T(8,128)(2,1)S(1)}, u32[]{:S(2)}, u32[]{:S(2)}) %collective-permute-start.2) | collective-permute-done | bytes 131104 | tf_op jit(solution)/shard_map/ppermute | solution.py:36
  22.2 2.5 %collective-permute-done.5 = bf16[144,1024]{1,0:T(8,128)(2,1)S(1)} collective-permute-done((bf16[144,1024]{1,0:T(8,128)(2,1)S(1)}, bf16[144,1024]{1,0:T(8,128)(2,1)S(1)}, u32[]{:S(2)}, u32[]{:S(2)}) %collective-permute-start.5) | collective-permute-done | bytes 294944 | tf_op jit(solution)/shard_map/ppermute | solution.py:55
  24.8 2.6 %collective-permute-start.8 = (bf16[144,1024]{1,0:T(8,128)(2,1)S(1)}, bf16[144,1024]{1,0:T(8,128)(2,1)S(1)}, u32[]{:S(2)}, u32[]{:S(2)}) collective-permute-start(bf16[144,1024]{1,0:T(8,128)(2,1)S(1)} %broadcast_select_fusion.q0), channel_id=1, source_target_pairs={{0,192},{8,200},{16,208},{24,216},{32,224},{40,232},{48,240},{56,2... | collective-permute-start | bytes 884744 | tf_op jit(solution)/shard_map/ppermute | solution.py:32
  28.6 11.0 %collective-permute-done.8.q3 = bf16[144,1024]{1,0:T(8,128)(2,1)S(1)} collective-permute-done((bf16[144,1024]{1,0:T(8,128)(2,1)S(1)}, bf16[144,1024]{1,0:T(8,128)(2,1)S(1)}, u32[]{:S(2)}, u32[]{:S(2)}) %collective-permute-start.8) | collective-permute-done | bytes 294944 | tf_op jit(solution)/shard_map/ppermute | solution.py:32
  41.1 2.5 %collective-permute-done.6.q1 = bf16[144,1024]{1,0:T(8,128)(2,1)S(1)} collective-permute-done((bf16[144,1024]{1,0:T(8,128)(2,1)S(1)}, bf16[144,1024]{1,0:T(8,128)(2,1)S(1)}, u32[]{:S(2)}, u32[]{:S(2)}) %collective-permute-start.6) | collective-permute-done | bytes 294944 | tf_op jit(solution)/shard_map/ppermute | solution.py:32
  50.1 4.2 %all-to-all-start = ((f32[4,512,128]{2,1,0:T(8,128)}), f32[4,512,128]{2,1,0:T(8,128)S(1)}, u32[]{:S(2)}, u32[]{:S(2)}) async-start(f32[4,512,128]{2,1,0:T(8,128)} %copy-done.2), calls=%async_computation | async-start | bytes 2097152 | tf_op jit(solution)/shard_map/all_to_all | solution.py:330
  54.3 3.5 %shard_map.68 = (f32[5,4,512,128]{3,2,1,0:T(8,128)S(1)}, f32[4,16,128]{2,1,0:T(8,128)S(1)}) custom-call(s32[5]{0:T(128)S(1)} %stack.35.ids, bf16[512,1024]{1,0:T(8,128)(2,1)S(1)} %get-tuple-element.29.p, bf16[4,128,1024]{2,1,0:T(8,128)(2,1)S(1)} %get-tuple-element.30.q_all, s32[4,1,128]{2,1,0:T(1,128)S(1)} %get-tuple-element.28.pos), custom_call_target="tpu_custom_call" | custom-call | flops 536870912 | bytes 7374848 | tf_op jit(solution)/shard_map/pallas_call | solution.py:72
  57.8 2.3 %copy-done = f32[5,4,512,128]{3,2,1,0:T(8,128)} copy-done((f32[5,4,512,128]{3,2,1,0:T(8,128)}, f32[5,4,512,128]{3,2,1,0:T(8,128)S(1)}, u32[]{:S(2)}) %copy-start) | copy-done | bytes 5242904
  60.1 8.6 %all-to-all-done.pieces = f32[4,512,128]{2,1,0:T(8,128)S(1)} async-done(((f32[4,512,128]{2,1,0:T(8,128)}), f32[4,512,128]{2,1,0:T(8,128)S(1)}, u32[]{:S(2)}, u32[]{:S(2)}) %all-to-all-start) | async-done | bytes 1048608 | tf_op jit(solution)/shard_map/all_to_all | solution.py:330
  71.2 3.4 %all-to-all-start.1 = ((f32[8,72,128]{2,1,0:T(8,128)}), f32[8,72,128]{2,1,0:T(8,128)S(1)}, u32[]{:S(2)}, u32[]{:S(2)}) async-start(f32[8,72,128]{2,1,0:T(8,128)} %get-tuple-element.32), calls=%async_computation.1 | async-start | bytes 589824 | tf_op jit(solution)/shard_map/all_to_all | solution.py:340
  75.4 5.6 %all-to-all-done.1.stats = f32[8,72,128]{2,1,0:T(8,128)S(1)} async-done(((f32[8,72,128]{2,1,0:T(8,128)}), f32[8,72,128]{2,1,0:T(8,128)S(1)}, u32[]{:S(2)}, u32[]{:S(2)}) %all-to-all-start.1) | async-done | bytes 294944 | tf_op jit(solution)/shard_map/all_to_all | solution.py:340
  86.1 3.6 %collective-permute-done.9.t1 = bf16[528,128]{1,0:T(8,128)(2,1)S(1)} collective-permute-done((bf16[528,128]{1,0:T(8,128)(2,1)S(1)}, bf16[528,128]{1,0:T(8,128)(2,1)S(1)}, u32[]{:S(2)}, u32[]{:S(2)}) %collective-permute-start.9) | collective-permute-done | bytes 135200 | tf_op jit(solution)/shard_map/ppermute | solution.py:42
  90.5 2.5 %copy-done.1 = f32[5,4,512,128]{3,2,1,0:T(8,128)S(1)} copy-done((f32[5,4,512,128]{3,2,1,0:T(8,128)S(1)}, f32[5,4,512,128]{3,2,1,0:T(8,128)}, u32[]{:S(2)}) %copy-start.1) | copy-done | bytes 5242904
  93.0 4.6 %shard_map.71 = (f32[128,1024]{1,0:T(8,128)S(1)}, bf16[128,1024]{1,0:T(8,128)(2,1)S(1)}, bf16[128,1024]{1,0:T(8,128)(2,1)S(1)}, bf16[128,1024]{1,0:T(8,128)(2,1)...) custom-call(s32[5]{0:T(128)S(1)} %stack.35.ids, f32[7]{0:T(128)S(1)} %copy-done.11, ...), custom_call_target="tpu_custom_call" | custom-call | flops 1073741824 | bytes 10799104 | tf_op jit(solution)/shard_map/pallas_call | solution.py:72
  99.6 3.4 %collective-permute-done.16 = bf16[128,1024]{1,0:T(8,128)(2,1)S(1)} collective-permute-done((bf16[128,1024]{1,0:T(8,128)(2,1)S(1)}, bf16[128,1024]{1,0:T(8,128)(2,1)S(1)}, u32[]{:S(2)}, u32[]{:S(2)}) %collective-permute-start.16) | collective-permute-done | bytes 262176 | tf_op jit(solution)/shard_map/ppermute | solution.py:32
  103.0 2.4 %collective-permute-done.17 = bf16[128,1024]{1,0:T(8,128)(2,1)S(1)} collective-permute-done((bf16[128,1024]{1,0:T(8,128)(2,1)S(1)}, bf16[128,1024]{1,0:T(8,128)(2,1)S(1)}, u32[]{:S(2)}, u32[]{:S(2)}) %collective-permute-start.17) | collective-permute-done | bytes 262176 | tf_op jit(solution)/shard_map/ppermute | solution.py:32
  105.4 6.5 %collective-permute-done.18 = bf16[128,1024]{1,0:T(8,128)(2,1)S(1)} collective-permute-done((bf16[128,1024]{1,0:T(8,128)(2,1)S(1)}, bf16[128,1024]{1,0:T(8,128)(2,1)S(1)}, u32[]{:S(2)}, u32[]{:S(2)}) %collective-permute-start.18) | collective-permute-done | bytes 262176 | tf_op jit(solution)/shard_map/ppermute | solution.py:32
  112.0 2.7 %collective-permute-start.19 = (bf16[128,1024]{1,0:T(8,128)(2,1)S(1)}, bf16[128,1024]{1,0:T(8,128)(2,1)S(1)}, u32[]{:S(2)}, u32[]{:S(2)}) collective-permute-start(bf16[128,1024]{1,0:T(8,128)(2,1)S(1)} %fusion.6), channel_id=1, source_target_pairs={{1,9},{3,11},{5,13},{7,15},{8,0},{10,2},{12,4},{14,6},{17,25},{19,... | collective-permute-start | bytes 786440 | tf_op jit(solution)/shard_map/ppermute | solution.py:55
  115.9 2.1 %collective-permute-done.19 = bf16[128,1024]{1,0:T(8,128)(2,1)S(1)} collective-permute-done((bf16[128,1024]{1,0:T(8,128)(2,1)S(1)}, bf16[128,1024]{1,0:T(8,128)(2,1)S(1)}, u32[]{:S(2)}, u32[]{:S(2)}) %collective-permute-start.19) | collective-permute-done | bytes 262176 | tf_op jit(solution)/shard_map/ppermute | solution.py:55
  118.2 4.9 %collective-permute-start.20 = (bf16[128,512]{1,0:T(8,128)(2,1)S(1)}, bf16[128,512]{1,0:T(8,128)(2,1)S(1)}, u32[]{:S(2)}, u32[]{:S(2)}) collective-permute-start(bf16[128,512]{1,0:T(8,128)(2,1)S(1)} %broadcast_select_fusion.1), channel_id=1, source_target_pairs={{0,1},{1,0},{2,3},{3,2},{4,5},{5,4},{6,7},{7,6},{8,9},{9,8},{10,11... | collective-permute-start | bytes 393224 | tf_op jit(solution)/shard_map/ppermute | solution.py:46
  128.5 8.4 %collective-permute-done.13 = bf16[144,512]{1,0:T(8,128)(2,1)S(1)} collective-permute-done((bf16[144,512]{1,0:T(8,128)(2,1)S(1)}, bf16[144,512]{1,0:T(8,128)(2,1)S(1)}, u32[]{:S(2)}, u32[]{:S(2)}) %collective-permute-start.13) | collective-permute-done | bytes 147488 | tf_op jit(solution)/shard_map/ppermute | solution.py:36
  137.0 5.6 %collective-permute-done.15 = bf16[144,512]{1,0:T(8,128)(2,1)S(1)} collective-permute-done((bf16[144,512]{1,0:T(8,128)(2,1)S(1)}, bf16[144,512]{1,0:T(8,128)(2,1)S(1)}, u32[]{:S(2)}, u32[]{:S(2)}) %collective-permute-start.15) | collective-permute-done | bytes 147488 | tf_op jit(solution)/shard_map/ppermute | solution.py:36
  (72 shorter events, 36.1 us)
Async XLA Ops:
  0.6 16.9 %collective-permute-start.1 = (bf16[128,512]{1,0:T(8,128)(2,1)}, bf16[128,512]{1,0:T(8,128)(2,1)S(1)}, u32[]{:S(2)}, u32[]{:S(2)}) collective-permute-start(bf16[128,512]{1,0:T(8,128)(2,1)} %param.5), channel_id=1, source_target_pairs={{0,32},{8,40},{16,48},{24,56},{32,0},{40,8},{48,16},{56,24},{64,96... | collective-permute-start | bytes 393224 | tf_op jit(solution)/shard_map/ppermute | solution.py:36
  8.5 9.1 %collective-permute-start = (bf16[128,512]{1,0:T(8,128)(2,1)}, bf16[128,512]{1,0:T(8,128)(2,1)S(1)}, u32[]{:S(2)}, u32[]{:S(2)}) collective-permute-start(bf16[128,512]{1,0:T(8,128)(2,1)} %param.5), channel_id=1, source_target_pairs={{0,16},{8,24},{16,32},{24,40},{32,48},{40,56},{48,0},{56,8},{64,80... | collective-permute-start | bytes 393224 | tf_op jit(solution)/shard_map/ppermute | solution.py:36
  9.6 11.9 %collective-permute-start.2 = (bf16[128,512]{1,0:T(8,128)(2,1)}, bf16[128,512]{1,0:T(8,128)(2,1)S(1)}, u32[]{:S(2)}, u32[]{:S(2)}) collective-permute-start(bf16[128,512]{1,0:T(8,128)(2,1)} %param.5), channel_id=1, source_target_pairs={{0,48},{8,56},{16,0},{24,8},{32,16},{40,24},{48,32},{56,40},{64,11... | collective-permute-start | bytes 393224 | tf_op jit(solution)/shard_map/ppermute | solution.py:36
  12.0 3.1 %collective-permute-start.4 = (bf16[128,512]{1,0:T(8,128)(2,1)}, bf16[128,512]{1,0:T(8,128)(2,1)S(1)}, u32[]{:S(2)}, u32[]{:S(2)}) collective-permute-start(bf16[128,512]{1,0:T(8,128)(2,1)} %param.4), channel_id=1, source_target_pairs={{0,1},{1,0},{2,3},{3,2},{4,5},{5,4},{6,7},{7,6},{8,9},{9,8},{10,11... | collective-permute-start | bytes 393224 | tf_op jit(solution)/shard_map/ppermute | solution.py:46
  16.1 64.9 %copy-start.11 = (f32[7]{0:T(128)S(1)}, f32[7]{0:T(128)}, u32[]{:S(2)}) copy-start(f32[7]{0:T(128)} %weight.3) | copy-start | bytes 88
  16.2 8.6 %collective-permute-start.5 = (bf16[144,1024]{1,0:T(8,128)(2,1)S(1)}, bf16[144,1024]{1,0:T(8,128)(2,1)S(1)}, u32[]{:S(2)}, u32[]{:S(2)}) collective-permute-start(bf16[144,1024]{1,0:T(8,128)(2,1)S(1)} %pad_maximum_fusion), channel_id=1, source_target_pairs={{0,8},{2,10},{4,12},{6,14},{9,1},{11,3},{13,5},{15,7},{16,24},{18,... | collective-permute-start | bytes 884744 | tf_op jit(solution)/shard_map/ppermute | solution.py:55
  21.6 7.0 %collective-permute-start.3 = (bf16[512,512]{1,0:T(8,128)(2,1)S(1)}, bf16[512,512]{1,0:T(8,128)(2,1)S(1)}, u32[]{:S(2)}, u32[]{:S(2)}) collective-permute-start(bf16[512,512]{1,0:T(8,128)(2,1)S(1)} %constant_dynamic-update-slice_fusion.p_own), channel_id=1, source_target_pairs={{0,1},{1,0},{2,3},{3,2},{4,5},{5,4},{6,7},{7,6},{8,9},{9,8},{10,11... | collective-permute-start | bytes 1572872 | tf_op jit(solution)/shard_map/ppermute | solution.py:46
  24.8 14.8 %collective-permute-start.8 = (bf16[144,1024]{1,0:T(8,128)(2,1)S(1)}, bf16[144,1024]{1,0:T(8,128)(2,1)S(1)}, u32[]{:S(2)}, u32[]{:S(2)}) collective-permute-start(bf16[144,1024]{1,0:T(8,128)(2,1)S(1)} %broadcast_select_fusion.q0), channel_id=1, source_target_pairs={{0,192},{8,200},{16,208},{24,216},{32,224},{40,232},{48,240},{56,2... | collective-permute-start | bytes 884744 | tf_op jit(solution)/shard_map/ppermute | solution.py:32
  27.4 13.0 %collective-permute-start.7 = (bf16[144,1024]{1,0:T(8,128)(2,1)S(1)}, bf16[144,1024]{1,0:T(8,128)(2,1)S(1)}, u32[]{:S(2)}, u32[]{:S(2)}) collective-permute-start(bf16[144,1024]{1,0:T(8,128)(2,1)S(1)} %broadcast_select_fusion.q0), channel_id=1, source_target_pairs={{0,128},{8,136},{16,144},{24,152},{32,160},{40,168},{48,176},{56,1... | collective-permute-start | bytes 884744 | tf_op jit(solution)/shard_map/ppermute | solution.py:32
  27.9 15.7 %collective-permute-start.6 = (bf16[144,1024]{1,0:T(8,128)(2,1)S(1)}, bf16[144,1024]{1,0:T(8,128)(2,1)S(1)}, u32[]{:S(2)}, u32[]{:S(2)}) collective-permute-start(bf16[144,1024]{1,0:T(8,128)(2,1)S(1)} %broadcast_select_fusion.q0), channel_id=1, source_target_pairs={{0,64},{8,72},{16,80},{24,88},{32,96},{40,104},{48,112},{56,120},{... | collective-permute-start | bytes 884744 | tf_op jit(solution)/shard_map/ppermute | solution.py:32
  50.1 18.7 %all-to-all-start = ((f32[4,512,128]{2,1,0:T(8,128)}), f32[4,512,128]{2,1,0:T(8,128)S(1)}, u32[]{:S(2)}, u32[]{:S(2)}) async-start(f32[4,512,128]{2,1,0:T(8,128)} %copy-done.2), calls=%async_computation | async-start | bytes 2097152 | tf_op jit(solution)/shard_map/all_to_all | solution.py:330
  71.2 9.8 %all-to-all-start.1 = ((f32[8,72,128]{2,1,0:T(8,128)}), f32[8,72,128]{2,1,0:T(8,128)S(1)}, u32[]{:S(2)}, u32[]{:S(2)}) async-start(f32[8,72,128]{2,1,0:T(8,128)} %get-tuple-element.32), calls=%async_computation.1 | async-start | bytes 589824 | tf_op jit(solution)/shard_map/all_to_all | solution.py:340
  83.0 6.6 %collective-permute-start.9 = (bf16[528,128]{1,0:T(8,128)(2,1)S(1)}, bf16[528,128]{1,0:T(8,128)(2,1)S(1)}, u32[]{:S(2)}, u32[]{:S(2)}) collective-permute-start(bf16[528,128]{1,0:T(8,128)(2,1)S(1)} %get-tuple-element.35), channel_id=1, source_target_pairs={{0,2},{1,3},{2,4},{3,5},{4,6},{5,7},{6,0},{7,1},{8,10},{9,11},{10,... | collective-permute-start | bytes 405512 | tf_op jit(solution)/shard_map/ppermute | solution.py:42
  83.4 6.2 %collective-permute-start.10 = (bf16[528,128]{1,0:T(8,128)(2,1)S(1)}, bf16[528,128]{1,0:T(8,128)(2,1)S(1)}, u32[]{:S(2)}, u32[]{:S(2)}) collective-permute-start(bf16[528,128]{1,0:T(8,128)(2,1)S(1)} %get-tuple-element.36), channel_id=1, source_target_pairs={{0,4},{1,5},{2,6},{3,7},{4,0},{5,1},{6,2},{7,3},{8,12},{9,13},{10,... | collective-permute-start | bytes 405512 | tf_op jit(solution)/shard_map/ppermute | solution.py:42
  85.2 5.4 %collective-permute-start.11 = (bf16[528,128]{1,0:T(8,128)(2,1)S(1)}, bf16[528,128]{1,0:T(8,128)(2,1)S(1)}, u32[]{:S(2)}, u32[]{:S(2)}) collective-permute-start(bf16[528,128]{1,0:T(8,128)(2,1)S(1)} %get-tuple-element.37), channel_id=1, source_target_pairs={{0,6},{1,7},{2,0},{3,1},{4,2},{5,3},{6,4},{7,5},{8,14},{9,15},{10,... | collective-permute-start | bytes 405512 | tf_op jit(solution)/shard_map/ppermute | solution.py:42
  97.7 5.3 %collective-permute-start.16 = (bf16[128,1024]{1,0:T(8,128)(2,1)S(1)}, bf16[128,1024]{1,0:T(8,128)(2,1)S(1)}, u32[]{:S(2)}, u32[]{:S(2)}) collective-permute-start(bf16[128,1024]{1,0:T(8,128)(2,1)S(1)} %get-tuple-element.47), channel_id=1, source_target_pairs={{0,192},{8,200},{16,208},{24,216},{32,224},{40,232},{48,240},{56,2... | collective-permute-start | bytes 786440 | tf_op jit(solution)/shard_map/ppermute | solution.py:32
  98.5 6.8 %collective-permute-start.17 = (bf16[128,1024]{1,0:T(8,128)(2,1)S(1)}, bf16[128,1024]{1,0:T(8,128)(2,1)S(1)}, u32[]{:S(2)}, u32[]{:S(2)}) collective-permute-start(bf16[128,1024]{1,0:T(8,128)(2,1)S(1)} %get-tuple-element.48), channel_id=1, source_target_pairs={{0,128},{8,136},{16,144},{24,152},{32,160},{40,168},{48,176},{56,1... | collective-permute-start | bytes 786440 | tf_op jit(solution)/shard_map/ppermute | solution.py:32
  99.4 12.4 %collective-permute-start.18 = (bf16[128,1024]{1,0:T(8,128)(2,1)S(1)}, bf16[128,1024]{1,0:T(8,128)(2,1)S(1)}, u32[]{:S(2)}, u32[]{:S(2)}) collective-permute-start(bf16[128,1024]{1,0:T(8,128)(2,1)S(1)} %get-tuple-element.49), channel_id=1, source_target_pairs={{0,64},{8,72},{16,80},{24,88},{32,96},{40,104},{48,112},{56,120},{... | collective-permute-start | bytes 786440 | tf_op jit(solution)/shard_map/ppermute | solution.py:32
  112.0 6.0 %collective-permute-start.19 = (bf16[128,1024]{1,0:T(8,128)(2,1)S(1)}, bf16[128,1024]{1,0:T(8,128)(2,1)S(1)}, u32[]{:S(2)}, u32[]{:S(2)}) collective-permute-start(bf16[128,1024]{1,0:T(8,128)(2,1)S(1)} %fusion.6), channel_id=1, source_target_pairs={{1,9},{3,11},{5,13},{7,15},{8,0},{10,2},{12,4},{14,6},{17,25},{19,... | collective-permute-start | bytes 786440 | tf_op jit(solution)/shard_map/ppermute | solution.py:55
  114.7 8.4 %collective-permute-start.12 = (bf16[528,512]{1,0:T(8,128)(2,1)S(1)}, bf16[528,512]{1,0:T(8,128)(2,1)S(1)}, u32[]{:S(2)}, u32[]{:S(2)}) collective-permute-start(bf16[528,512]{1,0:T(8,128)(2,1)S(1)} %get-tuple-element.41.own_message), channel_id=1, source_target_pairs={{0,1},{1,0},{2,3},{3,2},{4,5},{5,4},{6,7},{7,6},{8,9},{9,8},{10,11... | collective-permute-start | bytes 1622024 | tf_op jit(solution)/shard_map/ppermute | solution.py:46
  118.2 9.6 %collective-permute-start.20 = (bf16[128,512]{1,0:T(8,128)(2,1)S(1)}, bf16[128,512]{1,0:T(8,128)(2,1)S(1)}, u32[]{:S(2)}, u32[]{:S(2)}) collective-permute-start(bf16[128,512]{1,0:T(8,128)(2,1)S(1)} %broadcast_select_fusion.1), channel_id=1, source_target_pairs={{0,1},{1,0},{2,3},{3,2},{4,5},{5,4},{6,7},{7,6},{8,9},{9,8},{10,11... | collective-permute-start | bytes 393224 | tf_op jit(solution)/shard_map/ppermute | solution.py:46
  123.2 13.7 %collective-permute-start.13 = (bf16[144,512]{1,0:T(8,128)(2,1)S(1)}, bf16[144,512]{1,0:T(8,128)(2,1)S(1)}, u32[]{:S(2)}, u32[]{:S(2)}) collective-permute-start(bf16[144,512]{1,0:T(8,128)(2,1)S(1)} %get-tuple-element.43), channel_id=1, source_target_pairs={{0,48},{8,56},{16,0},{24,8},{32,16},{40,24},{48,32},{56,40},{64,11... | collective-permute-start | bytes 442376 | tf_op jit(solution)/shard_map/ppermute | solution.py:36
  125.0 11.9 %collective-permute-start.14 = (bf16[144,512]{1,0:T(8,128)(2,1)S(1)}, bf16[144,512]{1,0:T(8,128)(2,1)S(1)}, u32[]{:S(2)}, u32[]{:S(2)}) collective-permute-start(bf16[144,512]{1,0:T(8,128)(2,1)S(1)} %get-tuple-element.44), channel_id=1, source_target_pairs={{0,32},{8,40},{16,48},{24,56},{32,0},{40,8},{48,16},{56,24},{64,96... | collective-permute-start | bytes 442376 | tf_op jit(solution)/shard_map/ppermute | solution.py:36
  127.0 15.5 %collective-permute-start.15 = (bf16[144,512]{1,0:T(8,128)(2,1)S(1)}, bf16[144,512]{1,0:T(8,128)(2,1)S(1)}, u32[]{:S(2)}, u32[]{:S(2)}) collective-permute-start(bf16[144,512]{1,0:T(8,128)(2,1)S(1)} %get-tuple-element.45), channel_id=1, source_target_pairs={{0,16},{8,24},{16,32},{24,40},{32,48},{40,56},{48,0},{56,8},{64,80... | collective-permute-start | bytes 442376 | tf_op jit(solution)/shard_map/ppermute | solution.py:36
  (11 other events, 12.7 us)

commit v2 on v1

--- a/solution.py
+++ b/solution.py
@@ -46,12 +46,13 @@
     return lax.ppermute(a, "feat", [(f, f ^ 1) for f in range(FEAT)])
 
 
-def move_zh(a, first):
+def move_square(a, rule):
     pairs = []
     for b in range(BATCH):
         for f in range(FEAT):
-            if (b % 2 == f % 2) == first:
-                pairs.append((b * FEAT + f, (b ^ 1) * FEAT + f))
+            to = rule(b % 2, f % 2)
+            if to is not None:
+                pairs.append((b * FEAT + f, (b - b % 2 + to[0]) * FEAT + f - f % 2 + to[1]))
     return lax.ppermute(a, BOTH, pairs)
 
 
@@ -65,7 +66,7 @@
     return jax.ShapeDtypeStruct(dims_dtype[:-1], dims_dtype[-1])
 
 
-def call(body, smem, args, outs, scratch=(), flops=0):
+def call(body, smem, args, outs, scratch=(), flops=0, grant=8):
     vmem = pl.BlockSpec(memory_space=pltpu.VMEM)
     scalar = pl.BlockSpec(memory_space=pltpu.SMEM)
     moved = sum(a.size * a.dtype.itemsize for a in (*args, *outs))
@@ -78,7 +79,7 @@
         cost_estimate=pl.CostEstimate(
             flops=flops, bytes_accessed=moved, transcendentals=0
         ),
-        compiler_params=pltpu.CompilerParams(vmem_limit_bytes=40 << 20),
+        compiler_params=pltpu.CompilerParams(vmem_limit_bytes=grant << 20),
     )(*smem, *args)
 
 
@@ -89,19 +90,43 @@
     return (block << bits) + (rows & (n - 1)) == pos
 
 
-def score_kernel(ids, p_own, p_other, q0, q1, q2, q3, partial, p, q_all, pos):
-    n = q_all.shape[1]
-    width = p_own.shape[1]
-
-    @pl.when(ids[CORE] == 0)
-    def _():
-        p[:, :width] = p_own[...]
-        p[:, width:] = p_other[...]
-
-    @pl.when(ids[CORE] != 0)
-    def _():
-        p[:, :width] = p_other[...]
-        p[:, width:] = p_own[...]
+def pack_kernel(ids, own, near, far, out):
+    n, width = near.shape
+    same = ids[ZH] == ids[CORE]
+
+    def put(first, second, rows):
+        out[:n, :width] = first[:n]
+        out[:n, width:] = second[:n]
+        out[n:, :width] = rows[n:]
+
+    out[n:, width:] = jnp.zeros((EXTRA, width), bf16)
+    for core in (0, 1):
+        for matches in (True, False):
+            a, b = (own, near) if matches else (near, far)
+            if core:
+                a, b = b, a
+
+            @pl.when((ids[CORE] == core) & (same == matches))
+            def _():
+                put(a, b, own if matches else far)
+
+
+def score_kernel(
+    ids, p0, p1, p2, p3, o0, o1, o2, o3, q0, q1, q2, q3, partial, p, q_all, pos
+):
+    n, width = p0.shape
+    for s, (own, other) in enumerate(zip((p0, p1, p2, p3), (o0, o1, o2, o3))):
+        rows = slice(s * n, s * n + n)
+
+        @pl.when(ids[CORE] == 0)
+        def _():
+            p[rows, :width] = own[...]
+            p[rows, width:] = other[...]
+
+        @pl.when(ids[CORE] != 0)
+        def _():
+            p[rows, :width] = other[...]
+            p[rows, width:] = own[...]
 
     for s, q in enumerate((q0, q1, q2, q3)):
         j = (ids[X] + 4 - s) & 3
@@ -137,7 +162,7 @@
         stats[j] = jnp.concatenate(tops + sums + picks + [tops[0]], axis=0)
 
 
-def owner_kernel(ids, pieces, pos, low_stats, e_high, message):
+def owner_kernel(ids, pieces, pos, low_stats, e_high, message, local):
     n = pos.shape[2]
     hot = find_positives(ids, pos[ids[Y]], n)
     sum5 = pieces[0] + pieces[1]
@@ -158,6 +183,7 @@
         for j in range(4):
             message[i, 16 * j : 16 * j + 16] = low_stats[j]
         message[i, 64:72] = high
+    local[...] = message[0]
 
 
 def put_terms(ref, row, v):
@@ -229,10 +255,10 @@
 
 def grad_kernel(
     ids, weight, t0, t1, t2, t3, e_low, rates, pos, p, q_all,
-    gq0, gq1, gq2, gq3, gp_own, gp_message, tails, gq,
+    gq0, gq1, gq2, gq3, gp0, gp1, gp2, gp3, row, tails, gq, gp,
 ):
     n = pos.shape[2]
-    width = gp_own.shape[1]
+    wide = gp0.shape[1]
     on = ids[Y] == 0
     loss = jnp.zeros((1, n), f32)
     for t, ref in enumerate((t0, t1, t2, t3)):
@@ -245,48 +271,53 @@
             scale = jnp.where(on, weight[k] * FACTORS[k], 0.0)
             acc = acc + (e_low[k, j] * rates[j, k : k + 1] - jnp.where(hot, scale, 0.0))
             tails[k, :, lanes] = acc.astype(bf16)
-
-    q = q_all[...].reshape(4 * n, 2 * width)
+    row[...] = jnp.broadcast_to(loss, row.shape)
+
+    q = q_all[...].reshape(4 * n, wide)
     first = lax.broadcasted_iota(jnp.int32, (4 * n, PAIR), 1) < SMALLEST
 
-    def by_span(fn):
-        yield 0, PAIR, jnp.where(first, fn(0, 0, PAIR), fn(1, 0, PAIR))
+    def fill(out, fn):
+        out[:, :PAIR] = jnp.where(first, fn(0, 0, PAIR), fn(1, 0, PAIR))
         for k in range(2, LOW):
             begin, end = SPANS[k]
-            yield begin, end, fn(k, begin, end)
-
-    for begin, end, v in by_span(lambda k, a, b: dot(tails[k], q[:, a:b], 1, 0)):
-        mine = (begin < width) == (ids[CORE] == 0)
-        at = begin % width
-
-        @pl.when(mine)
-        def _():
-            gp_own[:, at : at + end - begin] = v
-
-        @pl.when(jnp.logical_not(mine))
-        def _():
-            gp_message[: 4 * n, at : at + end - begin] = v.astype(bf16)
-
-    gp_message[4 * n :] = jnp.zeros((EXTRA, width), bf16)
-    put_terms(gp_message, 4 * n, loss)
-    for begin, end, v in by_span(lambda k, a, b: dot(tails[k], p[:, a:b], 0, 0)):
-        gq[:, begin:end] = v
+            out[:, begin:end] = fn(k, begin, end)
+
+    fill(gq, lambda k, a, b: dot(tails[k], p[:, a:b], 0, 0))
     for s, out in enumerate((gq0, gq1, gq2, gq3)):
         j = (ids[X] + 4 - s) & 3
         out[...] = gq[pl.ds(pl.multiple_of(j * n, n), n), :].astype(out.dtype)
-
-
-def core_sum_kernel(gp_own, own_message, other_message, own, m1, m2, m3, loss):
+    fill(gp, lambda k, a, b: dot(tails[k], q[:, a:b], 1, 0))
+    for s, out in enumerate((gp0, gp1, gp2, gp3)):
+        out[:n] = gp[s * n : s * n + n].astype(out.dtype)
+        if s:
+            out[n:] = jnp.zeros((EXTRA, wide), bf16)
+            put_terms(out, n, loss)
+
+
+def passage_kernel(ids, gp0, g1, g2, g3, row, own, message, loss):
     n, width = own.shape
-    total = get_terms(own_message, 4 * n, n) + get_terms(other_message, 4 * n, n)
+    total = row[0:1]
+    for g in (g1, g2, g3):
+        total += get_terms(g, n, n)
     loss[...] = jnp.broadcast_to(total, loss.shape)
-    for s, out in enumerate((own, m1, m2, m3)):
-        rows = slice(s * n, s * n + n)
-        v = gp_own[rows] + other_message[rows].astype(f32)
-        out[:n] = v.astype(out.dtype)
-        if s:
-            out[n:] = jnp.zeros((EXTRA, width), bf16)
-            put_terms(out, n, total)
+    message[n:] = jnp.zeros((EXTRA, width), bf16)
+    put_terms(message, n, total)
+
+    def half(c):
+        lanes = slice(c * width, c * width + width)
+        return gp0[:, lanes] + (
+            g1[:n, lanes].astype(f32) + g2[:n, lanes].astype(f32) + g3[:n, lanes].astype(f32)
+        )
+
+    @pl.when(ids[CORE] == 0)
+    def _():
+        own[...] = half(0)
+        message[:n] = half(1).astype(bf16)
+
+    @pl.when(ids[CORE] != 0)
+    def _():
+        own[...] = half(1)
+        message[:n] = half(0).astype(bf16)
 
 
 def per_device(queries, passages, positives, level_weight):
@@ -298,27 +329,22 @@
     same = bi % 2 == core
     ids = jnp.stack([bi // 8, fi // 2, bi % 8 // 2, bi % 2, core]).astype(jnp.int32)
 
-    q_core = swap_core(queries)
     rows = jnp.stack([positives // 64, positives % 64]).astype(bf16)
-    q_chip = jnp.concatenate(
-        [
-            jnp.concatenate(
-                [jnp.where(core == 0, queries, q_core), jnp.where(core == 0, q_core, queries)],
-                axis=1,
-            ),
-            jnp.pad(rows, ((0, EXTRA - 2), (0, wide - n))),
-        ],
-        axis=0,
-    )
-    q_msg = jnp.where(same, q_chip, move_zh(q_chip, True))
+    rows = jnp.pad(rows, ((0, EXTRA - 2), (0, width - n)))
+    q_row = jnp.concatenate([queries, rows], axis=0)
+    near = move_square(queries, lambda h, c: (1 - h, c) if h == c else (h, 1 - c))
+    far = move_square(q_row, lambda h, c: None if h == c else (1 - h, 1 - c))
+    (q_msg,) = call(
+        pack_kernel, [ids], [q_row, near, far], [shape(n + EXTRA, wide, bf16)]
+    )
     q_msgs = [q_msg] + [shift_x(q_msg, s) for s in (1, 2, 3)]
 
-    p_half = jnp.concatenate([passages] + [shift_zl(passages, s) for s in (1, 2, 3)], axis=0)
-    p_other = swap_core(p_half)
+    p_own = [passages] + [shift_zl(passages, s) for s in (1, 2, 3)]
+    p_other = [swap_core(a) for a in p_own]
 
     tile = 4 * n * 4 * n
     partial, p, q, pos = call(
-        score_kernel, [ids], [p_half, p_other, *q_msgs],
+        score_kernel, [ids], [*p_own, *p_other, *q_msgs],
         [
             shape(4, 4 * n, n, f32),
             shape(4 * n, wide, bf16),
@@ -333,46 +359,45 @@
         [shape(LOW, 4, 4 * n, n, f32), shape(4, 16, n, f32)],
         flops=2 * tile * wide,
     )
-    e_high, message = call(
+    e_high, message, local = call(
         owner_kernel, [ids], [pieces, pos, low_stats],
-        [shape(2, 4 * n, n, f32), shape(8, 72, n, f32)],
+        [shape(2, 4 * n, n, f32), shape(8, 72, n, f32), shape(72, n, f32)],
     )
     stats = lax.all_to_all(message, "batch", 0, 0, axis_index_groups=XZH_GROUPS)
     *tails, rates = call(
-        tail_kernel, [ids, level_weight], [stats, message[0], e_high, pos],
+        tail_kernel, [ids, level_weight], [stats, local, e_high, pos],
         [shape(4 * n + EXTRA, n, bf16)] * 4 + [shape(4, 8, n, f32)],
     )
     tails = [tails[0]] + [shift_y(tails[t], t) for t in (1, 2, 3)]
-    *gq, gp_own, gp_message = call(
+    gq0, gq1, gq2, gq3, gp0, gp1, gp2, gp3, row = call(
         grad_kernel, [ids, level_weight], [*tails, e_low, rates, pos, p, q],
         [shape(n, wide, f32)]
         + [shape(n, wide, bf16)] * 3
-        + [shape(4 * n, width, f32), shape(4 * n + EXTRA, width, bf16)],
-        scratch=[pltpu.VMEM((LOW, 4 * n, 4 * n), bf16), pltpu.VMEM((4 * n, wide), f32)],
-        flops=4 * tile * wide,
-    )
-
-    own, *messages, loss_row = call(
-        core_sum_kernel, [], [gp_own, gp_message, swap_core(gp_message)],
-        [shape(n, width, f32)] + [shape(n + EXTRA, width, bf16)] * 3 + [shape(8, n, f32)],
-    )
-    grad_passages = own
-    loss_row = loss_row[0]
-    for s, message in zip((1, 2, 3), messages):
-        other = shift_zl(message, -s).astype(f32)
-        grad_passages = grad_passages + other[:n]
-        loss_row = loss_row + (other[n, :n] + other[n + 1, :n] + other[n + 2, :n])
+        + [shape(n, wide, f32)]
+        + [shape(n + EXTRA, wide, bf16)] * 3
+        + [shape(8, n, f32)],
+        scratch=[pltpu.VMEM((LOW, 4 * n, 4 * n), bf16)] + [pltpu.VMEM((4 * n, wide), f32)] * 2,
+        flops=4 * tile * wide, grant=20,
+    )
+    gq = [shift_x(g, -s) for s, g in enumerate((gq1, gq2, gq3), 1)]
+    gp = [shift_zl(g, -s) for s, g in enumerate((gp1, gp2, gp3), 1)]
+
+    own, message, loss_row = call(
+        passage_kernel, [ids], [gp0, *gp, row],
+        [shape(n, width, f32), shape(n + EXTRA, width, bf16), shape(8, n, f32)],
+    )
+    other = swap_core(message).astype(f32)
+    grad_passages = (own + other[:n]).astype(bf16)
+    loss_row = loss_row[0] + (other[n, :n] + other[n + 1, :n] + other[n + 2, :n])
     loss = jnp.sum(loss_row) / (n * BATCH)
 
-    gq_sum = gq[0]
-    for s in (1, 2, 3):
-        gq_sum = gq_sum + shift_x(gq[s], -s).astype(f32)
-    gq_sum = gq_sum + move_zh(gq_sum.astype(bf16), False).astype(f32)
-    gq_sum = gq_sum.astype(bf16)
+    gq_sum = gq0 + sum(g.astype(f32) for g in gq)
+    far = move_square(gq_sum.astype(bf16), lambda h, c: None if h == c else (1 - h, c))
+    gq_sum = (gq_sum + far.astype(f32)).astype(bf16)
     left, right = gq_sum[:, :width], gq_sum[:, width:]
     other = swap_core(jnp.where(core == 0, right, left))
     grad_queries = jnp.where(same, jnp.where(core == 0, left, right), other)
-    return loss, grad_queries, grad_passages.astype(bf16)
+    return loss, grad_queries, grad_passages
 
 
 def solution(mesh):

time: 146 us -> 128 us (0.88)
  waiting for transfers between devices: 67.1 us -> 40.1 us
  blocking collectives: 0 us -> 10.4 us
  local copies, waits for them, and re-layouts: 14.5 us -> 6.8 us
  starting transfers between devices: 44.5 us -> 51.2 us
    ppermute x6, waiting for transfers between devices: 25.8 us -> 11.4 us  [shift_x(): lax.ppermute(a, 'batch', [(b, (b + 8 * s) % BATCH) for b in range(BATCH)])]
    all_to_all x0 -> x1, blocking collectives: none -> 10.4 us  [per_device(): stats = lax.all_to_all(message, 'batch', 0, 0, axis_index_groups=XZH_GROUPS)]
    ppermute x4 -> x6, starting transfers between devices: 8.2 us -> 15.4 us  [swap_core(): return lax.ppermute(a, 'feat', [(f, f ^ 1) for f in range(FEAT)])]
    unnamed x27 -> x10, local copies, waits for them, and re-layouts: 13.6 us -> 6.71 us
    ppermute x6, waiting for transfers between devices: 18 us -> 12.4 us  [shift_zl(): lax.ppermute(a, 'batch', [(b, b // 8 * 8 + (b + 2 * s) % 8) for b in rang...]
    all_to_all x1 -> x0, waiting for transfers between devices: 5.58 us -> none  [per_device(): stats = lax.all_to_all(message, 'batch', 0, 0, axis_index_groups=XZH_GROUPS)]
    ppermute x2 -> x3, waiting for transfers between devices: 4.6 us -> 0.01 us  [move_square(): return lax.ppermute(a, BOTH, pairs)]
    ppermute x2 -> x3, starting transfers between devices: 4 us -> 7.66 us  [move_square(): return lax.ppermute(a, BOTH, pairs)]
  transfers between devices with their start and end apart: 23 -> 25, of which waited for: 15 -> 13; matrix products, arithmetic and copies ran while one was open for 3% -> 1% of each run, Pallas kernels for 2% -> 4%
where the time goes in v2:
time: 128 us
  starting transfers between devices  51.2 us (40%)
  waiting for transfers between devices  40.1 us (31%)
  Pallas kernels  12.7 us (10%)
  blocking collectives  10.4 us (8%)
  local copies, waits for them, and re-layouts  6.8 us (5%)
  other arithmetic  3.95 us (3%)
  between operations  2.57 us (2%)
    ppermute x6, starting transfers between devices, swap_core(): return lax.ppermute(a, 'feat', [(f, f ^ 1) for f in range(FEAT)])  15.4 us
    ppermute x6, starting transfers between devices, shift_zl(): lax.ppermute(a, 'batch', [(b, b // 8 * 8 + (b + 2 * s) % 8) for b in rang...  14.6 us
    pallas_call x7, Pallas kernels, call(): pl.pallas_call(body, out_shape=outs, in_specs=[scalar] * len(smem) + [vme...  12.7 us
    ppermute x6, waiting for transfers between devices, shift_zl(): lax.ppermute(a, 'batch', [(b, b // 8 * 8 + (b + 2 * s) % 8) for b in rang...  12.4 us
    ppermute x6, waiting for transfers between devices, shift_x(): lax.ppermute(a, 'batch', [(b, (b + 8 * s) % BATCH) for b in range(BATCH)])  11.4 us
    all_to_all x1, blocking collectives, per_device(): stats = lax.all_to_all(message, 'batch', 0, 0, axis_index_groups=XZH_GROUPS)  10.4 us
    all_to_all x1, waiting for transfers between devices, per_device(): pieces = lax.all_to_all(partial, 'feat', 0, 0, axis_index_groups=Y_GROUPS)  7.98 us
    ppermute x3, starting transfers between devices, move_square(): return lax.ppermute(a, BOTH, pairs)  7.66 us
  transfers between devices with their start and end apart: 25, of which 13 were waited for; matrix products, arithmetic and copies ran while one was open for 1% of the time, Pallas kernels for 4%

profile of v2, /device:TPU:1, one launch (start us, length us, event | category | flops | bytes accessed | tf_op | source)
XLA Modules:
  0.0 127.7 jit_solution(3569601633013007780)
XLA Ops:
  2.2 4.9 %collective-permute-start.8 = (bf16[144,512]{1,0:T(8,128)(2,1)S(1)}, bf16[144,512]{1,0:T(8,128)(2,1)S(1)}, u32[]{:S(2)}, u32[]{:S(2)}) collective-permute-start(bf16[144,512]{1,0:T(8,128)(2,1)S(1)} %pad_maximum_fusion.own), channel_id=1, source_target_pairs={{1,8},{3,10},{5,12},{7,14},{8,1},{10,3},{12,5},{14,7},{17,24},{19,... | collective-permute-start | bytes 442376 | tf_op jit(solution)/shard_map/ppermute | solution.py:56
  7.3 5.2 %collective-permute-start.2 = (bf16[128,512]{1,0:T(8,128)(2,1)}, bf16[128,512]{1,0:T(8,128)(2,1)S(1)}, u32[]{:S(2)}, u32[]{:S(2)}) collective-permute-start(bf16[128,512]{1,0:T(8,128)(2,1)} %p0.1), channel_id=1, source_target_pairs={{0,48},{8,56},{16,0},{24,8},{32,16},{40,24},{48,32},{56,40},{64,11... | collective-permute-start | bytes 393224 | tf_op jit(solution)/shard_map/ppermute | solution.py:36
  13.7 2.1 %collective-permute-start = (bf16[128,512]{1,0:T(8,128)(2,1)}, bf16[128,512]{1,0:T(8,128)(2,1)S(1)}, u32[]{:S(2)}, u32[]{:S(2)}) collective-permute-start(bf16[128,512]{1,0:T(8,128)(2,1)} %p0.1), channel_id=1, source_target_pairs={{0,16},{8,24},{16,32},{24,40},{32,48},{40,56},{48,0},{56,8},{64,80... | collective-permute-start | bytes 393224 | tf_op jit(solution)/shard_map/ppermute | solution.py:36
  16.4 2.6 %collective-permute-start.11 = (bf16[144,1024]{1,0:T(8,128)(2,1)S(1)}, bf16[144,1024]{1,0:T(8,128)(2,1)S(1)}, u32[]{:S(2)}, u32[]{:S(2)}) collective-permute-start(bf16[144,1024]{1,0:T(8,128)(2,1)S(1)} %shard_map.67.q0), channel_id=1, source_target_pairs={{0,192},{8,200},{16,208},{24,216},{32,224},{40,232},{48,240},{56,2... | collective-permute-start | bytes 884744 | tf_op jit(solution)/shard_map/ppermute | solution.py:32
  19.5 3.8 %collective-permute-done.2.p3 = bf16[128,512]{1,0:T(8,128)(2,1)S(1)} collective-permute-done((bf16[128,512]{1,0:T(8,128)(2,1)}, bf16[128,512]{1,0:T(8,128)(2,1)S(1)}, u32[]{:S(2)}, u32[]{:S(2)}) %collective-permute-start.2) | collective-permute-done | bytes 131104 | tf_op jit(solution)/shard_map/ppermute | solution.py:36
  23.3 1.2 collective-permute-start.9
  24.6 1.9 %collective-permute-start.3 = (bf16[128,512]{1,0:T(8,128)(2,1)}, bf16[128,512]{1,0:T(8,128)(2,1)S(1)}, u32[]{:S(2)}, u32[]{:S(2)}) collective-permute-start(bf16[128,512]{1,0:T(8,128)(2,1)} %p0.1), channel_id=1, source_target_pairs={{0,1},{1,0},{2,3},{3,2},{4,5},{5,4},{6,7},{7,6},{8,9},{9,8},{10,11... | collective-permute-start | bytes 393224 | tf_op jit(solution)/shard_map/ppermute | solution.py:46
  29.4 5.9 %collective-permute-done.9.q1 = bf16[144,1024]{1,0:T(8,128)(2,1)S(1)} collective-permute-done((bf16[144,1024]{1,0:T(8,128)(2,1)S(1)}, bf16[144,1024]{1,0:T(8,128)(2,1)S(1)}, u32[]{:S(2)}, u32[]{:S(2)}) %collective-permute-start.9) | collective-permute-done | bytes 294944 | tf_op jit(solution)/shard_map/ppermute | solution.py:32
  36.2 2.0 %shard_map.68 = (f32[4,512,128]{2,1,0:T(8,128)S(1)}, bf16[512,1024]{1,0:T(8,128)(2,1)S(1)}, bf16[4,128,1024]{2,1,0:T(8,128)(2,1)S(1)}, s32[4,1,128]{2,1,0:T(1,128)S(1)}) custom-call(s32[5]{0:T(128)S(1)} %stack.35.ids, bf16[128,512]{1,0:T(8,128)(2,1)S(1)} %copy-done.3, bf16[128,512]{1,0:T(8,128)(2,1)S(1)} %collective-permute-done.p1, ...), custom_call_target="tpu_custom_call" | custom-call | flops 536870912 | bytes 5376000 | tf_op jit(solution)/shard_map/pallas_call | solution.py:73
  39.1 4.2 %all-to-all-start = ((f32[4,512,128]{2,1,0:T(8,128)}), f32[4,512,128]{2,1,0:T(8,128)S(1)}, u32[]{:S(2)}, u32[]{:S(2)}) async-start(f32[4,512,128]{2,1,0:T(8,128)} %copy-done.2), calls=%async_computation | async-start | bytes 2097152 | tf_op jit(solution)/shard_map/all_to_all | solution.py:356
  43.3 3.6 %shard_map.69 = (f32[5,4,512,128]{3,2,1,0:T(8,128)S(1)}, f32[4,16,128]{2,1,0:T(8,128)S(1)}) custom-call(s32[5]{0:T(128)S(1)} %stack.35.ids, bf16[512,1024]{1,0:T(8,128)(2,1)S(1)} %get-tuple-element.31.p, bf16[4,128,1024]{2,1,0:T(8,128)(2,1)S(1)} %get-tuple-element.32.q_all, s32[4,1,128]{2,1,0:T(1,128)S(1)} %get-tuple-element.30.pos), custom_call_target="tpu_custom_call" | custom-call | flops 536870912 | bytes 7374848 | tf_op jit(solution)/shard_map/pallas_call | solution.py:73
  46.9 2.3 %copy-done = f32[5,4,512,128]{3,2,1,0:T(8,128)} copy-done((f32[5,4,512,128]{3,2,1,0:T(8,128)}, f32[5,4,512,128]{3,2,1,0:T(8,128)S(1)}, u32[]{:S(2)}) %copy-start) | copy-done | bytes 5242904
  49.2 8.0 %all-to-all-done.pieces = f32[4,512,128]{2,1,0:T(8,128)S(1)} async-done(((f32[4,512,128]{2,1,0:T(8,128)}), f32[4,512,128]{2,1,0:T(8,128)S(1)}, u32[]{:S(2)}, u32[]{:S(2)}) %all-to-all-start) | async-done | bytes 1048608 | tf_op jit(solution)/shard_map/all_to_all | solution.py:356
  58.2 10.4 %all_to_all.10.stats = f32[8,72,128]{2,1,0:T(8,128)S(1)} all-to-all(f32[8,72,128]{2,1,0:T(8,128)S(1)} %get-tuple-element.34), channel_id=1, replica_groups={{0,8,64,72,128,136,192,200},{16,24,80,88,144,152,208,216},{32,40,96,104..., dimensions={0} | all-to-all | bytes 589824 | tf_op jit(solution)/shard_map/all_to_all | solution.py:366
  69.9 1.8 %collective-permute-start.13 = (bf16[528,128]{1,0:T(8,128)(2,1)S(1)}, bf16[528,128]{1,0:T(8,128)(2,1)S(1)}, u32[]{:S(2)}, u32[]{:S(2)}) collective-permute-start(bf16[528,128]{1,0:T(8,128)(2,1)S(1)} %get-tuple-element.39), channel_id=1, source_target_pairs={{0,4},{1,5},{2,6},{3,7},{4,0},{5,1},{6,2},{7,3},{8,12},{9,13},{10,... | collective-permute-start | bytes 405512 | tf_op jit(solution)/shard_map/ppermute | solution.py:42
  72.4 3.7 %collective-permute-done.12.t1 = bf16[528,128]{1,0:T(8,128)(2,1)S(1)} collective-permute-done((bf16[528,128]{1,0:T(8,128)(2,1)S(1)}, bf16[528,128]{1,0:T(8,128)(2,1)S(1)}, u32[]{:S(2)}, u32[]{:S(2)}) %collective-permute-start.12) | collective-permute-done | bytes 135200 | tf_op jit(solution)/shard_map/ppermute | solution.py:42
  77.0 2.5 %copy-done.1 = f32[5,4,512,128]{3,2,1,0:T(8,128)S(1)} copy-done((f32[5,4,512,128]{3,2,1,0:T(8,128)S(1)}, f32[5,4,512,128]{3,2,1,0:T(8,128)}, u32[]{:S(2)}) %copy-start.1) | copy-done | bytes 5242904
  79.5 4.0 %shard_map.72 = (f32[128,1024]{1,0:T(8,128)S(1)}, bf16[128,1024]{1,0:T(8,128)(2,1)S(1)}, bf16[128,1024]{1,0:T(8,128)(2,1)S(1)}, bf16[128,1024]{1,0:T(8,128)(2,1)...) custom-call(s32[5]{0:T(128)S(1)} %stack.35.ids, ...), custom_call_target="tpu_custom_call" | custom-call | flops 1073741824 | bytes 10622976 | tf_op jit(solution)/shard_map/pallas_call | solution.py:73
  85.8 1.3 %collective-permute-start.15 = (bf16[144,1024]{1,0:T(8,128)(2,1)S(1)}, bf16[144,1024]{1,0:T(8,128)(2,1)S(1)}, u32[]{:S(2)}, u32[]{:S(2)}) collective-permute-start(bf16[144,1024]{1,0:T(8,128)(2,1)S(1)} %get-tuple-element.44), channel_id=1, source_target_pairs={{0,48},{8,56},{16,0},{24,8},{32,16},{40,24},{48,32},{56,40},{64,11... | collective-permute-start | bytes 884744 | tf_op jit(solution)/shard_map/ppermute | solution.py:36
  87.1 4.3 %collective-permute-start.16 = (bf16[144,1024]{1,0:T(8,128)(2,1)S(1)}, bf16[144,1024]{1,0:T(8,128)(2,1)S(1)}, u32[]{:S(2)}, u32[]{:S(2)}) collective-permute-start(bf16[144,1024]{1,0:T(8,128)(2,1)S(1)} %get-tuple-element.45), channel_id=1, source_target_pairs={{0,32},{8,40},{16,48},{24,56},{32,0},{40,8},{48,16},{56,24},{64,96... | collective-permute-start | bytes 884744 | tf_op jit(solution)/shard_map/ppermute | solution.py:36
  92.0 5.5 %collective-permute-done.21 = bf16[128,1024]{1,0:T(8,128)(2,1)S(1)} collective-permute-done((bf16[128,1024]{1,0:T(8,128)(2,1)S(1)}, bf16[128,1024]{1,0:T(8,128)(2,1)S(1)}, u32[]{:S(2)}, u32[]{:S(2)}) %collective-permute-start.21) | collective-permute-done | bytes 262176 | tf_op jit(solution)/shard_map/ppermute | solution.py:32
  97.6 2.6 %collective-permute-start.22 = (bf16[128,1024]{1,0:T(8,128)(2,1)S(1)}, bf16[128,1024]{1,0:T(8,128)(2,1)S(1)}, u32[]{:S(2)}, u32[]{:S(2)}) collective-permute-start(bf16[128,1024]{1,0:T(8,128)(2,1)S(1)} %fusion.1), channel_id=1, source_target_pairs={{1,9},{3,11},{5,13},{7,15},{8,0},{10,2},{12,4},{14,6},{17,25},{19,... | collective-permute-start | bytes 786440 | tf_op jit(solution)/shard_map/ppermute | solution.py:56
  100.2 7.7 %collective-permute-done.15.g1 = bf16[144,1024]{1,0:T(8,128)(2,1)S(1)} collective-permute-done((bf16[144,1024]{1,0:T(8,128)(2,1)S(1)}, bf16[144,1024]{1,0:T(8,128)(2,1)S(1)}, u32[]{:S(2)}, u32[]{:S(2)}) %collective-permute-start.15) | collective-permute-done | bytes 294944 | tf_op jit(solution)/shard_map/ppermute | solution.py:36
  109.5 12.5 %collective-permute-start.18 = (bf16[144,512]{1,0:T(8,128)(2,1)S(1)}, bf16[144,512]{1,0:T(8,128)(2,1)S(1)}, u32[]{:S(2)}, u32[]{:S(2)}) collective-permute-start(bf16[144,512]{1,0:T(8,128)(2,1)S(1)} %get-tuple-element.49), channel_id=1, source_target_pairs={{0,1},{1,0},{2,3},{3,2},{4,5},{5,4},{6,7},{7,6},{8,9},{9,8},{10,11... | collective-permute-start | bytes 442376 | tf_op jit(solution)/shard_map/ppermute | solution.py:46
  (55 shorter events, 21.3 us)
Async XLA Ops:
  2.2 13.6 %collective-permute-start.8 = (bf16[144,512]{1,0:T(8,128)(2,1)S(1)}, bf16[144,512]{1,0:T(8,128)(2,1)S(1)}, u32[]{:S(2)}, u32[]{:S(2)}) collective-permute-start(bf16[144,512]{1,0:T(8,128)(2,1)S(1)} %pad_maximum_fusion.own), channel_id=1, source_target_pairs={{1,8},{3,10},{5,12},{7,14},{8,1},{10,3},{12,5},{14,7},{17,24},{19,... | collective-permute-start | bytes 442376 | tf_op jit(solution)/shard_map/ppermute | solution.py:56
  7.2 8.6 %collective-permute-start.7 = (bf16[128,512]{1,0:T(8,128)(2,1)}, bf16[128,512]{1,0:T(8,128)(2,1)S(1)}, u32[]{:S(2)}, u32[]{:S(2)}) collective-permute-start(bf16[128,512]{1,0:T(8,128)(2,1)} %param.4), channel_id=1, source_target_pairs={{0,8},{1,0},{2,10},{3,2},{4,12},{5,4},{6,14},{7,6},{8,9},{9,1},{10... | collective-permute-start | bytes 393224 | tf_op jit(solution)/shard_map/ppermute | solution.py:56
  7.3 16.1 %collective-permute-start.2 = (bf16[128,512]{1,0:T(8,128)(2,1)}, bf16[128,512]{1,0:T(8,128)(2,1)S(1)}, u32[]{:S(2)}, u32[]{:S(2)}) collective-permute-start(bf16[128,512]{1,0:T(8,128)(2,1)} %p0.1), channel_id=1, source_target_pairs={{0,48},{8,56},{16,0},{24,8},{32,16},{40,24},{48,32},{56,40},{64,11... | collective-permute-start | bytes 393224 | tf_op jit(solution)/shard_map/ppermute | solution.py:36
  12.5 12.1 %collective-permute-start.1 = (bf16[128,512]{1,0:T(8,128)(2,1)}, bf16[128,512]{1,0:T(8,128)(2,1)S(1)}, u32[]{:S(2)}, u32[]{:S(2)}) collective-permute-start(bf16[128,512]{1,0:T(8,128)(2,1)} %p0.1), channel_id=1, source_target_pairs={{0,32},{8,40},{16,48},{24,56},{32,0},{40,8},{48,16},{56,24},{64,96... | collective-permute-start | bytes 393224 | tf_op jit(solution)/shard_map/ppermute | solution.py:36
  13.7 12.8 %collective-permute-start = (bf16[128,512]{1,0:T(8,128)(2,1)}, bf16[128,512]{1,0:T(8,128)(2,1)S(1)}, u32[]{:S(2)}, u32[]{:S(2)}) collective-permute-start(bf16[128,512]{1,0:T(8,128)(2,1)} %p0.1), channel_id=1, source_target_pairs={{0,16},{8,24},{16,32},{24,40},{32,48},{40,56},{48,0},{56,8},{64,80... | collective-permute-start | bytes 393224 | tf_op jit(solution)/shard_map/ppermute | solution.py:36
  16.4 12.9 %collective-permute-start.11 = (bf16[144,1024]{1,0:T(8,128)(2,1)S(1)}, bf16[144,1024]{1,0:T(8,128)(2,1)S(1)}, u32[]{:S(2)}, u32[]{:S(2)}) collective-permute-start(bf16[144,1024]{1,0:T(8,128)(2,1)S(1)} %shard_map.67.q0), channel_id=1, source_target_pairs={{0,192},{8,200},{16,208},{24,216},{32,224},{40,232},{48,240},{56,2... | collective-permute-start | bytes 884744 | tf_op jit(solution)/shard_map/ppermute | solution.py:32
  19.0 10.4 %collective-permute-start.10 = (bf16[144,1024]{1,0:T(8,128)(2,1)S(1)}, bf16[144,1024]{1,0:T(8,128)(2,1)S(1)}, u32[]{:S(2)}, u32[]{:S(2)}) collective-permute-start(bf16[144,1024]{1,0:T(8,128)(2,1)S(1)} %shard_map.67.q0), channel_id=1, source_target_pairs={{0,128},{8,136},{16,144},{24,152},{32,160},{40,168},{48,176},{56,1... | collective-permute-start | bytes 884744 | tf_op jit(solution)/shard_map/ppermute | solution.py:32
  23.3 11.9 %collective-permute-start.9 = (bf16[144,1024]{1,0:T(8,128)(2,1)S(1)}, bf16[144,1024]{1,0:T(8,128)(2,1)S(1)}, u32[]{:S(2)}, u32[]{:S(2)}) collective-permute-start(bf16[144,1024]{1,0:T(8,128)(2,1)S(1)} %shard_map.67.q0), channel_id=1, source_target_pairs={{0,64},{8,72},{16,80},{24,88},{32,96},{40,104},{48,112},{56,120},{... | collective-permute-start | bytes 884744 | tf_op jit(solution)/shard_map/ppermute | solution.py:32
  24.6 3.1 %collective-permute-start.3 = (bf16[128,512]{1,0:T(8,128)(2,1)}, bf16[128,512]{1,0:T(8,128)(2,1)S(1)}, u32[]{:S(2)}, u32[]{:S(2)}) collective-permute-start(bf16[128,512]{1,0:T(8,128)(2,1)} %p0.1), channel_id=1, source_target_pairs={{0,1},{1,0},{2,3},{3,2},{4,5},{5,4},{6,7},{7,6},{8,9},{9,8},{10,11... | collective-permute-start | bytes 393224 | tf_op jit(solution)/shard_map/ppermute | solution.py:46
  26.4 1.6 %collective-permute-start.6 = (bf16[128,512]{1,0:T(8,128)(2,1)S(1)}, bf16[128,512]{1,0:T(8,128)(2,1)S(1)}, u32[]{:S(2)}, u32[]{:S(2)}) collective-permute-start(bf16[128,512]{1,0:T(8,128)(2,1)S(1)} %collective-permute-done.2.p3), channel_id=1, source_target_pairs={{0,1},{1,0},{2,3},{3,2},{4,5},{5,4},{6,7},{7,6},{8,9},{9,8},{10,11... | collective-permute-start | bytes 393224 | tf_op jit(solution)/shard_map/ppermute | solution.py:46
  28.0 1.3 %collective-permute-start.4 = (bf16[128,512]{1,0:T(8,128)(2,1)S(1)}, bf16[128,512]{1,0:T(8,128)(2,1)S(1)}, u32[]{:S(2)}, u32[]{:S(2)}) collective-permute-start(bf16[128,512]{1,0:T(8,128)(2,1)S(1)} %collective-permute-done.p1), channel_id=1, source_target_pairs={{0,1},{1,0},{2,3},{3,2},{4,5},{5,4},{6,7},{7,6},{8,9},{9,8},{10,11... | collective-permute-start | bytes 393224 | tf_op jit(solution)/shard_map/ppermute | solution.py:46
  39.1 18.1 %all-to-all-start = ((f32[4,512,128]{2,1,0:T(8,128)}), f32[4,512,128]{2,1,0:T(8,128)S(1)}, u32[]{:S(2)}, u32[]{:S(2)}) async-start(f32[4,512,128]{2,1,0:T(8,128)} %copy-done.2), calls=%async_computation | async-start | bytes 2097152 | tf_op jit(solution)/shard_map/all_to_all | solution.py:356
  69.5 6.6 %collective-permute-start.12 = (bf16[528,128]{1,0:T(8,128)(2,1)S(1)}, bf16[528,128]{1,0:T(8,128)(2,1)S(1)}, u32[]{:S(2)}, u32[]{:S(2)}) collective-permute-start(bf16[528,128]{1,0:T(8,128)(2,1)S(1)} %get-tuple-element.38), channel_id=1, source_target_pairs={{0,2},{1,3},{2,4},{3,5},{4,6},{5,7},{6,0},{7,1},{8,10},{9,11},{10,... | collective-permute-start | bytes 405512 | tf_op jit(solution)/shard_map/ppermute | solution.py:42
  69.9 6.2 %collective-permute-start.13 = (bf16[528,128]{1,0:T(8,128)(2,1)S(1)}, bf16[528,128]{1,0:T(8,128)(2,1)S(1)}, u32[]{:S(2)}, u32[]{:S(2)}) collective-permute-start(bf16[528,128]{1,0:T(8,128)(2,1)S(1)} %get-tuple-element.39), channel_id=1, source_target_pairs={{0,4},{1,5},{2,6},{3,7},{4,0},{5,1},{6,2},{7,3},{8,12},{9,13},{10,... | collective-permute-start | bytes 405512 | tf_op jit(solution)/shard_map/ppermute | solution.py:42
  71.7 5.4 %collective-permute-start.14 = (bf16[528,128]{1,0:T(8,128)(2,1)S(1)}, bf16[528,128]{1,0:T(8,128)(2,1)S(1)}, u32[]{:S(2)}, u32[]{:S(2)}) collective-permute-start(bf16[528,128]{1,0:T(8,128)(2,1)S(1)} %get-tuple-element.40), channel_id=1, source_target_pairs={{0,6},{1,7},{2,0},{3,1},{4,2},{5,3},{6,4},{7,5},{8,14},{9,15},{10,... | collective-permute-start | bytes 405512 | tf_op jit(solution)/shard_map/ppermute | solution.py:42
  83.6 7.9 %collective-permute-start.19 = (bf16[128,1024]{1,0:T(8,128)(2,1)S(1)}, bf16[128,1024]{1,0:T(8,128)(2,1)S(1)}, u32[]{:S(2)}, u32[]{:S(2)}) collective-permute-start(bf16[128,1024]{1,0:T(8,128)(2,1)S(1)} %get-tuple-element.51), channel_id=1, source_target_pairs={{0,192},{8,200},{16,208},{24,216},{32,224},{40,232},{48,240},{56,2... | collective-permute-start | bytes 786440 | tf_op jit(solution)/shard_map/ppermute | solution.py:32
  84.6 7.3 %collective-permute-start.20 = (bf16[128,1024]{1,0:T(8,128)(2,1)S(1)}, bf16[128,1024]{1,0:T(8,128)(2,1)S(1)}, u32[]{:S(2)}, u32[]{:S(2)}) collective-permute-start(bf16[128,1024]{1,0:T(8,128)(2,1)S(1)} %get-tuple-element.52), channel_id=1, source_target_pairs={{0,128},{8,136},{16,144},{24,152},{32,160},{40,168},{48,176},{56,1... | collective-permute-start | bytes 786440 | tf_op jit(solution)/shard_map/ppermute | solution.py:32
  85.8 11.6 %collective-permute-start.21 = (bf16[128,1024]{1,0:T(8,128)(2,1)S(1)}, bf16[128,1024]{1,0:T(8,128)(2,1)S(1)}, u32[]{:S(2)}, u32[]{:S(2)}) collective-permute-start(bf16[128,1024]{1,0:T(8,128)(2,1)S(1)} %get-tuple-element.53), channel_id=1, source_target_pairs={{0,64},{8,72},{16,80},{24,88},{32,96},{40,104},{48,112},{56,120},{... | collective-permute-start | bytes 786440 | tf_op jit(solution)/shard_map/ppermute | solution.py:32
  85.8 22.1 %collective-permute-start.15 = (bf16[144,1024]{1,0:T(8,128)(2,1)S(1)}, bf16[144,1024]{1,0:T(8,128)(2,1)S(1)}, u32[]{:S(2)}, u32[]{:S(2)}) collective-permute-start(bf16[144,1024]{1,0:T(8,128)(2,1)S(1)} %get-tuple-element.44), channel_id=1, source_target_pairs={{0,48},{8,56},{16,0},{24,8},{32,16},{40,24},{48,32},{56,40},{64,11... | collective-permute-start | bytes 884744 | tf_op jit(solution)/shard_map/ppermute | solution.py:36
  87.1 20.7 %collective-permute-start.16 = (bf16[144,1024]{1,0:T(8,128)(2,1)S(1)}, bf16[144,1024]{1,0:T(8,128)(2,1)S(1)}, u32[]{:S(2)}, u32[]{:S(2)}) collective-permute-start(bf16[144,1024]{1,0:T(8,128)(2,1)S(1)} %get-tuple-element.45), channel_id=1, source_target_pairs={{0,32},{8,40},{16,48},{24,56},{32,0},{40,8},{48,16},{56,24},{64,96... | collective-permute-start | bytes 884744 | tf_op jit(solution)/shard_map/ppermute | solution.py:36
  91.4 17.4 %collective-permute-start.17 = (bf16[144,1024]{1,0:T(8,128)(2,1)S(1)}, bf16[144,1024]{1,0:T(8,128)(2,1)S(1)}, u32[]{:S(2)}, u32[]{:S(2)}) collective-permute-start(bf16[144,1024]{1,0:T(8,128)(2,1)S(1)} %get-tuple-element.46), channel_id=1, source_target_pairs={{0,16},{8,24},{16,32},{24,40},{32,48},{40,56},{48,0},{56,8},{64,80... | collective-permute-start | bytes 884744 | tf_op jit(solution)/shard_map/ppermute | solution.py:36
  97.6 26.6 %collective-permute-start.22 = (bf16[128,1024]{1,0:T(8,128)(2,1)S(1)}, bf16[128,1024]{1,0:T(8,128)(2,1)S(1)}, u32[]{:S(2)}, u32[]{:S(2)}) collective-permute-start(bf16[128,1024]{1,0:T(8,128)(2,1)S(1)} %fusion.1), channel_id=1, source_target_pairs={{1,9},{3,11},{5,13},{7,15},{8,0},{10,2},{12,4},{14,6},{17,25},{19,... | collective-permute-start | bytes 786440 | tf_op jit(solution)/shard_map/ppermute | solution.py:56
  109.5 13.5 %collective-permute-start.18 = (bf16[144,512]{1,0:T(8,128)(2,1)S(1)}, bf16[144,512]{1,0:T(8,128)(2,1)S(1)}, u32[]{:S(2)}, u32[]{:S(2)}) collective-permute-start(bf16[144,512]{1,0:T(8,128)(2,1)S(1)} %get-tuple-element.49), channel_id=1, source_target_pairs={{0,1},{1,0},{2,3},{3,2},{4,5},{5,4},{6,7},{7,6},{8,9},{9,8},{10,11... | collective-permute-start | bytes 442376 | tf_op jit(solution)/shard_map/ppermute | solution.py:46
  124.5 1.4 %collective-permute-start.23 = (bf16[128,512]{1,0:T(8,128)(2,1)S(1)}, bf16[128,512]{1,0:T(8,128)(2,1)S(1)}, u32[]{:S(2)}, u32[]{:S(2)}) collective-permute-start(bf16[128,512]{1,0:T(8,128)(2,1)S(1)} %broadcast_select_fusion), channel_id=1, source_target_pairs={{0,1},{1,0},{2,3},{3,2},{4,5},{5,4},{6,7},{7,6},{8,9},{9,8},{10,11... | collective-permute-start | bytes 393224 | tf_op jit(solution)/shard_map/ppermute | solution.py:46
  (6 other events, 76.0 us)

commit v3 on v2

--- a/solution.py
+++ b/solution.py
@@ -21,7 +21,6 @@
 FEAT = 8
 BOTH = ("batch", "feat")
 XZH_GROUPS = [[x * 8 + zl * 2 + zh for x in range(4) for zh in range(2)] for zl in range(4)]
-Y_GROUPS = [[y * 2 + c for y in range(4)] for c in range(2)]
 X, Y, ZL, ZH, CORE = range(5)
 
 f32 = jnp.float32
@@ -66,14 +65,16 @@
     return jax.ShapeDtypeStruct(dims_dtype[:-1], dims_dtype[-1])
 
 
-def call(body, smem, args, outs, scratch=(), flops=0, grant=8):
+def call(body, smem, args, outs, scratch=(), flops=0, grant=8, unread=0):
     vmem = pl.BlockSpec(memory_space=pltpu.VMEM)
     scalar = pl.BlockSpec(memory_space=pltpu.SMEM)
     moved = sum(a.size * a.dtype.itemsize for a in (*args, *outs))
     return pl.pallas_call(
         body,
         out_shape=outs,
-        in_specs=[scalar] * len(smem) + [vmem] * len(args),
+        in_specs=[scalar] * len(smem)
+        + [vmem] * (len(args) - unread)
+        + [pl.BlockSpec(memory_space=pl.ANY)] * unread,
         out_specs=[vmem] * len(outs),
         scratch_shapes=list(scratch),
         cost_estimate=pl.CostEstimate(
@@ -112,7 +113,7 @@
 
 
 def score_kernel(
-    ids, p0, p1, p2, p3, o0, o1, o2, o3, q0, q1, q2, q3, partial, p, q_all, pos
+    ids, p0, p1, p2, p3, o0, o1, o2, o3, q0, q1, q2, q3, s0, s1, s2, s3, p, q_all, pos
 ):
     n, width = p0.shape
     for s, (own, other) in enumerate(zip((p0, p1, p2, p3), (o0, o1, o2, o3))):
@@ -133,7 +134,8 @@
         q_all[j] = q[:n]
         digits = q[n:, :n].astype(f32)
         pos[j] = (digits[0:1] * 64.0 + digits[1:2]).astype(jnp.int32)
-        partial[j] = dot(p[...], q[:n], 1, 1)
+    for t, out in enumerate((s0, s1, s2, s3)):
+        out[...] = dot(p[...], q_all[(ids[Y] + t) & 3], 1, 1)
 
 
 def low_kernel(ids, p, q_all, pos, e_low, stats):
@@ -162,11 +164,15 @@
         stats[j] = jnp.concatenate(tops + sums + picks + [tops[0]], axis=0)
 
 
-def owner_kernel(ids, pieces, pos, low_stats, e_high, message, local):
+def owner_kernel(ids, s0, s1, s2, s3, pos, low_stats, e_high, message, local):
     n = pos.shape[2]
     hot = find_positives(ids, pos[ids[Y]], n)
-    sum5 = pieces[0] + pieces[1]
-    sum6 = sum5 + (pieces[2] + pieces[3])
+    sum5 = sum6 = None
+    for t, ref in enumerate((s0, s1, s2, s3)):
+        v = ref[...]
+        part = jnp.where(((ids[Y] + 4 - t) & 3) <= 1, v, 0.0)
+        sum5 = part if t == 0 else sum5 + part
+        sum6 = v if t == 0 else sum6 + v
     rows = []
     for i, total in enumerate((sum5, sum6)):
         scores = total * FACTORS[LOW + i]
@@ -253,27 +259,19 @@
     return v[0:1] + v[1:2] + v[2:3]
 
 
-def grad_kernel(
-    ids, weight, t0, t1, t2, t3, e_low, rates, pos, p, q_all,
-    gq0, gq1, gq2, gq3, gp0, gp1, gp2, gp3, row, tails, gq, gp,
-):
+def low_grad_kernel(ids, weight, e_low, rates, pos, p, q_all, gq, gp, tails):
     n = pos.shape[2]
-    wide = gp0.shape[1]
     on = ids[Y] == 0
-    loss = jnp.zeros((1, n), f32)
-    for t, ref in enumerate((t0, t1, t2, t3)):
-        j = (ids[Y] + 4 - t) & 3
-        lanes = pl.ds(pl.multiple_of(j * n, n), n)
-        loss += get_terms(ref, 4 * n, n)
+    for j in range(4):
         hot = find_positives(ids, pos[j], n)
-        acc = ref[: 4 * n].astype(f32)
+        acc = None
         for k in reversed(range(LOW)):
             scale = jnp.where(on, weight[k] * FACTORS[k], 0.0)
-            acc = acc + (e_low[k, j] * rates[j, k : k + 1] - jnp.where(hot, scale, 0.0))
-            tails[k, :, lanes] = acc.astype(bf16)
-    row[...] = jnp.broadcast_to(loss, row.shape)
-
-    q = q_all[...].reshape(4 * n, wide)
+            g = e_low[k, j] * rates[j, k : k + 1] - jnp.where(hot, scale, 0.0)
+            acc = g if acc is None else acc + g
+            tails[k, :, j * n : j * n + n] = acc.astype(bf16)
+
+    q = q_all[...].reshape(4 * n, q_all.shape[2])
     first = lax.broadcasted_iota(jnp.int32, (4 * n, PAIR), 1) < SMALLEST
 
     def fill(out, fn):
@@ -283,41 +281,61 @@
             out[:, begin:end] = fn(k, begin, end)
 
     fill(gq, lambda k, a, b: dot(tails[k], p[:, a:b], 0, 0))
+    fill(gp, lambda k, a, b: dot(tails[k], q[:, a:b], 1, 0))
+
+
+def grad_kernel(
+    ids, t0, t1, t2, t3, gq_low, gp_low, p, q_all,
+    gq0, gq1, gq2, gq3, own, message, row, tail, gq,
+):
+    n, wide = gq0.shape
+    width = own.shape[1]
+    loss = jnp.zeros((1, n), f32)
+    for t, ref in enumerate((t0, t1, t2, t3)):
+        j = (ids[Y] + 4 - t) & 3
+        tail[:, pl.ds(pl.multiple_of(j * n, n), n)] = ref[: 4 * n]
+        loss += get_terms(ref, 4 * n, n)
+    row[...] = jnp.broadcast_to(loss, row.shape)
+
+    q = q_all[...].reshape(4 * n, wide)
+    message[4 * n :] = jnp.zeros((EXTRA, width), bf16)
+    put_terms(message, 4 * n, loss)
+    for c in (0, 1):
+        lanes = slice(c * width, c * width + width)
+        gp = dot(tail[...], q[:, lanes], 1, 0) + gp_low[:, lanes]
+
+        @pl.when(ids[CORE] == c)
+        def _():
+            own[...] = gp
+
+        @pl.when(ids[CORE] != c)
+        def _():
+            message[: 4 * n] = gp.astype(bf16)
+
+    gq[...] = dot(tail[...], p[...], 0, 0) + gq_low[...]
     for s, out in enumerate((gq0, gq1, gq2, gq3)):
         j = (ids[X] + 4 - s) & 3
         out[...] = gq[pl.ds(pl.multiple_of(j * n, n), n), :].astype(out.dtype)
-    fill(gp, lambda k, a, b: dot(tails[k], q[:, a:b], 1, 0))
-    for s, out in enumerate((gp0, gp1, gp2, gp3)):
-        out[:n] = gp[s * n : s * n + n].astype(out.dtype)
+
+
+def core_sum_kernel(gp_own, row, other, own, m1, m2, m3, loss):
+    n, width = own.shape
+    total = row[0:1] + get_terms(other, 4 * n, n)
+    loss[...] = jnp.broadcast_to(total, loss.shape)
+    for s, out in enumerate((own, m1, m2, m3)):
+        rows = slice(s * n, s * n + n)
+        v = gp_own[rows] + other[rows].astype(f32)
+        out[:n] = v.astype(out.dtype)
         if s:
-            out[n:] = jnp.zeros((EXTRA, wide), bf16)
-            put_terms(out, n, loss)
-
-
-def passage_kernel(ids, gp0, g1, g2, g3, row, own, message, loss):
-    n, width = own.shape
-    total = row[0:1]
-    for g in (g1, g2, g3):
-        total += get_terms(g, n, n)
-    loss[...] = jnp.broadcast_to(total, loss.shape)
-    message[n:] = jnp.zeros((EXTRA, width), bf16)
-    put_terms(message, n, total)
-
-    def half(c):
-        lanes = slice(c * width, c * width + width)
-        return gp0[:, lanes] + (
-            g1[:n, lanes].astype(f32) + g2[:n, lanes].astype(f32) + g3[:n, lanes].astype(f32)
-        )
-
-    @pl.when(ids[CORE] == 0)
-    def _():
-        own[...] = half(0)
-        message[:n] = half(1).astype(bf16)
-
-    @pl.when(ids[CORE] != 0)
-    def _():
-        own[...] = half(1)
-        message[:n] = half(0).astype(bf16)
+            out[n:] = jnp.zeros((EXTRA, width), bf16)
+            put_terms(out, n, total)
+
+
+def query_sum_kernel(gq0, g1, g2, g3, *refs):
+    total, message = refs[-2:]
+    v = gq0[...] + (g1[...].astype(f32) + g2[...].astype(f32) + g3[...].astype(f32))
+    total[...] = v
+    message[...] = v.astype(bf16)
 
 
 def per_device(queries, passages, positives, level_weight):
@@ -343,24 +361,24 @@
     p_other = [swap_core(a) for a in p_own]
 
     tile = 4 * n * 4 * n
-    partial, p, q, pos = call(
+    *partial, p, q, pos = call(
         score_kernel, [ids], [*p_own, *p_other, *q_msgs],
-        [
-            shape(4, 4 * n, n, f32),
+        [shape(4 * n, n, f32)] * 4
+        + [
             shape(4 * n, wide, bf16),
             shape(4, n, wide, bf16),
             shape(4, 1, n, jnp.int32),
         ],
         flops=2 * tile * wide,
     )
-    pieces = lax.all_to_all(partial, "feat", 0, 0, axis_index_groups=Y_GROUPS)
+    pieces = [partial[0]] + [shift_y(partial[t], t) for t in (1, 2, 3)]
     e_low, low_stats = call(
         low_kernel, [ids], [p, q, pos],
         [shape(LOW, 4, 4 * n, n, f32), shape(4, 16, n, f32)],
         flops=2 * tile * wide,
     )
     e_high, message, local = call(
-        owner_kernel, [ids], [pieces, pos, low_stats],
+        owner_kernel, [ids], [*pieces, pos, low_stats],
         [shape(2, 4 * n, n, f32), shape(8, 72, n, f32), shape(72, n, f32)],
     )
     stats = lax.all_to_all(message, "batch", 0, 0, axis_index_groups=XZH_GROUPS)
@@ -369,35 +387,45 @@
         [shape(4 * n + EXTRA, n, bf16)] * 4 + [shape(4, 8, n, f32)],
     )
     tails = [tails[0]] + [shift_y(tails[t], t) for t in (1, 2, 3)]
-    gq0, gq1, gq2, gq3, gp0, gp1, gp2, gp3, row = call(
-        grad_kernel, [ids, level_weight], [*tails, e_low, rates, pos, p, q],
+    gq_low, gp_low = call(
+        low_grad_kernel, [ids, level_weight], [e_low, rates, pos, p, q],
+        [shape(4 * n, wide, f32)] * 2,
+        scratch=[pltpu.VMEM((LOW, 4 * n, 4 * n), bf16)],
+        flops=4 * tile * wide, grant=12,
+    )
+    gq0, gq1, gq2, gq3, gp_own, message, row = call(
+        grad_kernel, [ids], [*tails, gq_low, gp_low, p, q],
         [shape(n, wide, f32)]
         + [shape(n, wide, bf16)] * 3
-        + [shape(n, wide, f32)]
-        + [shape(n + EXTRA, wide, bf16)] * 3
-        + [shape(8, n, f32)],
-        scratch=[pltpu.VMEM((LOW, 4 * n, 4 * n), bf16)] + [pltpu.VMEM((4 * n, wide), f32)] * 2,
-        flops=4 * tile * wide, grant=20,
+        + [
+            shape(4 * n, width, f32),
+            shape(4 * n + EXTRA, width, bf16),
+            shape(8, n, f32),
+        ],
+        scratch=[pltpu.VMEM((4 * n, 4 * n), bf16), pltpu.VMEM((4 * n, wide), f32)],
+        flops=4 * tile * wide, grant=12,
     )
     gq = [shift_x(g, -s) for s, g in enumerate((gq1, gq2, gq3), 1)]
-    gp = [shift_zl(g, -s) for s, g in enumerate((gp1, gp2, gp3), 1)]
-
-    own, message, loss_row = call(
-        passage_kernel, [ids], [gp0, *gp, row],
-        [shape(n, width, f32), shape(n + EXTRA, width, bf16), shape(8, n, f32)],
-    )
-    other = swap_core(message).astype(f32)
-    grad_passages = (own + other[:n]).astype(bf16)
-    loss_row = loss_row[0] + (other[n, :n] + other[n + 1, :n] + other[n + 2, :n])
-    loss = jnp.sum(loss_row) / (n * BATCH)
-
-    gq_sum = gq0 + sum(g.astype(f32) for g in gq)
-    far = move_square(gq_sum.astype(bf16), lambda h, c: None if h == c else (1 - h, c))
+
+    own, *messages, loss_row = call(
+        core_sum_kernel, [], [gp_own, row, swap_core(message)],
+        [shape(n, width, f32)] + [shape(n + EXTRA, width, bf16)] * 3 + [shape(8, n, f32)],
+    )
+    gp = [shift_zl(m, -s) for s, m in enumerate(messages, 1)]
+    gq_sum, gq_message = call(
+        query_sum_kernel, [], [gq0, *gq, *messages],
+        [shape(n, wide, f32), shape(n, wide, bf16)], unread=3,
+    )
+    far = move_square(gq_message, lambda h, c: None if h == c else (1 - h, c))
     gq_sum = (gq_sum + far.astype(f32)).astype(bf16)
     left, right = gq_sum[:, :width], gq_sum[:, width:]
     other = swap_core(jnp.where(core == 0, right, left))
     grad_queries = jnp.where(same, jnp.where(core == 0, left, right), other)
-    return loss, grad_queries, grad_passages
+
+    grad_passages = own + sum(g[:n].astype(f32) for g in gp)
+    loss_row = loss_row[0] + sum(jnp.sum(g[n : n + 3, :n].astype(f32), axis=0) for g in gp)
+    loss = jnp.sum(loss_row) / (n * BATCH)
+    return loss, grad_queries, grad_passages.astype(bf16)
 
 
 def solution(mesh):

time: 128 us -> 109 us (0.85)
  waiting for transfers between devices: 40.1 us -> 18.2 us
  local copies, waits for them, and re-layouts: 6.8 us -> 1 us
  blocking collectives: 10.4 us -> 15 us
  starting transfers between devices: 51.2 us -> 54.1 us
  Pallas kernels: 12.7 us -> 14.5 us
    ppermute x6, waiting for transfers between devices: 12.4 us -> 0.8 us  [shift_zl(): lax.ppermute(a, 'batch', [(b, b // 8 * 8 + (b + 2 * s) % 8) for b in rang...]
    all_to_all x1 -> x0, waiting for transfers between devices: 7.98 us -> none  [per_device(): pieces = lax.all_to_all(partial, 'feat', 0, 0, axis_index_groups=Y_GROUPS)]
    ppermute x3 -> x6, starting transfers between devices: 2.86 us -> 9.45 us  [shift_y(): lax.ppermute(a, 'feat', [(f, (f + 2 * s) % FEAT) for f in range(FEAT)])]
    unnamed x10 -> x4, local copies, waits for them, and re-layouts: 6.71 us -> 0.91 us
    all_to_all x1, blocking collectives: 10.4 us -> 15 us  [per_device(): stats = lax.all_to_all(message, 'batch', 0, 0, axis_index_groups=XZH_GROUPS)]
    ppermute x6, waiting for transfers between devices: 11.4 us -> 7.16 us  [shift_x(): lax.ppermute(a, 'batch', [(b, (b + 8 * s) % BATCH) for b in range(BATCH)])]
    all_to_all x1 -> x0, starting transfers between devices: 4.18 us -> none  [per_device(): pieces = lax.all_to_all(partial, 'feat', 0, 0, axis_index_groups=Y_GROUPS)]
    ppermute x6, starting transfers between devices: 15.4 us -> 11.9 us  [swap_core(): return lax.ppermute(a, 'feat', [(f, f ^ 1) for f in range(FEAT)])]
  transfers between devices with their start and end apart: 25 -> 27, of which waited for: 13 -> 13; matrix products, arithmetic and copies ran while one was open for 1% -> 1% of each run, Pallas kernels for 4% -> 7%
where the time goes in v3:
time: 109 us
  starting transfers between devices  54.1 us (50%)
  waiting for transfers between devices  18.2 us (17%)
  blocking collectives  15 us (14%)
  Pallas kernels  14.5 us (13%)
  other arithmetic  3.73 us (3%)
  between operations  2.58 us (2%)
    ppermute x6, starting transfers between devices, shift_zl(): lax.ppermute(a, 'batch', [(b, b // 8 * 8 + (b + 2 * s) % 8) for b in rang...  17.6 us
    all_to_all x1, blocking collectives, per_device(): stats = lax.all_to_all(message, 'batch', 0, 0, axis_index_groups=XZH_GROUPS)  15 us
    pallas_call x9, Pallas kernels, call(): pl.pallas_call(body, out_shape=outs, in_specs=[scalar] * len(smem) + [vme...  14.5 us
    ppermute x6, starting transfers between devices, swap_core(): return lax.ppermute(a, 'feat', [(f, f ^ 1) for f in range(FEAT)])  11.9 us
    ppermute x6, starting transfers between devices, shift_y(): lax.ppermute(a, 'feat', [(f, (f + 2 * s) % FEAT) for f in range(FEAT)])  9.45 us
    ppermute x6, starting transfers between devices, shift_x(): lax.ppermute(a, 'batch', [(b, (b + 8 * s) % BATCH) for b in range(BATCH)])  7.83 us
    ppermute x3, starting transfers between devices, move_square(): return lax.ppermute(a, BOTH, pairs)  7.35 us
    ppermute x6, waiting for transfers between devices, shift_x(): lax.ppermute(a, 'batch', [(b, (b + 8 * s) % BATCH) for b in range(BATCH)])  7.16 us
  transfers between devices with their start and end apart: 27, of which 13 were waited for; matrix products, arithmetic and copies ran while one was open for 1% of the time, Pallas kernels for 7%

profile of v3, /device:TPU:1, one launch (start us, length us, event | category | flops | bytes accessed | tf_op | source)
XLA Modules:
  0.0 109.0 jit_solution(16751217189629507665)
XLA Ops:
  2.2 4.9 %collective-permute-start.8 = (bf16[144,512]{1,0:T(8,128)(2,1)S(1)}, bf16[144,512]{1,0:T(8,128)(2,1)S(1)}, u32[]{:S(2)}, u32[]{:S(2)}) collective-permute-start(bf16[144,512]{1,0:T(8,128)(2,1)S(1)} %pad_maximum_fusion.own), channel_id=1, source_target_pairs={{1,8},{3,10},{5,12},{7,14},{8,1},{10,3},{12,5},{14,7},{17,24},{19,... | collective-permute-start | bytes 442376 | tf_op jit(solution)/shard_map/ppermute | solution.py:55
  7.3 3.1 %collective-permute-start = (bf16[128,512]{1,0:T(8,128)(2,1)}, bf16[128,512]{1,0:T(8,128)(2,1)S(1)}, u32[]{:S(2)}, u32[]{:S(2)}) collective-permute-start(bf16[128,512]{1,0:T(8,128)(2,1)} %p0.1), channel_id=1, source_target_pairs={{0,16},{8,24},{16,32},{24,40},{32,48},{40,56},{48,0},{56,8},{64,80... | collective-permute-start | bytes 393224 | tf_op jit(solution)/shard_map/ppermute | solution.py:35
  10.3 4.2 %collective-permute-start.1 = (bf16[128,512]{1,0:T(8,128)(2,1)}, bf16[128,512]{1,0:T(8,128)(2,1)S(1)}, u32[]{:S(2)}, u32[]{:S(2)}) collective-permute-start(bf16[128,512]{1,0:T(8,128)(2,1)} %p0.1), channel_id=1, source_target_pairs={{0,32},{8,40},{16,48},{24,56},{32,0},{40,8},{48,16},{56,24},{64,96... | collective-permute-start | bytes 393224 | tf_op jit(solution)/shard_map/ppermute | solution.py:35
  14.6 2.4 %collective-permute-start.2 = (bf16[128,512]{1,0:T(8,128)(2,1)}, bf16[128,512]{1,0:T(8,128)(2,1)S(1)}, u32[]{:S(2)}, u32[]{:S(2)}) collective-permute-start(bf16[128,512]{1,0:T(8,128)(2,1)} %p0.1), channel_id=1, source_target_pairs={{0,48},{8,56},{16,0},{24,8},{32,16},{40,24},{48,32},{56,40},{64,11... | collective-permute-start | bytes 393224 | tf_op jit(solution)/shard_map/ppermute | solution.py:35
  18.9 2.5 %collective-permute-start.10 = (bf16[144,1024]{1,0:T(8,128)(2,1)S(1)}, bf16[144,1024]{1,0:T(8,128)(2,1)S(1)}, u32[]{:S(2)}, u32[]{:S(2)}) collective-permute-start(bf16[144,1024]{1,0:T(8,128)(2,1)S(1)} %shard_map.67.q0), channel_id=1, source_target_pairs={{0,128},{8,136},{16,144},{24,152},{32,160},{40,168},{48,176},{56,1... | collective-permute-start | bytes 884744 | tf_op jit(solution)/shard_map/ppermute | solution.py:31
  21.4 2.0 %collective-permute-start.11 = (bf16[144,1024]{1,0:T(8,128)(2,1)S(1)}, bf16[144,1024]{1,0:T(8,128)(2,1)S(1)}, u32[]{:S(2)}, u32[]{:S(2)}) collective-permute-start(bf16[144,1024]{1,0:T(8,128)(2,1)S(1)} %shard_map.67.q0), channel_id=1, source_target_pairs={{0,192},{8,200},{16,208},{24,216},{32,224},{40,232},{48,240},{56,2... | collective-permute-start | bytes 884744 | tf_op jit(solution)/shard_map/ppermute | solution.py:31
  24.2 5.1 %collective-permute-start.3 = (bf16[128,512]{1,0:T(8,128)(2,1)}, bf16[128,512]{1,0:T(8,128)(2,1)S(1)}, u32[]{:S(2)}, u32[]{:S(2)}) collective-permute-start(bf16[128,512]{1,0:T(8,128)(2,1)} %p0.1), channel_id=1, source_target_pairs={{0,1},{1,0},{2,3},{3,2},{4,5},{5,4},{6,7},{7,6},{8,9},{9,8},{10,11... | collective-permute-start | bytes 393224 | tf_op jit(solution)/shard_map/ppermute | solution.py:45
  34.0 2.0 %shard_map.68 = (f32[512,128]{1,0:T(8,128)S(1)}, f32[512,128]{1,0:T(8,128)S(1)}, f32[512,128]{1,0:T(8,128)S(1)}, f32[512,128]{1,0:T(8,128)S(1)}, bf16[512,1024]{...) custom-call(s32[5]{0:T(128)S(1)} %stack.35.ids, bf16[128,512]{1,0:T(8,128)(2,1)S(1)} %copy-done, ...), custom_call_target="tpu_custom_call" | custom-call | flops 536870912 | bytes 5376000 | tf_op jit(solution)/shard_map/pallas_call | solution.py:72
  36.0 1.4 %collective-permute-start.12 = (f32[512,128]{1,0:T(8,128)S(1)}, f32[512,128]{1,0:T(8,128)S(1)}, u32[]{:S(2)}, u32[]{:S(2)}) collective-permute-start(f32[512,128]{1,0:T(8,128)S(1)} %get-tuple-element.37), channel_id=1, source_target_pairs={{0,2},{1,3},{2,4},{3,5},{4,6},{5,7},{6,0},{7,1},{8,10},{9,11},{10,... | collective-permute-start | bytes 786440 | tf_op jit(solution)/shard_map/ppermute | solution.py:41
  37.4 2.6 %collective-permute-start.13 = (f32[512,128]{1,0:T(8,128)S(1)}, f32[512,128]{1,0:T(8,128)S(1)}, u32[]{:S(2)}, u32[]{:S(2)}) collective-permute-start(f32[512,128]{1,0:T(8,128)S(1)} %get-tuple-element.38), channel_id=1, source_target_pairs={{0,4},{1,5},{2,6},{3,7},{4,0},{5,1},{6,2},{7,3},{8,12},{9,13},{10,... | collective-permute-start | bytes 786440 | tf_op jit(solution)/shard_map/ppermute | solution.py:41
  41.1 3.7 %shard_map.69 = (f32[5,4,512,128]{3,2,1,0:T(8,128)S(1)}, f32[4,16,128]{2,1,0:T(8,128)S(1)}) custom-call(s32[5]{0:T(128)S(1)} %stack.35.ids, bf16[512,1024]{1,0:T(8,128)(2,1)S(1)} %get-tuple-element.41.p, bf16[4,128,1024]{2,1,0:T(8,128)(2,1)S(1)} %get-tuple-element.42.q_all, s32[4,1,128]{2,1,0:T(1,128)S(1)} %get-tuple-element.40.pos), custom_call_target="tpu_custom_call" | custom-call | flops 536870912 | bytes 7374848 | tf_op jit(solution)/shard_map/pallas_call | solution.py:72
  44.8 4.4 %collective-permute-done.13.s2 = f32[512,128]{1,0:T(8,128)S(1)} collective-permute-done((f32[512,128]{1,0:T(8,128)S(1)}, f32[512,128]{1,0:T(8,128)S(1)}, u32[]{:S(2)}, u32[]{:S(2)}) %collective-permute-start.13) | collective-permute-done | bytes 262176 | tf_op jit(solution)/shard_map/ppermute | solution.py:41
  50.4 15.0 %all_to_all.5.stats = f32[8,72,128]{2,1,0:T(8,128)S(1)} all-to-all(f32[8,72,128]{2,1,0:T(8,128)S(1)} %get-tuple-element.44), channel_id=1, replica_groups={{0,8,64,72,128,136,192,200},{16,24,80,88,144,152,208,216},{32,40,96,104..., dimensions={0} | all-to-all | bytes 589824 | tf_op jit(solution)/shard_map/all_to_all | solution.py:384
  67.5 3.2 %collective-permute-start.16 = (bf16[528,128]{1,0:T(8,128)(2,1)S(1)}, bf16[528,128]{1,0:T(8,128)(2,1)S(1)}, u32[]{:S(2)}, u32[]{:S(2)}) collective-permute-start(bf16[528,128]{1,0:T(8,128)(2,1)S(1)} %get-tuple-element.49), channel_id=1, source_target_pairs={{0,4},{1,5},{2,6},{3,7},{4,0},{5,1},{6,2},{7,3},{8,12},{9,13},{10,... | collective-permute-start | bytes 405512 | tf_op jit(solution)/shard_map/ppermute | solution.py:41
  70.7 3.4 %shard_map.72 = (f32[512,1024]{1,0:T(8,128)S(1)}, f32[512,1024]{1,0:T(8,128)S(1)}) custom-call(s32[5]{0:T(128)S(1)} %stack.35.ids, f32[7]{0:T(128)S(1)} %copy-done.1, f32[5,4,512,128]{3,2,1,0:T(8,128)S(1)} %get-tuple-element.51.e_low, f32[4,8,128]{2,1,0:T(8,128)S(1)} %get-tuple-element.52.rates, s32[4,1,128]{2,1,0:T(1,128)S(1)} %get-tuple-element.40.pos, ...), custom_call_target="tpu_custom_call" | custom-call | flops 1073741824 | bytes 11552768 | tf_op jit(solution)/shard_map/pallas_call | solution.py:72
  75.3 2.5 %shard_map.73 = (f32[128,1024]{1,0:T(8,128)S(1)}, bf16[128,1024]{1,0:T(8,128)(2,1)S(1)}, bf16[128,1024]{1,0:T(8,128)(2,1)S(1)}, bf16[128,1024]{1,0:T(8,128)(2,1)...) custom-call(s32[5]{0:T(128)S(1)} %stack.35.ids, ...), custom_call_target="tpu_custom_call" | custom-call | flops 1073741824 | bytes 9736192 | tf_op jit(solution)/shard_map/pallas_call | solution.py:72
  77.9 2.9 %collective-permute-start.18 = (bf16[528,512]{1,0:T(8,128)(2,1)S(1)}, bf16[528,512]{1,0:T(8,128)(2,1)S(1)}, u32[]{:S(2)}, u32[]{:S(2)}) collective-permute-start(bf16[528,512]{1,0:T(8,128)(2,1)S(1)} %get-tuple-element.57), channel_id=1, source_target_pairs={{0,1},{1,0},{2,3},{3,2},{4,5},{5,4},{6,7},{7,6},{8,9},{9,8},{10,11... | collective-permute-start | bytes 1622024 | tf_op jit(solution)/shard_map/ppermute | solution.py:45
  83.2 3.5 %collective-permute-start.19 = (bf16[144,512]{1,0:T(8,128)(2,1)S(1)}, bf16[144,512]{1,0:T(8,128)(2,1)S(1)}, u32[]{:S(2)}, u32[]{:S(2)}) collective-permute-start(bf16[144,512]{1,0:T(8,128)(2,1)S(1)} %get-tuple-element.59.refs_0_), channel_id=1, source_target_pairs={{0,48},{8,56},{16,0},{24,8},{32,16},{40,24},{48,32},{56,40},{64,11... | collective-permute-start | bytes 442376 | tf_op jit(solution)/shard_map/ppermute | solution.py:35
  86.7 2.0 %collective-permute-done.22.g1 = bf16[128,1024]{1,0:T(8,128)(2,1)S(1)} collective-permute-done((bf16[128,1024]{1,0:T(8,128)(2,1)S(1)}, bf16[128,1024]{1,0:T(8,128)(2,1)S(1)}, u32[]{:S(2)}, u32[]{:S(2)}) %collective-permute-start.22) | collective-permute-done | bytes 262176 | tf_op jit(solution)/shard_map/ppermute | solution.py:31
  88.7 4.3 %collective-permute-start.20 = (bf16[144,512]{1,0:T(8,128)(2,1)S(1)}, bf16[144,512]{1,0:T(8,128)(2,1)S(1)}, u32[]{:S(2)}, u32[]{:S(2)}) collective-permute-start(bf16[144,512]{1,0:T(8,128)(2,1)S(1)} %get-tuple-element.60.refs_1_), channel_id=1, source_target_pairs={{0,32},{8,40},{16,48},{24,56},{32,0},{40,8},{48,16},{56,24},{64,96... | collective-permute-start | bytes 442376 | tf_op jit(solution)/shard_map/ppermute | solution.py:35
  93.0 4.2 %collective-permute-done.24.g3 = bf16[128,1024]{1,0:T(8,128)(2,1)S(1)} collective-permute-done((bf16[128,1024]{1,0:T(8,128)(2,1)S(1)}, bf16[128,1024]{1,0:T(8,128)(2,1)S(1)}, u32[]{:S(2)}, u32[]{:S(2)}) %collective-permute-start.24) | collective-permute-done | bytes 262176 | tf_op jit(solution)/shard_map/ppermute | solution.py:31
  97.3 2.3 %collective-permute-start.25 = (bf16[128,1024]{1,0:T(8,128)(2,1)S(1)}, bf16[128,1024]{1,0:T(8,128)(2,1)S(1)}, u32[]{:S(2)}, u32[]{:S(2)}) collective-permute-start(bf16[128,1024]{1,0:T(8,128)(2,1)S(1)} %get-tuple-element.67), channel_id=1, source_target_pairs={{1,9},{3,11},{5,13},{7,15},{8,0},{10,2},{12,4},{14,6},{17,25},{19,... | collective-permute-start | bytes 786440 | tf_op jit(solution)/shard_map/ppermute | solution.py:55
  101.0 1.9 %collective-permute-done.25 = bf16[128,1024]{1,0:T(8,128)(2,1)S(1)} collective-permute-done((bf16[128,1024]{1,0:T(8,128)(2,1)S(1)}, bf16[128,1024]{1,0:T(8,128)(2,1)S(1)}, u32[]{:S(2)}, u32[]{:S(2)}) %collective-permute-start.25) | collective-permute-done | bytes 262176 | tf_op jit(solution)/shard_map/ppermute | solution.py:55
  103.0 3.2 %collective-permute-start.26 = (bf16[128,512]{1,0:T(8,128)(2,1)S(1)}, bf16[128,512]{1,0:T(8,128)(2,1)S(1)}, u32[]{:S(2)}, u32[]{:S(2)}) collective-permute-start(bf16[128,512]{1,0:T(8,128)(2,1)S(1)} %broadcast_select_fusion), channel_id=1, source_target_pairs={{0,1},{1,0},{2,3},{3,2},{4,5},{5,4},{6,7},{7,6},{8,9},{9,8},{10,11... | collective-permute-start | bytes 393224 | tf_op jit(solution)/shard_map/ppermute | solution.py:45
  (56 shorter events, 19.7 us)
Async XLA Ops:
  2.2 14.8 %collective-permute-start.8 = (bf16[144,512]{1,0:T(8,128)(2,1)S(1)}, bf16[144,512]{1,0:T(8,128)(2,1)S(1)}, u32[]{:S(2)}, u32[]{:S(2)}) collective-permute-start(bf16[144,512]{1,0:T(8,128)(2,1)S(1)} %pad_maximum_fusion.own), channel_id=1, source_target_pairs={{1,8},{3,10},{5,12},{7,14},{8,1},{10,3},{12,5},{14,7},{17,24},{19,... | collective-permute-start | bytes 442376 | tf_op jit(solution)/shard_map/ppermute | solution.py:55
  7.2 9.9 %collective-permute-start.7 = (bf16[128,512]{1,0:T(8,128)(2,1)}, bf16[128,512]{1,0:T(8,128)(2,1)S(1)}, u32[]{:S(2)}, u32[]{:S(2)}) collective-permute-start(bf16[128,512]{1,0:T(8,128)(2,1)} %param.4), channel_id=1, source_target_pairs={{0,8},{1,0},{2,10},{3,2},{4,12},{5,4},{6,14},{7,6},{8,9},{9,1},{10... | collective-permute-start | bytes 393224 | tf_op jit(solution)/shard_map/ppermute | solution.py:55
  7.3 14.1 %collective-permute-start = (bf16[128,512]{1,0:T(8,128)(2,1)}, bf16[128,512]{1,0:T(8,128)(2,1)S(1)}, u32[]{:S(2)}, u32[]{:S(2)}) collective-permute-start(bf16[128,512]{1,0:T(8,128)(2,1)} %p0.1), channel_id=1, source_target_pairs={{0,16},{8,24},{16,32},{24,40},{32,48},{40,56},{48,0},{56,8},{64,80... | collective-permute-start | bytes 393224 | tf_op jit(solution)/shard_map/ppermute | solution.py:35
  10.3 13.8 %collective-permute-start.1 = (bf16[128,512]{1,0:T(8,128)(2,1)}, bf16[128,512]{1,0:T(8,128)(2,1)S(1)}, u32[]{:S(2)}, u32[]{:S(2)}) collective-permute-start(bf16[128,512]{1,0:T(8,128)(2,1)} %p0.1), channel_id=1, source_target_pairs={{0,32},{8,40},{16,48},{24,56},{32,0},{40,8},{48,16},{56,24},{64,96... | collective-permute-start | bytes 393224 | tf_op jit(solution)/shard_map/ppermute | solution.py:35
  14.6 14.7 %collective-permute-start.2 = (bf16[128,512]{1,0:T(8,128)(2,1)}, bf16[128,512]{1,0:T(8,128)(2,1)S(1)}, u32[]{:S(2)}, u32[]{:S(2)}) collective-permute-start(bf16[128,512]{1,0:T(8,128)(2,1)} %p0.1), channel_id=1, source_target_pairs={{0,48},{8,56},{16,0},{24,8},{32,16},{40,24},{48,32},{56,40},{64,11... | collective-permute-start | bytes 393224 | tf_op jit(solution)/shard_map/ppermute | solution.py:35
  17.6 14.6 %collective-permute-start.9 = (bf16[144,1024]{1,0:T(8,128)(2,1)S(1)}, bf16[144,1024]{1,0:T(8,128)(2,1)S(1)}, u32[]{:S(2)}, u32[]{:S(2)}) collective-permute-start(bf16[144,1024]{1,0:T(8,128)(2,1)S(1)} %shard_map.67.q0), channel_id=1, source_target_pairs={{0,64},{8,72},{16,80},{24,88},{32,96},{40,104},{48,112},{56,120},{... | collective-permute-start | bytes 884744 | tf_op jit(solution)/shard_map/ppermute | solution.py:31
  18.9 14.2 %collective-permute-start.10 = (bf16[144,1024]{1,0:T(8,128)(2,1)S(1)}, bf16[144,1024]{1,0:T(8,128)(2,1)S(1)}, u32[]{:S(2)}, u32[]{:S(2)}) collective-permute-start(bf16[144,1024]{1,0:T(8,128)(2,1)S(1)} %shard_map.67.q0), channel_id=1, source_target_pairs={{0,128},{8,136},{16,144},{24,152},{32,160},{40,168},{48,176},{56,1... | collective-permute-start | bytes 884744 | tf_op jit(solution)/shard_map/ppermute | solution.py:31
  21.4 11.8 %collective-permute-start.11 = (bf16[144,1024]{1,0:T(8,128)(2,1)S(1)}, bf16[144,1024]{1,0:T(8,128)(2,1)S(1)}, u32[]{:S(2)}, u32[]{:S(2)}) collective-permute-start(bf16[144,1024]{1,0:T(8,128)(2,1)S(1)} %shard_map.67.q0), channel_id=1, source_target_pairs={{0,192},{8,200},{16,208},{24,216},{32,224},{40,232},{48,240},{56,2... | collective-permute-start | bytes 884744 | tf_op jit(solution)/shard_map/ppermute | solution.py:31
  24.2 6.3 %collective-permute-start.3 = (bf16[128,512]{1,0:T(8,128)(2,1)}, bf16[128,512]{1,0:T(8,128)(2,1)S(1)}, u32[]{:S(2)}, u32[]{:S(2)}) collective-permute-start(bf16[128,512]{1,0:T(8,128)(2,1)} %p0.1), channel_id=1, source_target_pairs={{0,1},{1,0},{2,3},{3,2},{4,5},{5,4},{6,7},{7,6},{8,9},{9,8},{10,11... | collective-permute-start | bytes 393224 | tf_op jit(solution)/shard_map/ppermute | solution.py:45
  36.0 8.8 %collective-permute-start.12 = (f32[512,128]{1,0:T(8,128)S(1)}, f32[512,128]{1,0:T(8,128)S(1)}, u32[]{:S(2)}, u32[]{:S(2)}) collective-permute-start(f32[512,128]{1,0:T(8,128)S(1)} %get-tuple-element.37), channel_id=1, source_target_pairs={{0,2},{1,3},{2,4},{3,5},{4,6},{5,7},{6,0},{7,1},{8,10},{9,11},{10,... | collective-permute-start | bytes 786440 | tf_op jit(solution)/shard_map/ppermute | solution.py:41
  37.4 11.7 %collective-permute-start.13 = (f32[512,128]{1,0:T(8,128)S(1)}, f32[512,128]{1,0:T(8,128)S(1)}, u32[]{:S(2)}, u32[]{:S(2)}) collective-permute-start(f32[512,128]{1,0:T(8,128)S(1)} %get-tuple-element.38), channel_id=1, source_target_pairs={{0,4},{1,5},{2,6},{3,7},{4,0},{5,1},{6,2},{7,3},{8,12},{9,13},{10,... | collective-permute-start | bytes 786440 | tf_op jit(solution)/shard_map/ppermute | solution.py:41
  40.0 9.3 %collective-permute-start.14 = (f32[512,128]{1,0:T(8,128)S(1)}, f32[512,128]{1,0:T(8,128)S(1)}, u32[]{:S(2)}, u32[]{:S(2)}) collective-permute-start(f32[512,128]{1,0:T(8,128)S(1)} %get-tuple-element.39), channel_id=1, source_target_pairs={{0,6},{1,7},{2,0},{3,1},{4,2},{5,3},{6,4},{7,5},{8,14},{9,15},{10,... | collective-permute-start | bytes 786440 | tf_op jit(solution)/shard_map/ppermute | solution.py:41
  66.3 7.8 %collective-permute-start.15 = (bf16[528,128]{1,0:T(8,128)(2,1)S(1)}, bf16[528,128]{1,0:T(8,128)(2,1)S(1)}, u32[]{:S(2)}, u32[]{:S(2)}) collective-permute-start(bf16[528,128]{1,0:T(8,128)(2,1)S(1)} %get-tuple-element.48), channel_id=1, source_target_pairs={{0,2},{1,3},{2,4},{3,5},{4,6},{5,7},{6,0},{7,1},{8,10},{9,11},{10,... | collective-permute-start | bytes 405512 | tf_op jit(solution)/shard_map/ppermute | solution.py:41
  67.5 7.6 %collective-permute-start.16 = (bf16[528,128]{1,0:T(8,128)(2,1)S(1)}, bf16[528,128]{1,0:T(8,128)(2,1)S(1)}, u32[]{:S(2)}, u32[]{:S(2)}) collective-permute-start(bf16[528,128]{1,0:T(8,128)(2,1)S(1)} %get-tuple-element.49), channel_id=1, source_target_pairs={{0,4},{1,5},{2,6},{3,7},{4,0},{5,1},{6,2},{7,3},{8,12},{9,13},{10,... | collective-permute-start | bytes 405512 | tf_op jit(solution)/shard_map/ppermute | solution.py:41
  70.7 4.6 %collective-permute-start.17 = (bf16[528,128]{1,0:T(8,128)(2,1)S(1)}, bf16[528,128]{1,0:T(8,128)(2,1)S(1)}, u32[]{:S(2)}, u32[]{:S(2)}) collective-permute-start(bf16[528,128]{1,0:T(8,128)(2,1)S(1)} %get-tuple-element.50), channel_id=1, source_target_pairs={{0,6},{1,7},{2,0},{3,1},{4,2},{5,3},{6,4},{7,5},{8,14},{9,15},{10,... | collective-permute-start | bytes 405512 | tf_op jit(solution)/shard_map/ppermute | solution.py:41
  77.9 5.0 %collective-permute-start.18 = (bf16[528,512]{1,0:T(8,128)(2,1)S(1)}, bf16[528,512]{1,0:T(8,128)(2,1)S(1)}, u32[]{:S(2)}, u32[]{:S(2)}) collective-permute-start(bf16[528,512]{1,0:T(8,128)(2,1)S(1)} %get-tuple-element.57), channel_id=1, source_target_pairs={{0,1},{1,0},{2,3},{3,2},{4,5},{5,4},{6,7},{7,6},{8,9},{9,8},{10,11... | collective-permute-start | bytes 1622024 | tf_op jit(solution)/shard_map/ppermute | solution.py:45
  80.8 7.9 %collective-permute-start.22 = (bf16[128,1024]{1,0:T(8,128)(2,1)S(1)}, bf16[128,1024]{1,0:T(8,128)(2,1)S(1)}, u32[]{:S(2)}, u32[]{:S(2)}) collective-permute-start(bf16[128,1024]{1,0:T(8,128)(2,1)S(1)} %get-tuple-element.63), channel_id=1, source_target_pairs={{0,192},{8,200},{16,208},{24,216},{32,224},{40,232},{48,240},{56,2... | collective-permute-start | bytes 786440 | tf_op jit(solution)/shard_map/ppermute | solution.py:31
  81.8 11.1 %collective-permute-start.23 = (bf16[128,1024]{1,0:T(8,128)(2,1)S(1)}, bf16[128,1024]{1,0:T(8,128)(2,1)S(1)}, u32[]{:S(2)}, u32[]{:S(2)}) collective-permute-start(bf16[128,1024]{1,0:T(8,128)(2,1)S(1)} %get-tuple-element.64), channel_id=1, source_target_pairs={{0,128},{8,136},{16,144},{24,152},{32,160},{40,168},{48,176},{56,1... | collective-permute-start | bytes 786440 | tf_op jit(solution)/shard_map/ppermute | solution.py:31
  82.9 14.3 %collective-permute-start.24 = (bf16[128,1024]{1,0:T(8,128)(2,1)S(1)}, bf16[128,1024]{1,0:T(8,128)(2,1)S(1)}, u32[]{:S(2)}, u32[]{:S(2)}) collective-permute-start(bf16[128,1024]{1,0:T(8,128)(2,1)S(1)} %get-tuple-element.65), channel_id=1, source_target_pairs={{0,64},{8,72},{16,80},{24,88},{32,96},{40,104},{48,112},{56,120},{... | collective-permute-start | bytes 786440 | tf_op jit(solution)/shard_map/ppermute | solution.py:31
  83.0 16.6 %collective-permute-start.21 = (bf16[144,512]{1,0:T(8,128)(2,1)S(1)}, bf16[144,512]{1,0:T(8,128)(2,1)S(1)}, u32[]{:S(2)}, u32[]{:S(2)}) collective-permute-start(bf16[144,512]{1,0:T(8,128)(2,1)S(1)} %get-tuple-element.61.refs_2_), channel_id=1, source_target_pairs={{0,16},{8,24},{16,32},{24,40},{32,48},{40,56},{48,0},{56,8},{64,80... | collective-permute-start | bytes 442376 | tf_op jit(solution)/shard_map/ppermute | solution.py:35
  83.2 16.5 %collective-permute-start.19 = (bf16[144,512]{1,0:T(8,128)(2,1)S(1)}, bf16[144,512]{1,0:T(8,128)(2,1)S(1)}, u32[]{:S(2)}, u32[]{:S(2)}) collective-permute-start(bf16[144,512]{1,0:T(8,128)(2,1)S(1)} %get-tuple-element.59.refs_0_), channel_id=1, source_target_pairs={{0,48},{8,56},{16,0},{24,8},{32,16},{40,24},{48,32},{56,40},{64,11... | collective-permute-start | bytes 442376 | tf_op jit(solution)/shard_map/ppermute | solution.py:35
  88.7 11.0 %collective-permute-start.20 = (bf16[144,512]{1,0:T(8,128)(2,1)S(1)}, bf16[144,512]{1,0:T(8,128)(2,1)S(1)}, u32[]{:S(2)}, u32[]{:S(2)}) collective-permute-start(bf16[144,512]{1,0:T(8,128)(2,1)S(1)} %get-tuple-element.60.refs_1_), channel_id=1, source_target_pairs={{0,32},{8,40},{16,48},{24,56},{32,0},{40,8},{48,16},{56,24},{64,96... | collective-permute-start | bytes 442376 | tf_op jit(solution)/shard_map/ppermute | solution.py:35
  97.3 5.6 %collective-permute-start.25 = (bf16[128,1024]{1,0:T(8,128)(2,1)S(1)}, bf16[128,1024]{1,0:T(8,128)(2,1)S(1)}, u32[]{:S(2)}, u32[]{:S(2)}) collective-permute-start(bf16[128,1024]{1,0:T(8,128)(2,1)S(1)} %get-tuple-element.67), channel_id=1, source_target_pairs={{1,9},{3,11},{5,13},{7,15},{8,0},{10,2},{12,4},{14,6},{17,25},{19,... | collective-permute-start | bytes 786440 | tf_op jit(solution)/shard_map/ppermute | solution.py:55
  103.0 4.2 %collective-permute-start.26 = (bf16[128,512]{1,0:T(8,128)(2,1)S(1)}, bf16[128,512]{1,0:T(8,128)(2,1)S(1)}, u32[]{:S(2)}, u32[]{:S(2)}) collective-permute-start(bf16[128,512]{1,0:T(8,128)(2,1)S(1)} %broadcast_select_fusion), channel_id=1, source_target_pairs={{0,1},{1,0},{2,3},{3,2},{4,5},{5,4},{6,7},{7,6},{8,9},{9,8},{10,11... | collective-permute-start | bytes 393224 | tf_op jit(solution)/shard_map/ppermute | solution.py:45
  (5 other events, 34.5 us)

commit v4 on v3

v4 whole, which is shorter than its diff:
```python
import math

import jax
import jax.numpy as jnp
from jax import lax
from jax.experimental import pallas as pl
from jax.experimental.pallas import tpu as pltpu
from jax.sharding import PartitionSpec as P

SMALLEST = 64
LEVELS = 7
LOW = 5
SHARPNESS = 3.0
WIDTHS = [SMALLEST * 2**k for k in range(LEVELS)]
FACTORS = [SHARPNESS / math.sqrt(w) for w in WIDTHS]
SPANS = list(zip([0] + WIDTHS[: LOW - 1], WIDTHS[:LOW]))
EXTRA = 16
PAIR = 2 * SMALLEST

BATCH = 32
FEAT = 8
BOTH = ("batch", "feat")
STAT_GROUPS = [
    [(x * 8 + zl * 2 + zh) * FEAT + y * 2 + c for zl in range(4) for c in range(2)]
    for x in range(4) for zh in range(2) for y in range(4)
]
X, Y, ZL, ZH, CORE = range(5)

f32 = jnp.float32
bf16 = jnp.bfloat16


def shift_x(a, s):
    return lax.ppermute(a, "batch", [(b, (b + 8 * s) % BATCH) for b in range(BATCH)])


def shift_zl(a, s):
    return lax.ppermute(
        a, "batch", [(b, b // 8 * 8 + (b + 2 * s) % 8) for b in range(BATCH)]
    )


def shift_y(a, s):
    return lax.ppermute(a, "feat", [(f, (f + 2 * s) % FEAT) for f in range(FEAT)])


def swap_core(a):
    return lax.ppermute(a, "feat", [(f, f ^ 1) for f in range(FEAT)])


def move_square(a, rule):
    pairs = []
    for b in range(BATCH):
        for f in range(FEAT):
            to = rule(b % 2, f % 2)
            if to is not None:
                pairs.append((b * FEAT + f, (b - b % 2 + to[0]) * FEAT + f - f % 2 + to[1]))
    return lax.ppermute(a, BOTH, pairs)


def dot(a, b, ca, cb):
    return lax.dot_general(
        a, b, (((ca,), (cb,)), ((), ())), preferred_element_type=f32
    )


def shape(*dims_dtype):
    return jax.ShapeDtypeStruct(dims_dtype[:-1], dims_dtype[-1])


def call(body, smem, args, outs, scratch=(), flops=0, grant=8, unread=0):
    vmem = pl.BlockSpec(memory_space=pltpu.VMEM)
    scalar = pl.BlockSpec(memory_space=pltpu.SMEM)
    moved = sum(a.size * a.dtype.itemsize for a in (*args, *outs))
    return pl.pallas_call(
        body,
        out_shape=outs,
        in_specs=[scalar] * len(smem)
        + [vmem] * (len(args) - unread)
        + [pl.BlockSpec(memory_space=pl.ANY)] * unread,
        out_specs=[vmem] * len(outs),
        scratch_shapes=list(scratch),
        cost_estimate=pl.CostEstimate(
            flops=flops, bytes_accessed=moved, transcendentals=0
        ),
        compiler_params=pltpu.CompilerParams(vmem_limit_bytes=grant << 20),
    )(*smem, *args)


def find_positives(ids, pos, n):
    rows = lax.broadcasted_iota(jnp.int32, (4 * n, n), 0)
    bits = n.bit_length() - 1
    block = ((ids[X] + 4 - (rows >> bits)) & 3) * 8 + ids[ZL] * 2 + ids[CORE]
    return (block << bits) + (rows & (n - 1)) == pos


def pack_kernel(ids, own, near, far, q_row, out, late):
    n, width = near.shape
    same = ids[ZH] == ids[CORE]
    late[...] = q_row[...]
    for core in (0, 1):
        for matches in (True, False):
            a, b = (own, near) if matches else (near, far)
            if core:
                a, b = b, a

            @pl.when((ids[CORE] == core) & (same == matches))
            def _():
                out[:, :width] = a[...]
                out[:, width:] = b[...]


def score_kernel(
    ids, p0, p1, p2, p3, q0, q1, q2, q3, o0, o1, o2, o3, s0, s1, s2, s3, p, q_all, pos
):
    n, wide = p0.shape
    width = wide // 2
    for s, block in enumerate((p0, p1, p2, p3)):
        p[s * n : s * n + n] = block[...]
    for s, (own, other) in enumerate(zip((q0, q1, q2, q3), (o0, o1, o2, o3))):
        j = (ids[ZL] + 4 - s) & 3
        digits = own[n:, :n].astype(f32)
        pos[j] = (digits[0:1] * 64.0 + digits[1:2]).astype(jnp.int32)

        @pl.when(ids[CORE] == 0)
        def _():
            q_all[j, :, :width] = own[:n]
            q_all[j, :, width:] = other[:n]

        @pl.when(ids[CORE] != 0)
        def _():
            q_all[j, :, :width] = other[:n]
            q_all[j, :, width:] = own[:n]

    for t, out in enumerate((s0, s1, s2, s3)):
        out[...] = dot(p[...], q_all[(ids[Y] + t) & 3], 1, 1)


def level(scores, hot, weight):
    top = jnp.max(scores, axis=0, keepdims=True)
    e = jnp.exp(scores - top)
    lse = top + jnp.log(jnp.sum(e, axis=0, keepdims=True))
    picked = weight * jnp.sum(jnp.where(hot, scores, 0.0), axis=0, keepdims=True)
    return e, top, lse, picked


def low_kernel(ids, weight, p, q_all, pos, e_low, stats, tops):
    n = q_all.shape[1]
    first = lax.broadcasted_iota(jnp.int32, (n, PAIR), 1) < SMALLEST
    for j in range(4):
        hot = find_positives(ids, pos[j], n)
        rows, lses, total = [], [], jnp.zeros((1, n), f32)
        running = None
        for k, (begin, end) in enumerate(SPANS):
            if k == 0:
                q_part = q_all[j, :, :PAIR]
                q_part = jnp.where(first, q_part, jnp.zeros_like(q_part))
                running = dot(p[:, :PAIR], q_part, 1, 1)
            elif k == 1:
                running = dot(p[:, :PAIR], q_all[j, :, :PAIR], 1, 1)
            else:
                running = running + dot(p[:, begin:end], q_all[j, :, begin:end], 1, 1)
            e_low[k, j], top, lse, picked = level(running * FACTORS[k], hot, weight[k])
            rows.append(top)
            lses.append(lse)
            total += picked
        tops[j] = jnp.concatenate(rows + rows[:3], axis=0)
        stats[j] = jnp.concatenate(lses + [total, total, total], axis=0)


def owner_kernel(ids, weight, s0, s1, s2, s3, pos, low_stats, e_high, message, tops):
    n = pos.shape[2]
    hot = find_positives(ids, pos[ids[Y]], n)
    sum5 = sum6 = None
    for t, ref in enumerate((s0, s1, s2, s3)):
        v = ref[...]
        part = jnp.where(((ids[Y] + 4 - t) & 3) <= 1, v, 0.0)
        sum5 = part if t == 0 else sum5 + part
        sum6 = v if t == 0 else sum6 + v
    e_high[0], top5, lse5, picked5 = level(sum5 * FACTORS[5], hot, weight[5])
    e_high[1], top6, lse6, picked6 = level(sum6 * FACTORS[6], hot, weight[6])
    tops[...] = jnp.concatenate([top5, top6] * 4, axis=0)
    high = jnp.concatenate([lse5, lse6] + [picked5 + picked6] * 6, axis=0)
    for i in range(8):
        for j in range(4):
            message[i, 8 * j : 8 * j + 8] = low_stats[j]
        message[i, 32:] = high


def put_terms(ref, row, v):
    hi = v.astype(bf16).astype(f32)
    mid = (v - hi).astype(bf16).astype(f32)
    lo = v - hi - mid
    zero = jnp.zeros((EXTRA - 3, v.shape[1]), f32)
    ref[row:, : v.shape[1]] = jnp.concatenate([hi, mid, lo, zero], axis=0).astype(bf16)


def tail_kernel(ids, weight, stats, low_tops, tops, e_high, pos, m0, m1, m2, m3, rates):
    n = pos.shape[2]

    def merged(at, levels):
        lse = stats[:, at : at + levels]
        best = jnp.max(lse, axis=0)
        mass = jnp.sum(jnp.exp(lse - best[None]), axis=0)
        return best + jnp.log(mass), jnp.sum(stats[:, at + levels : at + levels + 1], axis=0)

    on = ids[Y] == 0
    loss = jnp.zeros((1, n), f32)
    for j in range(4):
        lse, picked = merged(8 * j, LOW)
        loss -= picked
        rows = []
        for k in range(LOW):
            loss += weight[k] * lse[k : k + 1]
            scale = jnp.where(on, weight[k] * FACTORS[k], 0.0)
            rows.append(scale * jnp.exp(low_tops[j, k : k + 1] - lse[k : k + 1]))
        rates[j] = jnp.concatenate(rows + rows[:3], axis=0)

    hot = find_positives(ids, pos[ids[Y]], n)
    lse, picked = merged(32, 2)
    loss = jnp.where(on, loss, 0.0) - picked
    tail = None
    tails = []
    for i in (1, 0):
        loss += weight[LOW + i] * lse[i : i + 1]
        scale = weight[LOW + i] * FACTORS[LOW + i]
        rate = scale * jnp.exp(tops[i : i + 1] - lse[i : i + 1])
        g = e_high[i] * rate - jnp.where(hot, scale, 0.0)
        tail = g if tail is None else tail + g
        tails.append(tail.astype(bf16))
    lane = lax.broadcasted_iota(jnp.int32, (1, n), 1)
    mine = ids[X] * 8 + ids[ZH] * 4 + ids[Y]
    loss = jnp.where(lane == mine, jnp.sum(loss, axis=1, keepdims=True), 0.0)
    for t, m in enumerate((m0, m1, m2, m3)):
        narrow = ((ids[Y] + t) & 3) <= 1

        @pl.when(narrow)
        def _():
            m[: 4 * n] = tails[1]

        @pl.when(jnp.logical_not(narrow))
        def _():
            m[: 4 * n] = tails[0]

        put_terms(m, 4 * n, loss)


def get_terms(ref, row, lanes):
    v = ref[row:, :lanes].astype(f32)
    return v[0:1] + v[1:2] + v[2:3]


def low_grad_kernel(ids, weight, e_low, rates, pos, p, q_all, gq, gp, tails):
    n = pos.shape[2]
    on = ids[Y] == 0
    for j in range(4):
        hot = find_positives(ids, pos[j], n)
        acc = None
        for k in reversed(range(LOW)):
            scale = jnp.where(on, weight[k] * FACTORS[k], 0.0)
            g = e_low[k, j] * rates[j, k : k + 1] - jnp.where(hot, scale, 0.0)
            acc = g if acc is None else acc + g
            tails[k, :, j * n : j * n + n] = acc.astype(bf16)

    q = q_all[...].reshape(4 * n, q_all.shape[2])
    first = lax.broadcasted_iota(jnp.int32, (4 * n, PAIR), 1) < SMALLEST

    def fill(out, fn):
        out[:, :PAIR] = jnp.where(first, fn(0, 0, PAIR), fn(1, 0, PAIR))
        for k in range(2, LOW):
            begin, end = SPANS[k]
            out[:, begin:end] = fn(k, begin, end)

    fill(gq, lambda k, a, b: dot(tails[k], p[:, a:b], 0, 0))
    fill(gp, lambda k, a, b: dot(tails[k], q[:, a:b], 1, 0))


def grad_kernel(
    ids, t0, t1, t2, t3, gq_low, gp_low, p, q_all,
    gp0, gp1, gp2, gp3, own, message, row, tail,
):
    n, wide = gp0.shape
    width = own.shape[1]
    loss = jnp.zeros((1, n), f32)
    for t, ref in enumerate((t0, t1, t2, t3)):
        j = (ids[Y] + 4 - t) & 3
        tail[:, pl.ds(pl.multiple_of(j * n, n), n)] = ref[: 4 * n]
        loss += get_terms(ref, 4 * n, n)
    row[...] = jnp.broadcast_to(loss, row.shape)

    q = q_all[...].reshape(4 * n, wide)
    for s, out in enumerate((gp0, gp1, gp2, gp3)):
        rows = slice(s * n, s * n + n)
        out[:n] = (dot(tail[rows], q, 1, 0) + gp_low[rows]).astype(out.dtype)
        if s:
            out[n:] = jnp.zeros((EXTRA, wide), bf16)
            put_terms(out, n, loss)

    for c in (0, 1):
        lanes = slice(c * width, c * width + width)
        gq = dot(tail[...], p[:, lanes], 0, 0) + gq_low[:, lanes]

        @pl.when(ids[CORE] == c)
        def _():
            own[...] = gq

        @pl.when(ids[CORE] != c)
        def _():
            message[...] = gq.astype(bf16)


def core_sum_kernel(ids, gq_own, other, own, m1, m2, m3):
    n = own.shape[0]
    for s, out in enumerate((own, m1, m2, m3)):
        j = (ids[ZL] + 4 - s) & 3
        rows = pl.ds(pl.multiple_of(j * n, n), n)
        out[...] = (gq_own[rows, :] + other[rows, :].astype(f32)).astype(out.dtype)


def passage_sum_kernel(ids, gp0, g1, g2, g3, row, m1, m2, m3, own, near, far, loss):
    n, width = own.shape
    total = row[0:1]
    for g in (g1, g2, g3):
        total += get_terms(g, n, n)
    loss[...] = jnp.broadcast_to(total, loss.shape)
    same = ids[ZH] == ids[CORE]
    for c in (0, 1):
        lanes = slice(c * width, c * width + width)
        v = gp0[:, lanes] + (
            g1[:n, lanes].astype(f32) + g2[:n, lanes].astype(f32) + g3[:n, lanes].astype(f32)
        )

        @pl.when(ids[CORE] == c)
        def _():
            own[...] = v

        @pl.when((ids[CORE] == c) != same)
        def _():
            near[:n] = v.astype(bf16)

        @pl.when(ids[CORE] != c)
        def _():
            far[:n] = v.astype(bf16)

    for out in (near, far):
        out[n:] = jnp.zeros((EXTRA, width), bf16)
        put_terms(out, n, total)


def per_device(queries, passages, positives, level_weight):
    n, width = queries.shape
    wide = 2 * width
    bi = lax.axis_index("batch")
    fi = lax.axis_index("feat")
    core = fi % 2
    same = bi % 2 == core
    ids = jnp.stack([bi // 8, fi // 2, bi % 8 // 2, bi % 2, core]).astype(jnp.int32)

    near = move_square(passages, lambda h, c: (1 - h, c) if h == c else (h, 1 - c))
    far = move_square(passages, lambda h, c: None if h == c else (1 - h, 1 - c))
    rows = jnp.stack([positives // 64, positives % 64]).astype(bf16)
    rows = jnp.pad(rows, ((0, EXTRA - 2), (0, width - n)))
    q_row = jnp.concatenate([queries, rows], axis=0)
    p_block, q_late = call(
        pack_kernel, [ids], [passages, near, far, q_row],
        [shape(n, wide, bf16), shape(n + EXTRA, width, bf16)],
    )
    p_blocks = [p_block] + [shift_x(p_block, s) for s in (1, 2, 3)]

    q_own = [q_row, shift_zl(q_row, 1), shift_zl(q_late, 2), shift_zl(q_row, 3)]
    q_other = [swap_core(a) for a in q_own]

    tile = 4 * n * 4 * n
    *partial, p, q, pos = call(
        score_kernel, [ids], [*p_blocks, *q_own, *q_other],
        [shape(4 * n, n, f32)] * 4
        + [
            shape(4 * n, wide, bf16),
            shape(4, n, wide, bf16),
            shape(4, 1, n, jnp.int32),
        ],
        flops=2 * tile * wide,
    )
    pieces = [partial[0]] + [shift_y(partial[t], t) for t in (1, 2, 3)]
    e_low, low_stats, low_tops = call(
        low_kernel, [ids, level_weight], [p, q, pos],
        [shape(LOW, 4, 4 * n, n, f32), shape(4, 8, n, f32), shape(4, 8, n, f32)],
        flops=2 * tile * wide,
    )
    e_high, message, tops = call(
        owner_kernel, [ids, level_weight], [*pieces, pos, low_stats],
        [shape(2, 4 * n, n, f32), shape(8, 40, n, f32), shape(8, n, f32)],
    )
    stats = lax.all_to_all(message, BOTH, 0, 0, axis_index_groups=STAT_GROUPS)
    *tails, rates = call(
        tail_kernel, [ids, level_weight], [stats, low_tops, tops, e_high, pos],
        [shape(4 * n + EXTRA, n, bf16)] * 4 + [shape(4, 8, n, f32)],
    )
    tails = [tails[0]] + [shift_y(tails[t], t) for t in (1, 2, 3)]
    gq_low, gp_low = call(
        low_grad_kernel, [ids, level_weight], [e_low, rates, pos, p, q],
        [shape(4 * n, wide, f32)] * 2,
        scratch=[pltpu.VMEM((LOW, 4 * n, 4 * n), bf16)],
        flops=4 * tile * wide, grant=12,
    )
    gp0, gp1, gp2, gp3, gq_own, message, row = call(
        grad_kernel, [ids], [*tails, gq_low, gp_low, p, q],
        [shape(n, wide, f32)]
        + [shape(n + EXTRA, wide, bf16)] * 3
        + [
            shape(4 * n, width, f32),
            shape(4 * n, width, bf16),
            shape(8, n, f32),
        ],
        scratch=[pltpu.VMEM((4 * n, 4 * n), bf16)],
        flops=4 * tile * wide, grant=12,
    )
    gp = [shift_x(g, -s) for s, g in enumerate((gp1, gp2, gp3), 1)]
    own, *messages = call(
        core_sum_kernel, [ids], [gq_own, swap_core(message)],
        [shape(n, width, f32)] + [shape(n, width, bf16)] * 3,
    )
    gq = [shift_zl(m, -s) for s, m in enumerate(messages, 1)]
    gp_own, near, far, loss_row = call(
        passage_sum_kernel, [ids], [gp0, *gp, row, *messages],
        [shape(n, width, f32)] + [shape(n + EXTRA, width, bf16)] * 2 + [shape(8, n, f32)],
        unread=3,
    )
    near = move_square(near, lambda h, c: (h, 1 - c) if h == c else (1 - h, c)).astype(f32)
    far = move_square(far, lambda h, c: None if h == c else (1 - h, 1 - c)).astype(f32)
    grad_queries = own + sum(g.astype(f32) for g in gq)
    grad_passages = near[:n] + jnp.where(same, gp_own, far[:n])
    loss_other = jnp.where(same, near[n : n + 3, :n], far[n : n + 3, :n])
    loss = jnp.sum(loss_row[0] + jnp.sum(loss_other, axis=0)) / (n * BATCH)
    return loss, grad_queries.astype(bf16), grad_passages.astype(bf16)
def solution(mesh):
    in_specs = (P("batch", "feat"), P("batch", "feat"), P("batch"), P())
    out_specs = (P(), P("batch", "feat"), P("batch", "feat"))
    return jax.shard_map(
        per_device, mesh=mesh, in_specs=in_specs, out_specs=out_specs, check_vma=False
    )
```

time: 109 us -> 115 us (1.055)
  waiting for transfers between devices: 18.2 us -> 37.4 us
  starting transfers between devices: 54.1 us -> 41.3 us
  blocking collectives: 15 us -> 13.5 us
    ppermute x6, waiting for transfers between devices: 7.16 us -> 19.4 us  [shift_x(): lax.ppermute(a, 'batch', [(b, (b + 8 * s) % BATCH) for b in range(BATCH)])]
    ppermute x6 -> x5, starting transfers between devices: 11.9 us -> 3.5 us  [swap_core(): return lax.ppermute(a, 'feat', [(f, f ^ 1) for f in range(FEAT)])]
    ppermute x3 -> x4, waiting for transfers between devices: 1.95 us -> 7.74 us  [move_square(): return lax.ppermute(a, BOTH, pairs)]
    ppermute x6, starting transfers between devices: 7.83 us -> 5.09 us  [shift_x(): lax.ppermute(a, 'batch', [(b, (b + 8 * s) % BATCH) for b in range(BATCH)])]
    ppermute x6, starting transfers between devices: 17.6 us -> 15.6 us  [shift_zl(): lax.ppermute(a, 'batch', [(b, b // 8 * 8 + (b + 2 * s) % 8) for b in rang...]
    ppermute x6, waiting for transfers between devices: 0.8 us -> 2.51 us  [shift_zl(): lax.ppermute(a, 'batch', [(b, b // 8 * 8 + (b + 2 * s) % 8) for b in rang...]
    ppermute x6 -> x5, waiting for transfers between devices: 2.57 us -> 0.92 us  [swap_core(): return lax.ppermute(a, 'feat', [(f, f ^ 1) for f in range(FEAT)])]
    all_to_all x1, blocking collectives: 15 us -> 13.5 us  [per_device(): stats = lax.all_to_all(message, BOTH, 0, 0, axis_index_groups=STAT_GROUPS)]
  transfers between devices with their start and end apart: 27 -> 27, of which waited for: 13 -> 14; matrix products, arithmetic and copies ran while one was open for 1% -> 1% of each run, Pallas kernels for 7% -> 8%
where the time goes in v4:
time: 115 us
  starting transfers between devices  41.3 us (36%)
  waiting for transfers between devices  37.4 us (33%)
  Pallas kernels  15.4 us (13%)
  blocking collectives  13.5 us (12%)
  other arithmetic  3.71 us (3%)
  between operations  2.65 us (2%)
    ppermute x6, waiting for transfers between devices, shift_x(): lax.ppermute(a, 'batch', [(b, (b + 8 * s) % BATCH) for b in range(BATCH)])  19.4 us
    ppermute x6, starting transfers between devices, shift_zl(): lax.ppermute(a, 'batch', [(b, b // 8 * 8 + (b + 2 * s) % 8) for b in rang...  15.6 us
    pallas_call x9, Pallas kernels, call(): pl.pallas_call(body, out_shape=outs, in_specs=[scalar] * len(smem) + [vme...  15.4 us
    all_to_all x1, blocking collectives, per_device(): stats = lax.all_to_all(message, BOTH, 0, 0, axis_index_groups=STAT_GROUPS)  13.5 us
    ppermute x6, starting transfers between devices, shift_y(): lax.ppermute(a, 'feat', [(f, (f + 2 * s) % FEAT) for f in range(FEAT)])  9.51 us
    ppermute x4, waiting for transfers between devices, move_square(): return lax.ppermute(a, BOTH, pairs)  7.74 us
    ppermute x4, starting transfers between devices, move_square(): return lax.ppermute(a, BOTH, pairs)  7.57 us
    ppermute x6, waiting for transfers between devices, shift_y(): lax.ppermute(a, 'feat', [(f, (f + 2 * s) % FEAT) for f in range(FEAT)])  6.82 us
  transfers between devices with their start and end apart: 27, of which 14 were waited for; matrix products, arithmetic and copies ran while one was open for 1% of the time, Pallas kernels for 8%

profile of v4, /device:TPU:1, one launch (start us, length us, event | category | flops | bytes accessed | tf_op | source)
XLA Modules:
  0.0 114.9 jit_solution(12280255137827153611)
XLA Ops:
  2.2 6.9 %collective-permute-start.7 = (bf16[144,512]{1,0:T(8,128)(2,1)S(1)}, bf16[144,512]{1,0:T(8,128)(2,1)S(1)}, u32[]{:S(2)}, u32[]{:S(2)}) collective-permute-start(bf16[144,512]{1,0:T(8,128)(2,1)S(1)} %pad_maximum_fusion.q_row.q0), channel_id=1, source_target_pairs={{0,48},{8,56},{16,0},{24,8},{32,16},{40,24},{48,32},{56,40},{64,11... | collective-permute-start | bytes 442376 | tf_op jit(solution)/shard_map/ppermute | solution.py:38
  10.1 2.5 %collective-permute-start.1 = (bf16[128,512]{1,0:T(8,128)(2,1)}, bf16[128,512]{1,0:T(8,128)(2,1)S(1)}, u32[]{:S(2)}, u32[]{:S(2)}) collective-permute-start(bf16[128,512]{1,0:T(8,128)(2,1)} %own.1), channel_id=1, source_target_pairs={{1,8},{3,10},{5,12},{7,14},{8,1},{10,3},{12,5},{14,7},{17,24},{19,... | collective-permute-start | bytes 393224 | tf_op jit(solution)/shard_map/ppermute | solution.py:58
  13.0 5.3 %collective-permute-done.near = bf16[128,512]{1,0:T(8,128)(2,1)S(1)} collective-permute-done((bf16[128,512]{1,0:T(8,128)(2,1)}, bf16[128,512]{1,0:T(8,128)(2,1)S(1)}, u32[]{:S(2)}, u32[]{:S(2)}) %collective-permute-start) | collective-permute-done | bytes 131104 | tf_op jit(solution)/shard_map/ppermute | solution.py:58
  20.0 3.0 %collective-permute-start.6 = (bf16[144,512]{1,0:T(8,128)(2,1)S(1)}, bf16[144,512]{1,0:T(8,128)(2,1)S(1)}, u32[]{:S(2)}, u32[]{:S(2)}) collective-permute-start(bf16[144,512]{1,0:T(8,128)(2,1)S(1)} %get-tuple-element.41), channel_id=1, source_target_pairs={{0,32},{8,40},{16,48},{24,56},{32,0},{40,8},{48,16},{56,24},{64,96... | collective-permute-start | bytes 442376 | tf_op jit(solution)/shard_map/ppermute | solution.py:38
  23.1 2.5 %collective-permute-start.4 = (bf16[128,1024]{1,0:T(8,128)(2,1)S(1)}, bf16[128,1024]{1,0:T(8,128)(2,1)S(1)}, u32[]{:S(2)}, u32[]{:S(2)}) collective-permute-start(bf16[128,1024]{1,0:T(8,128)(2,1)S(1)} %get-tuple-element.40.p0), channel_id=1, source_target_pairs={{0,192},{8,200},{16,208},{24,216},{32,224},{40,232},{48,240},{56,2... | collective-permute-start | bytes 786440 | tf_op jit(solution)/shard_map/ppermute | solution.py:34
  26.7 2.5 %collective-permute-done.6.q2 = bf16[144,512]{1,0:T(8,128)(2,1)S(1)} collective-permute-done((bf16[144,512]{1,0:T(8,128)(2,1)S(1)}, bf16[144,512]{1,0:T(8,128)(2,1)S(1)}, u32[]{:S(2)}, u32[]{:S(2)}) %collective-permute-start.6) | collective-permute-done | bytes 147488 | tf_op jit(solution)/shard_map/ppermute | solution.py:38
  31.5 2.6 %collective-permute-done.3.p2 = bf16[128,1024]{1,0:T(8,128)(2,1)S(1)} collective-permute-done((bf16[128,1024]{1,0:T(8,128)(2,1)S(1)}, bf16[128,1024]{1,0:T(8,128)(2,1)S(1)}, u32[]{:S(2)}, u32[]{:S(2)}) %collective-permute-start.3) | collective-permute-done | bytes 262176 | tf_op jit(solution)/shard_map/ppermute | solution.py:34
  34.2 6.8 %collective-permute-done.2.p1 = bf16[128,1024]{1,0:T(8,128)(2,1)S(1)} collective-permute-done((bf16[128,1024]{1,0:T(8,128)(2,1)S(1)}, bf16[128,1024]{1,0:T(8,128)(2,1)S(1)}, u32[]{:S(2)}, u32[]{:S(2)}) %collective-permute-start.2) | collective-permute-done | bytes 262176 | tf_op jit(solution)/shard_map/ppermute | solution.py:34
  40.9 2.0 %shard_map.68 = (f32[512,128]{1,0:T(8,128)S(1)}, f32[512,128]{1,0:T(8,128)S(1)}, f32[512,128]{1,0:T(8,128)S(1)}, f32[512,128]{1,0:T(8,128)S(1)}, bf16[512,1024]{...) custom-call(s32[5]{0:T(128)S(1)} %stack.35.ids, ...), custom_call_target="tpu_custom_call" | custom-call | flops 536870912 | bytes 5376000 | tf_op jit(solution)/shard_map/pallas_call | solution.py:75
  42.9 1.4 %collective-permute-start.12 = (f32[512,128]{1,0:T(8,128)S(1)}, f32[512,128]{1,0:T(8,128)S(1)}, u32[]{:S(2)}, u32[]{:S(2)}) collective-permute-start(f32[512,128]{1,0:T(8,128)S(1)} %get-tuple-element.43), channel_id=1, source_target_pairs={{0,2},{1,3},{2,4},{3,5},{4,6},{5,7},{6,0},{7,1},{8,10},{9,11},{10,... | collective-permute-start | bytes 786440 | tf_op jit(solution)/shard_map/ppermute | solution.py:44
  44.3 2.6 %collective-permute-start.13 = (f32[512,128]{1,0:T(8,128)S(1)}, f32[512,128]{1,0:T(8,128)S(1)}, u32[]{:S(2)}, u32[]{:S(2)}) collective-permute-start(f32[512,128]{1,0:T(8,128)S(1)} %get-tuple-element.44), channel_id=1, source_target_pairs={{0,4},{1,5},{2,6},{3,7},{4,0},{5,1},{6,2},{7,3},{8,12},{9,13},{10,... | collective-permute-start | bytes 786440 | tf_op jit(solution)/shard_map/ppermute | solution.py:44
  48.0 3.7 %shard_map.69 = (f32[5,4,512,128]{3,2,1,0:T(8,128)S(1)}, f32[4,8,128]{2,1,0:T(8,128)S(1)}, f32[4,8,128]{2,1,0:T(8,128)S(1)}) custom-call(s32[5]{0:T(128)S(1)} %stack.35.ids, f32[7]{0:T(128)S(1)} %copy-done.1, bf16[512,1024]{1,0:T(8,128)(2,1)S(1)} %get-tuple-element.47.p, bf16[4,128,1024]{2,1,0:T(8,128)(2,1)S(1)} %get-tuple-element.48.q_all, ...), custom_call_target="tpu_custom_call" | custom-call | flops 536870912 | bytes 7374848 | tf_op jit(solution)/shard_map/pallas_call | solution.py:75
  51.7 6.7 %collective-permute-done.13.s2 = f32[512,128]{1,0:T(8,128)S(1)} collective-permute-done((f32[512,128]{1,0:T(8,128)S(1)}, f32[512,128]{1,0:T(8,128)S(1)}, u32[]{:S(2)}, u32[]{:S(2)}) %collective-permute-start.13) | collective-permute-done | bytes 262176 | tf_op jit(solution)/shard_map/ppermute | solution.py:44
  59.5 13.5 %all_to_all.5.stats = f32[8,40,128]{2,1,0:T(8,128)S(1)} all-to-all(f32[8,40,128]{2,1,0:T(8,128)S(1)} %get-tuple-element.50), channel_id=1, replica_groups={{0,1,16,17,32,33,48,49},{2,3,18,19,34,35,50,51},{4,5,20,21,36,37,52,53}..., dimensions={0} | all-to-all | bytes 327680 | tf_op jit(solution)/shard_map/all_to_all | solution.py:394
  75.0 2.1 %collective-permute-start.16 = (bf16[528,128]{1,0:T(8,128)(2,1)S(1)}, bf16[528,128]{1,0:T(8,128)(2,1)S(1)}, u32[]{:S(2)}, u32[]{:S(2)}) collective-permute-start(bf16[528,128]{1,0:T(8,128)(2,1)S(1)} %get-tuple-element.56), channel_id=1, source_target_pairs={{0,4},{1,5},{2,6},{3,7},{4,0},{5,1},{6,2},{7,3},{8,12},{9,13},{10,... | collective-permute-start | bytes 405512 | tf_op jit(solution)/shard_map/ppermute | solution.py:44
  77.1 1.3 %collective-permute-start.17 = (bf16[528,128]{1,0:T(8,128)(2,1)S(1)}, bf16[528,128]{1,0:T(8,128)(2,1)S(1)}, u32[]{:S(2)}, u32[]{:S(2)}) collective-permute-start(bf16[528,128]{1,0:T(8,128)(2,1)S(1)} %get-tuple-element.57), channel_id=1, source_target_pairs={{0,6},{1,7},{2,0},{3,1},{4,2},{5,3},{6,4},{7,5},{8,14},{9,15},{10,... | collective-permute-start | bytes 405512 | tf_op jit(solution)/shard_map/ppermute | solution.py:44
  78.4 3.4 %shard_map.72 = (f32[512,1024]{1,0:T(8,128)S(1)}, f32[512,1024]{1,0:T(8,128)S(1)}) custom-call(s32[5]{0:T(128)S(1)} %stack.35.ids, f32[7]{0:T(128)S(1)} %copy-done.1, f32[5,4,512,128]{3,2,1,0:T(8,128)S(1)} %get-tuple-element.58.e_low, f32[4,8,128]{2,1,0:T(8,128)S(1)} %get-tuple-element.59.rates, s32[4,1,128]{2,1,0:T(1,128)S(1)} %get-tuple-element.46.pos, ...), custom_call_target="tpu_custom_call" | custom-call | flops 1073741824 | bytes 11552768 | tf_op jit(solution)/shard_map/pallas_call | solution.py:75
  81.9 2.3 %shard_map.73 = (f32[128,1024]{1,0:T(8,128)S(1)}, bf16[144,1024]{1,0:T(8,128)(2,1)S(1)}, bf16[144,1024]{1,0:T(8,128)(2,1)S(1)}, bf16[144,1024]{1,0:T(8,128)(2,1)...) custom-call(s32[5]{0:T(128)S(1)} %stack.35.ids, ...), custom_call_target="tpu_custom_call" | custom-call | flops 1073741824 | bytes 9818112 | tf_op jit(solution)/shard_map/pallas_call | solution.py:75
  84.2 2.9 %collective-permute-start.21 = (bf16[512,512]{1,0:T(8,128)(2,1)S(1)}, bf16[512,512]{1,0:T(8,128)(2,1)S(1)}, u32[]{:S(2)}, u32[]{:S(2)}) collective-permute-start(bf16[512,512]{1,0:T(8,128)(2,1)S(1)} %get-tuple-element.68), channel_id=1, source_target_pairs={{0,1},{1,0},{2,3},{3,2},{4,5},{5,4},{6,7},{7,6},{8,9},{9,8},{10,11... | collective-permute-start | bytes 1572872 | tf_op jit(solution)/shard_map/ppermute | solution.py:48
  90.2 3.6 %collective-permute-start.25 = (bf16[128,512]{1,0:T(8,128)(2,1)S(1)}, bf16[128,512]{1,0:T(8,128)(2,1)S(1)}, u32[]{:S(2)}, u32[]{:S(2)}) collective-permute-start(bf16[128,512]{1,0:T(8,128)(2,1)S(1)} %get-tuple-element.70.m2), channel_id=1, source_target_pairs={{0,32},{8,40},{16,48},{24,56},{32,0},{40,8},{48,16},{56,24},{64,96... | collective-permute-start | bytes 393224 | tf_op jit(solution)/shard_map/ppermute | solution.py:38
  93.8 1.9 %collective-permute-done.18.g1 = bf16[144,1024]{1,0:T(8,128)(2,1)S(1)} collective-permute-done((bf16[144,1024]{1,0:T(8,128)(2,1)S(1)}, bf16[144,1024]{1,0:T(8,128)(2,1)S(1)}, u32[]{:S(2)}, u32[]{:S(2)}) %collective-permute-start.18) | collective-permute-done | bytes 294944 | tf_op jit(solution)/shard_map/ppermute | solution.py:34
  97.1 6.8 %collective-permute-done.20.g3 = bf16[144,1024]{1,0:T(8,128)(2,1)S(1)} collective-permute-done((bf16[144,1024]{1,0:T(8,128)(2,1)S(1)}, bf16[144,1024]{1,0:T(8,128)(2,1)S(1)}, u32[]{:S(2)}, u32[]{:S(2)}) %collective-permute-start.20) | collective-permute-done | bytes 294944 | tf_op jit(solution)/shard_map/ppermute | solution.py:34
  105.3 3.4 %collective-permute-start.23 = (bf16[144,512]{1,0:T(8,128)(2,1)S(1)}, bf16[144,512]{1,0:T(8,128)(2,1)S(1)}, u32[]{:S(2)}, u32[]{:S(2)}) collective-permute-start(bf16[144,512]{1,0:T(8,128)(2,1)S(1)} %get-tuple-element.74), channel_id=1, source_target_pairs={{1,8},{3,10},{5,12},{7,14},{8,1},{10,3},{12,5},{14,7},{17,24},{19,... | collective-permute-start | bytes 442376 | tf_op jit(solution)/shard_map/ppermute | solution.py:58
  109.6 2.2 %collective-permute-done.23 = bf16[144,512]{1,0:T(8,128)(2,1)S(1)} collective-permute-done((bf16[144,512]{1,0:T(8,128)(2,1)S(1)}, bf16[144,512]{1,0:T(8,128)(2,1)S(1)}, u32[]{:S(2)}, u32[]{:S(2)}) %collective-permute-start.23) | collective-permute-done | bytes 147488 | tf_op jit(solution)/shard_map/ppermute | solution.py:58
  (54 shorter events, 20.2 us)
Async XLA Ops:
  2.2 20.8 %collective-permute-start.7 = (bf16[144,512]{1,0:T(8,128)(2,1)S(1)}, bf16[144,512]{1,0:T(8,128)(2,1)S(1)}, u32[]{:S(2)}, u32[]{:S(2)}) collective-permute-start(bf16[144,512]{1,0:T(8,128)(2,1)S(1)} %pad_maximum_fusion.q_row.q0), channel_id=1, source_target_pairs={{0,48},{8,56},{16,0},{24,8},{32,16},{40,24},{48,32},{56,40},{64,11... | collective-permute-start | bytes 442376 | tf_op jit(solution)/shard_map/ppermute | solution.py:38
  9.2 9.1 %collective-permute-start = (bf16[128,512]{1,0:T(8,128)(2,1)}, bf16[128,512]{1,0:T(8,128)(2,1)S(1)}, u32[]{:S(2)}, u32[]{:S(2)}) collective-permute-start(bf16[128,512]{1,0:T(8,128)(2,1)} %own.1), channel_id=1, source_target_pairs={{0,8},{1,0},{2,10},{3,2},{4,12},{5,4},{6,14},{7,6},{8,9},{9,1},{10... | collective-permute-start | bytes 393224 | tf_op jit(solution)/shard_map/ppermute | solution.py:58
  10.1 8.4 %collective-permute-start.1 = (bf16[128,512]{1,0:T(8,128)(2,1)}, bf16[128,512]{1,0:T(8,128)(2,1)S(1)}, u32[]{:S(2)}, u32[]{:S(2)}) collective-permute-start(bf16[128,512]{1,0:T(8,128)(2,1)} %own.1), channel_id=1, source_target_pairs={{1,8},{3,10},{5,12},{7,14},{8,1},{10,3},{12,5},{14,7},{17,24},{19,... | collective-permute-start | bytes 393224 | tf_op jit(solution)/shard_map/ppermute | solution.py:58
  12.7 12.9 %collective-permute-start.8 = (bf16[144,512]{1,0:T(8,128)(2,1)S(1)}, bf16[144,512]{1,0:T(8,128)(2,1)S(1)}, u32[]{:S(2)}, u32[]{:S(2)}) collective-permute-start(bf16[144,512]{1,0:T(8,128)(2,1)S(1)} %pad_maximum_fusion.q_row.q0), channel_id=1, source_target_pairs={{0,1},{1,0},{2,3},{3,2},{4,5},{5,4},{6,7},{7,6},{8,9},{9,8},{10,11... | collective-permute-start | bytes 442376 | tf_op jit(solution)/shard_map/ppermute | solution.py:48
  12.8 13.3 %collective-permute-start.5 = (bf16[144,512]{1,0:T(8,128)(2,1)S(1)}, bf16[144,512]{1,0:T(8,128)(2,1)S(1)}, u32[]{:S(2)}, u32[]{:S(2)}) collective-permute-start(bf16[144,512]{1,0:T(8,128)(2,1)S(1)} %pad_maximum_fusion.q_row.q0), channel_id=1, source_target_pairs={{0,16},{8,24},{16,32},{24,40},{32,48},{40,56},{48,0},{56,8},{64,80... | collective-permute-start | bytes 442376 | tf_op jit(solution)/shard_map/ppermute | solution.py:38
  20.0 9.2 %collective-permute-start.6 = (bf16[144,512]{1,0:T(8,128)(2,1)S(1)}, bf16[144,512]{1,0:T(8,128)(2,1)S(1)}, u32[]{:S(2)}, u32[]{:S(2)}) collective-permute-start(bf16[144,512]{1,0:T(8,128)(2,1)S(1)} %get-tuple-element.41), channel_id=1, source_target_pairs={{0,32},{8,40},{16,48},{24,56},{32,0},{40,8},{48,16},{56,24},{64,96... | collective-permute-start | bytes 442376 | tf_op jit(solution)/shard_map/ppermute | solution.py:38
  23.1 6.1 %collective-permute-start.11 = (bf16[144,512]{1,0:T(8,128)(2,1)S(1)}, bf16[144,512]{1,0:T(8,128)(2,1)S(1)}, u32[]{:S(2)}, u32[]{:S(2)}) collective-permute-start(bf16[144,512]{1,0:T(8,128)(2,1)S(1)} %collective-permute-done.7.q3), channel_id=1, source_target_pairs={{0,1},{1,0},{2,3},{3,2},{4,5},{5,4},{6,7},{7,6},{8,9},{9,8},{10,11... | collective-permute-start | bytes 442376 | tf_op jit(solution)/shard_map/ppermute | solution.py:48
  23.1 8.4 %collective-permute-start.4 = (bf16[128,1024]{1,0:T(8,128)(2,1)S(1)}, bf16[128,1024]{1,0:T(8,128)(2,1)S(1)}, u32[]{:S(2)}, u32[]{:S(2)}) collective-permute-start(bf16[128,1024]{1,0:T(8,128)(2,1)S(1)} %get-tuple-element.40.p0), channel_id=1, source_target_pairs={{0,192},{8,200},{16,208},{24,216},{32,224},{40,232},{48,240},{56,2... | collective-permute-start | bytes 786440 | tf_op jit(solution)/shard_map/ppermute | solution.py:34
  25.6 8.6 %collective-permute-start.3 = (bf16[128,1024]{1,0:T(8,128)(2,1)S(1)}, bf16[128,1024]{1,0:T(8,128)(2,1)S(1)}, u32[]{:S(2)}, u32[]{:S(2)}) collective-permute-start(bf16[128,1024]{1,0:T(8,128)(2,1)S(1)} %get-tuple-element.40.p0), channel_id=1, source_target_pairs={{0,128},{8,136},{16,144},{24,152},{32,160},{40,168},{48,176},{56,1... | collective-permute-start | bytes 786440 | tf_op jit(solution)/shard_map/ppermute | solution.py:34
  26.1 14.8 %collective-permute-start.2 = (bf16[128,1024]{1,0:T(8,128)(2,1)S(1)}, bf16[128,1024]{1,0:T(8,128)(2,1)S(1)}, u32[]{:S(2)}, u32[]{:S(2)}) collective-permute-start(bf16[128,1024]{1,0:T(8,128)(2,1)S(1)} %get-tuple-element.40.p0), channel_id=1, source_target_pairs={{0,64},{8,72},{16,80},{24,88},{32,96},{40,104},{48,112},{56,120},{... | collective-permute-start | bytes 786440 | tf_op jit(solution)/shard_map/ppermute | solution.py:34
  29.2 11.7 %collective-permute-start.10 = (bf16[144,512]{1,0:T(8,128)(2,1)S(1)}, bf16[144,512]{1,0:T(8,128)(2,1)S(1)}, u32[]{:S(2)}, u32[]{:S(2)}) collective-permute-start(bf16[144,512]{1,0:T(8,128)(2,1)S(1)} %collective-permute-done.6.q2), channel_id=1, source_target_pairs={{0,1},{1,0},{2,3},{3,2},{4,5},{5,4},{6,7},{7,6},{8,9},{9,8},{10,11... | collective-permute-start | bytes 442376 | tf_op jit(solution)/shard_map/ppermute | solution.py:48
  42.9 8.8 %collective-permute-start.12 = (f32[512,128]{1,0:T(8,128)S(1)}, f32[512,128]{1,0:T(8,128)S(1)}, u32[]{:S(2)}, u32[]{:S(2)}) collective-permute-start(f32[512,128]{1,0:T(8,128)S(1)} %get-tuple-element.43), channel_id=1, source_target_pairs={{0,2},{1,3},{2,4},{3,5},{4,6},{5,7},{6,0},{7,1},{8,10},{9,11},{10,... | collective-permute-start | bytes 786440 | tf_op jit(solution)/shard_map/ppermute | solution.py:44
  44.3 14.2 %collective-permute-start.13 = (f32[512,128]{1,0:T(8,128)S(1)}, f32[512,128]{1,0:T(8,128)S(1)}, u32[]{:S(2)}, u32[]{:S(2)}) collective-permute-start(f32[512,128]{1,0:T(8,128)S(1)} %get-tuple-element.44), channel_id=1, source_target_pairs={{0,4},{1,5},{2,6},{3,7},{4,0},{5,1},{6,2},{7,3},{8,12},{9,13},{10,... | collective-permute-start | bytes 786440 | tf_op jit(solution)/shard_map/ppermute | solution.py:44
  46.9 11.5 %collective-permute-start.14 = (f32[512,128]{1,0:T(8,128)S(1)}, f32[512,128]{1,0:T(8,128)S(1)}, u32[]{:S(2)}, u32[]{:S(2)}) collective-permute-start(f32[512,128]{1,0:T(8,128)S(1)} %get-tuple-element.45), channel_id=1, source_target_pairs={{0,6},{1,7},{2,0},{3,1},{4,2},{5,3},{6,4},{7,5},{8,14},{9,15},{10,... | collective-permute-start | bytes 786440 | tf_op jit(solution)/shard_map/ppermute | solution.py:44
  73.9 7.9 %collective-permute-start.15 = (bf16[528,128]{1,0:T(8,128)(2,1)S(1)}, bf16[528,128]{1,0:T(8,128)(2,1)S(1)}, u32[]{:S(2)}, u32[]{:S(2)}) collective-permute-start(bf16[528,128]{1,0:T(8,128)(2,1)S(1)} %get-tuple-element.55), channel_id=1, source_target_pairs={{0,2},{1,3},{2,4},{3,5},{4,6},{5,7},{6,0},{7,1},{8,10},{9,11},{10,... | collective-permute-start | bytes 405512 | tf_op jit(solution)/shard_map/ppermute | solution.py:44
  75.0 6.9 %collective-permute-start.16 = (bf16[528,128]{1,0:T(8,128)(2,1)S(1)}, bf16[528,128]{1,0:T(8,128)(2,1)S(1)}, u32[]{:S(2)}, u32[]{:S(2)}) collective-permute-start(bf16[528,128]{1,0:T(8,128)(2,1)S(1)} %get-tuple-element.56), channel_id=1, source_target_pairs={{0,4},{1,5},{2,6},{3,7},{4,0},{5,1},{6,2},{7,3},{8,12},{9,13},{10,... | collective-permute-start | bytes 405512 | tf_op jit(solution)/shard_map/ppermute | solution.py:44
  87.1 8.6 %collective-permute-start.18 = (bf16[144,1024]{1,0:T(8,128)(2,1)S(1)}, bf16[144,1024]{1,0:T(8,128)(2,1)S(1)}, u32[]{:S(2)}, u32[]{:S(2)}) collective-permute-start(bf16[144,1024]{1,0:T(8,128)(2,1)S(1)} %get-tuple-element.63), channel_id=1, source_target_pairs={{0,192},{8,200},{16,208},{24,216},{32,224},{40,232},{48,240},{56,2... | collective-permute-start | bytes 884744 | tf_op jit(solution)/shard_map/ppermute | solution.py:34
  87.1 10.0 %collective-permute-start.19 = (bf16[144,1024]{1,0:T(8,128)(2,1)S(1)}, bf16[144,1024]{1,0:T(8,128)(2,1)S(1)}, u32[]{:S(2)}, u32[]{:S(2)}) collective-permute-start(bf16[144,1024]{1,0:T(8,128)(2,1)S(1)} %get-tuple-element.64), channel_id=1, source_target_pairs={{0,128},{8,136},{16,144},{24,152},{32,160},{40,168},{48,176},{56,1... | collective-permute-start | bytes 884744 | tf_op jit(solution)/shard_map/ppermute | solution.py:34
  87.7 16.3 %collective-permute-start.20 = (bf16[144,1024]{1,0:T(8,128)(2,1)S(1)}, bf16[144,1024]{1,0:T(8,128)(2,1)S(1)}, u32[]{:S(2)}, u32[]{:S(2)}) collective-permute-start(bf16[144,1024]{1,0:T(8,128)(2,1)S(1)} %get-tuple-element.65), channel_id=1, source_target_pairs={{0,64},{8,72},{16,80},{24,88},{32,96},{40,104},{48,112},{56,120},{... | collective-permute-start | bytes 884744 | tf_op jit(solution)/shard_map/ppermute | solution.py:34
  89.3 19.5 %collective-permute-start.24 = (bf16[128,512]{1,0:T(8,128)(2,1)S(1)}, bf16[128,512]{1,0:T(8,128)(2,1)S(1)}, u32[]{:S(2)}, u32[]{:S(2)}) collective-permute-start(bf16[128,512]{1,0:T(8,128)(2,1)S(1)} %get-tuple-element.69.m1), channel_id=1, source_target_pairs={{0,48},{8,56},{16,0},{24,8},{32,16},{40,24},{48,32},{56,40},{64,11... | collective-permute-start | bytes 393224 | tf_op jit(solution)/shard_map/ppermute | solution.py:38
  90.2 18.6 %collective-permute-start.25 = (bf16[128,512]{1,0:T(8,128)(2,1)S(1)}, bf16[128,512]{1,0:T(8,128)(2,1)S(1)}, u32[]{:S(2)}, u32[]{:S(2)}) collective-permute-start(bf16[128,512]{1,0:T(8,128)(2,1)S(1)} %get-tuple-element.70.m2), channel_id=1, source_target_pairs={{0,32},{8,40},{16,48},{24,56},{32,0},{40,8},{48,16},{56,24},{64,96... | collective-permute-start | bytes 393224 | tf_op jit(solution)/shard_map/ppermute | solution.py:38
  95.7 13.1 %collective-permute-start.26 = (bf16[128,512]{1,0:T(8,128)(2,1)S(1)}, bf16[128,512]{1,0:T(8,128)(2,1)S(1)}, u32[]{:S(2)}, u32[]{:S(2)}) collective-permute-start(bf16[128,512]{1,0:T(8,128)(2,1)S(1)} %get-tuple-element.71.m3), channel_id=1, source_target_pairs={{0,16},{8,24},{16,32},{24,40},{32,48},{40,56},{48,0},{56,8},{64,80... | collective-permute-start | bytes 393224 | tf_op jit(solution)/shard_map/ppermute | solution.py:38
  104.7 4.9 %collective-permute-start.22 = (bf16[144,512]{1,0:T(8,128)(2,1)S(1)}, bf16[144,512]{1,0:T(8,128)(2,1)S(1)}, u32[]{:S(2)}, u32[]{:S(2)}) collective-permute-start(bf16[144,512]{1,0:T(8,128)(2,1)S(1)} %get-tuple-element.73), channel_id=1, source_target_pairs={{0,1},{1,9},{2,3},{3,11},{4,5},{5,13},{6,7},{7,15},{8,0},{9,8},{10... | collective-permute-start | bytes 442376 | tf_op jit(solution)/shard_map/ppermute | solution.py:58
  105.3 6.5 %collective-permute-start.23 = (bf16[144,512]{1,0:T(8,128)(2,1)S(1)}, bf16[144,512]{1,0:T(8,128)(2,1)S(1)}, u32[]{:S(2)}, u32[]{:S(2)}) collective-permute-start(bf16[144,512]{1,0:T(8,128)(2,1)S(1)} %get-tuple-element.74), channel_id=1, source_target_pairs={{1,8},{3,10},{5,12},{7,14},{8,1},{10,3},{12,5},{14,7},{17,24},{19,... | collective-permute-start | bytes 442376 | tf_op jit(solution)/shard_map/ppermute | solution.py:58
  (5 other events, 58.9 us)

commit v5 on v4

--- a/solution.py
+++ b/solution.py
@@ -20,10 +20,7 @@
 BATCH = 32
 FEAT = 8
 BOTH = ("batch", "feat")
-STAT_GROUPS = [
-    [(x * 8 + zl * 2 + zh) * FEAT + y * 2 + c for zl in range(4) for c in range(2)]
-    for x in range(4) for zh in range(2) for y in range(4)
-]
+XZH_GROUPS = [[x * 8 + zl * 2 + zh for x in range(4) for zh in range(2)] for zl in range(4)]
 X, Y, ZL, ZH, CORE = range(5)
 
 f32 = jnp.float32
@@ -68,7 +65,7 @@
     return jax.ShapeDtypeStruct(dims_dtype[:-1], dims_dtype[-1])
 
 
-def call(body, smem, args, outs, scratch=(), flops=0, grant=8, unread=0):
+def call(body, smem, args, outs, scratch=(), flops=0, grant=8, in_place=0):
     vmem = pl.BlockSpec(memory_space=pltpu.VMEM)
     scalar = pl.BlockSpec(memory_space=pltpu.SMEM)
     moved = sum(a.size * a.dtype.itemsize for a in (*args, *outs))
@@ -76,8 +73,8 @@
         body,
         out_shape=outs,
         in_specs=[scalar] * len(smem)
-        + [vmem] * (len(args) - unread)
-        + [pl.BlockSpec(memory_space=pl.ANY)] * unread,
+        + [vmem] * (len(args) - in_place)
+        + [pl.BlockSpec(memory_space=pl.ANY)] * in_place,
         out_specs=[vmem] * len(outs),
         scratch_shapes=list(scratch),
         cost_estimate=pl.CostEstimate(
@@ -90,14 +87,20 @@
 def find_positives(ids, pos, n):
     rows = lax.broadcasted_iota(jnp.int32, (4 * n, n), 0)
     bits = n.bit_length() - 1
-    block = ((ids[X] + 4 - (rows >> bits)) & 3) * 8 + ids[ZL] * 2 + ids[CORE]
+    block = ids[X] * 8 + ids[ZH] + 2 * ((ids[ZL] + 4 - (rows >> bits)) & 3)
     return (block << bits) + (rows & (n - 1)) == pos
 
 
-def pack_kernel(ids, own, near, far, q_row, out, late):
+def pack_kernel(ids, own, near, far, out):
     n, width = near.shape
     same = ids[ZH] == ids[CORE]
-    late[...] = q_row[...]
+
+    def put(first, second, rows):
+        out[:n, :width] = first[:n]
+        out[:n, width:] = second[:n]
+        out[n:, :width] = rows[n:]
+
+    out[n:, width:] = jnp.zeros((EXTRA, width), bf16)
     for core in (0, 1):
         for matches in (True, False):
             a, b = (own, near) if matches else (near, far)
@@ -106,32 +109,36 @@
 
             @pl.when((ids[CORE] == core) & (same == matches))
             def _():
-                out[:, :width] = a[...]
-                out[:, width:] = b[...]
+                put(a, b, own if matches else far)
 
 
 def score_kernel(
-    ids, p0, p1, p2, p3, q0, q1, q2, q3, o0, o1, o2, o3, s0, s1, s2, s3, p, q_all, pos
+    ids, p1, p2, p3, o0, o1, o2, o3, q0, q1, q2, q3, p0_hbm,
+    s0, s1, s2, s3, p, q_all, pos, p0, arrived,
 ):
-    n, wide = p0.shape
-    width = wide // 2
-    for s, block in enumerate((p0, p1, p2, p3)):
-        p[s * n : s * n + n] = block[...]
-    for s, (own, other) in enumerate(zip((q0, q1, q2, q3), (o0, o1, o2, o3))):
-        j = (ids[ZL] + 4 - s) & 3
-        digits = own[n:, :n].astype(f32)
+    n, width = p1.shape
+    copy = pltpu.make_async_copy(p0_hbm, p0, arrived)
+    copy.start()
+    for s, (own, other) in enumerate(zip((p1, p2, p3, p0), (o1, o2, o3, o0))):
+        rows = slice((s + 1) % 4 * n, (s + 1) % 4 * n + n)
+        if s == 3:
+            copy.wait()
+
+        @pl.when(ids[CORE] == 0)
+        def _():
+            p[rows, :width] = own[...]
+            p[rows, width:] = other[...]
+
+        @pl.when(ids[CORE] != 0)
+        def _():
+            p[rows, :width] = other[...]
+            p[rows, width:] = own[...]
+
+    for s, q in enumerate((q0, q1, q2, q3)):
+        j = (ids[X] + 4 - s) & 3
+        q_all[j] = q[:n]
+        digits = q[n:, :n].astype(f32)
         pos[j] = (digits[0:1] * 64.0 + digits[1:2]).astype(jnp.int32)
-
-        @pl.when(ids[CORE] == 0)
-        def _():
-            q_all[j, :, :width] = own[:n]
-            q_all[j, :, width:] = other[:n]
-
-        @pl.when(ids[CORE] != 0)
-        def _():
-            q_all[j, :, :width] = other[:n]
-            q_all[j, :, width:] = own[:n]
-
     for t, out in enumerate((s0, s1, s2, s3)):
         out[...] = dot(p[...], q_all[(ids[Y] + t) & 3], 1, 1)
 
@@ -229,7 +236,7 @@
         tail = g if tail is None else tail + g
         tails.append(tail.astype(bf16))
     lane = lax.broadcasted_iota(jnp.int32, (1, n), 1)
-    mine = ids[X] * 8 + ids[ZH] * 4 + ids[Y]
+    mine = ids[ZL] * FEAT + ids[Y] * 2 + ids[CORE]
     loss = jnp.where(lane == mine, jnp.sum(loss, axis=1, keepdims=True), 0.0)
     for t, m in enumerate((m0, m1, m2, m3)):
         narrow = ((ids[Y] + t) & 3) <= 1
@@ -275,59 +282,59 @@
     fill(gp, lambda k, a, b: dot(tails[k], q[:, a:b], 1, 0))
 
 
-def grad_kernel(
-    ids, t0, t1, t2, t3, gq_low, gp_low, p, q_all,
-    gp0, gp1, gp2, gp3, own, message, row, tail,
-):
-    n, wide = gp0.shape
-    width = own.shape[1]
+def query_grad_kernel(ids, t0, t1, t2, t3, gq_low, p, gq0, gq1, gq2, gq3, tail, row, gq):
+    n, wide = gq0.shape
     loss = jnp.zeros((1, n), f32)
     for t, ref in enumerate((t0, t1, t2, t3)):
         j = (ids[Y] + 4 - t) & 3
         tail[:, pl.ds(pl.multiple_of(j * n, n), n)] = ref[: 4 * n]
         loss += get_terms(ref, 4 * n, n)
     row[...] = jnp.broadcast_to(loss, row.shape)
-
-    q = q_all[...].reshape(4 * n, wide)
-    for s, out in enumerate((gp0, gp1, gp2, gp3)):
-        rows = slice(s * n, s * n + n)
-        out[:n] = (dot(tail[rows], q, 1, 0) + gp_low[rows]).astype(out.dtype)
-        if s:
-            out[n:] = jnp.zeros((EXTRA, wide), bf16)
-            put_terms(out, n, loss)
-
+    gq[...] = dot(tail[...], p[...], 0, 0) + gq_low[...]
+    for s, out in enumerate((gq0, gq1, gq2, gq3)):
+        j = (ids[X] + 4 - s) & 3
+        out[...] = gq[pl.ds(pl.multiple_of(j * n, n), n), :].astype(out.dtype)
+
+
+def passage_grad_kernel(ids, tail, row, gp_low, q_all, own, message):
+    n = q_all.shape[1]
+    width = own.shape[1]
+    q = q_all[...].reshape(4 * n, 2 * width)
+    message[4 * n :] = jnp.zeros((EXTRA, width), bf16)
+    put_terms(message, 4 * n, row[0:1])
     for c in (0, 1):
         lanes = slice(c * width, c * width + width)
-        gq = dot(tail[...], p[:, lanes], 0, 0) + gq_low[:, lanes]
+        gp = dot(tail[...], q[:, lanes], 1, 0) + gp_low[:, lanes]
 
         @pl.when(ids[CORE] == c)
         def _():
-            own[...] = gq
+            own[...] = gp
 
         @pl.when(ids[CORE] != c)
         def _():
-            message[...] = gq.astype(bf16)
-
-
-def core_sum_kernel(ids, gq_own, other, own, m1, m2, m3):
-    n = own.shape[0]
+            message[: 4 * n] = gp.astype(bf16)
+
+
+def core_sum_kernel(gp_own, row, other, own, m1, m2, m3, loss):
+    n, width = own.shape
+    total = row[0:1] + get_terms(other, 4 * n, n)
+    loss[...] = jnp.broadcast_to(total, loss.shape)
     for s, out in enumerate((own, m1, m2, m3)):
-        j = (ids[ZL] + 4 - s) & 3
-        rows = pl.ds(pl.multiple_of(j * n, n), n)
-        out[...] = (gq_own[rows, :] + other[rows, :].astype(f32)).astype(out.dtype)
-
-
-def passage_sum_kernel(ids, gp0, g1, g2, g3, row, m1, m2, m3, own, near, far, loss):
-    n, width = own.shape
-    total = row[0:1]
-    for g in (g1, g2, g3):
-        total += get_terms(g, n, n)
-    loss[...] = jnp.broadcast_to(total, loss.shape)
+        rows = slice(s * n, s * n + n)
+        v = gp_own[rows] + other[rows].astype(f32)
+        out[:n] = v.astype(out.dtype)
+        if s:
+            out[n:] = jnp.zeros((EXTRA, width), bf16)
+            put_terms(out, n, total)
+
+
+def query_sum_kernel(ids, gq0, g1, g2, g3, m1, m2, m3, own, near, far):
+    width = own.shape[1]
     same = ids[ZH] == ids[CORE]
     for c in (0, 1):
         lanes = slice(c * width, c * width + width)
-        v = gp0[:, lanes] + (
-            g1[:n, lanes].astype(f32) + g2[:n, lanes].astype(f32) + g3[:n, lanes].astype(f32)
+        v = gq0[:, lanes] + (
+            g1[:, lanes].astype(f32) + g2[:, lanes].astype(f32) + g3[:, lanes].astype(f32)
         )
 
         @pl.when(ids[CORE] == c)
@@ -336,15 +343,11 @@
 
         @pl.when((ids[CORE] == c) != same)
         def _():
-            near[:n] = v.astype(bf16)
+            near[...] = v.astype(bf16)
 
         @pl.when(ids[CORE] != c)
         def _():
-            far[:n] = v.astype(bf16)
-
-    for out in (near, far):
-        out[n:] = jnp.zeros((EXTRA, width), bf16)
-        put_terms(out, n, total)
+            far[...] = v.astype(bf16)
 
 
 def per_device(queries, passages, positives, level_weight):
@@ -356,30 +359,31 @@
     same = bi % 2 == core
     ids = jnp.stack([bi // 8, fi // 2, bi % 8 // 2, bi % 2, core]).astype(jnp.int32)
 
-    near = move_square(passages, lambda h, c: (1 - h, c) if h == c else (h, 1 - c))
-    far = move_square(passages, lambda h, c: None if h == c else (1 - h, 1 - c))
     rows = jnp.stack([positives // 64, positives % 64]).astype(bf16)
     rows = jnp.pad(rows, ((0, EXTRA - 2), (0, width - n)))
     q_row = jnp.concatenate([queries, rows], axis=0)
-    p_block, q_late = call(
-        pack_kernel, [ids], [passages, near, far, q_row],
-        [shape(n, wide, bf16), shape(n + EXTRA, width, bf16)],
-    )
-    p_blocks = [p_block] + [shift_x(p_block, s) for s in (1, 2, 3)]
-
-    q_own = [q_row, shift_zl(q_row, 1), shift_zl(q_late, 2), shift_zl(q_row, 3)]
-    q_other = [swap_core(a) for a in q_own]
+    near = move_square(queries, lambda h, c: (1 - h, c) if h == c else (h, 1 - c))
+    far = move_square(q_row, lambda h, c: None if h == c else (1 - h, 1 - c))
+    (q_msg,) = call(
+        pack_kernel, [ids], [q_row, near, far], [shape(n + EXTRA, wide, bf16)]
+    )
+    q_msgs = [q_msg] + [shift_x(q_msg, s) for s in (1, 2, 3)]
+
+    p_next, p_before = shift_zl(passages, 1), shift_zl(passages, 3)
+    p_own = [passages, p_next, shift_zl(p_next, 1), p_before]
+    p_other = [swap_core(a) for a in p_own]
 
     tile = 4 * n * 4 * n
     *partial, p, q, pos = call(
-        score_kernel, [ids], [*p_blocks, *q_own, *q_other],
+        score_kernel, [ids], [*p_own[1:], *p_other, *q_msgs, passages],
         [shape(4 * n, n, f32)] * 4
         + [
             shape(4 * n, wide, bf16),
             shape(4, n, wide, bf16),
             shape(4, 1, n, jnp.int32),
         ],
-        flops=2 * tile * wide,
+        scratch=[pltpu.VMEM((n, width), bf16), pltpu.SemaphoreType.DMA],
+        flops=2 * tile * wide, in_place=1,
     )
     pieces = [partial[0]] + [shift_y(partial[t], t) for t in (1, 2, 3)]
     e_low, low_stats, low_tops = call(
@@ -391,7 +395,7 @@
         owner_kernel, [ids, level_weight], [*pieces, pos, low_stats],
         [shape(2, 4 * n, n, f32), shape(8, 40, n, f32), shape(8, n, f32)],
     )
-    stats = lax.all_to_all(message, BOTH, 0, 0, axis_index_groups=STAT_GROUPS)
+    stats = lax.all_to_all(message, "batch", 0, 0, axis_index_groups=XZH_GROUPS)
     *tails, rates = call(
         tail_kernel, [ids, level_weight], [stats, low_tops, tops, e_high, pos],
         [shape(4 * n + EXTRA, n, bf16)] * 4 + [shape(4, 8, n, f32)],
@@ -403,36 +407,40 @@
         scratch=[pltpu.VMEM((LOW, 4 * n, 4 * n), bf16)],
         flops=4 * tile * wide, grant=12,
     )
-    gp0, gp1, gp2, gp3, gq_own, message, row = call(
-        grad_kernel, [ids], [*tails, gq_low, gp_low, p, q],
+    gq0, gq1, gq2, gq3, tail, row = call(
+        query_grad_kernel, [ids], [*tails, gq_low, p],
         [shape(n, wide, f32)]
-        + [shape(n + EXTRA, wide, bf16)] * 3
-        + [
-            shape(4 * n, width, f32),
-            shape(4 * n, width, bf16),
-            shape(8, n, f32),
-        ],
-        scratch=[pltpu.VMEM((4 * n, 4 * n), bf16)],
-        flops=4 * tile * wide, grant=12,
-    )
-    gp = [shift_x(g, -s) for s, g in enumerate((gp1, gp2, gp3), 1)]
-    own, *messages = call(
-        core_sum_kernel, [ids], [gq_own, swap_core(message)],
-        [shape(n, width, f32)] + [shape(n, width, bf16)] * 3,
-    )
-    gq = [shift_zl(m, -s) for s, m in enumerate(messages, 1)]
-    gp_own, near, far, loss_row = call(
-        passage_sum_kernel, [ids], [gp0, *gp, row, *messages],
-        [shape(n, width, f32)] + [shape(n + EXTRA, width, bf16)] * 2 + [shape(8, n, f32)],
-        unread=3,
+        + [shape(n, wide, bf16)] * 3
+        + [shape(4 * n, 4 * n, bf16), shape(8, n, f32)],
+        scratch=[pltpu.VMEM((4 * n, wide), f32)],
+        flops=2 * tile * wide,
+    )
+    gp_own, message = call(
+        passage_grad_kernel, [ids], [tail, row, gp_low, q],
+        [shape(4 * n, width, f32), shape(4 * n + EXTRA, width, bf16)],
+        flops=2 * tile * wide,
+    )
+    gq = [shift_x(g, -s) for s, g in enumerate((gq1, gq2, gq3), 1)]
+
+    own, *messages, loss_row = call(
+        core_sum_kernel, [], [gp_own, row, swap_core(message)],
+        [shape(n, width, f32)] + [shape(n + EXTRA, width, bf16)] * 3 + [shape(8, n, f32)],
+    )
+    gp = [shift_zl(m, -s) for s, m in enumerate(messages, 1)]
+    gq_own, near, far = call(
+        query_sum_kernel, [ids], [gq0, *gq, *messages],
+        [shape(n, width, f32)] + [shape(n, width, bf16)] * 2, in_place=3,
     )
     near = move_square(near, lambda h, c: (h, 1 - c) if h == c else (1 - h, c)).astype(f32)
     far = move_square(far, lambda h, c: None if h == c else (1 - h, 1 - c)).astype(f32)
-    grad_queries = own + sum(g.astype(f32) for g in gq)
-    grad_passages = near[:n] + jnp.where(same, gp_own, far[:n])
-    loss_other = jnp.where(same, near[n : n + 3, :n], far[n : n + 3, :n])
-    loss = jnp.sum(loss_row[0] + jnp.sum(loss_other, axis=0)) / (n * BATCH)
-    return loss, grad_queries.astype(bf16), grad_passages.astype(bf16)
+    grad_queries = (near + jnp.where(same, gq_own, far)).astype(bf16)
+
+    grad_passages = own + sum(g[:n].astype(f32) for g in gp)
+    loss_row = loss_row[0] + sum(jnp.sum(g[n : n + 3, :n].astype(f32), axis=0) for g in gp)
+    loss = jnp.sum(loss_row) / (n * BATCH)
+    return loss, grad_queries, grad_passages.astype(bf16)
+
+
 def solution(mesh):
     in_specs = (P("batch", "feat"), P("batch", "feat"), P("batch"), P())
     out_specs = (P(), P("batch", "feat"), P("batch", "feat"))

time: 115 us -> 123 us (1.070)
  waiting for transfers between devices: 37.4 us -> 45 us
  blocking collectives: 13.5 us -> 11.7 us
  starting transfers between devices: 41.3 us -> 42.7 us
    ppermute x6, waiting for transfers between devices: 2.51 us -> 16.8 us  [shift_zl(): lax.ppermute(a, 'batch', [(b, b // 8 * 8 + (b + 2 * s) % 8) for b in rang...]
    ppermute x6, starting transfers between devices: 15.6 us -> 9 us  [shift_zl(): lax.ppermute(a, 'batch', [(b, b // 8 * 8 + (b + 2 * s) % 8) for b in rang...]
    ppermute x5, starting transfers between devices: 3.5 us -> 9.04 us  [swap_core(): return lax.ppermute(a, 'feat', [(f, f ^ 1) for f in range(FEAT)])]
    ppermute x6, waiting for transfers between devices: 19.4 us -> 13.9 us  [shift_x(): lax.ppermute(a, 'batch', [(b, (b + 8 * s) % BATCH) for b in range(BATCH)])]
    ppermute x4, waiting for transfers between devices: 7.74 us -> 4.73 us  [move_square(): return lax.ppermute(a, BOTH, pairs)]
    all_to_all x1, blocking collectives: 13.5 us -> 11.7 us  [per_device(): stats = lax.all_to_all(message, 'batch', 0, 0, axis_index_groups=XZH_GROUPS)]
    ppermute x4, starting transfers between devices: 7.57 us -> 9.14 us  [move_square(): return lax.ppermute(a, BOTH, pairs)]
    pallas_call x9 -> x10, Pallas kernels: 15.4 us -> 15.8 us  [call(): pl.pallas_call(body, out_shape=outs, in_specs=[scalar] * len(smem) + [vme...]
  transfers between devices with their start and end apart: 27 -> 27, of which waited for: 14 -> 14; matrix products, arithmetic and copies ran while one was open for 1% -> 1% of each run, Pallas kernels for 8% -> 6%
where the time goes in v5:
time: 123 us; the launch traced here: 122 us
  waiting for transfers between devices  45 us (37%)
  starting transfers between devices  42.7 us (35%)
  Pallas kernels  15.8 us (13%)
  blocking collectives  11.7 us (10%)
  other arithmetic  3.69 us (3%)
  between operations  2.57 us (2%)
    ppermute x6, waiting for transfers between devices, shift_zl(): lax.ppermute(a, 'batch', [(b, b // 8 * 8 + (b + 2 * s) % 8) for b in rang...  16.8 us
    pallas_call x10, Pallas kernels, call(): pl.pallas_call(body, out_shape=outs, in_specs=[scalar] * len(smem) + [vme...  15.8 us
    ppermute x6, waiting for transfers between devices, shift_x(): lax.ppermute(a, 'batch', [(b, (b + 8 * s) % BATCH) for b in range(BATCH)])  13.9 us
    all_to_all x1, blocking collectives, per_device(): stats = lax.all_to_all(message, 'batch', 0, 0, axis_index_groups=XZH_GROUPS)  11.7 us
    ppermute x6, starting transfers between devices, shift_y(): lax.ppermute(a, 'feat', [(f, (f + 2 * s) % FEAT) for f in range(FEAT)])  9.22 us
    ppermute x4, starting transfers between devices, move_square(): return lax.ppermute(a, BOTH, pairs)  9.14 us
    ppermute x5, starting transfers between devices, swap_core(): return lax.ppermute(a, 'feat', [(f, f ^ 1) for f in range(FEAT)])  9.04 us
    ppermute x6, starting transfers between devices, shift_zl(): lax.ppermute(a, 'batch', [(b, b // 8 * 8 + (b + 2 * s) % 8) for b in rang...  9 us
  transfers between devices with their start and end apart: 27, of which 14 were waited for; matrix products, arithmetic and copies ran while one was open for 1% of the time, Pallas kernels for 6%

profile of v5, /device:TPU:1, one launch (start us, length us, event | category | flops | bytes accessed | tf_op | source)
XLA Modules:
  0.0 122.3 jit_solution(5967041537215753236)
XLA Ops:
  2.2 4.9 %collective-permute-start.8 = (bf16[144,512]{1,0:T(8,128)(2,1)S(1)}, bf16[144,512]{1,0:T(8,128)(2,1)S(1)}, u32[]{:S(2)}, u32[]{:S(2)}) collective-permute-start(bf16[144,512]{1,0:T(8,128)(2,1)S(1)} %pad_maximum_fusion.own), channel_id=1, source_target_pairs={{1,8},{3,10},{5,12},{7,14},{8,1},{10,3},{12,5},{14,7},{17,24},{19,... | collective-permute-start | bytes 442376 | tf_op jit(solution)/shard_map/ppermute | solution.py:55
  7.3 5.2 %collective-permute-start.2 = (bf16[128,512]{1,0:T(8,128)(2,1)}, bf16[128,512]{1,0:T(8,128)(2,1)S(1)}, u32[]{:S(2)}, u32[]{:S(2)}) collective-permute-start(bf16[128,512]{1,0:T(8,128)(2,1)} %p0_hbm.1), channel_id=1, source_target_pairs={{0,48},{8,56},{16,0},{24,8},{32,16},{40,24},{48,32},{56,40},{64,11... | collective-permute-start | bytes 393224 | tf_op jit(solution)/shard_map/ppermute | solution.py:35
  14.2 2.6 %collective-permute-start.11 = (bf16[144,1024]{1,0:T(8,128)(2,1)S(1)}, bf16[144,1024]{1,0:T(8,128)(2,1)S(1)}, u32[]{:S(2)}, u32[]{:S(2)}) collective-permute-start(bf16[144,1024]{1,0:T(8,128)(2,1)S(1)} %shard_map.67.q0), channel_id=1, source_target_pairs={{0,192},{8,200},{16,208},{24,216},{32,224},{40,232},{48,240},{56,2... | collective-permute-start | bytes 884744 | tf_op jit(solution)/shard_map/ppermute | solution.py:31
  19.8 3.7 %collective-permute-start.6 = (bf16[128,512]{1,0:T(8,128)(2,1)S(1)}, bf16[128,512]{1,0:T(8,128)(2,1)S(1)}, u32[]{:S(2)}, u32[]{:S(2)}) collective-permute-start(bf16[128,512]{1,0:T(8,128)(2,1)S(1)} %collective-permute-done.2.p3), channel_id=1, source_target_pairs={{0,1},{1,0},{2,3},{3,2},{4,5},{5,4},{6,7},{7,6},{8,9},{9,8},{10,11... | collective-permute-start | bytes 393224 | tf_op jit(solution)/shard_map/ppermute | solution.py:45
  24.9 7.5 %collective-permute-done.1.p2 = bf16[128,512]{1,0:T(8,128)(2,1)S(1)} collective-permute-done((bf16[128,512]{1,0:T(8,128)(2,1)S(1)}, bf16[128,512]{1,0:T(8,128)(2,1)S(1)}, u32[]{:S(2)}, u32[]{:S(2)}) %collective-permute-start.1) | collective-permute-done | bytes 131104 | tf_op jit(solution)/shard_map/ppermute | solution.py:35
  35.0 2.2 %shard_map.68 = (f32[512,128]{1,0:T(8,128)S(1)}, f32[512,128]{1,0:T(8,128)S(1)}, f32[512,128]{1,0:T(8,128)S(1)}, f32[512,128]{1,0:T(8,128)S(1)}, bf16[512,1024]{...) custom-call(s32[5]{0:T(128)S(1)} %stack.35.ids, ...), custom_call_target="tpu_custom_call" | custom-call | flops 536870912 | bytes 5376000 | tf_op jit(solution)/shard_map/pallas_call | solution.py:72
  38.6 2.6 %collective-permute-start.13 = (f32[512,128]{1,0:T(8,128)S(1)}, f32[512,128]{1,0:T(8,128)S(1)}, u32[]{:S(2)}, u32[]{:S(2)}) collective-permute-start(f32[512,128]{1,0:T(8,128)S(1)} %get-tuple-element.41), channel_id=1, source_target_pairs={{0,4},{1,5},{2,6},{3,7},{4,0},{5,1},{6,2},{7,3},{8,12},{9,13},{10,... | collective-permute-start | bytes 786440 | tf_op jit(solution)/shard_map/ppermute | solution.py:41
  42.2 3.7 %shard_map.69 = (f32[5,4,512,128]{3,2,1,0:T(8,128)S(1)}, f32[4,8,128]{2,1,0:T(8,128)S(1)}, f32[4,8,128]{2,1,0:T(8,128)S(1)}) custom-call(s32[5]{0:T(128)S(1)} %stack.35.ids, f32[7]{0:T(128)S(1)} %copy-done.1, bf16[512,1024]{1,0:T(8,128)(2,1)S(1)} %get-tuple-element.44.p, bf16[4,128,1024]{2,1,0:T(8,128)(2,1)S(1)} %get-tuple-element.45.q_all, ...), custom_call_target="tpu_custom_call" | custom-call | flops 536870912 | bytes 7374848 | tf_op jit(solution)/shard_map/pallas_call | solution.py:72
  46.1 6.7 %collective-permute-done.13.s2 = f32[512,128]{1,0:T(8,128)S(1)} collective-permute-done((f32[512,128]{1,0:T(8,128)S(1)}, f32[512,128]{1,0:T(8,128)S(1)}, u32[]{:S(2)}, u32[]{:S(2)}) %collective-permute-start.13) | collective-permute-done | bytes 262176 | tf_op jit(solution)/shard_map/ppermute | solution.py:41
  53.9 11.7 %all_to_all.5.stats = f32[8,40,128]{2,1,0:T(8,128)S(1)} all-to-all(f32[8,40,128]{2,1,0:T(8,128)S(1)} %get-tuple-element.47), channel_id=1, replica_groups={{0,8,64,72,128,136,192,200},{16,24,80,88,144,152,208,216},{32,40,96,104..., dimensions={0} | all-to-all | bytes 327680 | tf_op jit(solution)/shard_map/all_to_all | solution.py:398
  67.5 2.9 %collective-permute-start.16 = (bf16[528,128]{1,0:T(8,128)(2,1)S(1)}, bf16[528,128]{1,0:T(8,128)(2,1)S(1)}, u32[]{:S(2)}, u32[]{:S(2)}) collective-permute-start(bf16[528,128]{1,0:T(8,128)(2,1)S(1)} %get-tuple-element.53), channel_id=1, source_target_pairs={{0,4},{1,5},{2,6},{3,7},{4,0},{5,1},{6,2},{7,3},{8,12},{9,13},{10,... | collective-permute-start | bytes 405512 | tf_op jit(solution)/shard_map/ppermute | solution.py:41
  70.6 3.4 %shard_map.72 = (f32[512,1024]{1,0:T(8,128)S(1)}, f32[512,1024]{1,0:T(8,128)S(1)}) custom-call(s32[5]{0:T(128)S(1)} %stack.35.ids, f32[7]{0:T(128)S(1)} %copy-done.1, f32[5,4,512,128]{3,2,1,0:T(8,128)S(1)} %get-tuple-element.55.e_low, f32[4,8,128]{2,1,0:T(8,128)S(1)} %get-tuple-element.56.rates, s32[4,1,128]{2,1,0:T(1,128)S(1)} %get-tuple-element.43.pos, ...), custom_call_target="tpu_custom_call" | custom-call | flops 1073741824 | bytes 11552768 | tf_op jit(solution)/shard_map/pallas_call | solution.py:72
  74.7 1.5 %shard_map.73 = (f32[128,1024]{1,0:T(8,128)S(1)}, bf16[128,1024]{1,0:T(8,128)(2,1)S(1)}, bf16[128,1024]{1,0:T(8,128)(2,1)S(1)}, bf16[128,1024]{1,0:T(8,128)(2,1)...) custom-call(s32[5]{0:T(128)S(1)} %stack.35.ids, bf16[528,128]{1,0:T(8,128)(2,1)S(1)} %get-tuple-element.51.t0, ...), custom_call_target="tpu_custom_call" | custom-call | flops 536870912 | bytes 5525504 | tf_op jit(solution)/shard_map/pallas_call | solution.py:72
  76.2 1.6 %shard_map.74 = (f32[512,512]{1,0:T(8,128)S(1)}, bf16[528,512]{1,0:T(8,128)(2,1)S(1)}) custom-call(s32[5]{0:T(128)S(1)} %stack.35.ids, bf16[512,512]{1,0:T(8,128)(2,1)S(1)} %get-tuple-element.58.tail, f32[8,128]{1,0:T(8,128)S(1)} %get-tuple-element.59.row, f32[512,1024]{1,0:T(8,128)S(1)} %get-tuple-element.60.gp_low, ...), custom_call_target="tpu_custom_call" | custom-call | flops 536870912 | bytes 5263360 | tf_op jit(solution)/shard_map/pallas_call | solution.py:72
  77.8 3.2 %collective-permute-start.18 = (bf16[528,512]{1,0:T(8,128)(2,1)S(1)}, bf16[528,512]{1,0:T(8,128)(2,1)S(1)}, u32[]{:S(2)}, u32[]{:S(2)}) collective-permute-start(bf16[528,512]{1,0:T(8,128)(2,1)S(1)} %get-tuple-element.62), channel_id=1, source_target_pairs={{0,1},{1,0},{2,3},{3,2},{4,5},{5,4},{6,7},{7,6},{8,9},{9,8},{10,11... | collective-permute-start | bytes 1622024 | tf_op jit(solution)/shard_map/ppermute | solution.py:45
  83.1 5.7 %collective-permute-done.22.g1 = bf16[128,1024]{1,0:T(8,128)(2,1)S(1)} collective-permute-done((bf16[128,1024]{1,0:T(8,128)(2,1)S(1)}, bf16[128,1024]{1,0:T(8,128)(2,1)S(1)}, u32[]{:S(2)}, u32[]{:S(2)}) %collective-permute-start.22) | collective-permute-done | bytes 262176 | tf_op jit(solution)/shard_map/ppermute | solution.py:31
  88.9 1.9 %collective-permute-done.23.g2 = bf16[128,1024]{1,0:T(8,128)(2,1)S(1)} collective-permute-done((bf16[128,1024]{1,0:T(8,128)(2,1)S(1)}, bf16[128,1024]{1,0:T(8,128)(2,1)S(1)}, u32[]{:S(2)}, u32[]{:S(2)}) %collective-permute-start.23) | collective-permute-done | bytes 262176 | tf_op jit(solution)/shard_map/ppermute | solution.py:31
  90.8 6.3 %collective-permute-done.24.g3 = bf16[128,1024]{1,0:T(8,128)(2,1)S(1)} collective-permute-done((bf16[128,1024]{1,0:T(8,128)(2,1)S(1)}, bf16[128,1024]{1,0:T(8,128)(2,1)S(1)}, u32[]{:S(2)}, u32[]{:S(2)}) %collective-permute-start.24) | collective-permute-done | bytes 262176 | tf_op jit(solution)/shard_map/ppermute | solution.py:31
  98.7 3.2 %collective-permute-start.26 = (bf16[128,512]{1,0:T(8,128)(2,1)S(1)}, bf16[128,512]{1,0:T(8,128)(2,1)S(1)}, u32[]{:S(2)}, u32[]{:S(2)}) collective-permute-start(bf16[128,512]{1,0:T(8,128)(2,1)S(1)} %get-tuple-element.73), channel_id=1, source_target_pairs={{1,8},{3,10},{5,12},{7,14},{8,1},{10,3},{12,5},{14,7},{17,24},{19,... | collective-permute-start | bytes 393224 | tf_op jit(solution)/shard_map/ppermute | solution.py:55
  102.6 1.6 %collective-permute-start.20 = (bf16[144,512]{1,0:T(8,128)(2,1)S(1)}, bf16[144,512]{1,0:T(8,128)(2,1)S(1)}, u32[]{:S(2)}, u32[]{:S(2)}) collective-permute-start(bf16[144,512]{1,0:T(8,128)(2,1)S(1)} %get-tuple-element.65.m2), channel_id=1, source_target_pairs={{0,32},{8,40},{16,48},{24,56},{32,0},{40,8},{48,16},{56,24},{64,96... | collective-permute-start | bytes 442376 | tf_op jit(solution)/shard_map/ppermute | solution.py:35
  104.1 1.6 %collective-permute-start.21 = (bf16[144,512]{1,0:T(8,128)(2,1)S(1)}, bf16[144,512]{1,0:T(8,128)(2,1)S(1)}, u32[]{:S(2)}, u32[]{:S(2)}) collective-permute-start(bf16[144,512]{1,0:T(8,128)(2,1)S(1)} %get-tuple-element.66.m3), channel_id=1, source_target_pairs={{0,16},{8,24},{16,32},{24,40},{32,48},{40,56},{48,0},{56,8},{64,80... | collective-permute-start | bytes 442376 | tf_op jit(solution)/shard_map/ppermute | solution.py:35
  105.7 4.7 %collective-permute-done.26 = bf16[128,512]{1,0:T(8,128)(2,1)S(1)} collective-permute-done((bf16[128,512]{1,0:T(8,128)(2,1)S(1)}, bf16[128,512]{1,0:T(8,128)(2,1)S(1)}, u32[]{:S(2)}, u32[]{:S(2)}) %collective-permute-start.26) | collective-permute-done | bytes 131104 | tf_op jit(solution)/shard_map/ppermute | solution.py:55
  111.2 6.3 %collective-permute-done.20 = bf16[144,512]{1,0:T(8,128)(2,1)S(1)} collective-permute-done((bf16[144,512]{1,0:T(8,128)(2,1)S(1)}, bf16[144,512]{1,0:T(8,128)(2,1)S(1)}, u32[]{:S(2)}, u32[]{:S(2)}) %collective-permute-start.20) | collective-permute-done | bytes 147488 | tf_op jit(solution)/shard_map/ppermute | solution.py:35
  117.6 1.6 %collective-permute-done.21 = bf16[144,512]{1,0:T(8,128)(2,1)S(1)} collective-permute-done((bf16[144,512]{1,0:T(8,128)(2,1)S(1)}, bf16[144,512]{1,0:T(8,128)(2,1)S(1)}, u32[]{:S(2)}, u32[]{:S(2)}) %collective-permute-start.21) | collective-permute-done | bytes 147488 | tf_op jit(solution)/shard_map/ppermute | solution.py:35
  (55 shorter events, 23.4 us)
Async XLA Ops:
  2.2 11.4 %collective-permute-start.8 = (bf16[144,512]{1,0:T(8,128)(2,1)S(1)}, bf16[144,512]{1,0:T(8,128)(2,1)S(1)}, u32[]{:S(2)}, u32[]{:S(2)}) collective-permute-start(bf16[144,512]{1,0:T(8,128)(2,1)S(1)} %pad_maximum_fusion.own), channel_id=1, source_target_pairs={{1,8},{3,10},{5,12},{7,14},{8,1},{10,3},{12,5},{14,7},{17,24},{19,... | collective-permute-start | bytes 442376 | tf_op jit(solution)/shard_map/ppermute | solution.py:55
  7.2 6.4 %collective-permute-start.7 = (bf16[128,512]{1,0:T(8,128)(2,1)}, bf16[128,512]{1,0:T(8,128)(2,1)S(1)}, u32[]{:S(2)}, u32[]{:S(2)}) collective-permute-start(bf16[128,512]{1,0:T(8,128)(2,1)} %param.4), channel_id=1, source_target_pairs={{0,8},{1,0},{2,10},{3,2},{4,12},{5,4},{6,14},{7,6},{8,9},{9,1},{10... | collective-permute-start | bytes 393224 | tf_op jit(solution)/shard_map/ppermute | solution.py:55
  7.3 10.4 %collective-permute-start.2 = (bf16[128,512]{1,0:T(8,128)(2,1)}, bf16[128,512]{1,0:T(8,128)(2,1)S(1)}, u32[]{:S(2)}, u32[]{:S(2)}) collective-permute-start(bf16[128,512]{1,0:T(8,128)(2,1)} %p0_hbm.1), channel_id=1, source_target_pairs={{0,48},{8,56},{16,0},{24,8},{32,16},{40,24},{48,32},{56,40},{64,11... | collective-permute-start | bytes 393224 | tf_op jit(solution)/shard_map/ppermute | solution.py:35
  12.5 7.3 %collective-permute-start = (bf16[128,512]{1,0:T(8,128)(2,1)}, bf16[128,512]{1,0:T(8,128)(2,1)S(1)}, u32[]{:S(2)}, u32[]{:S(2)}) collective-permute-start(bf16[128,512]{1,0:T(8,128)(2,1)} %p0_hbm.1), channel_id=1, source_target_pairs={{0,16},{8,24},{16,32},{24,40},{32,48},{40,56},{48,0},{56,8},{64,80... | collective-permute-start | bytes 393224 | tf_op jit(solution)/shard_map/ppermute | solution.py:35
  12.5 11.0 %collective-permute-start.3 = (bf16[128,512]{1,0:T(8,128)(2,1)}, bf16[128,512]{1,0:T(8,128)(2,1)S(1)}, u32[]{:S(2)}, u32[]{:S(2)}) collective-permute-start(bf16[128,512]{1,0:T(8,128)(2,1)} %p0_hbm.1), channel_id=1, source_target_pairs={{0,1},{1,0},{2,3},{3,2},{4,5},{5,4},{6,7},{7,6},{8,9},{9,8},{10,11... | collective-permute-start | bytes 393224 | tf_op jit(solution)/shard_map/ppermute | solution.py:45
  14.2 19.9 %collective-permute-start.11 = (bf16[144,1024]{1,0:T(8,128)(2,1)S(1)}, bf16[144,1024]{1,0:T(8,128)(2,1)S(1)}, u32[]{:S(2)}, u32[]{:S(2)}) collective-permute-start(bf16[144,1024]{1,0:T(8,128)(2,1)S(1)} %shard_map.67.q0), channel_id=1, source_target_pairs={{0,192},{8,200},{16,208},{24,216},{32,224},{40,232},{48,240},{56,2... | collective-permute-start | bytes 884744 | tf_op jit(solution)/shard_map/ppermute | solution.py:31
  16.8 17.3 %collective-permute-start.10 = (bf16[144,1024]{1,0:T(8,128)(2,1)S(1)}, bf16[144,1024]{1,0:T(8,128)(2,1)S(1)}, u32[]{:S(2)}, u32[]{:S(2)}) collective-permute-start(bf16[144,1024]{1,0:T(8,128)(2,1)S(1)} %shard_map.67.q0), channel_id=1, source_target_pairs={{0,128},{8,136},{16,144},{24,152},{32,160},{40,168},{48,176},{56,1... | collective-permute-start | bytes 884744 | tf_op jit(solution)/shard_map/ppermute | solution.py:31
  17.7 16.4 %collective-permute-start.9 = (bf16[144,1024]{1,0:T(8,128)(2,1)S(1)}, bf16[144,1024]{1,0:T(8,128)(2,1)S(1)}, u32[]{:S(2)}, u32[]{:S(2)}) collective-permute-start(bf16[144,1024]{1,0:T(8,128)(2,1)S(1)} %shard_map.67.q0), channel_id=1, source_target_pairs={{0,64},{8,72},{16,80},{24,88},{32,96},{40,104},{48,112},{56,120},{... | collective-permute-start | bytes 884744 | tf_op jit(solution)/shard_map/ppermute | solution.py:31
  23.5 8.8 %collective-permute-start.1 = (bf16[128,512]{1,0:T(8,128)(2,1)S(1)}, bf16[128,512]{1,0:T(8,128)(2,1)S(1)}, u32[]{:S(2)}, u32[]{:S(2)}) collective-permute-start(bf16[128,512]{1,0:T(8,128)(2,1)S(1)} %collective-permute-done.p1), channel_id=1, source_target_pairs={{0,16},{8,24},{16,32},{24,40},{32,48},{40,56},{48,0},{56,8},{64,80... | collective-permute-start | bytes 393224 | tf_op jit(solution)/shard_map/ppermute | solution.py:35
  24.5 8.6 %collective-permute-start.4 = (bf16[128,512]{1,0:T(8,128)(2,1)S(1)}, bf16[128,512]{1,0:T(8,128)(2,1)S(1)}, u32[]{:S(2)}, u32[]{:S(2)}) collective-permute-start(bf16[128,512]{1,0:T(8,128)(2,1)S(1)} %collective-permute-done.p1), channel_id=1, source_target_pairs={{0,1},{1,0},{2,3},{3,2},{4,5},{5,4},{6,7},{7,6},{8,9},{9,8},{10,11... | collective-permute-start | bytes 393224 | tf_op jit(solution)/shard_map/ppermute | solution.py:45
  37.2 8.9 %collective-permute-start.12 = (f32[512,128]{1,0:T(8,128)S(1)}, f32[512,128]{1,0:T(8,128)S(1)}, u32[]{:S(2)}, u32[]{:S(2)}) collective-permute-start(f32[512,128]{1,0:T(8,128)S(1)} %get-tuple-element.40), channel_id=1, source_target_pairs={{0,2},{1,3},{2,4},{3,5},{4,6},{5,7},{6,0},{7,1},{8,10},{9,11},{10,... | collective-permute-start | bytes 786440 | tf_op jit(solution)/shard_map/ppermute | solution.py:41
  38.6 14.3 %collective-permute-start.13 = (f32[512,128]{1,0:T(8,128)S(1)}, f32[512,128]{1,0:T(8,128)S(1)}, u32[]{:S(2)}, u32[]{:S(2)}) collective-permute-start(f32[512,128]{1,0:T(8,128)S(1)} %get-tuple-element.41), channel_id=1, source_target_pairs={{0,4},{1,5},{2,6},{3,7},{4,0},{5,1},{6,2},{7,3},{8,12},{9,13},{10,... | collective-permute-start | bytes 786440 | tf_op jit(solution)/shard_map/ppermute | solution.py:41
  41.2 11.7 %collective-permute-start.14 = (f32[512,128]{1,0:T(8,128)S(1)}, f32[512,128]{1,0:T(8,128)S(1)}, u32[]{:S(2)}, u32[]{:S(2)}) collective-permute-start(f32[512,128]{1,0:T(8,128)S(1)} %get-tuple-element.42), channel_id=1, source_target_pairs={{0,6},{1,7},{2,0},{3,1},{4,2},{5,3},{6,4},{7,5},{8,14},{9,15},{10,... | collective-permute-start | bytes 786440 | tf_op jit(solution)/shard_map/ppermute | solution.py:41
  66.5 7.6 %collective-permute-start.15 = (bf16[528,128]{1,0:T(8,128)(2,1)S(1)}, bf16[528,128]{1,0:T(8,128)(2,1)S(1)}, u32[]{:S(2)}, u32[]{:S(2)}) collective-permute-start(bf16[528,128]{1,0:T(8,128)(2,1)S(1)} %get-tuple-element.52), channel_id=1, source_target_pairs={{0,2},{1,3},{2,4},{3,5},{4,6},{5,7},{6,0},{7,1},{8,10},{9,11},{10,... | collective-permute-start | bytes 405512 | tf_op jit(solution)/shard_map/ppermute | solution.py:41
  67.5 7.2 %collective-permute-start.16 = (bf16[528,128]{1,0:T(8,128)(2,1)S(1)}, bf16[528,128]{1,0:T(8,128)(2,1)S(1)}, u32[]{:S(2)}, u32[]{:S(2)}) collective-permute-start(bf16[528,128]{1,0:T(8,128)(2,1)S(1)} %get-tuple-element.53), channel_id=1, source_target_pairs={{0,4},{1,5},{2,6},{3,7},{4,0},{5,1},{6,2},{7,3},{8,12},{9,13},{10,... | collective-permute-start | bytes 405512 | tf_op jit(solution)/shard_map/ppermute | solution.py:41
  77.8 5.2 %collective-permute-start.18 = (bf16[528,512]{1,0:T(8,128)(2,1)S(1)}, bf16[528,512]{1,0:T(8,128)(2,1)S(1)}, u32[]{:S(2)}, u32[]{:S(2)}) collective-permute-start(bf16[528,512]{1,0:T(8,128)(2,1)S(1)} %get-tuple-element.62), channel_id=1, source_target_pairs={{0,1},{1,0},{2,3},{3,2},{4,5},{5,4},{6,7},{7,6},{8,9},{9,8},{10,11... | collective-permute-start | bytes 1622024 | tf_op jit(solution)/shard_map/ppermute | solution.py:45
  81.0 7.9 %collective-permute-start.22 = (bf16[128,1024]{1,0:T(8,128)(2,1)S(1)}, bf16[128,1024]{1,0:T(8,128)(2,1)S(1)}, u32[]{:S(2)}, u32[]{:S(2)}) collective-permute-start(bf16[128,1024]{1,0:T(8,128)(2,1)S(1)} %get-tuple-element.68), channel_id=1, source_target_pairs={{0,192},{8,200},{16,208},{24,216},{32,224},{40,232},{48,240},{56,2... | collective-permute-start | bytes 786440 | tf_op jit(solution)/shard_map/ppermute | solution.py:31
  81.7 9.1 %collective-permute-start.23 = (bf16[128,1024]{1,0:T(8,128)(2,1)S(1)}, bf16[128,1024]{1,0:T(8,128)(2,1)S(1)}, u32[]{:S(2)}, u32[]{:S(2)}) collective-permute-start(bf16[128,1024]{1,0:T(8,128)(2,1)S(1)} %get-tuple-element.69), channel_id=1, source_target_pairs={{0,128},{8,136},{16,144},{24,152},{32,160},{40,168},{48,176},{56,1... | collective-permute-start | bytes 786440 | tf_op jit(solution)/shard_map/ppermute | solution.py:31
  82.9 14.2 %collective-permute-start.24 = (bf16[128,1024]{1,0:T(8,128)(2,1)S(1)}, bf16[128,1024]{1,0:T(8,128)(2,1)S(1)}, u32[]{:S(2)}, u32[]{:S(2)}) collective-permute-start(bf16[128,1024]{1,0:T(8,128)(2,1)S(1)} %get-tuple-element.70), channel_id=1, source_target_pairs={{0,64},{8,72},{16,80},{24,88},{32,96},{40,104},{48,112},{56,120},{... | collective-permute-start | bytes 786440 | tf_op jit(solution)/shard_map/ppermute | solution.py:31
  97.8 7.9 %collective-permute-start.25 = (bf16[128,512]{1,0:T(8,128)(2,1)S(1)}, bf16[128,512]{1,0:T(8,128)(2,1)S(1)}, u32[]{:S(2)}, u32[]{:S(2)}) collective-permute-start(bf16[128,512]{1,0:T(8,128)(2,1)S(1)} %get-tuple-element.71), channel_id=1, source_target_pairs={{0,1},{1,9},{2,3},{3,11},{4,5},{5,13},{6,7},{7,15},{8,0},{9,8},{10... | collective-permute-start | bytes 393224 | tf_op jit(solution)/shard_map/ppermute | solution.py:55
  98.7 11.8 %collective-permute-start.26 = (bf16[128,512]{1,0:T(8,128)(2,1)S(1)}, bf16[128,512]{1,0:T(8,128)(2,1)S(1)}, u32[]{:S(2)}, u32[]{:S(2)}) collective-permute-start(bf16[128,512]{1,0:T(8,128)(2,1)S(1)} %get-tuple-element.73), channel_id=1, source_target_pairs={{1,8},{3,10},{5,12},{7,14},{8,1},{10,3},{12,5},{14,7},{17,24},{19,... | collective-permute-start | bytes 393224 | tf_op jit(solution)/shard_map/ppermute | solution.py:55
  101.9 9.2 %collective-permute-start.19 = (bf16[144,512]{1,0:T(8,128)(2,1)S(1)}, bf16[144,512]{1,0:T(8,128)(2,1)S(1)}, u32[]{:S(2)}, u32[]{:S(2)}) collective-permute-start(bf16[144,512]{1,0:T(8,128)(2,1)S(1)} %get-tuple-element.64.m1), channel_id=1, source_target_pairs={{0,48},{8,56},{16,0},{24,8},{32,16},{40,24},{48,32},{56,40},{64,11... | collective-permute-start | bytes 442376 | tf_op jit(solution)/shard_map/ppermute | solution.py:35
  102.6 15.0 %collective-permute-start.20 = (bf16[144,512]{1,0:T(8,128)(2,1)S(1)}, bf16[144,512]{1,0:T(8,128)(2,1)S(1)}, u32[]{:S(2)}, u32[]{:S(2)}) collective-permute-start(bf16[144,512]{1,0:T(8,128)(2,1)S(1)} %get-tuple-element.65.m2), channel_id=1, source_target_pairs={{0,32},{8,40},{16,48},{24,56},{32,0},{40,8},{48,16},{56,24},{64,96... | collective-permute-start | bytes 442376 | tf_op jit(solution)/shard_map/ppermute | solution.py:35
  104.1 15.1 %collective-permute-start.21 = (bf16[144,512]{1,0:T(8,128)(2,1)S(1)}, bf16[144,512]{1,0:T(8,128)(2,1)S(1)}, u32[]{:S(2)}, u32[]{:S(2)}) collective-permute-start(bf16[144,512]{1,0:T(8,128)(2,1)S(1)} %get-tuple-element.66.m3), channel_id=1, source_target_pairs={{0,16},{8,24},{16,32},{24,40},{32,48},{40,56},{48,0},{56,8},{64,80... | collective-permute-start | bytes 442376 | tf_op jit(solution)/shard_map/ppermute | solution.py:35
  (5 other events, 53.3 us)

commit v6 on v5

--- a/solution.py
+++ b/solution.py
@@ -65,7 +65,7 @@
     return jax.ShapeDtypeStruct(dims_dtype[:-1], dims_dtype[-1])
 
 
-def call(body, smem, args, outs, scratch=(), flops=0, grant=8, in_place=0):
+def call(body, smem, args, outs, scratch=(), flops=0, grant=8, in_place=0, fixed=False):
     vmem = pl.BlockSpec(memory_space=pltpu.VMEM)
     scalar = pl.BlockSpec(memory_space=pltpu.SMEM)
     moved = sum(a.size * a.dtype.itemsize for a in (*args, *outs))
@@ -74,7 +74,7 @@
         out_shape=outs,
         in_specs=[scalar] * len(smem)
         + [vmem] * (len(args) - in_place)
-        + [pl.BlockSpec(memory_space=pl.ANY)] * in_place,
+        + [pl.BlockSpec(memory_space=pltpu.HBM if fixed else pl.ANY)] * in_place,
         out_specs=[vmem] * len(outs),
         scratch_shapes=list(scratch),
         cost_estimate=pl.CostEstimate(
@@ -112,27 +112,43 @@
                 put(a, b, own if matches else far)
 
 
+def digit_kernel(ids, positives, queries, out, arrived):
+    n, width = queries.shape
+    copy = pltpu.make_async_copy(queries, out.at[pl.ds(0, n)], arrived)
+    copy.start()
+    p = positives[...]
+    digits = jnp.concatenate([p >> 6, p & 63], axis=0).astype(f32)
+    out[n:] = jnp.zeros((EXTRA, width), bf16)
+    rows = jnp.concatenate([digits, jnp.zeros((EXTRA - 2, n), f32)], axis=0)
+    out[n:, :n] = rows.astype(bf16)
+    copy.wait()
+
+
+def gather_kernel(ids, after, before, own, out, arrived):
+    n = after.shape[0]
+    copy = pltpu.make_async_copy(own, out.at[pl.ds(0, n)], arrived)
+    copy.start()
+    out[n : 2 * n] = after[...]
+    out[2 * n :] = before[...]
+    copy.wait()
+
+
 def score_kernel(
-    ids, p1, p2, p3, o0, o1, o2, o3, q0, q1, q2, q3, p0_hbm,
-    s0, s1, s2, s3, p, q_all, pos, p0, arrived,
+    ids, near, other_near, far, other_far, q0, q1, q2, q3, s0, s1, s2, s3, p, q_all, pos
 ):
-    n, width = p1.shape
-    copy = pltpu.make_async_copy(p0_hbm, p0, arrived)
-    copy.start()
-    for s, (own, other) in enumerate(zip((p1, p2, p3, p0), (o1, o2, o3, o0))):
-        rows = slice((s + 1) % 4 * n, (s + 1) % 4 * n + n)
-        if s == 3:
-            copy.wait()
-
-        @pl.when(ids[CORE] == 0)
-        def _():
-            p[rows, :width] = own[...]
-            p[rows, width:] = other[...]
-
-        @pl.when(ids[CORE] != 0)
-        def _():
-            p[rows, :width] = other[...]
-            p[rows, width:] = own[...]
+    n, width = far.shape
+    for core in (0, 1):
+        for own, other, take, put in (
+            (near, other_near, slice(0, 2 * n), slice(0, 2 * n)),
+            (far, other_far, slice(0, n), slice(2 * n, 3 * n)),
+            (near, other_near, slice(2 * n, 3 * n), slice(3 * n, 4 * n)),
+        ):
+
+            @pl.when(ids[CORE] == core)
+            def _():
+                first, second = (other, own) if core else (own, other)
+                p[put, :width] = first[take]
+                p[put, width:] = second[take]
 
     for s, q in enumerate((q0, q1, q2, q3)):
         j = (ids[X] + 4 - s) & 3
@@ -282,54 +298,62 @@
     fill(gp, lambda k, a, b: dot(tails[k], q[:, a:b], 1, 0))
 
 
-def query_grad_kernel(ids, t0, t1, t2, t3, gq_low, p, gq0, gq1, gq2, gq3, tail, row, gq):
-    n, wide = gq0.shape
+def passage_grad_kernel(ids, t0, t1, t2, t3, gp_low, q_all, own, message, tail, row):
+    n = q_all.shape[1]
+    width = own.shape[1]
     loss = jnp.zeros((1, n), f32)
     for t, ref in enumerate((t0, t1, t2, t3)):
         j = (ids[Y] + 4 - t) & 3
         tail[:, pl.ds(pl.multiple_of(j * n, n), n)] = ref[: 4 * n]
         loss += get_terms(ref, 4 * n, n)
     row[...] = jnp.broadcast_to(loss, row.shape)
+    q = q_all[...].reshape(4 * n, 2 * width)
+    message[4 * n :] = jnp.zeros((EXTRA, width), bf16)
+    put_terms(message, 4 * n, loss)
+    for c in (0, 1):
+        lanes = slice(c * width, c * width + width)
+        gp = dot(tail[...], q[:, lanes], 1, 0) + gp_low[:, lanes]
+
+        @pl.when(ids[CORE] == c)
+        def _():
+            own[...] = gp
+
+        @pl.when(ids[CORE] != c)
+        def _():
+            message[: 4 * n] = gp.astype(bf16)
+
+
+def query_grad_kernel(ids, tail, gq_low, p, message, gq0, gq1, gq2, gq3, gq):
+    n = gq0.shape[0]
     gq[...] = dot(tail[...], p[...], 0, 0) + gq_low[...]
     for s, out in enumerate((gq0, gq1, gq2, gq3)):
         j = (ids[X] + 4 - s) & 3
         out[...] = gq[pl.ds(pl.multiple_of(j * n, n), n), :].astype(out.dtype)
 
 
-def passage_grad_kernel(ids, tail, row, gp_low, q_all, own, message):
-    n = q_all.shape[1]
-    width = own.shape[1]
-    q = q_all[...].reshape(4 * n, 2 * width)
-    message[4 * n :] = jnp.zeros((EXTRA, width), bf16)
-    put_terms(message, 4 * n, row[0:1])
-    for c in (0, 1):
-        lanes = slice(c * width, c * width + width)
-        gp = dot(tail[...], q[:, lanes], 1, 0) + gp_low[:, lanes]
-
-        @pl.when(ids[CORE] == c)
-        def _():
-            own[...] = gp
-
-        @pl.when(ids[CORE] != c)
-        def _():
-            message[: 4 * n] = gp.astype(bf16)
-
-
-def core_sum_kernel(gp_own, row, other, own, m1, m2, m3, loss):
+def core_sum_kernel(ids, gp_own, row, other, own, after, far, before, loss):
     n, width = own.shape
     total = row[0:1] + get_terms(other, 4 * n, n)
     loss[...] = jnp.broadcast_to(total, loss.shape)
-    for s, out in enumerate((own, m1, m2, m3)):
+    for s, out in enumerate((own, after, far, before)):
         rows = slice(s * n, s * n + n)
         v = gp_own[rows] + other[rows].astype(f32)
         out[:n] = v.astype(out.dtype)
-        if s:
+        if s >= 2:
             out[n:] = jnp.zeros((EXTRA, width), bf16)
             put_terms(out, n, total)
 
 
-def query_sum_kernel(ids, gq0, g1, g2, g3, m1, m2, m3, own, near, far):
-    width = own.shape[1]
+def middle_kernel(
+    ids, gq0, g1, g2, g3, gp_own, after, far_in, before_in, row,
+    own, near, far, relay, gp_sum, loss,
+):
+    n, width = own.shape
+    relay[n:] = jnp.zeros((EXTRA, width), bf16)
+    put_terms(relay, n, row[0:1] + get_terms(far_in, n, n))
+    relay[:n] = (after[...] + far_in[:n].astype(f32)).astype(bf16)
+    gp_sum[...] = gp_own[...] + before_in[:n].astype(f32)
+    loss[...] = jnp.broadcast_to(row[0:1] + get_terms(before_in, n, n), loss.shape)
     same = ids[ZH] == ids[CORE]
     for c in (0, 1):
         lanes = slice(c * width, c * width + width)
@@ -350,19 +374,35 @@
             far[...] = v.astype(bf16)
 
 
+def last_kernel(ids, gq_own, near, far, gp_sum, relay, row, gq, gp, loss):
+    n = gq.shape[0]
+
+    @pl.when(ids[ZH] == ids[CORE])
+    def _():
+        gq[...] = (gq_own[...] + near[...].astype(f32)).astype(bf16)
+
+    @pl.when(ids[ZH] != ids[CORE])
+    def _():
+        gq[...] = (far[...].astype(f32) + near[...].astype(f32)).astype(bf16)
+
+    gp[...] = (gp_sum[...] + relay[:n].astype(f32)).astype(bf16)
+    total = row[0:1] + get_terms(relay, n, n)
+    loss[...] = jnp.sum(total, axis=1, keepdims=True) * (1.0 / (n * BATCH))
+
+
 def per_device(queries, passages, positives, level_weight):
     n, width = queries.shape
     wide = 2 * width
     bi = lax.axis_index("batch")
     fi = lax.axis_index("feat")
-    core = fi % 2
-    same = bi % 2 == core
-    ids = jnp.stack([bi // 8, fi // 2, bi % 8 // 2, bi % 2, core]).astype(jnp.int32)
-
-    rows = jnp.stack([positives // 64, positives % 64]).astype(bf16)
-    rows = jnp.pad(rows, ((0, EXTRA - 2), (0, width - n)))
-    q_row = jnp.concatenate([queries, rows], axis=0)
+    ids = jnp.stack([bi // 8, fi // 2, bi % 8 // 2, bi % 2, fi % 2]).astype(jnp.int32)
+    dma = pltpu.SemaphoreType.DMA
+
     near = move_square(queries, lambda h, c: (1 - h, c) if h == c else (h, 1 - c))
+    (q_row,) = call(
+        digit_kernel, [ids], [positives.reshape(1, n), queries],
+        [shape(n + EXTRA, width, bf16)], scratch=[dma], in_place=1, fixed=True,
+    )
     far = move_square(q_row, lambda h, c: None if h == c else (1 - h, 1 - c))
     (q_msg,) = call(
         pack_kernel, [ids], [q_row, near, far], [shape(n + EXTRA, wide, bf16)]
@@ -370,20 +410,22 @@
     q_msgs = [q_msg] + [shift_x(q_msg, s) for s in (1, 2, 3)]
 
     p_next, p_before = shift_zl(passages, 1), shift_zl(passages, 3)
-    p_own = [passages, p_next, shift_zl(p_next, 1), p_before]
-    p_other = [swap_core(a) for a in p_own]
+    (p_near,) = call(
+        gather_kernel, [ids], [p_next, p_before, passages],
+        [shape(3 * n, width, bf16)], scratch=[dma], in_place=1, fixed=True,
+    )
+    p_far = shift_zl(p_next, 1)
 
     tile = 4 * n * 4 * n
     *partial, p, q, pos = call(
-        score_kernel, [ids], [*p_own[1:], *p_other, *q_msgs, passages],
+        score_kernel, [ids], [p_near, swap_core(p_near), p_far, swap_core(p_far), *q_msgs],
         [shape(4 * n, n, f32)] * 4
         + [
             shape(4 * n, wide, bf16),
             shape(4, n, wide, bf16),
             shape(4, 1, n, jnp.int32),
         ],
-        scratch=[pltpu.VMEM((n, width), bf16), pltpu.SemaphoreType.DMA],
-        flops=2 * tile * wide, in_place=1,
+        flops=2 * tile * wide,
     )
     pieces = [partial[0]] + [shift_y(partial[t], t) for t in (1, 2, 3)]
     e_low, low_stats, low_tops = call(
@@ -407,38 +449,45 @@
         scratch=[pltpu.VMEM((LOW, 4 * n, 4 * n), bf16)],
         flops=4 * tile * wide, grant=12,
     )
-    gq0, gq1, gq2, gq3, tail, row = call(
-        query_grad_kernel, [ids], [*tails, gq_low, p],
-        [shape(n, wide, f32)]
-        + [shape(n, wide, bf16)] * 3
-        + [shape(4 * n, 4 * n, bf16), shape(8, n, f32)],
+    gp_own, message, tail, row = call(
+        passage_grad_kernel, [ids], [*tails, gp_low, q],
+        [
+            shape(4 * n, width, f32),
+            shape(4 * n + EXTRA, width, bf16),
+            shape(4 * n, 4 * n, bf16),
+            shape(8, n, f32),
+        ],
+        flops=2 * tile * wide,
+    )
+    other = swap_core(message)
+    gq0, gq1, gq2, gq3 = call(
+        query_grad_kernel, [ids], [tail, gq_low, p, message],
+        [shape(n, wide, f32)] + [shape(n, wide, bf16)] * 3,
         scratch=[pltpu.VMEM((4 * n, wide), f32)],
-        flops=2 * tile * wide,
-    )
-    gp_own, message = call(
-        passage_grad_kernel, [ids], [tail, row, gp_low, q],
-        [shape(4 * n, width, f32), shape(4 * n + EXTRA, width, bf16)],
-        flops=2 * tile * wide,
+        flops=2 * tile * wide, in_place=1,
     )
     gq = [shift_x(g, -s) for s, g in enumerate((gq1, gq2, gq3), 1)]
-
-    own, *messages, loss_row = call(
-        core_sum_kernel, [], [gp_own, row, swap_core(message)],
-        [shape(n, width, f32)] + [shape(n + EXTRA, width, bf16)] * 3 + [shape(8, n, f32)],
-    )
-    gp = [shift_zl(m, -s) for s, m in enumerate(messages, 1)]
-    gq_own, near, far = call(
-        query_sum_kernel, [ids], [gq0, *gq, *messages],
-        [shape(n, width, f32)] + [shape(n, width, bf16)] * 2, in_place=3,
-    )
-    near = move_square(near, lambda h, c: (h, 1 - c) if h == c else (1 - h, c)).astype(f32)
-    far = move_square(far, lambda h, c: None if h == c else (1 - h, 1 - c)).astype(f32)
-    grad_queries = (near + jnp.where(same, gq_own, far)).astype(bf16)
-
-    grad_passages = own + sum(g[:n].astype(f32) for g in gp)
-    loss_row = loss_row[0] + sum(jnp.sum(g[n : n + 3, :n].astype(f32), axis=0) for g in gp)
-    loss = jnp.sum(loss_row) / (n * BATCH)
-    return loss, grad_queries, grad_passages.astype(bf16)
+    gp_own, after, far, before, row = call(
+        core_sum_kernel, [ids], [gp_own, row, other],
+        [shape(n, width, f32)] * 2
+        + [shape(n + EXTRA, width, bf16)] * 2
+        + [shape(8, n, f32)],
+    )
+    far_in, before_in = shift_zl(far, -1), shift_zl(before, 1)
+    gq_own, near, far, relay, gp_sum, row = call(
+        middle_kernel, [ids], [gq0, *gq, gp_own, after, far_in, before_in, row],
+        [shape(n, width, f32)]
+        + [shape(n, width, bf16)] * 2
+        + [shape(n + EXTRA, width, bf16), shape(n, width, f32), shape(8, n, f32)],
+    )
+    near = move_square(near, lambda h, c: (h, 1 - c) if h == c else (1 - h, c))
+    far = move_square(far, lambda h, c: None if h == c else (1 - h, 1 - c))
+    relay = shift_zl(relay, -1)
+    grad_queries, grad_passages, loss = call(
+        last_kernel, [ids], [gq_own, near, far, gp_sum, relay, row],
+        [shape(n, width, bf16), shape(n, width, bf16), shape(1, 1, f32)],
+    )
+    return loss.reshape(()), grad_queries, grad_passages
 
 
 def solution(mesh):

time: 123 us -> 111 us (0.902)
  waiting for transfers between devices: 45 us -> 35.8 us
  Pallas kernels: 15.8 us -> 19.6 us
  other arithmetic: 3.69 us -> 0 us
  blocking collectives: 11.7 us -> 8.67 us
  between operations: 2.57 us -> 0.79 us
  starting transfers between devices: 42.7 us -> 44.3 us
    ppermute x6, waiting for transfers between devices: 16.8 us -> 8.64 us  [shift_zl(): lax.ppermute(a, 'batch', [(b, b // 8 * 8 + (b + 2 * s) % 8) for b in rang...]
    ppermute x6, starting transfers between devices: 9 us -> 15.4 us  [shift_zl(): lax.ppermute(a, 'batch', [(b, b // 8 * 8 + (b + 2 * s) % 8) for b in rang...]
    ppermute x5 -> x3, starting transfers between devices: 9.04 us -> 4.85 us  [swap_core(): return lax.ppermute(a, 'feat', [(f, f ^ 1) for f in range(FEAT)])]
    pallas_call x10 -> x13, Pallas kernels: 15.8 us -> 19.6 us  [call(): pl.pallas_call(body, out_shape=outs, in_specs=[scalar] * len(smem) + [vme...]
    all_to_all x1, blocking collectives: 11.7 us -> 8.67 us  [per_device(): stats = lax.all_to_all(message, 'batch', 0, 0, axis_index_groups=XZH_GROUPS)]
    ppermute x6, waiting for transfers between devices: 13.9 us -> 11.8 us  [shift_x(): lax.ppermute(a, 'batch', [(b, (b + 8 * s) % BATCH) for b in range(BATCH)])]
    ppermute x4, waiting for transfers between devices: 4.73 us -> 6.58 us  [move_square(): return lax.ppermute(a, BOTH, pairs)]
    convert_element_type x2 -> x0, other arithmetic: 1.43 us -> none  [the longest x1 0.72 us: per_device(): return (loss, grad_queries, grad_passages.astype(bf16))]
  transfers between devices with their start and end apart: 27 -> 25, of which waited for: 14 -> 12; matrix products, arithmetic and copies ran while one was open for 1% -> 0% of each run, Pallas kernels for 6% -> 11%
where the time goes in v6:
time: 111 us
  starting transfers between devices  44.3 us (40%)
  waiting for transfers between devices  35.8 us (32%)
  Pallas kernels  19.6 us (18%)
  blocking collectives  8.67 us (8%)
  local copies, waits for them, and re-layouts  1.65 us (1%)
    pallas_call x13, Pallas kernels, call(): pl.pallas_call(body, out_shape=outs, in_specs=[scalar] * len(smem) + [vme...  19.6 us
    ppermute x6, starting transfers between devices, shift_zl(): lax.ppermute(a, 'batch', [(b, b // 8 * 8 + (b + 2 * s) % 8) for b in rang...  15.4 us
    ppermute x6, waiting for transfers between devices, shift_x(): lax.ppermute(a, 'batch', [(b, (b + 8 * s) % BATCH) for b in range(BATCH)])  11.8 us
    ppermute x6, starting transfers between devices, shift_y(): lax.ppermute(a, 'feat', [(f, (f + 2 * s) % FEAT) for f in range(FEAT)])  9.22 us
    all_to_all x1, blocking collectives, per_device(): stats = lax.all_to_all(message, 'batch', 0, 0, axis_index_groups=XZH_GROUPS)  8.67 us
    ppermute x6, waiting for transfers between devices, shift_zl(): lax.ppermute(a, 'batch', [(b, b // 8 * 8 + (b + 2 * s) % 8) for b in rang...  8.64 us
    ppermute x4, starting transfers between devices, move_square(): return lax.ppermute(a, BOTH, pairs)  7.87 us
    ppermute x6, waiting for transfers between devices, shift_y(): lax.ppermute(a, 'feat', [(f, (f + 2 * s) % FEAT) for f in range(FEAT)])  7.76 us
  transfers between devices with their start and end apart: 25, of which 12 were waited for; matrix products, arithmetic and copies ran while one was open for 0% of the time, Pallas kernels for 11%

profile of v6, /device:TPU:1, one launch (start us, length us, event | category | flops | bytes accessed | tf_op | source)
XLA Modules:
  0.0 110.9 jit_solution(9889289832920428038)
XLA Ops:
  0.6 3.9 %collective-permute-start = (bf16[128,512]{1,0:T(8,128)(2,1)}, bf16[128,512]{1,0:T(8,128)(2,1)S(1)}, u32[]{:S(2)}, u32[]{:S(2)}) collective-permute-start(bf16[128,512]{1,0:T(8,128)(2,1)} %own.1), channel_id=1, source_target_pairs={{0,16},{8,24},{16,32},{24,40},{32,48},{40,56},{48,0},{56,8},{64,80... | collective-permute-start | bytes 393224 | tf_op jit(solution)/shard_map/ppermute | solution.py:35
  4.5 3.1 %collective-permute-start.1 = (bf16[128,512]{1,0:T(8,128)(2,1)}, bf16[128,512]{1,0:T(8,128)(2,1)S(1)}, u32[]{:S(2)}, u32[]{:S(2)}) collective-permute-start(bf16[128,512]{1,0:T(8,128)(2,1)} %own.1), channel_id=1, source_target_pairs={{0,48},{8,56},{16,0},{24,8},{32,16},{40,24},{48,32},{56,40},{64,11... | collective-permute-start | bytes 393224 | tf_op jit(solution)/shard_map/ppermute | solution.py:35
  8.4 1.5 %shard_map.68.own = bf16[144,512]{1,0:T(8,128)(2,1)S(1)} custom-call(s32[5]{0:T(128)S(1)} %stack.23.ids, s32[1,128]{1,0:T(1,128)S(1)} %bitcast.7, bf16[128,512]{1,0:T(8,128)(2,1)} %queries.1), custom_call_target="tpu_custom_call" | custom-call | bytes 279040 | tf_op jit(solution)/shard_map/pallas_call | solution.py:72
  9.9 3.5 %collective-permute-start.6 = (bf16[144,512]{1,0:T(8,128)(2,1)S(1)}, bf16[144,512]{1,0:T(8,128)(2,1)S(1)}, u32[]{:S(2)}, u32[]{:S(2)}) collective-permute-start(bf16[144,512]{1,0:T(8,128)(2,1)S(1)} %shard_map.68.own), channel_id=1, source_target_pairs={{1,8},{3,10},{5,12},{7,14},{8,1},{10,3},{12,5},{14,7},{17,24},{19,... | collective-permute-start | bytes 442376 | tf_op jit(solution)/shard_map/ppermute | solution.py:55
  13.5 1.8 %collective-permute-done.1.before = bf16[128,512]{1,0:T(8,128)(2,1)S(1)} collective-permute-done((bf16[128,512]{1,0:T(8,128)(2,1)}, bf16[128,512]{1,0:T(8,128)(2,1)S(1)}, u32[]{:S(2)}, u32[]{:S(2)}) %collective-permute-start.1) | collective-permute-done | bytes 131104 | tf_op jit(solution)/shard_map/ppermute | solution.py:35
  20.4 2.5 %collective-permute-start.8 = (bf16[144,1024]{1,0:T(8,128)(2,1)S(1)}, bf16[144,1024]{1,0:T(8,128)(2,1)S(1)}, u32[]{:S(2)}, u32[]{:S(2)}) collective-permute-start(bf16[144,1024]{1,0:T(8,128)(2,1)S(1)} %shard_map.69.q0), channel_id=1, source_target_pairs={{0,128},{8,136},{16,144},{24,152},{32,160},{40,168},{48,176},{56,1... | collective-permute-start | bytes 884744 | tf_op jit(solution)/shard_map/ppermute | solution.py:31
  24.0 3.0 %collective-permute-start.3 = (bf16[128,512]{1,0:T(8,128)(2,1)S(1)}, bf16[128,512]{1,0:T(8,128)(2,1)S(1)}, u32[]{:S(2)}, u32[]{:S(2)}) collective-permute-start(bf16[128,512]{1,0:T(8,128)(2,1)S(1)} %collective-permute-done.after), channel_id=1, source_target_pairs={{0,16},{8,24},{16,32},{24,40},{32,48},{40,56},{48,0},{56,8},{64,80... | collective-permute-start | bytes 393224 | tf_op jit(solution)/shard_map/ppermute | solution.py:35
  27.0 6.8 %collective-permute-done.3.far = bf16[128,512]{1,0:T(8,128)(2,1)S(1)} collective-permute-done((bf16[128,512]{1,0:T(8,128)(2,1)S(1)}, bf16[128,512]{1,0:T(8,128)(2,1)S(1)}, u32[]{:S(2)}, u32[]{:S(2)}) %collective-permute-start.3) | collective-permute-done | bytes 131104 | tf_op jit(solution)/shard_map/ppermute | solution.py:35
  36.7 2.0 %shard_map.70 = (f32[512,128]{1,0:T(8,128)S(1)}, f32[512,128]{1,0:T(8,128)S(1)}, f32[512,128]{1,0:T(8,128)S(1)}, f32[512,128]{1,0:T(8,128)S(1)}, bf16[512,1024]{...) custom-call(s32[5]{0:T(128)S(1)} %stack.23.ids, bf16[384,512]{1,0:T(8,128)(2,1)S(1)} %shard_map.67.near, ...), custom_call_target="tpu_custom_call" | custom-call | flops 536870912 | bytes 5376000 | tf_op jit(solution)/shard_map/pallas_call | solution.py:72
  40.1 2.6 %collective-permute-start.11 = (f32[512,128]{1,0:T(8,128)S(1)}, f32[512,128]{1,0:T(8,128)S(1)}, u32[]{:S(2)}, u32[]{:S(2)}) collective-permute-start(f32[512,128]{1,0:T(8,128)S(1)} %get-tuple-element.47), channel_id=1, source_target_pairs={{0,4},{1,5},{2,6},{3,7},{4,0},{5,1},{6,2},{7,3},{8,12},{9,13},{10,... | collective-permute-start | bytes 786440 | tf_op jit(solution)/shard_map/ppermute | solution.py:41
  43.8 3.7 %shard_map.71 = (f32[5,4,512,128]{3,2,1,0:T(8,128)S(1)}, f32[4,8,128]{2,1,0:T(8,128)S(1)}, f32[4,8,128]{2,1,0:T(8,128)S(1)}) custom-call(s32[5]{0:T(128)S(1)} %stack.23.ids, f32[7]{0:T(128)S(1)} %copy-done.1, bf16[512,1024]{1,0:T(8,128)(2,1)S(1)} %get-tuple-element.50.p, bf16[4,128,1024]{2,1,0:T(8,128)(2,1)S(1)} %get-tuple-element.51.q_all, ...), custom_call_target="tpu_custom_call" | custom-call | flops 536870912 | bytes 7374848 | tf_op jit(solution)/shard_map/pallas_call | solution.py:72
  47.6 6.7 %collective-permute-done.11.s2 = f32[512,128]{1,0:T(8,128)S(1)} collective-permute-done((f32[512,128]{1,0:T(8,128)S(1)}, f32[512,128]{1,0:T(8,128)S(1)}, u32[]{:S(2)}, u32[]{:S(2)}) %collective-permute-start.11) | collective-permute-done | bytes 262176 | tf_op jit(solution)/shard_map/ppermute | solution.py:41
  55.4 8.7 %all_to_all.5.stats = f32[8,40,128]{2,1,0:T(8,128)S(1)} all-to-all(f32[8,40,128]{2,1,0:T(8,128)S(1)} %get-tuple-element.53), channel_id=1, replica_groups={{0,8,64,72,128,136,192,200},{16,24,80,88,144,152,208,216},{32,40,96,104..., dimensions={0} | all-to-all | bytes 327680 | tf_op jit(solution)/shard_map/all_to_all | solution.py:440
  66.2 2.9 %collective-permute-start.14 = (bf16[528,128]{1,0:T(8,128)(2,1)S(1)}, bf16[528,128]{1,0:T(8,128)(2,1)S(1)}, u32[]{:S(2)}, u32[]{:S(2)}) collective-permute-start(bf16[528,128]{1,0:T(8,128)(2,1)S(1)} %get-tuple-element.59), channel_id=1, source_target_pairs={{0,4},{1,5},{2,6},{3,7},{4,0},{5,1},{6,2},{7,3},{8,12},{9,13},{10,... | collective-permute-start | bytes 405512 | tf_op jit(solution)/shard_map/ppermute | solution.py:41
  69.1 3.4 %shard_map.74 = (f32[512,1024]{1,0:T(8,128)S(1)}, f32[512,1024]{1,0:T(8,128)S(1)}) custom-call(s32[5]{0:T(128)S(1)} %stack.23.ids, f32[7]{0:T(128)S(1)} %copy-done.1, f32[5,4,512,128]{3,2,1,0:T(8,128)S(1)} %get-tuple-element.61.e_low, f32[4,8,128]{2,1,0:T(8,128)S(1)} %get-tuple-element.62.rates, s32[4,1,128]{2,1,0:T(1,128)S(1)} %get-tuple-element.49.pos, ...), custom_call_target="tpu_custom_call" | custom-call | flops 1073741824 | bytes 11552768 | tf_op jit(solution)/shard_map/pallas_call | solution.py:72
  73.5 1.6 %shard_map.75 = (f32[512,512]{1,0:T(8,128)S(1)}, bf16[528,512]{1,0:T(8,128)(2,1)S(1)}, bf16[512,512]{1,0:T(8,128)(2,1)S(1)}, f32[8,128]{1,0:T(8,128)S(1)}) custom-call(s32[5]{0:T(128)S(1)} %stack.23.ids, bf16[528,128]{1,0:T(8,128)(2,1)S(1)} %get-tuple-element.57.t0, bf16[528,128]{1,0:T(8,128)(2,1)S(1)} %collective-permute-done.13.t1, ...), custom_call_target="tpu_custom_call" | custom-call | flops 536870912 | bytes 5804032 | tf_op jit(solution)/shard_map/pallas_call | solution.py:72
  75.1 3.2 %collective-permute-start.19 = (bf16[528,512]{1,0:T(8,128)(2,1)S(1)}, bf16[528,512]{1,0:T(8,128)(2,1)S(1)}, u32[]{:S(2)}, u32[]{:S(2)}) collective-permute-start(bf16[528,512]{1,0:T(8,128)(2,1)S(1)} %get-tuple-element.66.message), channel_id=1, source_target_pairs={{0,1},{1,0},{2,3},{3,2},{4,5},{5,4},{6,7},{7,6},{8,9},{9,8},{10,11... | collective-permute-start | bytes 1622024 | tf_op jit(solution)/shard_map/ppermute | solution.py:45
  82.5 2.5 %collective-permute-start.20 = (bf16[144,512]{1,0:T(8,128)(2,1)S(1)}, bf16[144,512]{1,0:T(8,128)(2,1)S(1)}, u32[]{:S(2)}, u32[]{:S(2)}) collective-permute-start(bf16[144,512]{1,0:T(8,128)(2,1)S(1)} %get-tuple-element.75), channel_id=1, source_target_pairs={{0,48},{8,56},{16,0},{24,8},{32,16},{40,24},{48,32},{56,40},{64,11... | collective-permute-start | bytes 442376 | tf_op jit(solution)/shard_map/ppermute | solution.py:35
  85.4 2.3 %collective-permute-done.16.g1 = bf16[128,1024]{1,0:T(8,128)(2,1)S(1)} collective-permute-done((bf16[128,1024]{1,0:T(8,128)(2,1)S(1)}, bf16[128,1024]{1,0:T(8,128)(2,1)S(1)}, u32[]{:S(2)}, u32[]{:S(2)}) %collective-permute-start.16) | collective-permute-done | bytes 262176 | tf_op jit(solution)/shard_map/ppermute | solution.py:31
  87.7 1.9 %collective-permute-done.17.g2 = bf16[128,1024]{1,0:T(8,128)(2,1)S(1)} collective-permute-done((bf16[128,1024]{1,0:T(8,128)(2,1)S(1)}, bf16[128,1024]{1,0:T(8,128)(2,1)S(1)}, u32[]{:S(2)}, u32[]{:S(2)}) %collective-permute-start.17) | collective-permute-done | bytes 262176 | tf_op jit(solution)/shard_map/ppermute | solution.py:31
  89.6 6.2 %collective-permute-done.18.g3 = bf16[128,1024]{1,0:T(8,128)(2,1)S(1)} collective-permute-done((bf16[128,1024]{1,0:T(8,128)(2,1)S(1)}, bf16[128,1024]{1,0:T(8,128)(2,1)S(1)}, u32[]{:S(2)}, u32[]{:S(2)}) %collective-permute-start.18) | collective-permute-done | bytes 262176 | tf_op jit(solution)/shard_map/ppermute | solution.py:31
  96.7 2.5 %collective-permute-start.24 = (bf16[144,512]{1,0:T(8,128)(2,1)S(1)}, bf16[144,512]{1,0:T(8,128)(2,1)S(1)}, u32[]{:S(2)}, u32[]{:S(2)}) collective-permute-start(bf16[144,512]{1,0:T(8,128)(2,1)S(1)} %get-tuple-element.82), channel_id=1, source_target_pairs={{0,48},{8,56},{16,0},{24,8},{32,16},{40,24},{48,32},{56,40},{64,11... | collective-permute-start | bytes 442376 | tf_op jit(solution)/shard_map/ppermute | solution.py:35
  100.0 3.5 %collective-permute-start.23 = (bf16[128,512]{1,0:T(8,128)(2,1)S(1)}, bf16[128,512]{1,0:T(8,128)(2,1)S(1)}, u32[]{:S(2)}, u32[]{:S(2)}) collective-permute-start(bf16[128,512]{1,0:T(8,128)(2,1)S(1)} %get-tuple-element.80), channel_id=1, source_target_pairs={{1,8},{3,10},{5,12},{7,14},{8,1},{10,3},{12,5},{14,7},{17,24},{19,... | collective-permute-start | bytes 393224 | tf_op jit(solution)/shard_map/ppermute | solution.py:55
  103.5 6.1 %collective-permute-done.23.far = bf16[128,512]{1,0:T(8,128)(2,1)S(1)} collective-permute-done((bf16[128,512]{1,0:T(8,128)(2,1)S(1)}, bf16[128,512]{1,0:T(8,128)(2,1)S(1)}, u32[]{:S(2)}, u32[]{:S(2)}) %collective-permute-start.23) | collective-permute-done | bytes 131104 | tf_op jit(solution)/shard_map/ppermute | solution.py:55
  (47 shorter events, 24.3 us)
Async XLA Ops:
  0.6 12.8 %collective-permute-start = (bf16[128,512]{1,0:T(8,128)(2,1)}, bf16[128,512]{1,0:T(8,128)(2,1)S(1)}, u32[]{:S(2)}, u32[]{:S(2)}) collective-permute-start(bf16[128,512]{1,0:T(8,128)(2,1)} %own.1), channel_id=1, source_target_pairs={{0,16},{8,24},{16,32},{24,40},{32,48},{40,56},{48,0},{56,8},{64,80... | collective-permute-start | bytes 393224 | tf_op jit(solution)/shard_map/ppermute | solution.py:35
  4.5 10.7 %collective-permute-start.1 = (bf16[128,512]{1,0:T(8,128)(2,1)}, bf16[128,512]{1,0:T(8,128)(2,1)S(1)}, u32[]{:S(2)}, u32[]{:S(2)}) collective-permute-start(bf16[128,512]{1,0:T(8,128)(2,1)} %own.1), channel_id=1, source_target_pairs={{0,48},{8,56},{16,0},{24,8},{32,16},{40,24},{48,32},{56,40},{64,11... | collective-permute-start | bytes 393224 | tf_op jit(solution)/shard_map/ppermute | solution.py:35
  9.9 8.7 %collective-permute-start.6 = (bf16[144,512]{1,0:T(8,128)(2,1)S(1)}, bf16[144,512]{1,0:T(8,128)(2,1)S(1)}, u32[]{:S(2)}, u32[]{:S(2)}) collective-permute-start(bf16[144,512]{1,0:T(8,128)(2,1)S(1)} %shard_map.68.own), channel_id=1, source_target_pairs={{1,8},{3,10},{5,12},{7,14},{8,1},{10,3},{12,5},{14,7},{17,24},{19,... | collective-permute-start | bytes 442376 | tf_op jit(solution)/shard_map/ppermute | solution.py:55
  13.4 5.2 %collective-permute-start.5 = (bf16[128,512]{1,0:T(8,128)(2,1)}, bf16[128,512]{1,0:T(8,128)(2,1)S(1)}, u32[]{:S(2)}, u32[]{:S(2)}) collective-permute-start(bf16[128,512]{1,0:T(8,128)(2,1)} %queries.1), channel_id=1, source_target_pairs={{0,8},{1,0},{2,10},{3,2},{4,12},{5,4},{6,14},{7,6},{8,9},{9,1},{10... | collective-permute-start | bytes 393224 | tf_op jit(solution)/shard_map/ppermute | solution.py:55
  16.9 19.8 %collective-permute-start.2 = (bf16[384,512]{1,0:T(8,128)(2,1)S(1)}, bf16[384,512]{1,0:T(8,128)(2,1)S(1)}, u32[]{:S(2)}, u32[]{:S(2)}) collective-permute-start(bf16[384,512]{1,0:T(8,128)(2,1)S(1)} %shard_map.67.near), channel_id=1, source_target_pairs={{0,1},{1,0},{2,3},{3,2},{4,5},{5,4},{6,7},{7,6},{8,9},{9,8},{10,11... | collective-permute-start | bytes 1179656 | tf_op jit(solution)/shard_map/ppermute | solution.py:45
  19.1 16.2 %collective-permute-start.7 = (bf16[144,1024]{1,0:T(8,128)(2,1)S(1)}, bf16[144,1024]{1,0:T(8,128)(2,1)S(1)}, u32[]{:S(2)}, u32[]{:S(2)}) collective-permute-start(bf16[144,1024]{1,0:T(8,128)(2,1)S(1)} %shard_map.69.q0), channel_id=1, source_target_pairs={{0,64},{8,72},{16,80},{24,88},{32,96},{40,104},{48,112},{56,120},{... | collective-permute-start | bytes 884744 | tf_op jit(solution)/shard_map/ppermute | solution.py:31
  20.4 16.3 %collective-permute-start.8 = (bf16[144,1024]{1,0:T(8,128)(2,1)S(1)}, bf16[144,1024]{1,0:T(8,128)(2,1)S(1)}, u32[]{:S(2)}, u32[]{:S(2)}) collective-permute-start(bf16[144,1024]{1,0:T(8,128)(2,1)S(1)} %shard_map.69.q0), channel_id=1, source_target_pairs={{0,128},{8,136},{16,144},{24,152},{32,160},{40,168},{48,176},{56,1... | collective-permute-start | bytes 884744 | tf_op jit(solution)/shard_map/ppermute | solution.py:31
  22.9 13.9 %collective-permute-start.9 = (bf16[144,1024]{1,0:T(8,128)(2,1)S(1)}, bf16[144,1024]{1,0:T(8,128)(2,1)S(1)}, u32[]{:S(2)}, u32[]{:S(2)}) collective-permute-start(bf16[144,1024]{1,0:T(8,128)(2,1)S(1)} %shard_map.69.q0), channel_id=1, source_target_pairs={{0,192},{8,200},{16,208},{24,216},{32,224},{40,232},{48,240},{56,2... | collective-permute-start | bytes 884744 | tf_op jit(solution)/shard_map/ppermute | solution.py:31
  24.0 9.8 %collective-permute-start.3 = (bf16[128,512]{1,0:T(8,128)(2,1)S(1)}, bf16[128,512]{1,0:T(8,128)(2,1)S(1)}, u32[]{:S(2)}, u32[]{:S(2)}) collective-permute-start(bf16[128,512]{1,0:T(8,128)(2,1)S(1)} %collective-permute-done.after), channel_id=1, source_target_pairs={{0,16},{8,24},{16,32},{24,40},{32,48},{40,56},{48,0},{56,8},{64,80... | collective-permute-start | bytes 393224 | tf_op jit(solution)/shard_map/ppermute | solution.py:35
  38.7 8.9 %collective-permute-start.10 = (f32[512,128]{1,0:T(8,128)S(1)}, f32[512,128]{1,0:T(8,128)S(1)}, u32[]{:S(2)}, u32[]{:S(2)}) collective-permute-start(f32[512,128]{1,0:T(8,128)S(1)} %get-tuple-element.46), channel_id=1, source_target_pairs={{0,2},{1,3},{2,4},{3,5},{4,6},{5,7},{6,0},{7,1},{8,10},{9,11},{10,... | collective-permute-start | bytes 786440 | tf_op jit(solution)/shard_map/ppermute | solution.py:41
  40.1 14.2 %collective-permute-start.11 = (f32[512,128]{1,0:T(8,128)S(1)}, f32[512,128]{1,0:T(8,128)S(1)}, u32[]{:S(2)}, u32[]{:S(2)}) collective-permute-start(f32[512,128]{1,0:T(8,128)S(1)} %get-tuple-element.47), channel_id=1, source_target_pairs={{0,4},{1,5},{2,6},{3,7},{4,0},{5,1},{6,2},{7,3},{8,12},{9,13},{10,... | collective-permute-start | bytes 786440 | tf_op jit(solution)/shard_map/ppermute | solution.py:41
  42.7 11.6 %collective-permute-start.12 = (f32[512,128]{1,0:T(8,128)S(1)}, f32[512,128]{1,0:T(8,128)S(1)}, u32[]{:S(2)}, u32[]{:S(2)}) collective-permute-start(f32[512,128]{1,0:T(8,128)S(1)} %get-tuple-element.48), channel_id=1, source_target_pairs={{0,6},{1,7},{2,0},{3,1},{4,2},{5,3},{6,4},{7,5},{8,14},{9,15},{10,... | collective-permute-start | bytes 786440 | tf_op jit(solution)/shard_map/ppermute | solution.py:41
  65.0 7.6 %collective-permute-start.13 = (bf16[528,128]{1,0:T(8,128)(2,1)S(1)}, bf16[528,128]{1,0:T(8,128)(2,1)S(1)}, u32[]{:S(2)}, u32[]{:S(2)}) collective-permute-start(bf16[528,128]{1,0:T(8,128)(2,1)S(1)} %get-tuple-element.58), channel_id=1, source_target_pairs={{0,2},{1,3},{2,4},{3,5},{4,6},{5,7},{6,0},{7,1},{8,10},{9,11},{10,... | collective-permute-start | bytes 405512 | tf_op jit(solution)/shard_map/ppermute | solution.py:41
  66.2 7.2 %collective-permute-start.14 = (bf16[528,128]{1,0:T(8,128)(2,1)S(1)}, bf16[528,128]{1,0:T(8,128)(2,1)S(1)}, u32[]{:S(2)}, u32[]{:S(2)}) collective-permute-start(bf16[528,128]{1,0:T(8,128)(2,1)S(1)} %get-tuple-element.59), channel_id=1, source_target_pairs={{0,4},{1,5},{2,6},{3,7},{4,0},{5,1},{6,2},{7,3},{8,12},{9,13},{10,... | collective-permute-start | bytes 405512 | tf_op jit(solution)/shard_map/ppermute | solution.py:41
  69.1 4.3 %collective-permute-start.15 = (bf16[528,128]{1,0:T(8,128)(2,1)S(1)}, bf16[528,128]{1,0:T(8,128)(2,1)S(1)}, u32[]{:S(2)}, u32[]{:S(2)}) collective-permute-start(bf16[528,128]{1,0:T(8,128)(2,1)S(1)} %get-tuple-element.60), channel_id=1, source_target_pairs={{0,6},{1,7},{2,0},{3,1},{4,2},{5,3},{6,4},{7,5},{8,14},{9,15},{10,... | collective-permute-start | bytes 405512 | tf_op jit(solution)/shard_map/ppermute | solution.py:41
  75.1 6.7 %collective-permute-start.19 = (bf16[528,512]{1,0:T(8,128)(2,1)S(1)}, bf16[528,512]{1,0:T(8,128)(2,1)S(1)}, u32[]{:S(2)}, u32[]{:S(2)}) collective-permute-start(bf16[528,512]{1,0:T(8,128)(2,1)S(1)} %get-tuple-element.66.message), channel_id=1, source_target_pairs={{0,1},{1,0},{2,3},{3,2},{4,5},{5,4},{6,7},{7,6},{8,9},{9,8},{10,11... | collective-permute-start | bytes 1622024 | tf_op jit(solution)/shard_map/ppermute | solution.py:45
  79.7 8.0 %collective-permute-start.16 = (bf16[128,1024]{1,0:T(8,128)(2,1)S(1)}, bf16[128,1024]{1,0:T(8,128)(2,1)S(1)}, u32[]{:S(2)}, u32[]{:S(2)}) collective-permute-start(bf16[128,1024]{1,0:T(8,128)(2,1)S(1)} %get-tuple-element.68), channel_id=1, source_target_pairs={{0,192},{8,200},{16,208},{24,216},{32,224},{40,232},{48,240},{56,2... | collective-permute-start | bytes 786440 | tf_op jit(solution)/shard_map/ppermute | solution.py:31
  80.5 9.2 %collective-permute-start.17 = (bf16[128,1024]{1,0:T(8,128)(2,1)S(1)}, bf16[128,1024]{1,0:T(8,128)(2,1)S(1)}, u32[]{:S(2)}, u32[]{:S(2)}) collective-permute-start(bf16[128,1024]{1,0:T(8,128)(2,1)S(1)} %get-tuple-element.69), channel_id=1, source_target_pairs={{0,128},{8,136},{16,144},{24,152},{32,160},{40,168},{48,176},{56,1... | collective-permute-start | bytes 786440 | tf_op jit(solution)/shard_map/ppermute | solution.py:31
  81.7 14.2 %collective-permute-start.18 = (bf16[128,1024]{1,0:T(8,128)(2,1)S(1)}, bf16[128,1024]{1,0:T(8,128)(2,1)S(1)}, u32[]{:S(2)}, u32[]{:S(2)}) collective-permute-start(bf16[128,1024]{1,0:T(8,128)(2,1)S(1)} %get-tuple-element.70), channel_id=1, source_target_pairs={{0,64},{8,72},{16,80},{24,88},{32,96},{40,104},{48,112},{56,120},{... | collective-permute-start | bytes 786440 | tf_op jit(solution)/shard_map/ppermute | solution.py:31
  82.5 13.3 %collective-permute-start.20 = (bf16[144,512]{1,0:T(8,128)(2,1)S(1)}, bf16[144,512]{1,0:T(8,128)(2,1)S(1)}, u32[]{:S(2)}, u32[]{:S(2)}) collective-permute-start(bf16[144,512]{1,0:T(8,128)(2,1)S(1)} %get-tuple-element.75), channel_id=1, source_target_pairs={{0,48},{8,56},{16,0},{24,8},{32,16},{40,24},{48,32},{56,40},{64,11... | collective-permute-start | bytes 442376 | tf_op jit(solution)/shard_map/ppermute | solution.py:35
  85.0 10.8 %collective-permute-start.21 = (bf16[144,512]{1,0:T(8,128)(2,1)S(1)}, bf16[144,512]{1,0:T(8,128)(2,1)S(1)}, u32[]{:S(2)}, u32[]{:S(2)}) collective-permute-start(bf16[144,512]{1,0:T(8,128)(2,1)S(1)} %get-tuple-element.76), channel_id=1, source_target_pairs={{0,16},{8,24},{16,32},{24,40},{32,48},{40,56},{48,0},{56,8},{64,80... | collective-permute-start | bytes 442376 | tf_op jit(solution)/shard_map/ppermute | solution.py:35
  96.7 12.9 %collective-permute-start.24 = (bf16[144,512]{1,0:T(8,128)(2,1)S(1)}, bf16[144,512]{1,0:T(8,128)(2,1)S(1)}, u32[]{:S(2)}, u32[]{:S(2)}) collective-permute-start(bf16[144,512]{1,0:T(8,128)(2,1)S(1)} %get-tuple-element.82), channel_id=1, source_target_pairs={{0,48},{8,56},{16,0},{24,8},{32,16},{40,24},{48,32},{56,40},{64,11... | collective-permute-start | bytes 442376 | tf_op jit(solution)/shard_map/ppermute | solution.py:35
  99.2 4.3 %collective-permute-start.22 = (bf16[128,512]{1,0:T(8,128)(2,1)S(1)}, bf16[128,512]{1,0:T(8,128)(2,1)S(1)}, u32[]{:S(2)}, u32[]{:S(2)}) collective-permute-start(bf16[128,512]{1,0:T(8,128)(2,1)S(1)} %get-tuple-element.79), channel_id=1, source_target_pairs={{0,1},{1,9},{2,3},{3,11},{4,5},{5,13},{6,7},{7,15},{8,0},{9,8},{10... | collective-permute-start | bytes 393224 | tf_op jit(solution)/shard_map/ppermute | solution.py:55
  100.0 9.6 %collective-permute-start.23 = (bf16[128,512]{1,0:T(8,128)(2,1)S(1)}, bf16[128,512]{1,0:T(8,128)(2,1)S(1)}, u32[]{:S(2)}, u32[]{:S(2)}) collective-permute-start(bf16[128,512]{1,0:T(8,128)(2,1)S(1)} %get-tuple-element.80), channel_id=1, source_target_pairs={{1,8},{3,10},{5,12},{7,14},{8,1},{10,3},{12,5},{14,7},{17,24},{19,... | collective-permute-start | bytes 393224 | tf_op jit(solution)/shard_map/ppermute | solution.py:55
  (4 other events, 46.2 us)

commit v7 on v5

--- a/solution.py
+++ b/solution.py
@@ -14,6 +14,7 @@
 WIDTHS = [SMALLEST * 2**k for k in range(LEVELS)]
 FACTORS = [SHARPNESS / math.sqrt(w) for w in WIDTHS]
 SPANS = list(zip([0] + WIDTHS[: LOW - 1], WIDTHS[:LOW]))
+LONG = 20_000_000_000
 EXTRA = 16
 PAIR = 2 * SMALLEST
 
@@ -112,17 +113,16 @@
                 put(a, b, own if matches else far)
 
 
+def hold_kernel(ids, a, out):
+    out[...] = a[...]
+
+
 def score_kernel(
-    ids, p1, p2, p3, o0, o1, o2, o3, q0, q1, q2, q3, p0_hbm,
-    s0, s1, s2, s3, p, q_all, pos, p0, arrived,
+    ids, p0, p1, p2, p3, o0, o1, o2, o3, q0, q1, q2, q3, s0, s1, s2, s3, p, q_all, pos
 ):
-    n, width = p1.shape
-    copy = pltpu.make_async_copy(p0_hbm, p0, arrived)
-    copy.start()
-    for s, (own, other) in enumerate(zip((p1, p2, p3, p0), (o1, o2, o3, o0))):
-        rows = slice((s + 1) % 4 * n, (s + 1) % 4 * n + n)
-        if s == 3:
-            copy.wait()
+    n, width = p0.shape
+    for s, (own, other) in enumerate(zip((p0, p1, p2, p3), (o0, o1, o2, o3))):
+        rows = slice(s * n, s * n + n)
 
         @pl.when(ids[CORE] == 0)
         def _():
@@ -282,6 +282,25 @@
     fill(gp, lambda k, a, b: dot(tails[k], q[:, a:b], 1, 0))
 
 
+def passage_grad_kernel(ids, tail, row, gp_low, q_all, own, message):
+    n = q_all.shape[1]
+    width = own.shape[1]
+    q = q_all[...].reshape(4 * n, 2 * width)
+    message[4 * n :] = jnp.zeros((EXTRA, width), bf16)
+    put_terms(message, 4 * n, row[0:1])
+    for c in (0, 1):
+        lanes = slice(c * width, c * width + width)
+        gp = dot(tail[...], q[:, lanes], 1, 0) + gp_low[:, lanes]
+
+        @pl.when(ids[CORE] == c)
+        def _():
+            own[...] = gp
+
+        @pl.when(ids[CORE] != c)
+        def _():
+            message[: 4 * n] = gp.astype(bf16)
+
+
 def query_grad_kernel(ids, t0, t1, t2, t3, gq_low, p, gq0, gq1, gq2, gq3, tail, row, gq):
     n, wide = gq0.shape
     loss = jnp.zeros((1, n), f32)
@@ -296,26 +315,7 @@
         out[...] = gq[pl.ds(pl.multiple_of(j * n, n), n), :].astype(out.dtype)
 
 
-def passage_grad_kernel(ids, tail, row, gp_low, q_all, own, message):
-    n = q_all.shape[1]
-    width = own.shape[1]
-    q = q_all[...].reshape(4 * n, 2 * width)
-    message[4 * n :] = jnp.zeros((EXTRA, width), bf16)
-    put_terms(message, 4 * n, row[0:1])
-    for c in (0, 1):
-        lanes = slice(c * width, c * width + width)
-        gp = dot(tail[...], q[:, lanes], 1, 0) + gp_low[:, lanes]
-
-        @pl.when(ids[CORE] == c)
-        def _():
-            own[...] = gp
-
-        @pl.when(ids[CORE] != c)
-        def _():
-            message[: 4 * n] = gp.astype(bf16)
-
-
-def core_sum_kernel(gp_own, row, other, own, m1, m2, m3, loss):
+def core_sum_kernel(ids, gp_own, row, other, own, m1, m2, m3, loss):
     n, width = own.shape
     total = row[0:1] + get_terms(other, 4 * n, n)
     loss[...] = jnp.broadcast_to(total, loss.shape)
@@ -328,7 +328,7 @@
             put_terms(out, n, total)
 
 
-def query_sum_kernel(ids, gq0, g1, g2, g3, m1, m2, m3, own, near, far):
+def middle_kernel(ids, gq0, g1, g2, g3, m1, m2, m3, own, near, far):
     width = own.shape[1]
     same = ids[ZH] == ids[CORE]
     for c in (0, 1):
@@ -350,40 +350,58 @@
             far[...] = v.astype(bf16)
 
 
+def last_kernel(ids, gq_own, near, far, gp_own, row, m1, m2, m3, gq, gp, loss):
+    n = gq.shape[0]
+
+    @pl.when(ids[ZH] == ids[CORE])
+    def _():
+        gq[...] = (gq_own[...] + near[...].astype(f32)).astype(bf16)
+
+    @pl.when(ids[ZH] != ids[CORE])
+    def _():
+        gq[...] = (far[...].astype(f32) + near[...].astype(f32)).astype(bf16)
+
+    v = gp_own[...]
+    total = row[0:1]
+    for m in (m1, m2, m3):
+        v += m[:n].astype(f32)
+        total += get_terms(m, n, n)
+    gp[...] = v.astype(bf16)
+    loss[...] = jnp.sum(total, axis=1, keepdims=True) * (1.0 / (n * BATCH))
+
+
 def per_device(queries, passages, positives, level_weight):
     n, width = queries.shape
     wide = 2 * width
     bi = lax.axis_index("batch")
     fi = lax.axis_index("feat")
-    core = fi % 2
-    same = bi % 2 == core
-    ids = jnp.stack([bi // 8, fi // 2, bi % 8 // 2, bi % 2, core]).astype(jnp.int32)
-
-    rows = jnp.stack([positives // 64, positives % 64]).astype(bf16)
+    ids = jnp.stack([bi // 8, fi // 2, bi % 8 // 2, bi % 2, fi % 2]).astype(jnp.int32)
+
+    near = move_square(queries, lambda h, c: (1 - h, c) if h == c else (h, 1 - c))
+    rows = jnp.stack([positives >> 6, positives & 63]).astype(bf16)
     rows = jnp.pad(rows, ((0, EXTRA - 2), (0, width - n)))
     q_row = jnp.concatenate([queries, rows], axis=0)
-    near = move_square(queries, lambda h, c: (1 - h, c) if h == c else (h, 1 - c))
     far = move_square(q_row, lambda h, c: None if h == c else (1 - h, 1 - c))
     (q_msg,) = call(
         pack_kernel, [ids], [q_row, near, far], [shape(n + EXTRA, wide, bf16)]
     )
     q_msgs = [q_msg] + [shift_x(q_msg, s) for s in (1, 2, 3)]
 
+    (held,) = call(hold_kernel, [ids], [passages], [shape(n, width, bf16)])
     p_next, p_before = shift_zl(passages, 1), shift_zl(passages, 3)
-    p_own = [passages, p_next, shift_zl(p_next, 1), p_before]
+    p_own = [held, p_next, shift_zl(p_next, 1), p_before]
     p_other = [swap_core(a) for a in p_own]
 
     tile = 4 * n * 4 * n
     *partial, p, q, pos = call(
-        score_kernel, [ids], [*p_own[1:], *p_other, *q_msgs, passages],
+        score_kernel, [ids], [*p_own, *p_other, *q_msgs],
         [shape(4 * n, n, f32)] * 4
         + [
             shape(4 * n, wide, bf16),
             shape(4, n, wide, bf16),
             shape(4, 1, n, jnp.int32),
         ],
-        scratch=[pltpu.VMEM((n, width), bf16), pltpu.SemaphoreType.DMA],
-        flops=2 * tile * wide, in_place=1,
+        flops=2 * tile * wide,
     )
     pieces = [partial[0]] + [shift_y(partial[t], t) for t in (1, 2, 3)]
     e_low, low_stats, low_tops = call(
@@ -415,30 +433,28 @@
         scratch=[pltpu.VMEM((4 * n, wide), f32)],
         flops=2 * tile * wide,
     )
+    gq = [shift_x(g, -s) for s, g in enumerate((gq1, gq2, gq3), 1)]
     gp_own, message = call(
         passage_grad_kernel, [ids], [tail, row, gp_low, q],
         [shape(4 * n, width, f32), shape(4 * n + EXTRA, width, bf16)],
         flops=2 * tile * wide,
     )
-    gq = [shift_x(g, -s) for s, g in enumerate((gq1, gq2, gq3), 1)]
-
-    own, *messages, loss_row = call(
-        core_sum_kernel, [], [gp_own, row, swap_core(message)],
+    gp_own, *messages, row = call(
+        core_sum_kernel, [ids], [gp_own, row, swap_core(message)],
         [shape(n, width, f32)] + [shape(n + EXTRA, width, bf16)] * 3 + [shape(8, n, f32)],
     )
     gp = [shift_zl(m, -s) for s, m in enumerate(messages, 1)]
     gq_own, near, far = call(
-        query_sum_kernel, [ids], [gq0, *gq, *messages],
-        [shape(n, width, f32)] + [shape(n, width, bf16)] * 2, in_place=3,
-    )
-    near = move_square(near, lambda h, c: (h, 1 - c) if h == c else (1 - h, c)).astype(f32)
-    far = move_square(far, lambda h, c: None if h == c else (1 - h, 1 - c)).astype(f32)
-    grad_queries = (near + jnp.where(same, gq_own, far)).astype(bf16)
-
-    grad_passages = own + sum(g[:n].astype(f32) for g in gp)
-    loss_row = loss_row[0] + sum(jnp.sum(g[n : n + 3, :n].astype(f32), axis=0) for g in gp)
-    loss = jnp.sum(loss_row) / (n * BATCH)
-    return loss, grad_queries, grad_passages.astype(bf16)
+        middle_kernel, [ids], [gq0, *gq, *messages],
+        [shape(n, width, f32)] + [shape(n, width, bf16)] * 2, in_place=3, flops=LONG,
+    )
+    near = move_square(near, lambda h, c: (h, 1 - c) if h == c else (1 - h, c))
+    far = move_square(far, lambda h, c: None if h == c else (1 - h, 1 - c))
+    grad_queries, grad_passages, loss = call(
+        last_kernel, [ids], [gq_own, near, far, gp_own, row, *gp],
+        [shape(n, width, bf16), shape(n, width, bf16), shape(1, 1, f32)],
+    )
+    return loss.reshape(()), grad_queries, grad_passages
 
 
 def solution(mesh):

time: 123 us -> 103 us (0.84)
  waiting for transfers between devices: 45 us -> 27.4 us
  blocking collectives: 11.7 us -> 8.39 us
  starting transfers between devices: 42.7 us -> 45.3 us
  Pallas kernels: 15.8 us -> 18 us
  other arithmetic: 3.69 us -> 1.59 us
  between operations: 2.57 us -> 0.78 us
    ppermute x6, waiting for transfers between devices: 16.8 us -> 7 us  [shift_zl(): lax.ppermute(a, 'batch', [(b, b // 8 * 8 + (b + 2 * s) % 8) for b in rang...]
    ppermute x6, waiting for transfers between devices: 13.9 us -> 8.31 us  [shift_x(): lax.ppermute(a, 'batch', [(b, (b + 8 * s) % BATCH) for b in range(BATCH)])]
    all_to_all x1, blocking collectives: 11.7 us -> 8.39 us  [per_device(): stats = lax.all_to_all(message, 'batch', 0, 0, axis_index_groups=XZH_GROUPS)]
    pallas_call x10 -> x12, Pallas kernels: 15.8 us -> 18 us  [call(): pl.pallas_call(body, out_shape=outs, in_specs=[scalar] * len(smem) + [vme...]
    ppermute x6, starting transfers between devices: 6.3 us -> 8.23 us  [shift_x(): lax.ppermute(a, 'batch', [(b, (b + 8 * s) % BATCH) for b in range(BATCH)])]
    ppermute x4, waiting for transfers between devices: 4.73 us -> 3.1 us  [move_square(): return lax.ppermute(a, BOTH, pairs)]
    convert_element_type x2 -> x0, other arithmetic: 1.43 us -> none  [the longest x1 0.72 us: per_device(): return (loss, grad_queries, grad_passages.astype(bf16))]
    ppermute x6, starting transfers between devices: 9 us -> 10.4 us  [shift_zl(): lax.ppermute(a, 'batch', [(b, b // 8 * 8 + (b + 2 * s) % 8) for b in rang...]
  transfers between devices with their start and end apart: 27 -> 27, of which waited for: 14 -> 12; matrix products, arithmetic and copies ran while one was open for 1% -> 0% of each run, Pallas kernels for 6% -> 9%
where the time goes in v7:
time: 103 us; the launch traced here: 102 us
  starting transfers between devices  45.3 us (44%)
  waiting for transfers between devices  27.4 us (27%)
  Pallas kernels  18 us (17%)
  blocking collectives  8.39 us (8%)
  other arithmetic  1.59 us (2%)
    pallas_call x12, Pallas kernels, call(): pl.pallas_call(body, out_shape=outs, in_specs=[scalar] * len(smem) + [vme...  18 us
    ppermute x6, starting transfers between devices, shift_zl(): lax.ppermute(a, 'batch', [(b, b // 8 * 8 + (b + 2 * s) % 8) for b in rang...  10.4 us
    ppermute x6, starting transfers between devices, shift_y(): lax.ppermute(a, 'feat', [(f, (f + 2 * s) % FEAT) for f in range(FEAT)])  9.16 us
    ppermute x4, starting transfers between devices, move_square(): return lax.ppermute(a, BOTH, pairs)  9.14 us
    ppermute x5, starting transfers between devices, swap_core(): return lax.ppermute(a, 'feat', [(f, f ^ 1) for f in range(FEAT)])  8.46 us
    all_to_all x1, blocking collectives, per_device(): stats = lax.all_to_all(message, 'batch', 0, 0, axis_index_groups=XZH_GROUPS)  8.39 us
    ppermute x6, waiting for transfers between devices, shift_x(): lax.ppermute(a, 'batch', [(b, (b + 8 * s) % BATCH) for b in range(BATCH)])  8.31 us
    ppermute x6, starting transfers between devices, shift_x(): lax.ppermute(a, 'batch', [(b, (b + 8 * s) % BATCH) for b in range(BATCH)])  8.23 us
  transfers between devices with their start and end apart: 27, of which 12 were waited for; matrix products, arithmetic and copies ran while one was open for 0% of the time, Pallas kernels for 9%

profile of v7, /device:TPU:1, one launch (start us, length us, event | category | flops | bytes accessed | tf_op | source)
XLA Modules:
  0.0 102.5 jit_solution(13143123502476789077)
XLA Ops:
  2.2 4.9 %collective-permute-start.8 = (bf16[144,512]{1,0:T(8,128)(2,1)S(1)}, bf16[144,512]{1,0:T(8,128)(2,1)S(1)}, u32[]{:S(2)}, u32[]{:S(2)}) collective-permute-start(bf16[144,512]{1,0:T(8,128)(2,1)S(1)} %pad_maximum_fusion.own), channel_id=1, source_target_pairs={{1,8},{3,10},{5,12},{7,14},{8,1},{10,3},{12,5},{14,7},{17,24},{19,... | collective-permute-start | bytes 442376 | tf_op jit(solution)/shard_map/ppermute | solution.py:56
  7.3 3.1 %collective-permute-start = (bf16[128,512]{1,0:T(8,128)(2,1)}, bf16[128,512]{1,0:T(8,128)(2,1)S(1)}, u32[]{:S(2)}, u32[]{:S(2)}) collective-permute-start(bf16[128,512]{1,0:T(8,128)(2,1)} %a.1), channel_id=1, source_target_pairs={{0,16},{8,24},{16,32},{24,40},{32,48},{40,56},{48,0},{56,8},{64,80... | collective-permute-start | bytes 393224 | tf_op jit(solution)/shard_map/ppermute | solution.py:36
  10.4 2.2 %collective-permute-start.2 = (bf16[128,512]{1,0:T(8,128)(2,1)}, bf16[128,512]{1,0:T(8,128)(2,1)S(1)}, u32[]{:S(2)}, u32[]{:S(2)}) collective-permute-start(bf16[128,512]{1,0:T(8,128)(2,1)} %a.1), channel_id=1, source_target_pairs={{0,48},{8,56},{16,0},{24,8},{32,16},{40,24},{48,32},{56,40},{64,11... | collective-permute-start | bytes 393224 | tf_op jit(solution)/shard_map/ppermute | solution.py:36
  17.0 2.5 %collective-permute-start.10 = (bf16[144,1024]{1,0:T(8,128)(2,1)S(1)}, bf16[144,1024]{1,0:T(8,128)(2,1)S(1)}, u32[]{:S(2)}, u32[]{:S(2)}) collective-permute-start(bf16[144,1024]{1,0:T(8,128)(2,1)S(1)} %shard_map.68.q0), channel_id=1, source_target_pairs={{0,128},{8,136},{16,144},{24,152},{32,160},{40,168},{48,176},{56,1... | collective-permute-start | bytes 884744 | tf_op jit(solution)/shard_map/ppermute | solution.py:32
  19.5 1.4 %collective-permute-done.p1 = bf16[128,512]{1,0:T(8,128)(2,1)S(1)} collective-permute-done((bf16[128,512]{1,0:T(8,128)(2,1)}, bf16[128,512]{1,0:T(8,128)(2,1)S(1)}, u32[]{:S(2)}, u32[]{:S(2)}) %collective-permute-start) | collective-permute-done | bytes 131104 | tf_op jit(solution)/shard_map/ppermute | solution.py:36
  20.9 2.5 %collective-permute-start.11 = (bf16[144,1024]{1,0:T(8,128)(2,1)S(1)}, bf16[144,1024]{1,0:T(8,128)(2,1)S(1)}, u32[]{:S(2)}, u32[]{:S(2)}) collective-permute-start(bf16[144,1024]{1,0:T(8,128)(2,1)S(1)} %shard_map.68.q0), channel_id=1, source_target_pairs={{0,192},{8,200},{16,208},{24,216},{32,224},{40,232},{48,240},{56,2... | collective-permute-start | bytes 884744 | tf_op jit(solution)/shard_map/ppermute | solution.py:32
  23.4 2.0 %collective-permute-start.4 = (bf16[128,512]{1,0:T(8,128)(2,1)S(1)}, bf16[128,512]{1,0:T(8,128)(2,1)S(1)}, u32[]{:S(2)}, u32[]{:S(2)}) collective-permute-start(bf16[128,512]{1,0:T(8,128)(2,1)S(1)} %collective-permute-done.p1), channel_id=1, source_target_pairs={{0,1},{1,0},{2,3},{3,2},{4,5},{5,4},{6,7},{7,6},{8,9},{9,8},{10,11... | collective-permute-start | bytes 393224 | tf_op jit(solution)/shard_map/ppermute | solution.py:46
  25.4 5.6 %collective-permute-done.1.p2 = bf16[128,512]{1,0:T(8,128)(2,1)S(1)} collective-permute-done((bf16[128,512]{1,0:T(8,128)(2,1)S(1)}, bf16[128,512]{1,0:T(8,128)(2,1)S(1)}, u32[]{:S(2)}, u32[]{:S(2)}) %collective-permute-start.1) | collective-permute-done | bytes 131104 | tf_op jit(solution)/shard_map/ppermute | solution.py:36
  30.9 2.3 %collective-permute-start.6 = (bf16[128,512]{1,0:T(8,128)(2,1)S(1)}, bf16[128,512]{1,0:T(8,128)(2,1)S(1)}, u32[]{:S(2)}, u32[]{:S(2)}) collective-permute-start(bf16[128,512]{1,0:T(8,128)(2,1)S(1)} %collective-permute-done.2.p3), channel_id=1, source_target_pairs={{0,1},{1,0},{2,3},{3,2},{4,5},{5,4},{6,7},{7,6},{8,9},{9,8},{10,11... | collective-permute-start | bytes 393224 | tf_op jit(solution)/shard_map/ppermute | solution.py:46
  34.6 2.0 %shard_map.69 = (f32[512,128]{1,0:T(8,128)S(1)}, f32[512,128]{1,0:T(8,128)S(1)}, f32[512,128]{1,0:T(8,128)S(1)}, f32[512,128]{1,0:T(8,128)S(1)}, bf16[512,1024]{...) custom-call(s32[5]{0:T(128)S(1)} %stack.35.ids, bf16[128,512]{1,0:T(8,128)(2,1)S(1)} %shard_map.67.p0, ...), custom_call_target="tpu_custom_call" | custom-call | flops 536870912 | bytes 5376000 | tf_op jit(solution)/shard_map/pallas_call | solution.py:73
  38.0 2.6 %collective-permute-start.13 = (f32[512,128]{1,0:T(8,128)S(1)}, f32[512,128]{1,0:T(8,128)S(1)}, u32[]{:S(2)}, u32[]{:S(2)}) collective-permute-start(f32[512,128]{1,0:T(8,128)S(1)} %get-tuple-element.44), channel_id=1, source_target_pairs={{0,4},{1,5},{2,6},{3,7},{4,0},{5,1},{6,2},{7,3},{8,12},{9,13},{10,... | collective-permute-start | bytes 786440 | tf_op jit(solution)/shard_map/ppermute | solution.py:42
  41.6 3.7 %shard_map.70 = (f32[5,4,512,128]{3,2,1,0:T(8,128)S(1)}, f32[4,8,128]{2,1,0:T(8,128)S(1)}, f32[4,8,128]{2,1,0:T(8,128)S(1)}) custom-call(s32[5]{0:T(128)S(1)} %stack.35.ids, f32[7]{0:T(128)S(1)} %copy-done.1, bf16[512,1024]{1,0:T(8,128)(2,1)S(1)} %get-tuple-element.47.p, bf16[4,128,1024]{2,1,0:T(8,128)(2,1)S(1)} %get-tuple-element.48.q_all, ...), custom_call_target="tpu_custom_call" | custom-call | flops 536870912 | bytes 7374848 | tf_op jit(solution)/shard_map/pallas_call | solution.py:73
  45.7 6.7 %collective-permute-done.13.s2 = f32[512,128]{1,0:T(8,128)S(1)} collective-permute-done((f32[512,128]{1,0:T(8,128)S(1)}, f32[512,128]{1,0:T(8,128)S(1)}, u32[]{:S(2)}, u32[]{:S(2)}) %collective-permute-start.13) | collective-permute-done | bytes 262176 | tf_op jit(solution)/shard_map/ppermute | solution.py:42
  53.5 8.4 %all_to_all.5.stats = f32[8,40,128]{2,1,0:T(8,128)S(1)} all-to-all(f32[8,40,128]{2,1,0:T(8,128)S(1)} %get-tuple-element.50), channel_id=1, replica_groups={{0,8,64,72,128,136,192,200},{16,24,80,88,144,152,208,216},{32,40,96,104..., dimensions={0} | all-to-all | bytes 327680 | tf_op jit(solution)/shard_map/all_to_all | solution.py:416
  63.6 2.8 %collective-permute-start.16 = (bf16[528,128]{1,0:T(8,128)(2,1)S(1)}, bf16[528,128]{1,0:T(8,128)(2,1)S(1)}, u32[]{:S(2)}, u32[]{:S(2)}) collective-permute-start(bf16[528,128]{1,0:T(8,128)(2,1)S(1)} %get-tuple-element.56), channel_id=1, source_target_pairs={{0,4},{1,5},{2,6},{3,7},{4,0},{5,1},{6,2},{7,3},{8,12},{9,13},{10,... | collective-permute-start | bytes 405512 | tf_op jit(solution)/shard_map/ppermute | solution.py:42
  66.9 3.4 %shard_map.73 = (f32[512,1024]{1,0:T(8,128)S(1)}, f32[512,1024]{1,0:T(8,128)S(1)}) custom-call(s32[5]{0:T(128)S(1)} %stack.35.ids, f32[7]{0:T(128)S(1)} %copy-done.1, f32[5,4,512,128]{3,2,1,0:T(8,128)S(1)} %get-tuple-element.58.e_low, f32[4,8,128]{2,1,0:T(8,128)S(1)} %get-tuple-element.59.rates, s32[4,1,128]{2,1,0:T(1,128)S(1)} %get-tuple-element.46.pos, ...), custom_call_target="tpu_custom_call" | custom-call | flops 1073741824 | bytes 11552768 | tf_op jit(solution)/shard_map/pallas_call | solution.py:73
  70.8 1.5 %shard_map.74 = (f32[128,1024]{1,0:T(8,128)S(1)}, bf16[128,1024]{1,0:T(8,128)(2,1)S(1)}, bf16[128,1024]{1,0:T(8,128)(2,1)S(1)}, bf16[128,1024]{1,0:T(8,128)(2,1)...) custom-call(s32[5]{0:T(128)S(1)} %stack.35.ids, bf16[528,128]{1,0:T(8,128)(2,1)S(1)} %get-tuple-element.54.t0, ...), custom_call_target="tpu_custom_call" | custom-call | flops 536870912 | bytes 5525504 | tf_op jit(solution)/shard_map/pallas_call | solution.py:73
  72.3 1.6 %shard_map.75 = (f32[512,512]{1,0:T(8,128)S(1)}, bf16[528,512]{1,0:T(8,128)(2,1)S(1)}) custom-call(s32[5]{0:T(128)S(1)} %stack.35.ids, bf16[512,512]{1,0:T(8,128)(2,1)S(1)} %get-tuple-element.65.tail, f32[8,128]{1,0:T(8,128)S(1)} %get-tuple-element.66.row, f32[512,1024]{1,0:T(8,128)S(1)} %get-tuple-element.67.gp_low, ...), custom_call_target="tpu_custom_call" | custom-call | flops 536870912 | bytes 5263360 | tf_op jit(solution)/shard_map/pallas_call | solution.py:73
  73.9 3.2 %collective-permute-start.21 = (bf16[528,512]{1,0:T(8,128)(2,1)S(1)}, bf16[528,512]{1,0:T(8,128)(2,1)S(1)}, u32[]{:S(2)}, u32[]{:S(2)}) collective-permute-start(bf16[528,512]{1,0:T(8,128)(2,1)S(1)} %get-tuple-element.69), channel_id=1, source_target_pairs={{0,1},{1,0},{2,3},{3,2},{4,5},{5,4},{6,7},{7,6},{8,9},{9,8},{10,11... | collective-permute-start | bytes 1622024 | tf_op jit(solution)/shard_map/ppermute | solution.py:46
  79.8 1.5 %collective-permute-start.24 = (bf16[144,512]{1,0:T(8,128)(2,1)S(1)}, bf16[144,512]{1,0:T(8,128)(2,1)S(1)}, u32[]{:S(2)}, u32[]{:S(2)}) collective-permute-start(bf16[144,512]{1,0:T(8,128)(2,1)S(1)} %get-tuple-element.70.m1), channel_id=1, source_target_pairs={{0,48},{8,56},{16,0},{24,8},{32,16},{40,24},{48,32},{56,40},{64,11... | collective-permute-start | bytes 442376 | tf_op jit(solution)/shard_map/ppermute | solution.py:36
  81.3 2.5 %collective-permute-start.25 = (bf16[144,512]{1,0:T(8,128)(2,1)S(1)}, bf16[144,512]{1,0:T(8,128)(2,1)S(1)}, u32[]{:S(2)}, u32[]{:S(2)}) collective-permute-start(bf16[144,512]{1,0:T(8,128)(2,1)S(1)} %get-tuple-element.71.m2), channel_id=1, source_target_pairs={{0,32},{8,40},{16,48},{24,56},{32,0},{40,8},{48,16},{56,24},{64,96... | collective-permute-start | bytes 442376 | tf_op jit(solution)/shard_map/ppermute | solution.py:36
  86.9 6.3 %collective-permute-done.20.g3 = bf16[128,1024]{1,0:T(8,128)(2,1)S(1)} collective-permute-done((bf16[128,1024]{1,0:T(8,128)(2,1)S(1)}, bf16[128,1024]{1,0:T(8,128)(2,1)S(1)}, u32[]{:S(2)}, u32[]{:S(2)}) %collective-permute-start.20) | collective-permute-done | bytes 262176 | tf_op jit(solution)/shard_map/ppermute | solution.py:32
  94.8 3.2 %collective-permute-start.23 = (bf16[128,512]{1,0:T(8,128)(2,1)S(1)}, bf16[128,512]{1,0:T(8,128)(2,1)S(1)}, u32[]{:S(2)}, u32[]{:S(2)}) collective-permute-start(bf16[128,512]{1,0:T(8,128)(2,1)S(1)} %get-tuple-element.75), channel_id=1, source_target_pairs={{1,8},{3,10},{5,12},{7,14},{8,1},{10,3},{12,5},{14,7},{17,24},{19,... | collective-permute-start | bytes 393224 | tf_op jit(solution)/shard_map/ppermute | solution.py:56
  98.0 1.7 %collective-permute-done.22.near = bf16[128,512]{1,0:T(8,128)(2,1)S(1)} collective-permute-done((bf16[128,512]{1,0:T(8,128)(2,1)S(1)}, bf16[128,512]{1,0:T(8,128)(2,1)S(1)}, u32[]{:S(2)}, u32[]{:S(2)}) %collective-permute-start.22) | collective-permute-done | bytes 131104 | tf_op jit(solution)/shard_map/ppermute | solution.py:56
  (51 shorter events, 24.2 us)
Async XLA Ops:
  2.2 12.9 %collective-permute-start.8 = (bf16[144,512]{1,0:T(8,128)(2,1)S(1)}, bf16[144,512]{1,0:T(8,128)(2,1)S(1)}, u32[]{:S(2)}, u32[]{:S(2)}) collective-permute-start(bf16[144,512]{1,0:T(8,128)(2,1)S(1)} %pad_maximum_fusion.own), channel_id=1, source_target_pairs={{1,8},{3,10},{5,12},{7,14},{8,1},{10,3},{12,5},{14,7},{17,24},{19,... | collective-permute-start | bytes 442376 | tf_op jit(solution)/shard_map/ppermute | solution.py:56
  7.2 8.0 %collective-permute-start.7 = (bf16[128,512]{1,0:T(8,128)(2,1)}, bf16[128,512]{1,0:T(8,128)(2,1)S(1)}, u32[]{:S(2)}, u32[]{:S(2)}) collective-permute-start(bf16[128,512]{1,0:T(8,128)(2,1)} %param.4), channel_id=1, source_target_pairs={{0,8},{1,0},{2,10},{3,2},{4,12},{5,4},{6,14},{7,6},{8,9},{9,1},{10... | collective-permute-start | bytes 393224 | tf_op jit(solution)/shard_map/ppermute | solution.py:56
  7.3 13.6 %collective-permute-start = (bf16[128,512]{1,0:T(8,128)(2,1)}, bf16[128,512]{1,0:T(8,128)(2,1)S(1)}, u32[]{:S(2)}, u32[]{:S(2)}) collective-permute-start(bf16[128,512]{1,0:T(8,128)(2,1)} %a.1), channel_id=1, source_target_pairs={{0,16},{8,24},{16,32},{24,40},{32,48},{40,56},{48,0},{56,8},{64,80... | collective-permute-start | bytes 393224 | tf_op jit(solution)/shard_map/ppermute | solution.py:36
  10.4 13.0 %collective-permute-start.2 = (bf16[128,512]{1,0:T(8,128)(2,1)}, bf16[128,512]{1,0:T(8,128)(2,1)S(1)}, u32[]{:S(2)}, u32[]{:S(2)}) collective-permute-start(bf16[128,512]{1,0:T(8,128)(2,1)} %a.1), channel_id=1, source_target_pairs={{0,48},{8,56},{16,0},{24,8},{32,16},{40,24},{48,32},{56,40},{64,11... | collective-permute-start | bytes 393224 | tf_op jit(solution)/shard_map/ppermute | solution.py:36
  14.1 9.3 %collective-permute-start.3 = (bf16[128,512]{1,0:T(8,128)(2,1)S(1)}, bf16[128,512]{1,0:T(8,128)(2,1)S(1)}, u32[]{:S(2)}, u32[]{:S(2)}) collective-permute-start(bf16[128,512]{1,0:T(8,128)(2,1)S(1)} %shard_map.67.p0), channel_id=1, source_target_pairs={{0,1},{1,0},{2,3},{3,2},{4,5},{5,4},{6,7},{7,6},{8,9},{9,8},{10,11... | collective-permute-start | bytes 393224 | tf_op jit(solution)/shard_map/ppermute | solution.py:46
  15.8 18.8 %collective-permute-start.9 = (bf16[144,1024]{1,0:T(8,128)(2,1)S(1)}, bf16[144,1024]{1,0:T(8,128)(2,1)S(1)}, u32[]{:S(2)}, u32[]{:S(2)}) collective-permute-start(bf16[144,1024]{1,0:T(8,128)(2,1)S(1)} %shard_map.68.q0), channel_id=1, source_target_pairs={{0,64},{8,72},{16,80},{24,88},{32,96},{40,104},{48,112},{56,120},{... | collective-permute-start | bytes 884744 | tf_op jit(solution)/shard_map/ppermute | solution.py:32
  17.0 17.5 %collective-permute-start.10 = (bf16[144,1024]{1,0:T(8,128)(2,1)S(1)}, bf16[144,1024]{1,0:T(8,128)(2,1)S(1)}, u32[]{:S(2)}, u32[]{:S(2)}) collective-permute-start(bf16[144,1024]{1,0:T(8,128)(2,1)S(1)} %shard_map.68.q0), channel_id=1, source_target_pairs={{0,128},{8,136},{16,144},{24,152},{32,160},{40,168},{48,176},{56,1... | collective-permute-start | bytes 884744 | tf_op jit(solution)/shard_map/ppermute | solution.py:32
  20.9 13.6 %collective-permute-start.11 = (bf16[144,1024]{1,0:T(8,128)(2,1)S(1)}, bf16[144,1024]{1,0:T(8,128)(2,1)S(1)}, u32[]{:S(2)}, u32[]{:S(2)}) collective-permute-start(bf16[144,1024]{1,0:T(8,128)(2,1)S(1)} %shard_map.68.q0), channel_id=1, source_target_pairs={{0,192},{8,200},{16,208},{24,216},{32,224},{40,232},{48,240},{56,2... | collective-permute-start | bytes 884744 | tf_op jit(solution)/shard_map/ppermute | solution.py:32
  23.4 7.6 %collective-permute-start.1 = (bf16[128,512]{1,0:T(8,128)(2,1)S(1)}, bf16[128,512]{1,0:T(8,128)(2,1)S(1)}, u32[]{:S(2)}, u32[]{:S(2)}) collective-permute-start(bf16[128,512]{1,0:T(8,128)(2,1)S(1)} %collective-permute-done.p1), channel_id=1, source_target_pairs={{0,16},{8,24},{16,32},{24,40},{32,48},{40,56},{48,0},{56,8},{64,80... | collective-permute-start | bytes 393224 | tf_op jit(solution)/shard_map/ppermute | solution.py:36
  23.4 9.8 %collective-permute-start.4 = (bf16[128,512]{1,0:T(8,128)(2,1)S(1)}, bf16[128,512]{1,0:T(8,128)(2,1)S(1)}, u32[]{:S(2)}, u32[]{:S(2)}) collective-permute-start(bf16[128,512]{1,0:T(8,128)(2,1)S(1)} %collective-permute-done.p1), channel_id=1, source_target_pairs={{0,1},{1,0},{2,3},{3,2},{4,5},{5,4},{6,7},{7,6},{8,9},{9,8},{10,11... | collective-permute-start | bytes 393224 | tf_op jit(solution)/shard_map/ppermute | solution.py:46
  36.6 9.1 %collective-permute-start.12 = (f32[512,128]{1,0:T(8,128)S(1)}, f32[512,128]{1,0:T(8,128)S(1)}, u32[]{:S(2)}, u32[]{:S(2)}) collective-permute-start(f32[512,128]{1,0:T(8,128)S(1)} %get-tuple-element.43), channel_id=1, source_target_pairs={{0,2},{1,3},{2,4},{3,5},{4,6},{5,7},{6,0},{7,1},{8,10},{9,11},{10,... | collective-permute-start | bytes 786440 | tf_op jit(solution)/shard_map/ppermute | solution.py:42
  38.0 14.5 %collective-permute-start.13 = (f32[512,128]{1,0:T(8,128)S(1)}, f32[512,128]{1,0:T(8,128)S(1)}, u32[]{:S(2)}, u32[]{:S(2)}) collective-permute-start(f32[512,128]{1,0:T(8,128)S(1)} %get-tuple-element.44), channel_id=1, source_target_pairs={{0,4},{1,5},{2,6},{3,7},{4,0},{5,1},{6,2},{7,3},{8,12},{9,13},{10,... | collective-permute-start | bytes 786440 | tf_op jit(solution)/shard_map/ppermute | solution.py:42
  40.6 11.9 %collective-permute-start.14 = (f32[512,128]{1,0:T(8,128)S(1)}, f32[512,128]{1,0:T(8,128)S(1)}, u32[]{:S(2)}, u32[]{:S(2)}) collective-permute-start(f32[512,128]{1,0:T(8,128)S(1)} %get-tuple-element.45), channel_id=1, source_target_pairs={{0,6},{1,7},{2,0},{3,1},{4,2},{5,3},{6,4},{7,5},{8,14},{9,15},{10,... | collective-permute-start | bytes 786440 | tf_op jit(solution)/shard_map/ppermute | solution.py:42
  62.8 7.5 %collective-permute-start.15 = (bf16[528,128]{1,0:T(8,128)(2,1)S(1)}, bf16[528,128]{1,0:T(8,128)(2,1)S(1)}, u32[]{:S(2)}, u32[]{:S(2)}) collective-permute-start(bf16[528,128]{1,0:T(8,128)(2,1)S(1)} %get-tuple-element.55), channel_id=1, source_target_pairs={{0,2},{1,3},{2,4},{3,5},{4,6},{5,7},{6,0},{7,1},{8,10},{9,11},{10,... | collective-permute-start | bytes 405512 | tf_op jit(solution)/shard_map/ppermute | solution.py:42
  63.6 7.2 %collective-permute-start.16 = (bf16[528,128]{1,0:T(8,128)(2,1)S(1)}, bf16[528,128]{1,0:T(8,128)(2,1)S(1)}, u32[]{:S(2)}, u32[]{:S(2)}) collective-permute-start(bf16[528,128]{1,0:T(8,128)(2,1)S(1)} %get-tuple-element.56), channel_id=1, source_target_pairs={{0,4},{1,5},{2,6},{3,7},{4,0},{5,1},{6,2},{7,3},{8,12},{9,13},{10,... | collective-permute-start | bytes 405512 | tf_op jit(solution)/shard_map/ppermute | solution.py:42
  73.9 5.2 %collective-permute-start.21 = (bf16[528,512]{1,0:T(8,128)(2,1)S(1)}, bf16[528,512]{1,0:T(8,128)(2,1)S(1)}, u32[]{:S(2)}, u32[]{:S(2)}) collective-permute-start(bf16[528,512]{1,0:T(8,128)(2,1)S(1)} %get-tuple-element.69), channel_id=1, source_target_pairs={{0,1},{1,0},{2,3},{3,2},{4,5},{5,4},{6,7},{7,6},{8,9},{9,8},{10,11... | collective-permute-start | bytes 1622024 | tf_op jit(solution)/shard_map/ppermute | solution.py:46
  77.1 7.9 %collective-permute-start.18 = (bf16[128,1024]{1,0:T(8,128)(2,1)S(1)}, bf16[128,1024]{1,0:T(8,128)(2,1)S(1)}, u32[]{:S(2)}, u32[]{:S(2)}) collective-permute-start(bf16[128,1024]{1,0:T(8,128)(2,1)S(1)} %get-tuple-element.62), channel_id=1, source_target_pairs={{0,192},{8,200},{16,208},{24,216},{32,224},{40,232},{48,240},{56,2... | collective-permute-start | bytes 786440 | tf_op jit(solution)/shard_map/ppermute | solution.py:32
  77.8 9.1 %collective-permute-start.19 = (bf16[128,1024]{1,0:T(8,128)(2,1)S(1)}, bf16[128,1024]{1,0:T(8,128)(2,1)S(1)}, u32[]{:S(2)}, u32[]{:S(2)}) collective-permute-start(bf16[128,1024]{1,0:T(8,128)(2,1)S(1)} %get-tuple-element.63), channel_id=1, source_target_pairs={{0,128},{8,136},{16,144},{24,152},{32,160},{40,168},{48,176},{56,1... | collective-permute-start | bytes 786440 | tf_op jit(solution)/shard_map/ppermute | solution.py:32
  79.0 14.2 %collective-permute-start.20 = (bf16[128,1024]{1,0:T(8,128)(2,1)S(1)}, bf16[128,1024]{1,0:T(8,128)(2,1)S(1)}, u32[]{:S(2)}, u32[]{:S(2)}) collective-permute-start(bf16[128,1024]{1,0:T(8,128)(2,1)S(1)} %get-tuple-element.64), channel_id=1, source_target_pairs={{0,64},{8,72},{16,80},{24,88},{32,96},{40,104},{48,112},{56,120},{... | collective-permute-start | bytes 786440 | tf_op jit(solution)/shard_map/ppermute | solution.py:32
  79.8 21.3 %collective-permute-start.24 = (bf16[144,512]{1,0:T(8,128)(2,1)S(1)}, bf16[144,512]{1,0:T(8,128)(2,1)S(1)}, u32[]{:S(2)}, u32[]{:S(2)}) collective-permute-start(bf16[144,512]{1,0:T(8,128)(2,1)S(1)} %get-tuple-element.70.m1), channel_id=1, source_target_pairs={{0,48},{8,56},{16,0},{24,8},{32,16},{40,24},{48,32},{56,40},{64,11... | collective-permute-start | bytes 442376 | tf_op jit(solution)/shard_map/ppermute | solution.py:36
  81.3 19.8 %collective-permute-start.25 = (bf16[144,512]{1,0:T(8,128)(2,1)S(1)}, bf16[144,512]{1,0:T(8,128)(2,1)S(1)}, u32[]{:S(2)}, u32[]{:S(2)}) collective-permute-start(bf16[144,512]{1,0:T(8,128)(2,1)S(1)} %get-tuple-element.71.m2), channel_id=1, source_target_pairs={{0,32},{8,40},{16,48},{24,56},{32,0},{40,8},{48,16},{56,24},{64,96... | collective-permute-start | bytes 442376 | tf_op jit(solution)/shard_map/ppermute | solution.py:36
  85.0 16.1 %collective-permute-start.26 = (bf16[144,512]{1,0:T(8,128)(2,1)S(1)}, bf16[144,512]{1,0:T(8,128)(2,1)S(1)}, u32[]{:S(2)}, u32[]{:S(2)}) collective-permute-start(bf16[144,512]{1,0:T(8,128)(2,1)S(1)} %get-tuple-element.72.m3), channel_id=1, source_target_pairs={{0,16},{8,24},{16,32},{24,40},{32,48},{40,56},{48,0},{56,8},{64,80... | collective-permute-start | bytes 442376 | tf_op jit(solution)/shard_map/ppermute | solution.py:36
  93.9 5.8 %collective-permute-start.22 = (bf16[128,512]{1,0:T(8,128)(2,1)S(1)}, bf16[128,512]{1,0:T(8,128)(2,1)S(1)}, u32[]{:S(2)}, u32[]{:S(2)}) collective-permute-start(bf16[128,512]{1,0:T(8,128)(2,1)S(1)} %get-tuple-element.74), channel_id=1, source_target_pairs={{0,1},{1,9},{2,3},{3,11},{4,5},{5,13},{6,7},{7,15},{8,0},{9,8},{10... | collective-permute-start | bytes 393224 | tf_op jit(solution)/shard_map/ppermute | solution.py:56
  94.8 6.3 %collective-permute-start.23 = (bf16[128,512]{1,0:T(8,128)(2,1)S(1)}, bf16[128,512]{1,0:T(8,128)(2,1)S(1)}, u32[]{:S(2)}, u32[]{:S(2)}) collective-permute-start(bf16[128,512]{1,0:T(8,128)(2,1)S(1)} %get-tuple-element.75), channel_id=1, source_target_pairs={{1,8},{3,10},{5,12},{7,14},{8,1},{10,3},{12,5},{14,7},{17,24},{19,... | collective-permute-start | bytes 393224 | tf_op jit(solution)/shard_map/ppermute | solution.py:56
  (5 other events, 50.8 us)

commit v8 on v7

--- a/solution.py
+++ b/solution.py
@@ -14,7 +14,6 @@
 WIDTHS = [SMALLEST * 2**k for k in range(LEVELS)]
 FACTORS = [SHARPNESS / math.sqrt(w) for w in WIDTHS]
 SPANS = list(zip([0] + WIDTHS[: LOW - 1], WIDTHS[:LOW]))
-LONG = 20_000_000_000
 EXTRA = 16
 PAIR = 2 * SMALLEST
 
@@ -282,27 +281,12 @@
     fill(gp, lambda k, a, b: dot(tails[k], q[:, a:b], 1, 0))
 
 
-def passage_grad_kernel(ids, tail, row, gp_low, q_all, own, message):
-    n = q_all.shape[1]
+def grad_kernel(
+    ids, t0, t1, t2, t3, gq_low, gp_low, p, q_all,
+    gq0, gq1, gq2, gq3, own, message, row, tail, gq,
+):
+    n, wide = gq0.shape
     width = own.shape[1]
-    q = q_all[...].reshape(4 * n, 2 * width)
-    message[4 * n :] = jnp.zeros((EXTRA, width), bf16)
-    put_terms(message, 4 * n, row[0:1])
-    for c in (0, 1):
-        lanes = slice(c * width, c * width + width)
-        gp = dot(tail[...], q[:, lanes], 1, 0) + gp_low[:, lanes]
-
-        @pl.when(ids[CORE] == c)
-        def _():
-            own[...] = gp
-
-        @pl.when(ids[CORE] != c)
-        def _():
-            message[: 4 * n] = gp.astype(bf16)
-
-
-def query_grad_kernel(ids, t0, t1, t2, t3, gq_low, p, gq0, gq1, gq2, gq3, tail, row, gq):
-    n, wide = gq0.shape
     loss = jnp.zeros((1, n), f32)
     for t, ref in enumerate((t0, t1, t2, t3)):
         j = (ids[Y] + 4 - t) & 3
@@ -313,6 +297,21 @@
     for s, out in enumerate((gq0, gq1, gq2, gq3)):
         j = (ids[X] + 4 - s) & 3
         out[...] = gq[pl.ds(pl.multiple_of(j * n, n), n), :].astype(out.dtype)
+
+    q = q_all[...].reshape(4 * n, wide)
+    message[4 * n :] = jnp.zeros((EXTRA, width), bf16)
+    put_terms(message, 4 * n, loss)
+    for c in (0, 1):
+        lanes = slice(c * width, c * width + width)
+        gp = dot(tail[...], q[:, lanes], 1, 0) + gp_low[:, lanes]
+
+        @pl.when(ids[CORE] == c)
+        def _():
+            own[...] = gp
+
+        @pl.when(ids[CORE] != c)
+        def _():
+            message[: 4 * n] = gp.astype(bf16)
 
 
 def core_sum_kernel(ids, gp_own, row, other, own, m1, m2, m3, loss):
@@ -425,20 +424,19 @@
         scratch=[pltpu.VMEM((LOW, 4 * n, 4 * n), bf16)],
         flops=4 * tile * wide, grant=12,
     )
-    gq0, gq1, gq2, gq3, tail, row = call(
-        query_grad_kernel, [ids], [*tails, gq_low, p],
+    gq0, gq1, gq2, gq3, gp_own, message, row = call(
+        grad_kernel, [ids], [*tails, gq_low, gp_low, p, q],
         [shape(n, wide, f32)]
         + [shape(n, wide, bf16)] * 3
-        + [shape(4 * n, 4 * n, bf16), shape(8, n, f32)],
-        scratch=[pltpu.VMEM((4 * n, wide), f32)],
-        flops=2 * tile * wide,
+        + [
+            shape(4 * n, width, f32),
+            shape(4 * n + EXTRA, width, bf16),
+            shape(8, n, f32),
+        ],
+        scratch=[pltpu.VMEM((4 * n, 4 * n), bf16), pltpu.VMEM((4 * n, wide), f32)],
+        flops=4 * tile * wide, grant=12,
     )
     gq = [shift_x(g, -s) for s, g in enumerate((gq1, gq2, gq3), 1)]
-    gp_own, message = call(
-        passage_grad_kernel, [ids], [tail, row, gp_low, q],
-        [shape(4 * n, width, f32), shape(4 * n + EXTRA, width, bf16)],
-        flops=2 * tile * wide,
-    )
     gp_own, *messages, row = call(
         core_sum_kernel, [ids], [gp_own, row, swap_core(message)],
         [shape(n, width, f32)] + [shape(n + EXTRA, width, bf16)] * 3 + [shape(8, n, f32)],
@@ -446,7 +444,7 @@
     gp = [shift_zl(m, -s) for s, m in enumerate(messages, 1)]
     gq_own, near, far = call(
         middle_kernel, [ids], [gq0, *gq, *messages],
-        [shape(n, width, f32)] + [shape(n, width, bf16)] * 2, in_place=3, flops=LONG,
+        [shape(n, width, f32)] + [shape(n, width, bf16)] * 2, in_place=3,
     )
     near = move_square(near, lambda h, c: (h, 1 - c) if h == c else (1 - h, c))
     far = move_square(far, lambda h, c: None if h == c else (1 - h, 1 - c))

time: 103 us -> 102 us (level)
    pallas_call x12 -> x11, Pallas kernels: 18 us -> 17.3 us  [call(): pl.pallas_call(body, out_shape=outs, in_specs=[scalar] * len(smem) + [vme...]
where the time goes in v8:
time: 102 us
  starting transfers between devices  45.3 us (44%)
  waiting for transfers between devices  27.4 us (27%)
  Pallas kernels  17.3 us (17%)
  blocking collectives  8.39 us (8%)
  other arithmetic  1.59 us (2%)
    pallas_call x11, Pallas kernels, call(): pl.pallas_call(body, out_shape=outs, in_specs=[scalar] * len(smem) + [vme...  17.3 us
    ppermute x6, starting transfers between devices, shift_zl(): lax.ppermute(a, 'batch', [(b, b // 8 * 8 + (b + 2 * s) % 8) for b in rang...  10.3 us
    ppermute x6, starting transfers between devices, shift_y(): lax.ppermute(a, 'feat', [(f, (f + 2 * s) % FEAT) for f in range(FEAT)])  9.16 us
    ppermute x4, starting transfers between devices, move_square(): return lax.ppermute(a, BOTH, pairs)  9.14 us
    ppermute x5, starting transfers between devices, swap_core(): return lax.ppermute(a, 'feat', [(f, f ^ 1) for f in range(FEAT)])  8.46 us
    all_to_all x1, blocking collectives, per_device(): stats = lax.all_to_all(message, 'batch', 0, 0, axis_index_groups=XZH_GROUPS)  8.39 us
    ppermute x6, waiting for transfers between devices, shift_x(): lax.ppermute(a, 'batch', [(b, (b + 8 * s) % BATCH) for b in range(BATCH)])  8.34 us
    ppermute x6, starting transfers between devices, shift_x(): lax.ppermute(a, 'batch', [(b, (b + 8 * s) % BATCH) for b in range(BATCH)])  8.23 us
  transfers between devices with their start and end apart: 27, of which 12 were waited for; matrix products, arithmetic and copies ran while one was open for 0% of the time, Pallas kernels for 9%

profile of v8, /device:TPU:1, one launch (start us, length us, event | category | flops | bytes accessed | tf_op | source)
XLA Modules:
  0.0 101.8 jit_solution(4459162713387960327)
XLA Ops:
  2.2 4.9 %collective-permute-start.8 = (bf16[144,512]{1,0:T(8,128)(2,1)S(1)}, bf16[144,512]{1,0:T(8,128)(2,1)S(1)}, u32[]{:S(2)}, u32[]{:S(2)}) collective-permute-start(bf16[144,512]{1,0:T(8,128)(2,1)S(1)} %pad_maximum_fusion.own), channel_id=1, source_target_pairs={{1,8},{3,10},{5,12},{7,14},{8,1},{10,3},{12,5},{14,7},{17,24},{19,... | collective-permute-start | bytes 442376 | tf_op jit(solution)/shard_map/ppermute | solution.py:55
  7.3 3.1 %collective-permute-start = (bf16[128,512]{1,0:T(8,128)(2,1)}, bf16[128,512]{1,0:T(8,128)(2,1)S(1)}, u32[]{:S(2)}, u32[]{:S(2)}) collective-permute-start(bf16[128,512]{1,0:T(8,128)(2,1)} %a.1), channel_id=1, source_target_pairs={{0,16},{8,24},{16,32},{24,40},{32,48},{40,56},{48,0},{56,8},{64,80... | collective-permute-start | bytes 393224 | tf_op jit(solution)/shard_map/ppermute | solution.py:35
  10.4 2.2 %collective-permute-start.2 = (bf16[128,512]{1,0:T(8,128)(2,1)}, bf16[128,512]{1,0:T(8,128)(2,1)S(1)}, u32[]{:S(2)}, u32[]{:S(2)}) collective-permute-start(bf16[128,512]{1,0:T(8,128)(2,1)} %a.1), channel_id=1, source_target_pairs={{0,48},{8,56},{16,0},{24,8},{32,16},{40,24},{48,32},{56,40},{64,11... | collective-permute-start | bytes 393224 | tf_op jit(solution)/shard_map/ppermute | solution.py:35
  17.0 2.5 %collective-permute-start.10 = (bf16[144,1024]{1,0:T(8,128)(2,1)S(1)}, bf16[144,1024]{1,0:T(8,128)(2,1)S(1)}, u32[]{:S(2)}, u32[]{:S(2)}) collective-permute-start(bf16[144,1024]{1,0:T(8,128)(2,1)S(1)} %shard_map.68.q0), channel_id=1, source_target_pairs={{0,128},{8,136},{16,144},{24,152},{32,160},{40,168},{48,176},{56,1... | collective-permute-start | bytes 884744 | tf_op jit(solution)/shard_map/ppermute | solution.py:31
  19.5 1.4 %collective-permute-done.p1 = bf16[128,512]{1,0:T(8,128)(2,1)S(1)} collective-permute-done((bf16[128,512]{1,0:T(8,128)(2,1)}, bf16[128,512]{1,0:T(8,128)(2,1)S(1)}, u32[]{:S(2)}, u32[]{:S(2)}) %collective-permute-start) | collective-permute-done | bytes 131104 | tf_op jit(solution)/shard_map/ppermute | solution.py:35
  20.9 2.5 %collective-permute-start.11 = (bf16[144,1024]{1,0:T(8,128)(2,1)S(1)}, bf16[144,1024]{1,0:T(8,128)(2,1)S(1)}, u32[]{:S(2)}, u32[]{:S(2)}) collective-permute-start(bf16[144,1024]{1,0:T(8,128)(2,1)S(1)} %shard_map.68.q0), channel_id=1, source_target_pairs={{0,192},{8,200},{16,208},{24,216},{32,224},{40,232},{48,240},{56,2... | collective-permute-start | bytes 884744 | tf_op jit(solution)/shard_map/ppermute | solution.py:31
  23.4 2.0 %collective-permute-start.4 = (bf16[128,512]{1,0:T(8,128)(2,1)S(1)}, bf16[128,512]{1,0:T(8,128)(2,1)S(1)}, u32[]{:S(2)}, u32[]{:S(2)}) collective-permute-start(bf16[128,512]{1,0:T(8,128)(2,1)S(1)} %collective-permute-done.p1), channel_id=1, source_target_pairs={{0,1},{1,0},{2,3},{3,2},{4,5},{5,4},{6,7},{7,6},{8,9},{9,8},{10,11... | collective-permute-start | bytes 393224 | tf_op jit(solution)/shard_map/ppermute | solution.py:45
  25.4 5.6 %collective-permute-done.1.p2 = bf16[128,512]{1,0:T(8,128)(2,1)S(1)} collective-permute-done((bf16[128,512]{1,0:T(8,128)(2,1)S(1)}, bf16[128,512]{1,0:T(8,128)(2,1)S(1)}, u32[]{:S(2)}, u32[]{:S(2)}) %collective-permute-start.1) | collective-permute-done | bytes 131104 | tf_op jit(solution)/shard_map/ppermute | solution.py:35
  30.9 2.3 %collective-permute-start.6 = (bf16[128,512]{1,0:T(8,128)(2,1)S(1)}, bf16[128,512]{1,0:T(8,128)(2,1)S(1)}, u32[]{:S(2)}, u32[]{:S(2)}) collective-permute-start(bf16[128,512]{1,0:T(8,128)(2,1)S(1)} %collective-permute-done.2.p3), channel_id=1, source_target_pairs={{0,1},{1,0},{2,3},{3,2},{4,5},{5,4},{6,7},{7,6},{8,9},{9,8},{10,11... | collective-permute-start | bytes 393224 | tf_op jit(solution)/shard_map/ppermute | solution.py:45
  34.6 2.0 %shard_map.69 = (f32[512,128]{1,0:T(8,128)S(1)}, f32[512,128]{1,0:T(8,128)S(1)}, f32[512,128]{1,0:T(8,128)S(1)}, f32[512,128]{1,0:T(8,128)S(1)}, bf16[512,1024]{...) custom-call(s32[5]{0:T(128)S(1)} %stack.35.ids, bf16[128,512]{1,0:T(8,128)(2,1)S(1)} %shard_map.67.p0, ...), custom_call_target="tpu_custom_call" | custom-call | flops 536870912 | bytes 5376000 | tf_op jit(solution)/shard_map/pallas_call | solution.py:72
  38.0 2.6 %collective-permute-start.13 = (f32[512,128]{1,0:T(8,128)S(1)}, f32[512,128]{1,0:T(8,128)S(1)}, u32[]{:S(2)}, u32[]{:S(2)}) collective-permute-start(f32[512,128]{1,0:T(8,128)S(1)} %get-tuple-element.43), channel_id=1, source_target_pairs={{0,4},{1,5},{2,6},{3,7},{4,0},{5,1},{6,2},{7,3},{8,12},{9,13},{10,... | collective-permute-start | bytes 786440 | tf_op jit(solution)/shard_map/ppermute | solution.py:41
  41.6 3.7 %shard_map.70 = (f32[5,4,512,128]{3,2,1,0:T(8,128)S(1)}, f32[4,8,128]{2,1,0:T(8,128)S(1)}, f32[4,8,128]{2,1,0:T(8,128)S(1)}) custom-call(s32[5]{0:T(128)S(1)} %stack.35.ids, f32[7]{0:T(128)S(1)} %copy-done.1, bf16[512,1024]{1,0:T(8,128)(2,1)S(1)} %get-tuple-element.46.p, bf16[4,128,1024]{2,1,0:T(8,128)(2,1)S(1)} %get-tuple-element.47.q_all, ...), custom_call_target="tpu_custom_call" | custom-call | flops 536870912 | bytes 7374848 | tf_op jit(solution)/shard_map/pallas_call | solution.py:72
  45.7 6.7 %collective-permute-done.13.s2 = f32[512,128]{1,0:T(8,128)S(1)} collective-permute-done((f32[512,128]{1,0:T(8,128)S(1)}, f32[512,128]{1,0:T(8,128)S(1)}, u32[]{:S(2)}, u32[]{:S(2)}) %collective-permute-start.13) | collective-permute-done | bytes 262176 | tf_op jit(solution)/shard_map/ppermute | solution.py:41
  53.5 8.4 %all_to_all.5.stats = f32[8,40,128]{2,1,0:T(8,128)S(1)} all-to-all(f32[8,40,128]{2,1,0:T(8,128)S(1)} %get-tuple-element.49), channel_id=1, replica_groups={{0,8,64,72,128,136,192,200},{16,24,80,88,144,152,208,216},{32,40,96,104..., dimensions={0} | all-to-all | bytes 327680 | tf_op jit(solution)/shard_map/all_to_all | solution.py:415
  63.6 2.8 %collective-permute-start.16 = (bf16[528,128]{1,0:T(8,128)(2,1)S(1)}, bf16[528,128]{1,0:T(8,128)(2,1)S(1)}, u32[]{:S(2)}, u32[]{:S(2)}) collective-permute-start(bf16[528,128]{1,0:T(8,128)(2,1)S(1)} %get-tuple-element.55), channel_id=1, source_target_pairs={{0,4},{1,5},{2,6},{3,7},{4,0},{5,1},{6,2},{7,3},{8,12},{9,13},{10,... | collective-permute-start | bytes 405512 | tf_op jit(solution)/shard_map/ppermute | solution.py:41
  66.9 3.4 %shard_map.73 = (f32[512,1024]{1,0:T(8,128)S(1)}, f32[512,1024]{1,0:T(8,128)S(1)}) custom-call(s32[5]{0:T(128)S(1)} %stack.35.ids, f32[7]{0:T(128)S(1)} %copy-done.1, f32[5,4,512,128]{3,2,1,0:T(8,128)S(1)} %get-tuple-element.57.e_low, f32[4,8,128]{2,1,0:T(8,128)S(1)} %get-tuple-element.58.rates, s32[4,1,128]{2,1,0:T(1,128)S(1)} %get-tuple-element.45.pos, ...), custom_call_target="tpu_custom_call" | custom-call | flops 1073741824 | bytes 11552768 | tf_op jit(solution)/shard_map/pallas_call | solution.py:72
  70.8 2.4 %shard_map.74 = (f32[128,1024]{1,0:T(8,128)S(1)}, bf16[128,1024]{1,0:T(8,128)(2,1)S(1)}, bf16[128,1024]{1,0:T(8,128)(2,1)S(1)}, bf16[128,1024]{1,0:T(8,128)(2,1)...) custom-call(s32[5]{0:T(128)S(1)} %stack.35.ids, ...), custom_call_target="tpu_custom_call" | custom-call | flops 1073741824 | bytes 9736192 | tf_op jit(solution)/shard_map/pallas_call | solution.py:72
  73.2 3.2 %collective-permute-start.21 = (bf16[528,512]{1,0:T(8,128)(2,1)S(1)}, bf16[528,512]{1,0:T(8,128)(2,1)S(1)}, u32[]{:S(2)}, u32[]{:S(2)}) collective-permute-start(bf16[528,512]{1,0:T(8,128)(2,1)S(1)} %get-tuple-element.67), channel_id=1, source_target_pairs={{0,1},{1,0},{2,3},{3,2},{4,5},{5,4},{6,7},{7,6},{8,9},{9,8},{10,11... | collective-permute-start | bytes 1622024 | tf_op jit(solution)/shard_map/ppermute | solution.py:45
  79.1 1.5 %collective-permute-start.24 = (bf16[144,512]{1,0:T(8,128)(2,1)S(1)}, bf16[144,512]{1,0:T(8,128)(2,1)S(1)}, u32[]{:S(2)}, u32[]{:S(2)}) collective-permute-start(bf16[144,512]{1,0:T(8,128)(2,1)S(1)} %get-tuple-element.68.m1), channel_id=1, source_target_pairs={{0,48},{8,56},{16,0},{24,8},{32,16},{40,24},{48,32},{56,40},{64,11... | collective-permute-start | bytes 442376 | tf_op jit(solution)/shard_map/ppermute | solution.py:35
  80.6 2.5 %collective-permute-start.25 = (bf16[144,512]{1,0:T(8,128)(2,1)S(1)}, bf16[144,512]{1,0:T(8,128)(2,1)S(1)}, u32[]{:S(2)}, u32[]{:S(2)}) collective-permute-start(bf16[144,512]{1,0:T(8,128)(2,1)S(1)} %get-tuple-element.69.m2), channel_id=1, source_target_pairs={{0,32},{8,40},{16,48},{24,56},{32,0},{40,8},{48,16},{56,24},{64,96... | collective-permute-start | bytes 442376 | tf_op jit(solution)/shard_map/ppermute | solution.py:35
  86.2 6.3 %collective-permute-done.20.g3 = bf16[128,1024]{1,0:T(8,128)(2,1)S(1)} collective-permute-done((bf16[128,1024]{1,0:T(8,128)(2,1)S(1)}, bf16[128,1024]{1,0:T(8,128)(2,1)S(1)}, u32[]{:S(2)}, u32[]{:S(2)}) %collective-permute-start.20) | collective-permute-done | bytes 262176 | tf_op jit(solution)/shard_map/ppermute | solution.py:31
  94.1 3.2 %collective-permute-start.23 = (bf16[128,512]{1,0:T(8,128)(2,1)S(1)}, bf16[128,512]{1,0:T(8,128)(2,1)S(1)}, u32[]{:S(2)}, u32[]{:S(2)}) collective-permute-start(bf16[128,512]{1,0:T(8,128)(2,1)S(1)} %get-tuple-element.73), channel_id=1, source_target_pairs={{1,8},{3,10},{5,12},{7,14},{8,1},{10,3},{12,5},{14,7},{17,24},{19,... | collective-permute-start | bytes 393224 | tf_op jit(solution)/shard_map/ppermute | solution.py:55
  97.3 1.7 %collective-permute-done.22.near = bf16[128,512]{1,0:T(8,128)(2,1)S(1)} collective-permute-done((bf16[128,512]{1,0:T(8,128)(2,1)S(1)}, bf16[128,512]{1,0:T(8,128)(2,1)S(1)}, u32[]{:S(2)}, u32[]{:S(2)}) %collective-permute-start.22) | collective-permute-done | bytes 131104 | tf_op jit(solution)/shard_map/ppermute | solution.py:55
  99.0 1.4 %collective-permute-done.23.far = bf16[128,512]{1,0:T(8,128)(2,1)S(1)} collective-permute-done((bf16[128,512]{1,0:T(8,128)(2,1)S(1)}, bf16[128,512]{1,0:T(8,128)(2,1)S(1)}, u32[]{:S(2)}, u32[]{:S(2)}) %collective-permute-start.23) | collective-permute-done | bytes 131104 | tf_op jit(solution)/shard_map/ppermute | solution.py:55
  (50 shorter events, 22.8 us)
Async XLA Ops:
  2.2 12.9 %collective-permute-start.8 = (bf16[144,512]{1,0:T(8,128)(2,1)S(1)}, bf16[144,512]{1,0:T(8,128)(2,1)S(1)}, u32[]{:S(2)}, u32[]{:S(2)}) collective-permute-start(bf16[144,512]{1,0:T(8,128)(2,1)S(1)} %pad_maximum_fusion.own), channel_id=1, source_target_pairs={{1,8},{3,10},{5,12},{7,14},{8,1},{10,3},{12,5},{14,7},{17,24},{19,... | collective-permute-start | bytes 442376 | tf_op jit(solution)/shard_map/ppermute | solution.py:55
  7.2 8.0 %collective-permute-start.7 = (bf16[128,512]{1,0:T(8,128)(2,1)}, bf16[128,512]{1,0:T(8,128)(2,1)S(1)}, u32[]{:S(2)}, u32[]{:S(2)}) collective-permute-start(bf16[128,512]{1,0:T(8,128)(2,1)} %param.4), channel_id=1, source_target_pairs={{0,8},{1,0},{2,10},{3,2},{4,12},{5,4},{6,14},{7,6},{8,9},{9,1},{10... | collective-permute-start | bytes 393224 | tf_op jit(solution)/shard_map/ppermute | solution.py:55
  7.3 13.6 %collective-permute-start = (bf16[128,512]{1,0:T(8,128)(2,1)}, bf16[128,512]{1,0:T(8,128)(2,1)S(1)}, u32[]{:S(2)}, u32[]{:S(2)}) collective-permute-start(bf16[128,512]{1,0:T(8,128)(2,1)} %a.1), channel_id=1, source_target_pairs={{0,16},{8,24},{16,32},{24,40},{32,48},{40,56},{48,0},{56,8},{64,80... | collective-permute-start | bytes 393224 | tf_op jit(solution)/shard_map/ppermute | solution.py:35
  10.4 13.0 %collective-permute-start.2 = (bf16[128,512]{1,0:T(8,128)(2,1)}, bf16[128,512]{1,0:T(8,128)(2,1)S(1)}, u32[]{:S(2)}, u32[]{:S(2)}) collective-permute-start(bf16[128,512]{1,0:T(8,128)(2,1)} %a.1), channel_id=1, source_target_pairs={{0,48},{8,56},{16,0},{24,8},{32,16},{40,24},{48,32},{56,40},{64,11... | collective-permute-start | bytes 393224 | tf_op jit(solution)/shard_map/ppermute | solution.py:35
  14.1 9.3 %collective-permute-start.3 = (bf16[128,512]{1,0:T(8,128)(2,1)S(1)}, bf16[128,512]{1,0:T(8,128)(2,1)S(1)}, u32[]{:S(2)}, u32[]{:S(2)}) collective-permute-start(bf16[128,512]{1,0:T(8,128)(2,1)S(1)} %shard_map.67.p0), channel_id=1, source_target_pairs={{0,1},{1,0},{2,3},{3,2},{4,5},{5,4},{6,7},{7,6},{8,9},{9,8},{10,11... | collective-permute-start | bytes 393224 | tf_op jit(solution)/shard_map/ppermute | solution.py:45
  15.8 18.8 %collective-permute-start.9 = (bf16[144,1024]{1,0:T(8,128)(2,1)S(1)}, bf16[144,1024]{1,0:T(8,128)(2,1)S(1)}, u32[]{:S(2)}, u32[]{:S(2)}) collective-permute-start(bf16[144,1024]{1,0:T(8,128)(2,1)S(1)} %shard_map.68.q0), channel_id=1, source_target_pairs={{0,64},{8,72},{16,80},{24,88},{32,96},{40,104},{48,112},{56,120},{... | collective-permute-start | bytes 884744 | tf_op jit(solution)/shard_map/ppermute | solution.py:31
  17.0 17.5 %collective-permute-start.10 = (bf16[144,1024]{1,0:T(8,128)(2,1)S(1)}, bf16[144,1024]{1,0:T(8,128)(2,1)S(1)}, u32[]{:S(2)}, u32[]{:S(2)}) collective-permute-start(bf16[144,1024]{1,0:T(8,128)(2,1)S(1)} %shard_map.68.q0), channel_id=1, source_target_pairs={{0,128},{8,136},{16,144},{24,152},{32,160},{40,168},{48,176},{56,1... | collective-permute-start | bytes 884744 | tf_op jit(solution)/shard_map/ppermute | solution.py:31
  20.9 13.6 %collective-permute-start.11 = (bf16[144,1024]{1,0:T(8,128)(2,1)S(1)}, bf16[144,1024]{1,0:T(8,128)(2,1)S(1)}, u32[]{:S(2)}, u32[]{:S(2)}) collective-permute-start(bf16[144,1024]{1,0:T(8,128)(2,1)S(1)} %shard_map.68.q0), channel_id=1, source_target_pairs={{0,192},{8,200},{16,208},{24,216},{32,224},{40,232},{48,240},{56,2... | collective-permute-start | bytes 884744 | tf_op jit(solution)/shard_map/ppermute | solution.py:31
  23.4 7.6 %collective-permute-start.1 = (bf16[128,512]{1,0:T(8,128)(2,1)S(1)}, bf16[128,512]{1,0:T(8,128)(2,1)S(1)}, u32[]{:S(2)}, u32[]{:S(2)}) collective-permute-start(bf16[128,512]{1,0:T(8,128)(2,1)S(1)} %collective-permute-done.p1), channel_id=1, source_target_pairs={{0,16},{8,24},{16,32},{24,40},{32,48},{40,56},{48,0},{56,8},{64,80... | collective-permute-start | bytes 393224 | tf_op jit(solution)/shard_map/ppermute | solution.py:35
  23.4 9.8 %collective-permute-start.4 = (bf16[128,512]{1,0:T(8,128)(2,1)S(1)}, bf16[128,512]{1,0:T(8,128)(2,1)S(1)}, u32[]{:S(2)}, u32[]{:S(2)}) collective-permute-start(bf16[128,512]{1,0:T(8,128)(2,1)S(1)} %collective-permute-done.p1), channel_id=1, source_target_pairs={{0,1},{1,0},{2,3},{3,2},{4,5},{5,4},{6,7},{7,6},{8,9},{9,8},{10,11... | collective-permute-start | bytes 393224 | tf_op jit(solution)/shard_map/ppermute | solution.py:45
  36.6 9.1 %collective-permute-start.12 = (f32[512,128]{1,0:T(8,128)S(1)}, f32[512,128]{1,0:T(8,128)S(1)}, u32[]{:S(2)}, u32[]{:S(2)}) collective-permute-start(f32[512,128]{1,0:T(8,128)S(1)} %get-tuple-element.42), channel_id=1, source_target_pairs={{0,2},{1,3},{2,4},{3,5},{4,6},{5,7},{6,0},{7,1},{8,10},{9,11},{10,... | collective-permute-start | bytes 786440 | tf_op jit(solution)/shard_map/ppermute | solution.py:41
  38.0 14.5 %collective-permute-start.13 = (f32[512,128]{1,0:T(8,128)S(1)}, f32[512,128]{1,0:T(8,128)S(1)}, u32[]{:S(2)}, u32[]{:S(2)}) collective-permute-start(f32[512,128]{1,0:T(8,128)S(1)} %get-tuple-element.43), channel_id=1, source_target_pairs={{0,4},{1,5},{2,6},{3,7},{4,0},{5,1},{6,2},{7,3},{8,12},{9,13},{10,... | collective-permute-start | bytes 786440 | tf_op jit(solution)/shard_map/ppermute | solution.py:41
  40.6 11.9 %collective-permute-start.14 = (f32[512,128]{1,0:T(8,128)S(1)}, f32[512,128]{1,0:T(8,128)S(1)}, u32[]{:S(2)}, u32[]{:S(2)}) collective-permute-start(f32[512,128]{1,0:T(8,128)S(1)} %get-tuple-element.44), channel_id=1, source_target_pairs={{0,6},{1,7},{2,0},{3,1},{4,2},{5,3},{6,4},{7,5},{8,14},{9,15},{10,... | collective-permute-start | bytes 786440 | tf_op jit(solution)/shard_map/ppermute | solution.py:41
  62.8 7.5 %collective-permute-start.15 = (bf16[528,128]{1,0:T(8,128)(2,1)S(1)}, bf16[528,128]{1,0:T(8,128)(2,1)S(1)}, u32[]{:S(2)}, u32[]{:S(2)}) collective-permute-start(bf16[528,128]{1,0:T(8,128)(2,1)S(1)} %get-tuple-element.54), channel_id=1, source_target_pairs={{0,2},{1,3},{2,4},{3,5},{4,6},{5,7},{6,0},{7,1},{8,10},{9,11},{10,... | collective-permute-start | bytes 405512 | tf_op jit(solution)/shard_map/ppermute | solution.py:41
  63.6 7.2 %collective-permute-start.16 = (bf16[528,128]{1,0:T(8,128)(2,1)S(1)}, bf16[528,128]{1,0:T(8,128)(2,1)S(1)}, u32[]{:S(2)}, u32[]{:S(2)}) collective-permute-start(bf16[528,128]{1,0:T(8,128)(2,1)S(1)} %get-tuple-element.55), channel_id=1, source_target_pairs={{0,4},{1,5},{2,6},{3,7},{4,0},{5,1},{6,2},{7,3},{8,12},{9,13},{10,... | collective-permute-start | bytes 405512 | tf_op jit(solution)/shard_map/ppermute | solution.py:41
  73.2 5.2 %collective-permute-start.21 = (bf16[528,512]{1,0:T(8,128)(2,1)S(1)}, bf16[528,512]{1,0:T(8,128)(2,1)S(1)}, u32[]{:S(2)}, u32[]{:S(2)}) collective-permute-start(bf16[528,512]{1,0:T(8,128)(2,1)S(1)} %get-tuple-element.67), channel_id=1, source_target_pairs={{0,1},{1,0},{2,3},{3,2},{4,5},{5,4},{6,7},{7,6},{8,9},{9,8},{10,11... | collective-permute-start | bytes 1622024 | tf_op jit(solution)/shard_map/ppermute | solution.py:45
  76.4 7.9 %collective-permute-start.18 = (bf16[128,1024]{1,0:T(8,128)(2,1)S(1)}, bf16[128,1024]{1,0:T(8,128)(2,1)S(1)}, u32[]{:S(2)}, u32[]{:S(2)}) collective-permute-start(bf16[128,1024]{1,0:T(8,128)(2,1)S(1)} %get-tuple-element.62), channel_id=1, source_target_pairs={{0,192},{8,200},{16,208},{24,216},{32,224},{40,232},{48,240},{56,2... | collective-permute-start | bytes 786440 | tf_op jit(solution)/shard_map/ppermute | solution.py:31
  77.1 9.1 %collective-permute-start.19 = (bf16[128,1024]{1,0:T(8,128)(2,1)S(1)}, bf16[128,1024]{1,0:T(8,128)(2,1)S(1)}, u32[]{:S(2)}, u32[]{:S(2)}) collective-permute-start(bf16[128,1024]{1,0:T(8,128)(2,1)S(1)} %get-tuple-element.63), channel_id=1, source_target_pairs={{0,128},{8,136},{16,144},{24,152},{32,160},{40,168},{48,176},{56,1... | collective-permute-start | bytes 786440 | tf_op jit(solution)/shard_map/ppermute | solution.py:31
  78.3 14.2 %collective-permute-start.20 = (bf16[128,1024]{1,0:T(8,128)(2,1)S(1)}, bf16[128,1024]{1,0:T(8,128)(2,1)S(1)}, u32[]{:S(2)}, u32[]{:S(2)}) collective-permute-start(bf16[128,1024]{1,0:T(8,128)(2,1)S(1)} %get-tuple-element.64), channel_id=1, source_target_pairs={{0,64},{8,72},{16,80},{24,88},{32,96},{40,104},{48,112},{56,120},{... | collective-permute-start | bytes 786440 | tf_op jit(solution)/shard_map/ppermute | solution.py:31
  79.1 21.4 %collective-permute-start.24 = (bf16[144,512]{1,0:T(8,128)(2,1)S(1)}, bf16[144,512]{1,0:T(8,128)(2,1)S(1)}, u32[]{:S(2)}, u32[]{:S(2)}) collective-permute-start(bf16[144,512]{1,0:T(8,128)(2,1)S(1)} %get-tuple-element.68.m1), channel_id=1, source_target_pairs={{0,48},{8,56},{16,0},{24,8},{32,16},{40,24},{48,32},{56,40},{64,11... | collective-permute-start | bytes 442376 | tf_op jit(solution)/shard_map/ppermute | solution.py:35
  80.6 19.8 %collective-permute-start.25 = (bf16[144,512]{1,0:T(8,128)(2,1)S(1)}, bf16[144,512]{1,0:T(8,128)(2,1)S(1)}, u32[]{:S(2)}, u32[]{:S(2)}) collective-permute-start(bf16[144,512]{1,0:T(8,128)(2,1)S(1)} %get-tuple-element.69.m2), channel_id=1, source_target_pairs={{0,32},{8,40},{16,48},{24,56},{32,0},{40,8},{48,16},{56,24},{64,96... | collective-permute-start | bytes 442376 | tf_op jit(solution)/shard_map/ppermute | solution.py:35
  84.3 16.2 %collective-permute-start.26 = (bf16[144,512]{1,0:T(8,128)(2,1)S(1)}, bf16[144,512]{1,0:T(8,128)(2,1)S(1)}, u32[]{:S(2)}, u32[]{:S(2)}) collective-permute-start(bf16[144,512]{1,0:T(8,128)(2,1)S(1)} %get-tuple-element.70.m3), channel_id=1, source_target_pairs={{0,16},{8,24},{16,32},{24,40},{32,48},{40,56},{48,0},{56,8},{64,80... | collective-permute-start | bytes 442376 | tf_op jit(solution)/shard_map/ppermute | solution.py:35
  93.2 5.8 %collective-permute-start.22 = (bf16[128,512]{1,0:T(8,128)(2,1)S(1)}, bf16[128,512]{1,0:T(8,128)(2,1)S(1)}, u32[]{:S(2)}, u32[]{:S(2)}) collective-permute-start(bf16[128,512]{1,0:T(8,128)(2,1)S(1)} %get-tuple-element.72), channel_id=1, source_target_pairs={{0,1},{1,9},{2,3},{3,11},{4,5},{5,13},{6,7},{7,15},{8,0},{9,8},{10... | collective-permute-start | bytes 393224 | tf_op jit(solution)/shard_map/ppermute | solution.py:55
  94.1 6.3 %collective-permute-start.23 = (bf16[128,512]{1,0:T(8,128)(2,1)S(1)}, bf16[128,512]{1,0:T(8,128)(2,1)S(1)}, u32[]{:S(2)}, u32[]{:S(2)}) collective-permute-start(bf16[128,512]{1,0:T(8,128)(2,1)S(1)} %get-tuple-element.73), channel_id=1, source_target_pairs={{1,8},{3,10},{5,12},{7,14},{8,1},{10,3},{12,5},{14,7},{17,24},{19,... | collective-permute-start | bytes 393224 | tf_op jit(solution)/shard_map/ppermute | solution.py:55
  (5 other events, 50.8 us)

commit v9 on v8

--- a/solution.py
+++ b/solution.py
@@ -117,7 +117,7 @@
 
 
 def score_kernel(
-    ids, p0, p1, p2, p3, o0, o1, o2, o3, q0, q1, q2, q3, s0, s1, s2, s3, p, q_all, pos
+    ids, p0, p1, p2, p3, o0, o1, o2, o3, q0, q1, q2, q3, s0, s1, s2, s3, p, q_all, pos, partial
 ):
     n, width = p0.shape
     for s, (own, other) in enumerate(zip((p0, p1, p2, p3), (o0, o1, o2, o3))):
@@ -138,8 +138,10 @@
         q_all[j] = q[:n]
         digits = q[n:, :n].astype(f32)
         pos[j] = (digits[0:1] * 64.0 + digits[1:2]).astype(jnp.int32)
+    partial[...] = dot(p[...], q_all[...].reshape(4 * n, 2 * width), 1, 1)
     for t, out in enumerate((s0, s1, s2, s3)):
-        out[...] = dot(p[...], q_all[(ids[Y] + t) & 3], 1, 1)
+        j = (ids[Y] + t) & 3
+        out[...] = partial[:, pl.ds(pl.multiple_of(j * n, n), n)]
 
 
 def level(scores, hot, weight):
@@ -377,9 +379,12 @@
     ids = jnp.stack([bi // 8, fi // 2, bi % 8 // 2, bi % 2, fi % 2]).astype(jnp.int32)
 
     near = move_square(queries, lambda h, c: (1 - h, c) if h == c else (h, 1 - c))
-    rows = jnp.stack([positives >> 6, positives & 63]).astype(bf16)
-    rows = jnp.pad(rows, ((0, EXTRA - 2), (0, width - n)))
-    q_row = jnp.concatenate([queries, rows], axis=0)
+    row = lax.broadcasted_iota(jnp.int32, (n + EXTRA, width), 0)
+    digits = jnp.pad(positives, (0, width - n))[None, :]
+    digits = jnp.where(row == n, digits >> 6, jnp.where(row == n + 1, digits & 63, 0))
+    q_row = jnp.where(
+        row < n, jnp.pad(queries, ((0, EXTRA), (0, 0))), digits.astype(bf16)
+    )
     far = move_square(q_row, lambda h, c: None if h == c else (1 - h, 1 - c))
     (q_msg,) = call(
         pack_kernel, [ids], [q_row, near, far], [shape(n + EXTRA, wide, bf16)]
@@ -400,6 +405,7 @@
             shape(4, n, wide, bf16),
             shape(4, 1, n, jnp.int32),
         ],
+        scratch=[pltpu.VMEM((4 * n, 4 * n), f32)],
         flops=2 * tile * wide,
     )
     pieces = [partial[0]] + [shift_y(partial[t], t) for t in (1, 2, 3)]

time: 102 us -> 102 us (level)
    select_n x0 -> x1, other arithmetic: none -> 1.03 us  [per_device(): jnp.where(row < n, jnp.pad(queries, ((0, EXTRA), (0, 0))), digits.astype(...]
where the time goes in v9:
time: 102 us
  starting transfers between devices  45.4 us (45%)
  waiting for transfers between devices  27.4 us (27%)
  Pallas kernels  16.9 us (17%)
  blocking collectives  8.35 us (8%)
  other arithmetic  1.71 us (2%)
    pallas_call x11, Pallas kernels, call(): pl.pallas_call(body, out_shape=outs, in_specs=[scalar] * len(smem) + [vme...  16.9 us
    ppermute x6, starting transfers between devices, shift_zl(): lax.ppermute(a, 'batch', [(b, b // 8 * 8 + (b + 2 * s) % 8) for b in rang...  10.4 us
    ppermute x6, starting transfers between devices, shift_y(): lax.ppermute(a, 'feat', [(f, (f + 2 * s) % FEAT) for f in range(FEAT)])  9.18 us
    ppermute x4, starting transfers between devices, move_square(): return lax.ppermute(a, BOTH, pairs)  9.14 us
    ppermute x5, starting transfers between devices, swap_core(): return lax.ppermute(a, 'feat', [(f, f ^ 1) for f in range(FEAT)])  8.47 us
    all_to_all x1, blocking collectives, per_device(): stats = lax.all_to_all(message, 'batch', 0, 0, axis_index_groups=XZH_GROUPS)  8.35 us
    ppermute x6, waiting for transfers between devices, shift_x(): lax.ppermute(a, 'batch', [(b, (b + 8 * s) % BATCH) for b in range(BATCH)])  8.34 us
    ppermute x6, starting transfers between devices, shift_x(): lax.ppermute(a, 'batch', [(b, (b + 8 * s) % BATCH) for b in range(BATCH)])  8.22 us
  transfers between devices with their start and end apart: 27, of which 12 were waited for; matrix products, arithmetic and copies ran while one was open for 0% of the time, Pallas kernels for 9%

profile of v9, /device:TPU:1, one launch (start us, length us, event | category | flops | bytes accessed | tf_op | source)
XLA Modules:
  0.0 101.5 jit_solution(9938436418819691632)
XLA Ops:
  2.4 4.9 %collective-permute-start.8 = (bf16[144,512]{1,0:T(8,128)(2,1)S(1)}, bf16[144,512]{1,0:T(8,128)(2,1)S(1)}, u32[]{:S(2)}, u32[]{:S(2)}) collective-permute-start(bf16[144,512]{1,0:T(8,128)(2,1)S(1)} %fusion.own), channel_id=1, source_target_pairs={{1,8},{3,10},{5,12},{7,14},{8,1},{10,3},{12,5},{14,7},{17,24},{19,... | collective-permute-start | bytes 442376 | tf_op jit(solution)/shard_map/ppermute | solution.py:55
  7.4 3.1 %collective-permute-start = (bf16[128,512]{1,0:T(8,128)(2,1)}, bf16[128,512]{1,0:T(8,128)(2,1)S(1)}, u32[]{:S(2)}, u32[]{:S(2)}) collective-permute-start(bf16[128,512]{1,0:T(8,128)(2,1)} %a.1), channel_id=1, source_target_pairs={{0,16},{8,24},{16,32},{24,40},{32,48},{40,56},{48,0},{56,8},{64,80... | collective-permute-start | bytes 393224 | tf_op jit(solution)/shard_map/ppermute | solution.py:35
  10.5 2.2 %collective-permute-start.2 = (bf16[128,512]{1,0:T(8,128)(2,1)}, bf16[128,512]{1,0:T(8,128)(2,1)S(1)}, u32[]{:S(2)}, u32[]{:S(2)}) collective-permute-start(bf16[128,512]{1,0:T(8,128)(2,1)} %a.1), channel_id=1, source_target_pairs={{0,48},{8,56},{16,0},{24,8},{32,16},{40,24},{48,32},{56,40},{64,11... | collective-permute-start | bytes 393224 | tf_op jit(solution)/shard_map/ppermute | solution.py:35
  17.2 2.5 %collective-permute-start.10 = (bf16[144,1024]{1,0:T(8,128)(2,1)S(1)}, bf16[144,1024]{1,0:T(8,128)(2,1)S(1)}, u32[]{:S(2)}, u32[]{:S(2)}) collective-permute-start(bf16[144,1024]{1,0:T(8,128)(2,1)S(1)} %shard_map.68.q0), channel_id=1, source_target_pairs={{0,128},{8,136},{16,144},{24,152},{32,160},{40,168},{48,176},{56,1... | collective-permute-start | bytes 884744 | tf_op jit(solution)/shard_map/ppermute | solution.py:31
  19.6 1.4 %collective-permute-done.p1 = bf16[128,512]{1,0:T(8,128)(2,1)S(1)} collective-permute-done((bf16[128,512]{1,0:T(8,128)(2,1)}, bf16[128,512]{1,0:T(8,128)(2,1)S(1)}, u32[]{:S(2)}, u32[]{:S(2)}) %collective-permute-start) | collective-permute-done | bytes 131104 | tf_op jit(solution)/shard_map/ppermute | solution.py:35
  21.0 2.5 %collective-permute-start.11 = (bf16[144,1024]{1,0:T(8,128)(2,1)S(1)}, bf16[144,1024]{1,0:T(8,128)(2,1)S(1)}, u32[]{:S(2)}, u32[]{:S(2)}) collective-permute-start(bf16[144,1024]{1,0:T(8,128)(2,1)S(1)} %shard_map.68.q0), channel_id=1, source_target_pairs={{0,192},{8,200},{16,208},{24,216},{32,224},{40,232},{48,240},{56,2... | collective-permute-start | bytes 884744 | tf_op jit(solution)/shard_map/ppermute | solution.py:31
  23.5 2.0 %collective-permute-start.4 = (bf16[128,512]{1,0:T(8,128)(2,1)S(1)}, bf16[128,512]{1,0:T(8,128)(2,1)S(1)}, u32[]{:S(2)}, u32[]{:S(2)}) collective-permute-start(bf16[128,512]{1,0:T(8,128)(2,1)S(1)} %collective-permute-done.p1), channel_id=1, source_target_pairs={{0,1},{1,0},{2,3},{3,2},{4,5},{5,4},{6,7},{7,6},{8,9},{9,8},{10,11... | collective-permute-start | bytes 393224 | tf_op jit(solution)/shard_map/ppermute | solution.py:45
  25.5 5.6 %collective-permute-done.1.p2 = bf16[128,512]{1,0:T(8,128)(2,1)S(1)} collective-permute-done((bf16[128,512]{1,0:T(8,128)(2,1)S(1)}, bf16[128,512]{1,0:T(8,128)(2,1)S(1)}, u32[]{:S(2)}, u32[]{:S(2)}) %collective-permute-start.1) | collective-permute-done | bytes 131104 | tf_op jit(solution)/shard_map/ppermute | solution.py:35
  31.1 2.3 %collective-permute-start.6 = (bf16[128,512]{1,0:T(8,128)(2,1)S(1)}, bf16[128,512]{1,0:T(8,128)(2,1)S(1)}, u32[]{:S(2)}, u32[]{:S(2)}) collective-permute-start(bf16[128,512]{1,0:T(8,128)(2,1)S(1)} %collective-permute-done.2.p3), channel_id=1, source_target_pairs={{0,1},{1,0},{2,3},{3,2},{4,5},{5,4},{6,7},{7,6},{8,9},{9,8},{10,11... | collective-permute-start | bytes 393224 | tf_op jit(solution)/shard_map/ppermute | solution.py:45
  34.7 1.6 %shard_map.69 = (f32[512,128]{1,0:T(8,128)S(1)}, f32[512,128]{1,0:T(8,128)S(1)}, f32[512,128]{1,0:T(8,128)S(1)}, f32[512,128]{1,0:T(8,128)S(1)}, bf16[512,1024]{...) custom-call(s32[5]{0:T(128)S(1)} %stack.23.ids, bf16[128,512]{1,0:T(8,128)(2,1)S(1)} %shard_map.67.p0, ...), custom_call_target="tpu_custom_call" | custom-call | flops 536870912 | bytes 5376000 | tf_op jit(solution)/shard_map/pallas_call | solution.py:72
  37.7 2.6 %collective-permute-start.13 = (f32[512,128]{1,0:T(8,128)S(1)}, f32[512,128]{1,0:T(8,128)S(1)}, u32[]{:S(2)}, u32[]{:S(2)}) collective-permute-start(f32[512,128]{1,0:T(8,128)S(1)} %get-tuple-element.43), channel_id=1, source_target_pairs={{0,4},{1,5},{2,6},{3,7},{4,0},{5,1},{6,2},{7,3},{8,12},{9,13},{10,... | collective-permute-start | bytes 786440 | tf_op jit(solution)/shard_map/ppermute | solution.py:41
  41.4 3.7 %shard_map.70 = (f32[5,4,512,128]{3,2,1,0:T(8,128)S(1)}, f32[4,8,128]{2,1,0:T(8,128)S(1)}, f32[4,8,128]{2,1,0:T(8,128)S(1)}) custom-call(s32[5]{0:T(128)S(1)} %stack.23.ids, f32[7]{0:T(128)S(1)} %copy-done.1, bf16[512,1024]{1,0:T(8,128)(2,1)S(1)} %get-tuple-element.46.p, bf16[4,128,1024]{2,1,0:T(8,128)(2,1)S(1)} %get-tuple-element.47.q_all, ...), custom_call_target="tpu_custom_call" | custom-call | flops 536870912 | bytes 7374848 | tf_op jit(solution)/shard_map/pallas_call | solution.py:72
  45.5 6.7 %collective-permute-done.13.s2 = f32[512,128]{1,0:T(8,128)S(1)} collective-permute-done((f32[512,128]{1,0:T(8,128)S(1)}, f32[512,128]{1,0:T(8,128)S(1)}, u32[]{:S(2)}, u32[]{:S(2)}) %collective-permute-start.13) | collective-permute-done | bytes 262176 | tf_op jit(solution)/shard_map/ppermute | solution.py:41
  53.3 8.4 %all_to_all.5.stats = f32[8,40,128]{2,1,0:T(8,128)S(1)} all-to-all(f32[8,40,128]{2,1,0:T(8,128)S(1)} %get-tuple-element.49), channel_id=1, replica_groups={{0,8,64,72,128,136,192,200},{16,24,80,88,144,152,208,216},{32,40,96,104..., dimensions={0} | all-to-all | bytes 327680 | tf_op jit(solution)/shard_map/all_to_all | solution.py:421
  63.4 2.8 %collective-permute-start.16 = (bf16[528,128]{1,0:T(8,128)(2,1)S(1)}, bf16[528,128]{1,0:T(8,128)(2,1)S(1)}, u32[]{:S(2)}, u32[]{:S(2)}) collective-permute-start(bf16[528,128]{1,0:T(8,128)(2,1)S(1)} %get-tuple-element.55), channel_id=1, source_target_pairs={{0,4},{1,5},{2,6},{3,7},{4,0},{5,1},{6,2},{7,3},{8,12},{9,13},{10,... | collective-permute-start | bytes 405512 | tf_op jit(solution)/shard_map/ppermute | solution.py:41
  66.7 3.4 %shard_map.73 = (f32[512,1024]{1,0:T(8,128)S(1)}, f32[512,1024]{1,0:T(8,128)S(1)}) custom-call(s32[5]{0:T(128)S(1)} %stack.23.ids, f32[7]{0:T(128)S(1)} %copy-done.1, f32[5,4,512,128]{3,2,1,0:T(8,128)S(1)} %get-tuple-element.57.e_low, f32[4,8,128]{2,1,0:T(8,128)S(1)} %get-tuple-element.58.rates, s32[4,1,128]{2,1,0:T(1,128)S(1)} %get-tuple-element.45.pos, ...), custom_call_target="tpu_custom_call" | custom-call | flops 1073741824 | bytes 11552768 | tf_op jit(solution)/shard_map/pallas_call | solution.py:72
  70.6 2.4 %shard_map.74 = (f32[128,1024]{1,0:T(8,128)S(1)}, bf16[128,1024]{1,0:T(8,128)(2,1)S(1)}, bf16[128,1024]{1,0:T(8,128)(2,1)S(1)}, bf16[128,1024]{1,0:T(8,128)(2,1)...) custom-call(s32[5]{0:T(128)S(1)} %stack.23.ids, ...), custom_call_target="tpu_custom_call" | custom-call | flops 1073741824 | bytes 9736192 | tf_op jit(solution)/shard_map/pallas_call | solution.py:72
  73.0 3.2 %collective-permute-start.21 = (bf16[528,512]{1,0:T(8,128)(2,1)S(1)}, bf16[528,512]{1,0:T(8,128)(2,1)S(1)}, u32[]{:S(2)}, u32[]{:S(2)}) collective-permute-start(bf16[528,512]{1,0:T(8,128)(2,1)S(1)} %get-tuple-element.67), channel_id=1, source_target_pairs={{0,1},{1,0},{2,3},{3,2},{4,5},{5,4},{6,7},{7,6},{8,9},{9,8},{10,11... | collective-permute-start | bytes 1622024 | tf_op jit(solution)/shard_map/ppermute | solution.py:45
  78.8 1.5 %collective-permute-start.24 = (bf16[144,512]{1,0:T(8,128)(2,1)S(1)}, bf16[144,512]{1,0:T(8,128)(2,1)S(1)}, u32[]{:S(2)}, u32[]{:S(2)}) collective-permute-start(bf16[144,512]{1,0:T(8,128)(2,1)S(1)} %get-tuple-element.68.m1), channel_id=1, source_target_pairs={{0,48},{8,56},{16,0},{24,8},{32,16},{40,24},{48,32},{56,40},{64,11... | collective-permute-start | bytes 442376 | tf_op jit(solution)/shard_map/ppermute | solution.py:35
  80.4 2.5 %collective-permute-start.25 = (bf16[144,512]{1,0:T(8,128)(2,1)S(1)}, bf16[144,512]{1,0:T(8,128)(2,1)S(1)}, u32[]{:S(2)}, u32[]{:S(2)}) collective-permute-start(bf16[144,512]{1,0:T(8,128)(2,1)S(1)} %get-tuple-element.69.m2), channel_id=1, source_target_pairs={{0,32},{8,40},{16,48},{24,56},{32,0},{40,8},{48,16},{56,24},{64,96... | collective-permute-start | bytes 442376 | tf_op jit(solution)/shard_map/ppermute | solution.py:35
  86.0 6.3 %collective-permute-done.20.g3 = bf16[128,1024]{1,0:T(8,128)(2,1)S(1)} collective-permute-done((bf16[128,1024]{1,0:T(8,128)(2,1)S(1)}, bf16[128,1024]{1,0:T(8,128)(2,1)S(1)}, u32[]{:S(2)}, u32[]{:S(2)}) %collective-permute-start.20) | collective-permute-done | bytes 262176 | tf_op jit(solution)/shard_map/ppermute | solution.py:31
  93.8 3.3 %collective-permute-start.23 = (bf16[128,512]{1,0:T(8,128)(2,1)S(1)}, bf16[128,512]{1,0:T(8,128)(2,1)S(1)}, u32[]{:S(2)}, u32[]{:S(2)}) collective-permute-start(bf16[128,512]{1,0:T(8,128)(2,1)S(1)} %get-tuple-element.73), channel_id=1, source_target_pairs={{1,8},{3,10},{5,12},{7,14},{8,1},{10,3},{12,5},{14,7},{17,24},{19,... | collective-permute-start | bytes 393224 | tf_op jit(solution)/shard_map/ppermute | solution.py:55
  97.1 1.7 %collective-permute-done.22.near = bf16[128,512]{1,0:T(8,128)(2,1)S(1)} collective-permute-done((bf16[128,512]{1,0:T(8,128)(2,1)S(1)}, bf16[128,512]{1,0:T(8,128)(2,1)S(1)}, u32[]{:S(2)}, u32[]{:S(2)}) %collective-permute-start.22) | collective-permute-done | bytes 131104 | tf_op jit(solution)/shard_map/ppermute | solution.py:55
  98.8 1.4 %collective-permute-done.23.far = bf16[128,512]{1,0:T(8,128)(2,1)S(1)} collective-permute-done((bf16[128,512]{1,0:T(8,128)(2,1)S(1)}, bf16[128,512]{1,0:T(8,128)(2,1)S(1)}, u32[]{:S(2)}, u32[]{:S(2)}) %collective-permute-start.23) | collective-permute-done | bytes 131104 | tf_op jit(solution)/shard_map/ppermute | solution.py:55
  (51 shorter events, 22.9 us)
Async XLA Ops:
  2.4 12.9 %collective-permute-start.8 = (bf16[144,512]{1,0:T(8,128)(2,1)S(1)}, bf16[144,512]{1,0:T(8,128)(2,1)S(1)}, u32[]{:S(2)}, u32[]{:S(2)}) collective-permute-start(bf16[144,512]{1,0:T(8,128)(2,1)S(1)} %fusion.own), channel_id=1, source_target_pairs={{1,8},{3,10},{5,12},{7,14},{8,1},{10,3},{12,5},{14,7},{17,24},{19,... | collective-permute-start | bytes 442376 | tf_op jit(solution)/shard_map/ppermute | solution.py:55
  7.3 8.0 %collective-permute-start.7 = (bf16[128,512]{1,0:T(8,128)(2,1)}, bf16[128,512]{1,0:T(8,128)(2,1)S(1)}, u32[]{:S(2)}, u32[]{:S(2)}) collective-permute-start(bf16[128,512]{1,0:T(8,128)(2,1)} %param.4), channel_id=1, source_target_pairs={{0,8},{1,0},{2,10},{3,2},{4,12},{5,4},{6,14},{7,6},{8,9},{9,1},{10... | collective-permute-start | bytes 393224 | tf_op jit(solution)/shard_map/ppermute | solution.py:55
  7.4 13.6 %collective-permute-start = (bf16[128,512]{1,0:T(8,128)(2,1)}, bf16[128,512]{1,0:T(8,128)(2,1)S(1)}, u32[]{:S(2)}, u32[]{:S(2)}) collective-permute-start(bf16[128,512]{1,0:T(8,128)(2,1)} %a.1), channel_id=1, source_target_pairs={{0,16},{8,24},{16,32},{24,40},{32,48},{40,56},{48,0},{56,8},{64,80... | collective-permute-start | bytes 393224 | tf_op jit(solution)/shard_map/ppermute | solution.py:35
  10.5 13.0 %collective-permute-start.2 = (bf16[128,512]{1,0:T(8,128)(2,1)}, bf16[128,512]{1,0:T(8,128)(2,1)S(1)}, u32[]{:S(2)}, u32[]{:S(2)}) collective-permute-start(bf16[128,512]{1,0:T(8,128)(2,1)} %a.1), channel_id=1, source_target_pairs={{0,48},{8,56},{16,0},{24,8},{32,16},{40,24},{48,32},{56,40},{64,11... | collective-permute-start | bytes 393224 | tf_op jit(solution)/shard_map/ppermute | solution.py:35
  14.3 9.3 %collective-permute-start.3 = (bf16[128,512]{1,0:T(8,128)(2,1)S(1)}, bf16[128,512]{1,0:T(8,128)(2,1)S(1)}, u32[]{:S(2)}, u32[]{:S(2)}) collective-permute-start(bf16[128,512]{1,0:T(8,128)(2,1)S(1)} %shard_map.67.p0), channel_id=1, source_target_pairs={{0,1},{1,0},{2,3},{3,2},{4,5},{5,4},{6,7},{7,6},{8,9},{9,8},{10,11... | collective-permute-start | bytes 393224 | tf_op jit(solution)/shard_map/ppermute | solution.py:45
  15.9 18.8 %collective-permute-start.9 = (bf16[144,1024]{1,0:T(8,128)(2,1)S(1)}, bf16[144,1024]{1,0:T(8,128)(2,1)S(1)}, u32[]{:S(2)}, u32[]{:S(2)}) collective-permute-start(bf16[144,1024]{1,0:T(8,128)(2,1)S(1)} %shard_map.68.q0), channel_id=1, source_target_pairs={{0,64},{8,72},{16,80},{24,88},{32,96},{40,104},{48,112},{56,120},{... | collective-permute-start | bytes 884744 | tf_op jit(solution)/shard_map/ppermute | solution.py:31
  17.2 17.5 %collective-permute-start.10 = (bf16[144,1024]{1,0:T(8,128)(2,1)S(1)}, bf16[144,1024]{1,0:T(8,128)(2,1)S(1)}, u32[]{:S(2)}, u32[]{:S(2)}) collective-permute-start(bf16[144,1024]{1,0:T(8,128)(2,1)S(1)} %shard_map.68.q0), channel_id=1, source_target_pairs={{0,128},{8,136},{16,144},{24,152},{32,160},{40,168},{48,176},{56,1... | collective-permute-start | bytes 884744 | tf_op jit(solution)/shard_map/ppermute | solution.py:31
  21.0 13.6 %collective-permute-start.11 = (bf16[144,1024]{1,0:T(8,128)(2,1)S(1)}, bf16[144,1024]{1,0:T(8,128)(2,1)S(1)}, u32[]{:S(2)}, u32[]{:S(2)}) collective-permute-start(bf16[144,1024]{1,0:T(8,128)(2,1)S(1)} %shard_map.68.q0), channel_id=1, source_target_pairs={{0,192},{8,200},{16,208},{24,216},{32,224},{40,232},{48,240},{56,2... | collective-permute-start | bytes 884744 | tf_op jit(solution)/shard_map/ppermute | solution.py:31
  23.5 7.6 %collective-permute-start.1 = (bf16[128,512]{1,0:T(8,128)(2,1)S(1)}, bf16[128,512]{1,0:T(8,128)(2,1)S(1)}, u32[]{:S(2)}, u32[]{:S(2)}) collective-permute-start(bf16[128,512]{1,0:T(8,128)(2,1)S(1)} %collective-permute-done.p1), channel_id=1, source_target_pairs={{0,16},{8,24},{16,32},{24,40},{32,48},{40,56},{48,0},{56,8},{64,80... | collective-permute-start | bytes 393224 | tf_op jit(solution)/shard_map/ppermute | solution.py:35
  23.5 9.8 %collective-permute-start.4 = (bf16[128,512]{1,0:T(8,128)(2,1)S(1)}, bf16[128,512]{1,0:T(8,128)(2,1)S(1)}, u32[]{:S(2)}, u32[]{:S(2)}) collective-permute-start(bf16[128,512]{1,0:T(8,128)(2,1)S(1)} %collective-permute-done.p1), channel_id=1, source_target_pairs={{0,1},{1,0},{2,3},{3,2},{4,5},{5,4},{6,7},{7,6},{8,9},{9,8},{10,11... | collective-permute-start | bytes 393224 | tf_op jit(solution)/shard_map/ppermute | solution.py:45
  36.3 9.2 %collective-permute-start.12 = (f32[512,128]{1,0:T(8,128)S(1)}, f32[512,128]{1,0:T(8,128)S(1)}, u32[]{:S(2)}, u32[]{:S(2)}) collective-permute-start(f32[512,128]{1,0:T(8,128)S(1)} %get-tuple-element.42), channel_id=1, source_target_pairs={{0,2},{1,3},{2,4},{3,5},{4,6},{5,7},{6,0},{7,1},{8,10},{9,11},{10,... | collective-permute-start | bytes 786440 | tf_op jit(solution)/shard_map/ppermute | solution.py:41
  37.7 14.5 %collective-permute-start.13 = (f32[512,128]{1,0:T(8,128)S(1)}, f32[512,128]{1,0:T(8,128)S(1)}, u32[]{:S(2)}, u32[]{:S(2)}) collective-permute-start(f32[512,128]{1,0:T(8,128)S(1)} %get-tuple-element.43), channel_id=1, source_target_pairs={{0,4},{1,5},{2,6},{3,7},{4,0},{5,1},{6,2},{7,3},{8,12},{9,13},{10,... | collective-permute-start | bytes 786440 | tf_op jit(solution)/shard_map/ppermute | solution.py:41
  40.3 11.9 %collective-permute-start.14 = (f32[512,128]{1,0:T(8,128)S(1)}, f32[512,128]{1,0:T(8,128)S(1)}, u32[]{:S(2)}, u32[]{:S(2)}) collective-permute-start(f32[512,128]{1,0:T(8,128)S(1)} %get-tuple-element.44), channel_id=1, source_target_pairs={{0,6},{1,7},{2,0},{3,1},{4,2},{5,3},{6,4},{7,5},{8,14},{9,15},{10,... | collective-permute-start | bytes 786440 | tf_op jit(solution)/shard_map/ppermute | solution.py:41
  62.6 7.5 %collective-permute-start.15 = (bf16[528,128]{1,0:T(8,128)(2,1)S(1)}, bf16[528,128]{1,0:T(8,128)(2,1)S(1)}, u32[]{:S(2)}, u32[]{:S(2)}) collective-permute-start(bf16[528,128]{1,0:T(8,128)(2,1)S(1)} %get-tuple-element.54), channel_id=1, source_target_pairs={{0,2},{1,3},{2,4},{3,5},{4,6},{5,7},{6,0},{7,1},{8,10},{9,11},{10,... | collective-permute-start | bytes 405512 | tf_op jit(solution)/shard_map/ppermute | solution.py:41
  63.4 7.2 %collective-permute-start.16 = (bf16[528,128]{1,0:T(8,128)(2,1)S(1)}, bf16[528,128]{1,0:T(8,128)(2,1)S(1)}, u32[]{:S(2)}, u32[]{:S(2)}) collective-permute-start(bf16[528,128]{1,0:T(8,128)(2,1)S(1)} %get-tuple-element.55), channel_id=1, source_target_pairs={{0,4},{1,5},{2,6},{3,7},{4,0},{5,1},{6,2},{7,3},{8,12},{9,13},{10,... | collective-permute-start | bytes 405512 | tf_op jit(solution)/shard_map/ppermute | solution.py:41
  73.0 5.2 %collective-permute-start.21 = (bf16[528,512]{1,0:T(8,128)(2,1)S(1)}, bf16[528,512]{1,0:T(8,128)(2,1)S(1)}, u32[]{:S(2)}, u32[]{:S(2)}) collective-permute-start(bf16[528,512]{1,0:T(8,128)(2,1)S(1)} %get-tuple-element.67), channel_id=1, source_target_pairs={{0,1},{1,0},{2,3},{3,2},{4,5},{5,4},{6,7},{7,6},{8,9},{9,8},{10,11... | collective-permute-start | bytes 1622024 | tf_op jit(solution)/shard_map/ppermute | solution.py:45
  76.2 7.9 %collective-permute-start.18 = (bf16[128,1024]{1,0:T(8,128)(2,1)S(1)}, bf16[128,1024]{1,0:T(8,128)(2,1)S(1)}, u32[]{:S(2)}, u32[]{:S(2)}) collective-permute-start(bf16[128,1024]{1,0:T(8,128)(2,1)S(1)} %get-tuple-element.62), channel_id=1, source_target_pairs={{0,192},{8,200},{16,208},{24,216},{32,224},{40,232},{48,240},{56,2... | collective-permute-start | bytes 786440 | tf_op jit(solution)/shard_map/ppermute | solution.py:31
  76.9 9.1 %collective-permute-start.19 = (bf16[128,1024]{1,0:T(8,128)(2,1)S(1)}, bf16[128,1024]{1,0:T(8,128)(2,1)S(1)}, u32[]{:S(2)}, u32[]{:S(2)}) collective-permute-start(bf16[128,1024]{1,0:T(8,128)(2,1)S(1)} %get-tuple-element.63), channel_id=1, source_target_pairs={{0,128},{8,136},{16,144},{24,152},{32,160},{40,168},{48,176},{56,1... | collective-permute-start | bytes 786440 | tf_op jit(solution)/shard_map/ppermute | solution.py:31
  78.0 14.2 %collective-permute-start.20 = (bf16[128,1024]{1,0:T(8,128)(2,1)S(1)}, bf16[128,1024]{1,0:T(8,128)(2,1)S(1)}, u32[]{:S(2)}, u32[]{:S(2)}) collective-permute-start(bf16[128,1024]{1,0:T(8,128)(2,1)S(1)} %get-tuple-element.64), channel_id=1, source_target_pairs={{0,64},{8,72},{16,80},{24,88},{32,96},{40,104},{48,112},{56,120},{... | collective-permute-start | bytes 786440 | tf_op jit(solution)/shard_map/ppermute | solution.py:31
  78.8 21.4 %collective-permute-start.24 = (bf16[144,512]{1,0:T(8,128)(2,1)S(1)}, bf16[144,512]{1,0:T(8,128)(2,1)S(1)}, u32[]{:S(2)}, u32[]{:S(2)}) collective-permute-start(bf16[144,512]{1,0:T(8,128)(2,1)S(1)} %get-tuple-element.68.m1), channel_id=1, source_target_pairs={{0,48},{8,56},{16,0},{24,8},{32,16},{40,24},{48,32},{56,40},{64,11... | collective-permute-start | bytes 442376 | tf_op jit(solution)/shard_map/ppermute | solution.py:35
  80.4 19.8 %collective-permute-start.25 = (bf16[144,512]{1,0:T(8,128)(2,1)S(1)}, bf16[144,512]{1,0:T(8,128)(2,1)S(1)}, u32[]{:S(2)}, u32[]{:S(2)}) collective-permute-start(bf16[144,512]{1,0:T(8,128)(2,1)S(1)} %get-tuple-element.69.m2), channel_id=1, source_target_pairs={{0,32},{8,40},{16,48},{24,56},{32,0},{40,8},{48,16},{56,24},{64,96... | collective-permute-start | bytes 442376 | tf_op jit(solution)/shard_map/ppermute | solution.py:35
  84.1 16.1 %collective-permute-start.26 = (bf16[144,512]{1,0:T(8,128)(2,1)S(1)}, bf16[144,512]{1,0:T(8,128)(2,1)S(1)}, u32[]{:S(2)}, u32[]{:S(2)}) collective-permute-start(bf16[144,512]{1,0:T(8,128)(2,1)S(1)} %get-tuple-element.70.m3), channel_id=1, source_target_pairs={{0,16},{8,24},{16,32},{24,40},{32,48},{40,56},{48,0},{56,8},{64,80... | collective-permute-start | bytes 442376 | tf_op jit(solution)/shard_map/ppermute | solution.py:35
  93.0 5.8 %collective-permute-start.22 = (bf16[128,512]{1,0:T(8,128)(2,1)S(1)}, bf16[128,512]{1,0:T(8,128)(2,1)S(1)}, u32[]{:S(2)}, u32[]{:S(2)}) collective-permute-start(bf16[128,512]{1,0:T(8,128)(2,1)S(1)} %get-tuple-element.72), channel_id=1, source_target_pairs={{0,1},{1,9},{2,3},{3,11},{4,5},{5,13},{6,7},{7,15},{8,0},{9,8},{10... | collective-permute-start | bytes 393224 | tf_op jit(solution)/shard_map/ppermute | solution.py:55
  93.8 6.3 %collective-permute-start.23 = (bf16[128,512]{1,0:T(8,128)(2,1)S(1)}, bf16[128,512]{1,0:T(8,128)(2,1)S(1)}, u32[]{:S(2)}, u32[]{:S(2)}) collective-permute-start(bf16[128,512]{1,0:T(8,128)(2,1)S(1)} %get-tuple-element.73), channel_id=1, source_target_pairs={{1,8},{3,10},{5,12},{7,14},{8,1},{10,3},{12,5},{14,7},{17,24},{19,... | collective-permute-start | bytes 393224 | tf_op jit(solution)/shard_map/ppermute | solution.py:55
  (5 other events, 50.6 us)

commit v10 on v9

--- a/solution.py
+++ b/solution.py
@@ -274,10 +274,10 @@
     first = lax.broadcasted_iota(jnp.int32, (4 * n, PAIR), 1) < SMALLEST
 
     def fill(out, fn):
-        out[:, :PAIR] = jnp.where(first, fn(0, 0, PAIR), fn(1, 0, PAIR))
+        out[:, :PAIR] = jnp.where(first, fn(0, 0, PAIR), fn(1, 0, PAIR)).astype(bf16)
         for k in range(2, LOW):
             begin, end = SPANS[k]
-            out[:, begin:end] = fn(k, begin, end)
+            out[:, begin:end] = fn(k, begin, end).astype(bf16)
 
     fill(gq, lambda k, a, b: dot(tails[k], p[:, a:b], 0, 0))
     fill(gp, lambda k, a, b: dot(tails[k], q[:, a:b], 1, 0))
@@ -295,7 +295,7 @@
         tail[:, pl.ds(pl.multiple_of(j * n, n), n)] = ref[: 4 * n]
         loss += get_terms(ref, 4 * n, n)
     row[...] = jnp.broadcast_to(loss, row.shape)
-    gq[...] = dot(tail[...], p[...], 0, 0) + gq_low[...]
+    gq[...] = dot(tail[...], p[...], 0, 0) + gq_low[...].astype(f32)
     for s, out in enumerate((gq0, gq1, gq2, gq3)):
         j = (ids[X] + 4 - s) & 3
         out[...] = gq[pl.ds(pl.multiple_of(j * n, n), n), :].astype(out.dtype)
@@ -305,7 +305,7 @@
     put_terms(message, 4 * n, loss)
     for c in (0, 1):
         lanes = slice(c * width, c * width + width)
-        gp = dot(tail[...], q[:, lanes], 1, 0) + gp_low[:, lanes]
+        gp = dot(tail[...], q[:, lanes], 1, 0) + gp_low[:, lanes].astype(f32)
 
         @pl.when(ids[CORE] == c)
         def _():
@@ -426,7 +426,7 @@
     tails = [tails[0]] + [shift_y(tails[t], t) for t in (1, 2, 3)]
     gq_low, gp_low = call(
         low_grad_kernel, [ids, level_weight], [e_low, rates, pos, p, q],
-        [shape(4 * n, wide, f32)] * 2,
+        [shape(4 * n, wide, bf16)] * 2,
         scratch=[pltpu.VMEM((LOW, 4 * n, 4 * n), bf16)],
         flops=4 * tile * wide, grant=12,
     )

time: 102 us -> 102 us (level)
  transfers between devices with their start and end apart: 27 -> 27, of which waited for: 12 -> 11; matrix products, arithmetic and copies ran while one was open for 0% -> 0% of each run, Pallas kernels for 9% -> 9%
where the time goes in v10:
time: 102 us
  starting transfers between devices  45.3 us (44%)
  waiting for transfers between devices  26.7 us (26%)
  Pallas kernels  16.9 us (17%)
  blocking collectives  8.36 us (8%)
  other arithmetic  1.71 us (2%)
  local copies, waits for them, and re-layouts  1.65 us (2%)
    pallas_call x11, Pallas kernels, call(): pl.pallas_call(body, out_shape=outs, in_specs=[scalar] * len(smem) + [vme...  16.9 us
    ppermute x6, starting transfers between devices, shift_zl(): lax.ppermute(a, 'batch', [(b, b // 8 * 8 + (b + 2 * s) % 8) for b in rang...  10.3 us
    ppermute x6, starting transfers between devices, shift_y(): lax.ppermute(a, 'feat', [(f, (f + 2 * s) % FEAT) for f in range(FEAT)])  9.18 us
    ppermute x4, starting transfers between devices, move_square(): return lax.ppermute(a, BOTH, pairs)  9.14 us
    ppermute x5, starting transfers between devices, swap_core(): return lax.ppermute(a, 'feat', [(f, f ^ 1) for f in range(FEAT)])  8.49 us
    ppermute x6, waiting for transfers between devices, shift_x(): lax.ppermute(a, 'batch', [(b, (b + 8 * s) % BATCH) for b in range(BATCH)])  8.37 us
    all_to_all x1, blocking collectives, per_device(): stats = lax.all_to_all(message, 'batch', 0, 0, axis_index_groups=XZH_GROUPS)  8.36 us
    ppermute x6, starting transfers between devices, shift_x(): lax.ppermute(a, 'batch', [(b, (b + 8 * s) % BATCH) for b in range(BATCH)])  8.2 us
  transfers between devices with their start and end apart: 27, of which 11 were waited for; matrix products, arithmetic and copies ran while one was open for 0% of the time, Pallas kernels for 9%

profile of v10, /device:TPU:1, one launch (start us, length us, event | category | flops | bytes accessed | tf_op | source)
XLA Modules:
  0.0 101.5 jit_solution(18410149345569613031)
XLA Ops:
  2.4 4.9 %collective-permute-start.8 = (bf16[144,512]{1,0:T(8,128)(2,1)S(1)}, bf16[144,512]{1,0:T(8,128)(2,1)S(1)}, u32[]{:S(2)}, u32[]{:S(2)}) collective-permute-start(bf16[144,512]{1,0:T(8,128)(2,1)S(1)} %fusion.own), channel_id=1, source_target_pairs={{1,8},{3,10},{5,12},{7,14},{8,1},{10,3},{12,5},{14,7},{17,24},{19,... | collective-permute-start | bytes 442376 | tf_op jit(solution)/shard_map/ppermute | solution.py:55
  7.4 3.1 %collective-permute-start = (bf16[128,512]{1,0:T(8,128)(2,1)}, bf16[128,512]{1,0:T(8,128)(2,1)S(1)}, u32[]{:S(2)}, u32[]{:S(2)}) collective-permute-start(bf16[128,512]{1,0:T(8,128)(2,1)} %a.1), channel_id=1, source_target_pairs={{0,16},{8,24},{16,32},{24,40},{32,48},{40,56},{48,0},{56,8},{64,80... | collective-permute-start | bytes 393224 | tf_op jit(solution)/shard_map/ppermute | solution.py:35
  10.5 2.2 %collective-permute-start.2 = (bf16[128,512]{1,0:T(8,128)(2,1)}, bf16[128,512]{1,0:T(8,128)(2,1)S(1)}, u32[]{:S(2)}, u32[]{:S(2)}) collective-permute-start(bf16[128,512]{1,0:T(8,128)(2,1)} %a.1), channel_id=1, source_target_pairs={{0,48},{8,56},{16,0},{24,8},{32,16},{40,24},{48,32},{56,40},{64,11... | collective-permute-start | bytes 393224 | tf_op jit(solution)/shard_map/ppermute | solution.py:35
  17.2 2.5 %collective-permute-start.10 = (bf16[144,1024]{1,0:T(8,128)(2,1)S(1)}, bf16[144,1024]{1,0:T(8,128)(2,1)S(1)}, u32[]{:S(2)}, u32[]{:S(2)}) collective-permute-start(bf16[144,1024]{1,0:T(8,128)(2,1)S(1)} %shard_map.68.q0), channel_id=1, source_target_pairs={{0,128},{8,136},{16,144},{24,152},{32,160},{40,168},{48,176},{56,1... | collective-permute-start | bytes 884744 | tf_op jit(solution)/shard_map/ppermute | solution.py:31
  19.6 1.4 %collective-permute-done.p1 = bf16[128,512]{1,0:T(8,128)(2,1)S(1)} collective-permute-done((bf16[128,512]{1,0:T(8,128)(2,1)}, bf16[128,512]{1,0:T(8,128)(2,1)S(1)}, u32[]{:S(2)}, u32[]{:S(2)}) %collective-permute-start) | collective-permute-done | bytes 131104 | tf_op jit(solution)/shard_map/ppermute | solution.py:35
  21.0 2.5 %collective-permute-start.11 = (bf16[144,1024]{1,0:T(8,128)(2,1)S(1)}, bf16[144,1024]{1,0:T(8,128)(2,1)S(1)}, u32[]{:S(2)}, u32[]{:S(2)}) collective-permute-start(bf16[144,1024]{1,0:T(8,128)(2,1)S(1)} %shard_map.68.q0), channel_id=1, source_target_pairs={{0,192},{8,200},{16,208},{24,216},{32,224},{40,232},{48,240},{56,2... | collective-permute-start | bytes 884744 | tf_op jit(solution)/shard_map/ppermute | solution.py:31
  23.5 2.0 %collective-permute-start.4 = (bf16[128,512]{1,0:T(8,128)(2,1)S(1)}, bf16[128,512]{1,0:T(8,128)(2,1)S(1)}, u32[]{:S(2)}, u32[]{:S(2)}) collective-permute-start(bf16[128,512]{1,0:T(8,128)(2,1)S(1)} %collective-permute-done.p1), channel_id=1, source_target_pairs={{0,1},{1,0},{2,3},{3,2},{4,5},{5,4},{6,7},{7,6},{8,9},{9,8},{10,11... | collective-permute-start | bytes 393224 | tf_op jit(solution)/shard_map/ppermute | solution.py:45
  25.5 5.6 %collective-permute-done.1.p2 = bf16[128,512]{1,0:T(8,128)(2,1)S(1)} collective-permute-done((bf16[128,512]{1,0:T(8,128)(2,1)S(1)}, bf16[128,512]{1,0:T(8,128)(2,1)S(1)}, u32[]{:S(2)}, u32[]{:S(2)}) %collective-permute-start.1) | collective-permute-done | bytes 131104 | tf_op jit(solution)/shard_map/ppermute | solution.py:35
  31.1 2.3 %collective-permute-start.6 = (bf16[128,512]{1,0:T(8,128)(2,1)S(1)}, bf16[128,512]{1,0:T(8,128)(2,1)S(1)}, u32[]{:S(2)}, u32[]{:S(2)}) collective-permute-start(bf16[128,512]{1,0:T(8,128)(2,1)S(1)} %collective-permute-done.2.p3), channel_id=1, source_target_pairs={{0,1},{1,0},{2,3},{3,2},{4,5},{5,4},{6,7},{7,6},{8,9},{9,8},{10,11... | collective-permute-start | bytes 393224 | tf_op jit(solution)/shard_map/ppermute | solution.py:45
  34.7 1.6 %shard_map.69 = (f32[512,128]{1,0:T(8,128)S(1)}, f32[512,128]{1,0:T(8,128)S(1)}, f32[512,128]{1,0:T(8,128)S(1)}, f32[512,128]{1,0:T(8,128)S(1)}, bf16[512,1024]{...) custom-call(s32[5]{0:T(128)S(1)} %stack.23.ids, bf16[128,512]{1,0:T(8,128)(2,1)S(1)} %shard_map.67.p0, ...), custom_call_target="tpu_custom_call" | custom-call | flops 536870912 | bytes 5376000 | tf_op jit(solution)/shard_map/pallas_call | solution.py:72
  37.7 2.6 %collective-permute-start.13 = (f32[512,128]{1,0:T(8,128)S(1)}, f32[512,128]{1,0:T(8,128)S(1)}, u32[]{:S(2)}, u32[]{:S(2)}) collective-permute-start(f32[512,128]{1,0:T(8,128)S(1)} %get-tuple-element.43), channel_id=1, source_target_pairs={{0,4},{1,5},{2,6},{3,7},{4,0},{5,1},{6,2},{7,3},{8,12},{9,13},{10,... | collective-permute-start | bytes 786440 | tf_op jit(solution)/shard_map/ppermute | solution.py:41
  42.1 3.7 %shard_map.70 = (f32[5,4,512,128]{3,2,1,0:T(8,128)S(1)}, f32[4,8,128]{2,1,0:T(8,128)S(1)}, f32[4,8,128]{2,1,0:T(8,128)S(1)}) custom-call(s32[5]{0:T(128)S(1)} %stack.23.ids, f32[7]{0:T(128)S(1)} %copy-done.1, bf16[512,1024]{1,0:T(8,128)(2,1)S(1)} %get-tuple-element.46.p, bf16[4,128,1024]{2,1,0:T(8,128)(2,1)S(1)} %get-tuple-element.47.q_all, ...), custom_call_target="tpu_custom_call" | custom-call | flops 536870912 | bytes 7374848 | tf_op jit(solution)/shard_map/pallas_call | solution.py:72
  45.8 6.5 %collective-permute-done.13.s2 = f32[512,128]{1,0:T(8,128)S(1)} collective-permute-done((f32[512,128]{1,0:T(8,128)S(1)}, f32[512,128]{1,0:T(8,128)S(1)}, u32[]{:S(2)}, u32[]{:S(2)}) %collective-permute-start.13) | collective-permute-done | bytes 262176 | tf_op jit(solution)/shard_map/ppermute | solution.py:41
  53.3 8.4 %all_to_all.5.stats = f32[8,40,128]{2,1,0:T(8,128)S(1)} all-to-all(f32[8,40,128]{2,1,0:T(8,128)S(1)} %get-tuple-element.49), channel_id=1, replica_groups={{0,8,64,72,128,136,192,200},{16,24,80,88,144,152,208,216},{32,40,96,104..., dimensions={0} | all-to-all | bytes 327680 | tf_op jit(solution)/shard_map/all_to_all | solution.py:421
  63.4 2.8 %collective-permute-start.16 = (bf16[528,128]{1,0:T(8,128)(2,1)S(1)}, bf16[528,128]{1,0:T(8,128)(2,1)S(1)}, u32[]{:S(2)}, u32[]{:S(2)}) collective-permute-start(bf16[528,128]{1,0:T(8,128)(2,1)S(1)} %get-tuple-element.55), channel_id=1, source_target_pairs={{0,4},{1,5},{2,6},{3,7},{4,0},{5,1},{6,2},{7,3},{8,12},{9,13},{10,... | collective-permute-start | bytes 405512 | tf_op jit(solution)/shard_map/ppermute | solution.py:41
  66.7 3.4 %shard_map.73 = (bf16[512,1024]{1,0:T(8,128)(2,1)S(1)}, bf16[512,1024]{1,0:T(8,128)(2,1)S(1)}) custom-call(s32[5]{0:T(128)S(1)} %stack.23.ids, f32[7]{0:T(128)S(1)} %copy-done.2, f32[5,4,512,128]{3,2,1,0:T(8,128)S(1)} %get-tuple-element.57.e_low, f32[4,8,128]{2,1,0:T(8,128)S(1)} %get-tuple-element.58.rates, s32[4,1,128]{2,1,0:T(1,128)S(1)} %get-tuple-element.45.pos, ...), custom_call_target="tpu_custom_call" | custom-call | flops 1073741824 | bytes 9455616 | tf_op jit(solution)/shard_map/pallas_call | solution.py:72
  70.6 2.4 %shard_map.74 = (f32[128,1024]{1,0:T(8,128)S(1)}, bf16[128,1024]{1,0:T(8,128)(2,1)S(1)}, bf16[128,1024]{1,0:T(8,128)(2,1)S(1)}, bf16[128,1024]{1,0:T(8,128)(2,1)...) custom-call(s32[5]{0:T(128)S(1)} %stack.23.ids, ...), custom_call_target="tpu_custom_call" | custom-call | flops 1073741824 | bytes 7639040 | tf_op jit(solution)/shard_map/pallas_call | solution.py:72
  73.0 3.2 %collective-permute-start.21 = (bf16[528,512]{1,0:T(8,128)(2,1)S(1)}, bf16[528,512]{1,0:T(8,128)(2,1)S(1)}, u32[]{:S(2)}, u32[]{:S(2)}) collective-permute-start(bf16[528,512]{1,0:T(8,128)(2,1)S(1)} %get-tuple-element.67), channel_id=1, source_target_pairs={{0,1},{1,0},{2,3},{3,2},{4,5},{5,4},{6,7},{7,6},{8,9},{9,8},{10,11... | collective-permute-start | bytes 1622024 | tf_op jit(solution)/shard_map/ppermute | solution.py:45
  78.8 1.5 %collective-permute-start.24 = (bf16[144,512]{1,0:T(8,128)(2,1)S(1)}, bf16[144,512]{1,0:T(8,128)(2,1)S(1)}, u32[]{:S(2)}, u32[]{:S(2)}) collective-permute-start(bf16[144,512]{1,0:T(8,128)(2,1)S(1)} %get-tuple-element.68.m1), channel_id=1, source_target_pairs={{0,48},{8,56},{16,0},{24,8},{32,16},{40,24},{48,32},{56,40},{64,11... | collective-permute-start | bytes 442376 | tf_op jit(solution)/shard_map/ppermute | solution.py:35
  80.4 2.5 %collective-permute-start.25 = (bf16[144,512]{1,0:T(8,128)(2,1)S(1)}, bf16[144,512]{1,0:T(8,128)(2,1)S(1)}, u32[]{:S(2)}, u32[]{:S(2)}) collective-permute-start(bf16[144,512]{1,0:T(8,128)(2,1)S(1)} %get-tuple-element.69.m2), channel_id=1, source_target_pairs={{0,32},{8,40},{16,48},{24,56},{32,0},{40,8},{48,16},{56,24},{64,96... | collective-permute-start | bytes 442376 | tf_op jit(solution)/shard_map/ppermute | solution.py:35
  86.0 6.3 %collective-permute-done.20.g3 = bf16[128,1024]{1,0:T(8,128)(2,1)S(1)} collective-permute-done((bf16[128,1024]{1,0:T(8,128)(2,1)S(1)}, bf16[128,1024]{1,0:T(8,128)(2,1)S(1)}, u32[]{:S(2)}, u32[]{:S(2)}) %collective-permute-start.20) | collective-permute-done | bytes 262176 | tf_op jit(solution)/shard_map/ppermute | solution.py:31
  93.8 3.3 %collective-permute-start.23 = (bf16[128,512]{1,0:T(8,128)(2,1)S(1)}, bf16[128,512]{1,0:T(8,128)(2,1)S(1)}, u32[]{:S(2)}, u32[]{:S(2)}) collective-permute-start(bf16[128,512]{1,0:T(8,128)(2,1)S(1)} %get-tuple-element.73), channel_id=1, source_target_pairs={{1,8},{3,10},{5,12},{7,14},{8,1},{10,3},{12,5},{14,7},{17,24},{19,... | collective-permute-start | bytes 393224 | tf_op jit(solution)/shard_map/ppermute | solution.py:55
  97.1 1.7 %collective-permute-done.22.near = bf16[128,512]{1,0:T(8,128)(2,1)S(1)} collective-permute-done((bf16[128,512]{1,0:T(8,128)(2,1)S(1)}, bf16[128,512]{1,0:T(8,128)(2,1)S(1)}, u32[]{:S(2)}, u32[]{:S(2)}) %collective-permute-start.22) | collective-permute-done | bytes 131104 | tf_op jit(solution)/shard_map/ppermute | solution.py:55
  98.8 1.4 %collective-permute-done.23.far = bf16[128,512]{1,0:T(8,128)(2,1)S(1)} collective-permute-done((bf16[128,512]{1,0:T(8,128)(2,1)S(1)}, bf16[128,512]{1,0:T(8,128)(2,1)S(1)}, u32[]{:S(2)}, u32[]{:S(2)}) %collective-permute-start.23) | collective-permute-done | bytes 131104 | tf_op jit(solution)/shard_map/ppermute | solution.py:55
  (53 shorter events, 23.1 us)
Async XLA Ops:
  2.4 12.9 %collective-permute-start.8 = (bf16[144,512]{1,0:T(8,128)(2,1)S(1)}, bf16[144,512]{1,0:T(8,128)(2,1)S(1)}, u32[]{:S(2)}, u32[]{:S(2)}) collective-permute-start(bf16[144,512]{1,0:T(8,128)(2,1)S(1)} %fusion.own), channel_id=1, source_target_pairs={{1,8},{3,10},{5,12},{7,14},{8,1},{10,3},{12,5},{14,7},{17,24},{19,... | collective-permute-start | bytes 442376 | tf_op jit(solution)/shard_map/ppermute | solution.py:55
  7.3 8.0 %collective-permute-start.7 = (bf16[128,512]{1,0:T(8,128)(2,1)}, bf16[128,512]{1,0:T(8,128)(2,1)S(1)}, u32[]{:S(2)}, u32[]{:S(2)}) collective-permute-start(bf16[128,512]{1,0:T(8,128)(2,1)} %param.4), channel_id=1, source_target_pairs={{0,8},{1,0},{2,10},{3,2},{4,12},{5,4},{6,14},{7,6},{8,9},{9,1},{10... | collective-permute-start | bytes 393224 | tf_op jit(solution)/shard_map/ppermute | solution.py:55
  7.4 13.6 %collective-permute-start = (bf16[128,512]{1,0:T(8,128)(2,1)}, bf16[128,512]{1,0:T(8,128)(2,1)S(1)}, u32[]{:S(2)}, u32[]{:S(2)}) collective-permute-start(bf16[128,512]{1,0:T(8,128)(2,1)} %a.1), channel_id=1, source_target_pairs={{0,16},{8,24},{16,32},{24,40},{32,48},{40,56},{48,0},{56,8},{64,80... | collective-permute-start | bytes 393224 | tf_op jit(solution)/shard_map/ppermute | solution.py:35
  10.5 13.0 %collective-permute-start.2 = (bf16[128,512]{1,0:T(8,128)(2,1)}, bf16[128,512]{1,0:T(8,128)(2,1)S(1)}, u32[]{:S(2)}, u32[]{:S(2)}) collective-permute-start(bf16[128,512]{1,0:T(8,128)(2,1)} %a.1), channel_id=1, source_target_pairs={{0,48},{8,56},{16,0},{24,8},{32,16},{40,24},{48,32},{56,40},{64,11... | collective-permute-start | bytes 393224 | tf_op jit(solution)/shard_map/ppermute | solution.py:35
  14.3 9.3 %collective-permute-start.3 = (bf16[128,512]{1,0:T(8,128)(2,1)S(1)}, bf16[128,512]{1,0:T(8,128)(2,1)S(1)}, u32[]{:S(2)}, u32[]{:S(2)}) collective-permute-start(bf16[128,512]{1,0:T(8,128)(2,1)S(1)} %shard_map.67.p0), channel_id=1, source_target_pairs={{0,1},{1,0},{2,3},{3,2},{4,5},{5,4},{6,7},{7,6},{8,9},{9,8},{10,11... | collective-permute-start | bytes 393224 | tf_op jit(solution)/shard_map/ppermute | solution.py:45
  15.9 18.8 %collective-permute-start.9 = (bf16[144,1024]{1,0:T(8,128)(2,1)S(1)}, bf16[144,1024]{1,0:T(8,128)(2,1)S(1)}, u32[]{:S(2)}, u32[]{:S(2)}) collective-permute-start(bf16[144,1024]{1,0:T(8,128)(2,1)S(1)} %shard_map.68.q0), channel_id=1, source_target_pairs={{0,64},{8,72},{16,80},{24,88},{32,96},{40,104},{48,112},{56,120},{... | collective-permute-start | bytes 884744 | tf_op jit(solution)/shard_map/ppermute | solution.py:31
  17.2 17.5 %collective-permute-start.10 = (bf16[144,1024]{1,0:T(8,128)(2,1)S(1)}, bf16[144,1024]{1,0:T(8,128)(2,1)S(1)}, u32[]{:S(2)}, u32[]{:S(2)}) collective-permute-start(bf16[144,1024]{1,0:T(8,128)(2,1)S(1)} %shard_map.68.q0), channel_id=1, source_target_pairs={{0,128},{8,136},{16,144},{24,152},{32,160},{40,168},{48,176},{56,1... | collective-permute-start | bytes 884744 | tf_op jit(solution)/shard_map/ppermute | solution.py:31
  21.0 13.6 %collective-permute-start.11 = (bf16[144,1024]{1,0:T(8,128)(2,1)S(1)}, bf16[144,1024]{1,0:T(8,128)(2,1)S(1)}, u32[]{:S(2)}, u32[]{:S(2)}) collective-permute-start(bf16[144,1024]{1,0:T(8,128)(2,1)S(1)} %shard_map.68.q0), channel_id=1, source_target_pairs={{0,192},{8,200},{16,208},{24,216},{32,224},{40,232},{48,240},{56,2... | collective-permute-start | bytes 884744 | tf_op jit(solution)/shard_map/ppermute | solution.py:31
  23.5 7.6 %collective-permute-start.1 = (bf16[128,512]{1,0:T(8,128)(2,1)S(1)}, bf16[128,512]{1,0:T(8,128)(2,1)S(1)}, u32[]{:S(2)}, u32[]{:S(2)}) collective-permute-start(bf16[128,512]{1,0:T(8,128)(2,1)S(1)} %collective-permute-done.p1), channel_id=1, source_target_pairs={{0,16},{8,24},{16,32},{24,40},{32,48},{40,56},{48,0},{56,8},{64,80... | collective-permute-start | bytes 393224 | tf_op jit(solution)/shard_map/ppermute | solution.py:35
  23.5 9.8 %collective-permute-start.4 = (bf16[128,512]{1,0:T(8,128)(2,1)S(1)}, bf16[128,512]{1,0:T(8,128)(2,1)S(1)}, u32[]{:S(2)}, u32[]{:S(2)}) collective-permute-start(bf16[128,512]{1,0:T(8,128)(2,1)S(1)} %collective-permute-done.p1), channel_id=1, source_target_pairs={{0,1},{1,0},{2,3},{3,2},{4,5},{5,4},{6,7},{7,6},{8,9},{9,8},{10,11... | collective-permute-start | bytes 393224 | tf_op jit(solution)/shard_map/ppermute | solution.py:45
  36.3 9.4 %collective-permute-start.12 = (f32[512,128]{1,0:T(8,128)S(1)}, f32[512,128]{1,0:T(8,128)S(1)}, u32[]{:S(2)}, u32[]{:S(2)}) collective-permute-start(f32[512,128]{1,0:T(8,128)S(1)} %get-tuple-element.42), channel_id=1, source_target_pairs={{0,2},{1,3},{2,4},{3,5},{4,6},{5,7},{6,0},{7,1},{8,10},{9,11},{10,... | collective-permute-start | bytes 786440 | tf_op jit(solution)/shard_map/ppermute | solution.py:41
  37.7 14.5 %collective-permute-start.13 = (f32[512,128]{1,0:T(8,128)S(1)}, f32[512,128]{1,0:T(8,128)S(1)}, u32[]{:S(2)}, u32[]{:S(2)}) collective-permute-start(f32[512,128]{1,0:T(8,128)S(1)} %get-tuple-element.43), channel_id=1, source_target_pairs={{0,4},{1,5},{2,6},{3,7},{4,0},{5,1},{6,2},{7,3},{8,12},{9,13},{10,... | collective-permute-start | bytes 786440 | tf_op jit(solution)/shard_map/ppermute | solution.py:41
  40.3 11.9 %collective-permute-start.14 = (f32[512,128]{1,0:T(8,128)S(1)}, f32[512,128]{1,0:T(8,128)S(1)}, u32[]{:S(2)}, u32[]{:S(2)}) collective-permute-start(f32[512,128]{1,0:T(8,128)S(1)} %get-tuple-element.44), channel_id=1, source_target_pairs={{0,6},{1,7},{2,0},{3,1},{4,2},{5,3},{6,4},{7,5},{8,14},{9,15},{10,... | collective-permute-start | bytes 786440 | tf_op jit(solution)/shard_map/ppermute | solution.py:41
  62.6 7.5 %collective-permute-start.15 = (bf16[528,128]{1,0:T(8,128)(2,1)S(1)}, bf16[528,128]{1,0:T(8,128)(2,1)S(1)}, u32[]{:S(2)}, u32[]{:S(2)}) collective-permute-start(bf16[528,128]{1,0:T(8,128)(2,1)S(1)} %get-tuple-element.54), channel_id=1, source_target_pairs={{0,2},{1,3},{2,4},{3,5},{4,6},{5,7},{6,0},{7,1},{8,10},{9,11},{10,... | collective-permute-start | bytes 405512 | tf_op jit(solution)/shard_map/ppermute | solution.py:41
  63.4 7.2 %collective-permute-start.16 = (bf16[528,128]{1,0:T(8,128)(2,1)S(1)}, bf16[528,128]{1,0:T(8,128)(2,1)S(1)}, u32[]{:S(2)}, u32[]{:S(2)}) collective-permute-start(bf16[528,128]{1,0:T(8,128)(2,1)S(1)} %get-tuple-element.55), channel_id=1, source_target_pairs={{0,4},{1,5},{2,6},{3,7},{4,0},{5,1},{6,2},{7,3},{8,12},{9,13},{10,... | collective-permute-start | bytes 405512 | tf_op jit(solution)/shard_map/ppermute | solution.py:41
  73.0 5.2 %collective-permute-start.21 = (bf16[528,512]{1,0:T(8,128)(2,1)S(1)}, bf16[528,512]{1,0:T(8,128)(2,1)S(1)}, u32[]{:S(2)}, u32[]{:S(2)}) collective-permute-start(bf16[528,512]{1,0:T(8,128)(2,1)S(1)} %get-tuple-element.67), channel_id=1, source_target_pairs={{0,1},{1,0},{2,3},{3,2},{4,5},{5,4},{6,7},{7,6},{8,9},{9,8},{10,11... | collective-permute-start | bytes 1622024 | tf_op jit(solution)/shard_map/ppermute | solution.py:45
  76.2 7.9 %collective-permute-start.18 = (bf16[128,1024]{1,0:T(8,128)(2,1)S(1)}, bf16[128,1024]{1,0:T(8,128)(2,1)S(1)}, u32[]{:S(2)}, u32[]{:S(2)}) collective-permute-start(bf16[128,1024]{1,0:T(8,128)(2,1)S(1)} %get-tuple-element.62), channel_id=1, source_target_pairs={{0,192},{8,200},{16,208},{24,216},{32,224},{40,232},{48,240},{56,2... | collective-permute-start | bytes 786440 | tf_op jit(solution)/shard_map/ppermute | solution.py:31
  76.9 9.1 %collective-permute-start.19 = (bf16[128,1024]{1,0:T(8,128)(2,1)S(1)}, bf16[128,1024]{1,0:T(8,128)(2,1)S(1)}, u32[]{:S(2)}, u32[]{:S(2)}) collective-permute-start(bf16[128,1024]{1,0:T(8,128)(2,1)S(1)} %get-tuple-element.63), channel_id=1, source_target_pairs={{0,128},{8,136},{16,144},{24,152},{32,160},{40,168},{48,176},{56,1... | collective-permute-start | bytes 786440 | tf_op jit(solution)/shard_map/ppermute | solution.py:31
  78.1 14.2 %collective-permute-start.20 = (bf16[128,1024]{1,0:T(8,128)(2,1)S(1)}, bf16[128,1024]{1,0:T(8,128)(2,1)S(1)}, u32[]{:S(2)}, u32[]{:S(2)}) collective-permute-start(bf16[128,1024]{1,0:T(8,128)(2,1)S(1)} %get-tuple-element.64), channel_id=1, source_target_pairs={{0,64},{8,72},{16,80},{24,88},{32,96},{40,104},{48,112},{56,120},{... | collective-permute-start | bytes 786440 | tf_op jit(solution)/shard_map/ppermute | solution.py:31
  78.8 21.4 %collective-permute-start.24 = (bf16[144,512]{1,0:T(8,128)(2,1)S(1)}, bf16[144,512]{1,0:T(8,128)(2,1)S(1)}, u32[]{:S(2)}, u32[]{:S(2)}) collective-permute-start(bf16[144,512]{1,0:T(8,128)(2,1)S(1)} %get-tuple-element.68.m1), channel_id=1, source_target_pairs={{0,48},{8,56},{16,0},{24,8},{32,16},{40,24},{48,32},{56,40},{64,11... | collective-permute-start | bytes 442376 | tf_op jit(solution)/shard_map/ppermute | solution.py:35
  80.4 19.8 %collective-permute-start.25 = (bf16[144,512]{1,0:T(8,128)(2,1)S(1)}, bf16[144,512]{1,0:T(8,128)(2,1)S(1)}, u32[]{:S(2)}, u32[]{:S(2)}) collective-permute-start(bf16[144,512]{1,0:T(8,128)(2,1)S(1)} %get-tuple-element.69.m2), channel_id=1, source_target_pairs={{0,32},{8,40},{16,48},{24,56},{32,0},{40,8},{48,16},{56,24},{64,96... | collective-permute-start | bytes 442376 | tf_op jit(solution)/shard_map/ppermute | solution.py:35
  84.1 16.1 %collective-permute-start.26 = (bf16[144,512]{1,0:T(8,128)(2,1)S(1)}, bf16[144,512]{1,0:T(8,128)(2,1)S(1)}, u32[]{:S(2)}, u32[]{:S(2)}) collective-permute-start(bf16[144,512]{1,0:T(8,128)(2,1)S(1)} %get-tuple-element.70.m3), channel_id=1, source_target_pairs={{0,16},{8,24},{16,32},{24,40},{32,48},{40,56},{48,0},{56,8},{64,80... | collective-permute-start | bytes 442376 | tf_op jit(solution)/shard_map/ppermute | solution.py:35
  93.0 5.8 %collective-permute-start.22 = (bf16[128,512]{1,0:T(8,128)(2,1)S(1)}, bf16[128,512]{1,0:T(8,128)(2,1)S(1)}, u32[]{:S(2)}, u32[]{:S(2)}) collective-permute-start(bf16[128,512]{1,0:T(8,128)(2,1)S(1)} %get-tuple-element.72), channel_id=1, source_target_pairs={{0,1},{1,9},{2,3},{3,11},{4,5},{5,13},{6,7},{7,15},{8,0},{9,8},{10... | collective-permute-start | bytes 393224 | tf_op jit(solution)/shard_map/ppermute | solution.py:55
  93.8 6.3 %collective-permute-start.23 = (bf16[128,512]{1,0:T(8,128)(2,1)S(1)}, bf16[128,512]{1,0:T(8,128)(2,1)S(1)}, u32[]{:S(2)}, u32[]{:S(2)}) collective-permute-start(bf16[128,512]{1,0:T(8,128)(2,1)S(1)} %get-tuple-element.73), channel_id=1, source_target_pairs={{1,8},{3,10},{5,12},{7,14},{8,1},{10,3},{12,5},{14,7},{17,24},{19,... | collective-permute-start | bytes 393224 | tf_op jit(solution)/shard_map/ppermute | solution.py:55
  (6 other events, 76.5 us)
